TPU v7x, 256 devices: a whole 4x4x8 slice. The times are simulated.
256 devices in a mesh: slab: 64 (over y_lo, z, x), freq: 4 (over y_hi, core).
Axes of the slice: x: 4, y: 4 (y_hi: 2, y_lo: 2; y = y_hi * 2 + y_lo), z: 8, core: 2. Of those that a mesh axis runs over, the one named last changes fastest.
Arguments:
- source_field: bfloat16 [2, 8, 2048, 16, 256], P(None, 'freq', 'slab'), may hold values from -6 to 6
- receiver_field: bfloat16 [2, 8, 2048, 16, 256], P(None, 'freq', 'slab'), may hold values from -6 to 6
Outputs:
- extended: float32 [16, 65, 2048, 256], P('freq', None, 'slab')
All inputs are finite; a program needn't handle non-finite values.
Results may differ from a plain program's by a relative error of at most 0.0003.
Values may be sent and summed in bfloat16 or wider, within the bound.
No kernel may reach another device: no remote copies, remote signals or barrier semaphores. Data moves between devices by JAX's collectives and lax.ppermute only.
A program may use at most 128 MiB of HBM per device.

v0:
```python
import jax
import jax.numpy as jnp
from jax import lax
from jax.sharding import PartitionSpec as P

HMAX = 32


def extended(block, sides, width):
    for axis, dim in sides:
        count = lax.axis_size(axis)
        forward = [(i, i + 1) for i in range(count - 1)]
        backward = [(target, source) for source, target in forward]
        low = lax.ppermute(
            lax.slice_in_dim(block, block.shape[dim] - width, None, axis=dim), axis, forward
        )
        high = lax.ppermute(lax.slice_in_dim(block, 0, width, axis=dim), axis, backward)
        block = jnp.concatenate([low, block, high], axis=dim)
    return block


def with_rims(both_fields):
    return extended(both_fields, (("slab", 3),), HMAX)


def to_columns(both_fields):
    return lax.all_to_all(both_fields, "freq", split_axis=4, concat_axis=2, tiled=True)


def local_image(padded):
    slab_cells = padded.shape[3] - 2 * HMAX
    reordered = jnp.transpose(padded, (0, 1, 2, 4, 3, 5))
    source_block = reordered[0]
    receiver_block = reordered[1]
    pictures = []
    for offset_index in range(2 * HMAX + 1):
        source_start = 2 * HMAX - offset_index
        source_window = source_block[:, :, :, source_start : source_start + slab_cells, :]
        receiver_window = receiver_block[:, :, :, offset_index : offset_index + slab_cells, :]
        product = source_window.astype(jnp.float32) * receiver_window.astype(jnp.float32)
        pictures.append(0.25 * jnp.sum(product, axis=(0, 1)))
    return jnp.stack(pictures, axis=1)


def body(source_field, receiver_field):
    both_fields = jnp.stack([source_field, receiver_field])
    padded = with_rims(to_columns(both_fields))
    return local_image(padded)


def solution(mesh):
    in_specs = (P(None, "freq", "slab", None, None), P(None, "freq", "slab", None, None))
    out_specs = P("freq", None, "slab", None)
    return jax.shard_map(body, mesh=mesh, in_specs=in_specs, out_specs=out_specs, check_vma=False)
```

profile of v0, /device:TPU:8, one launch (start us, length us, event | category | flops | bytes accessed | tf_op | source)
XLA Modules:
  0.0 130.9 jit_solution(10341574554103837699)
XLA Ops:
  0.0 2.3 %copy_bitcast_fusion = (bf16[1,2,2,32,16,256]{5,3,2,1,0,4:T(8,128)(2,1)S(1)}, bf16[1,2,2,32,16,256]{5,3,2,1,0,4:T(8,128)(2,1)S(1)}) fusion(bf16[2,2,32,16,256]{4,3,2,1,0:T(8,128)(2,1)} %param.3, bf16[2,2,32,16,256]{4,3,2,1,0:T(8,128)(2,1)} %param.2), kind=kLoop, calls=%fused_computation.69 | loop fusion | bytes 4194304 | tf_op jit(solution)/shard_map/stack | solution.py:46
  2.3 0.2 pad_maximum_fusion
  2.5 30.6 %all_to_all.18 = bf16[2,2,2,32,16,256]{5,3,2,1,0,4:T(8,128)(2,1)S(1)} all-to-all(bf16[2,2,2,32,16,256]{5,3,2,1,0,4:T(8,128)(2,1)S(1)} %pad_maximum_fusion), channel_id=1, replica_groups=mesh['slab'=64,'freq'=4] {'freq'}, dimensions={4} | all-to-all | bytes 4194304 | tf_op jit(solution)/shard_map/all_to_all | solution.py:27
  33.0 0.2 copy.201
  33.3 3.4 %collective-permute-start = (bf16[2,2,8,32,4,256]{5,3,4,2,1,0:T(8,128)(2,1)S(1)}, bf16[2,2,8,32,4,256]{5,3,4,2,1,0:T(8,128)(2,1)S(1)}, u32[]{:S(2)}, u32[]{:S(2)}) collective-permute-start(bf16[2,2,8,32,4,256]{5,3,4,2,1,0:T(8,128)(2,1)S(1)} %bitcast.273), channel_id=1, source_target_pairs={{0,4},{4,8},{8,12},{12,16},{16,20},{20,24},{24,28},{28,32},{32,36}... | collective-permute-start | bytes 6291464 | tf_op jit(solution)/shard_map/ppermute | solution.py:14
  36.7 9.3 %collective-permute-start.1 = (bf16[2,2,8,32,4,256]{5,3,4,2,1,0:T(8,128)(2,1)S(1)}, bf16[2,2,8,32,4,256]{5,3,4,2,1,0:T(8,128)(2,1)S(1)}, u32[]{:S(2)}, u32[]{:S(2)}) collective-permute-start(bf16[2,2,8,32,4,256]{5,3,4,2,1,0:T(8,128)(2,1)S(1)} %bitcast.274), channel_id=1, source_target_pairs={{4,0},{8,4},{12,8},{16,12},{20,16},{24,20},{28,24},{32,28},{36,32}... | collective-permute-start | bytes 6291464 | tf_op jit(solution)/shard_map/ppermute | solution.py:17
  46.0 43.3 %collective-permute-done = bf16[2,2,8,32,4,256]{5,3,4,2,1,0:T(8,128)(2,1)S(1)} collective-permute-done((bf16[2,2,8,32,4,256]{5,3,4,2,1,0:T(8,128)(2,1)S(1)}, bf16[2,2,8,32,4,256]{5,3,4,2,1,0:T(8,128)(2,1)S(1)}, u32[]{:S(2)}, u32[]{:S(2)}) %collective-permute-start) | collective-permute-done | bytes 2097184 | tf_op jit(solution)/shard_map/ppermute | solution.py:14
  89.3 1.2 collective-permute-done.1
  90.5 5.1 %maximum_bitcast_fusion = bf16[2,2,8,4,96,256]{5,4,3,2,1,0:T(8,128)(2,1)S(1)} fusion(bf16[2,2,8,32,4,256]{5,3,4,2,1,0:T(8,128)(2,1)S(1)} %collective-permute-done.1, bf16[2,2,8,32,4,256]{5,3,4,2,1,0:T(8,128)(2,1)S(1)} %bitcast.275, bf16[2,2,8,32,4,256]{5,3,4,2,1,0:T(8,128)(2,1)S(1)} %collective-permute-done), kind=kLoop, calls=%fused_computation | loop fusion | flops 18874368 | bytes 12582912 | tf_op jit(solution)/shard_map/transpose | solution.py:32
  95.5 0.7 slice_bitcast_fusion.1
  96.3 1.1 multiply_reduce_fusion.63
  97.3 4.1 %multiply_reduce_fusion.54 = (f32[4,32,256]{2,1,0:T(8,128)S(1)}, f32[4,32,256]{2,1,0:T(8,128)S(1)}, f32[4,32,256]{2,1,0:T(8,128)S(1)}, f32[4,32,256]{2,1,0:T(8,1...) fusion(bf16[2,8,4,96,256]{4,3,2,1,0:T(8,128)(2,1)S(1)} %get-tup, ...), kind=kLoop, calls=%fused_computation.58 | loop fusion | flops 18579456 | bytes 20054016 | tf_op jit(solution)/shard_map/reduce_sum | solution.py:41
  101.4 4.0 %multiply_reduce_fusion.45 = (f32[4,32,256]{2,1,0:T(8,128)S(1)}, f32[4,32,256]{2,1,0:T(8,128)S(1)}, f32[4,32,256]{2,1,0:T(8,128)S(1)}, f32[4,32,256]{2,1,0:T(8,1...) fusion(bf16[2,8,4,96,256]{4,3,2,1,0:T(8,128)(2,1)S(1)} %get-tup, ...), kind=kLoop, calls=%fused_computation.49 | loop fusion | flops 18579456 | bytes 20054016 | tf_op jit(solution)/shard_map/reduce_sum | solution.py:41
  105.4 4.0 %multiply_reduce_fusion.36 = (f32[4,32,256]{2,1,0:T(8,128)S(1)}, f32[4,32,256]{2,1,0:T(8,128)S(1)}, f32[4,32,256]{2,1,0:T(8,128)S(1)}, f32[4,32,256]{2,1,0:T(8,1...) fusion(bf16[2,8,4,96,256]{4,3,2,1,0:T(8,128)(2,1)S(1)} %get-tup, ...), kind=kLoop, calls=%fused_computation.40 | loop fusion | flops 18579456 | bytes 20054016 | tf_op jit(solution)/shard_map/reduce_sum | solution.py:41
  109.5 4.0 %multiply_reduce_fusion.27 = (f32[4,32,256]{2,1,0:T(8,128)S(1)}, f32[4,32,256]{2,1,0:T(8,128)S(1)}, f32[4,32,256]{2,1,0:T(8,128)S(1)}, f32[4,32,256]{2,1,0:T(8,1...) fusion(bf16[2,8,4,96,256]{4,3,2,1,0:T(8,128)(2,1)S(1)} %get-tup, ...), kind=kLoop, calls=%fused_computation.31 | loop fusion | flops 18579456 | bytes 20054016 | tf_op jit(solution)/shard_map/reduce_sum | solution.py:41
  113.5 4.1 %multiply_reduce_fusion.18 = (f32[4,32,256]{2,1,0:T(8,128)S(1)}, f32[4,32,256]{2,1,0:T(8,128)S(1)}, f32[4,32,256]{2,1,0:T(8,128)S(1)}, f32[4,32,256]{2,1,0:T(8,1...) fusion(bf16[2,8,4,96,256]{4,3,2,1,0:T(8,128)(2,1)S(1)} %get-tup, ...), kind=kLoop, calls=%fused_computation.22 | loop fusion | flops 18579456 | bytes 20054016 | tf_op jit(solution)/shard_map/reduce_sum | solution.py:41
  117.6 4.2 %multiply_reduce_fusion.9 = (f32[4,32,256]{2,1,0:T(8,128)S(1)}, f32[4,32,256]{2,1,0:T(8,128)S(1)}, f32[4,32,256]{2,1,0:T(8,128)S(1)}, f32[4,32,256]{2,1,0:T(8,12...) fusion(bf16[2,8,4,96,256]{4,3,2,1,0:T(8,128)(2,1)S(1)} %get-tup, ...), kind=kLoop, calls=%fused_computation.13 | loop fusion | flops 18579456 | bytes 20054016 | tf_op jit(solution)/shard_map/reduce_sum | solution.py:41
  121.8 3.7 %multiply_reduce_fusion = (f32[4,32,256]{2,1,0:T(8,128)S(1)}, f32[4,32,256]{2,1,0:T(8,128)S(1)}, f32[4,32,256]{2,1,0:T(8,128)S(1)}, f32[4,32,256]{2,1,0:T(8,128)...) fusion(bf16[2,8,4,96,256]{4,3,2,1,0:T(8,128)(2,1)S(1)} %get-tup, ...), kind=kLoop, calls=%fused_computation.4 | loop fusion | flops 18579456 | bytes 20054016 | tf_op jit(solution)/shard_map/reduce_sum | solution.py:41
  126.8 0.0 copy-start
  126.8 3.4 %copy-done = f32[4,65,32,256]{3,2,1,0:T(8,128)} copy-done((f32[4,65,32,256]{3,2,1,0:T(8,128)}, f32[4,65,32,256]{3,2,1,0:T(8,128)S(1)}, u32[]{:S(2)}) %copy-start) | copy-done | bytes 8519704
  130.2 0.7 constant_dynamic-update-slice_fusion
  (64 shorter events, 0.8 us)
Async XLA Ops:
  33.3 56.0 %collective-permute-start = (bf16[2,2,8,32,4,256]{5,3,4,2,1,0:T(8,128)(2,1)S(1)}, bf16[2,2,8,32,4,256]{5,3,4,2,1,0:T(8,128)(2,1)S(1)}, u32[]{:S(2)}, u32[]{:S(2)}) collective-permute-start(bf16[2,2,8,32,4,256]{5,3,4,2,1,0:T(8,128)(2,1)S(1)} %bitcast.273), channel_id=1, source_target_pairs={{0,4},{4,8},{8,12},{12,16},{16,20},{20,24},{24,28},{28,32},{32,36}... | collective-permute-start | bytes 6291464 | tf_op jit(solution)/shard_map/ppermute | solution.py:14
  36.7 53.8 %collective-permute-start.1 = (bf16[2,2,8,32,4,256]{5,3,4,2,1,0:T(8,128)(2,1)S(1)}, bf16[2,2,8,32,4,256]{5,3,4,2,1,0:T(8,128)(2,1)S(1)}, u32[]{:S(2)}, u32[]{:S(2)}) collective-permute-start(bf16[2,2,8,32,4,256]{5,3,4,2,1,0:T(8,128)(2,1)S(1)} %bitcast.274), channel_id=1, source_target_pairs={{4,0},{8,4},{12,8},{16,12},{20,16},{24,20},{28,24},{32,28},{36,32}... | collective-permute-start | bytes 6291464 | tf_op jit(solution)/shard_map/ppermute | solution.py:17
  126.8 3.4 %copy-start = (f32[4,65,32,256]{3,2,1,0:T(8,128)}, f32[4,65,32,256]{3,2,1,0:T(8,128)S(1)}, u32[]{:S(2)}) copy-start(f32[4,65,32,256]{3,2,1,0:T(8,128)S(1)} %constant_dynamic-update-slice_fusion.1) | copy-start | bytes 25559044
where the time goes:
time: 132 us; the launch traced here: 131 us
  waiting for transfers between devices  44.5 us (34%)
  other arithmetic  35.9 us (27%)
  blocking collectives  30.6 us (23%)
  starting transfers between devices  12.7 us (10%)
  local copies, waits for them, and re-layouts  6.64 us (5%)
    ppermute x1, waiting for transfers between devices, extended(): lax.ppermute(lax.slice_in_dim(block, block.shape[dim] - width, None, axis...  43.3 us
    all_to_all x1, blocking collectives, to_columns(): lax.all_to_all(both_fields, 'freq', split_axis=4, concat_axis=2, tiled=True)  30.6 us
    reduce_sum x8, other arithmetic, local_image(): pictures.append(0.25 * jnp.sum(product, axis=(0, 1)))  29.2 us
    ppermute x1, starting transfers between devices, extended(): lax.ppermute(lax.slice_in_dim(block, 0, width, axis=dim), axis, backward)  9.27 us
    transpose x1, other arithmetic, local_image(): reordered = jnp.transpose(padded, (0, 1, 2, 4, 3, 5))  5.06 us
    unnamed x2, local copies, waits for them, and re-layouts  3.43 us
    ppermute x1, starting transfers between devices, extended(): lax.ppermute(lax.slice_in_dim(block, block.shape[dim] - width, None, axis...  3.4 us
  transfers between devices with their start and end apart: 2, of which 2 were waited for; matrix products, arithmetic and copies ran while one was open for 0% of the time, Pallas kernels for 0%

commit v1 on v0

v1 whole, which is shorter than its diff:
```python
import functools

import jax
import jax.numpy as jnp
from jax import lax
from jax.experimental import pallas as pl
from jax.experimental.pallas import tpu as pltpu
from jax.sharding import PartitionSpec as P

HMAX = 32
GROUPS = 4
ROWS = 16
LANES = 128


def regroup_kernel(group_ref, source_ref, receiver_ref, *out_refs):
    freqs, cells = source_ref.shape[1], source_ref.shape[2]

    def regroup(order):
        for field, ref in enumerate((source_ref, receiver_ref)):
            for f in range(freqs):

                def one_cell(x, _):
                    halves = [
                        [ref[c, f, x, :, zh * LANES : (zh + 1) * LANES].astype(jnp.float32) for zh in range(2)]
                        for c in range(2)
                    ]
                    for d in range(GROUPS):
                        q = order ^ d
                        rows = [halves[c][zh][4 * q : 4 * q + 4] for c in range(2) for zh in range(2)]
                        out_refs[d][field, f, x] = jnp.concatenate(rows, axis=0).astype(jnp.bfloat16)
                    return 0

                lax.fori_loop(0, cells, one_cell, 0, unroll=4)

    for order in range(GROUPS):
        pl.when(group_ref[0] == order)(functools.partial(regroup, order))


def regrouped(group, source_field, receiver_field):
    two, freqs, cells, _, _ = source_field.shape
    steps = 4
    spec_in = pl.BlockSpec((2, freqs, cells // steps, 16, 256), lambda i: (0, 0, i, 0, 0))
    spec_out = pl.BlockSpec((2, freqs, cells // steps, ROWS, LANES), lambda i: (0, 0, i, 0, 0))
    return pl.pallas_call(
        regroup_kernel,
        grid=(steps,),
        in_specs=[pl.BlockSpec(memory_space=pltpu.SMEM), spec_in, spec_in],
        out_specs=[spec_out] * GROUPS,
        out_shape=[jax.ShapeDtypeStruct((2, freqs, cells, ROWS, LANES), jnp.bfloat16)] * GROUPS,
        cost_estimate=pl.CostEstimate(flops=0, bytes_accessed=4 << 20, transcendentals=0),
    )(group, source_field, receiver_field)


TX = 8
TH = 5


def image_kernel(edge_ref, *refs):
    blocks = refs[: 3 * GROUPS]
    out_ref = refs[3 * GROUPS]
    raw, fields, turn, stage, in_sems, out_sems = refs[3 * GROUPS + 1 :]
    cells = blocks[0].shape[2]
    freqs = blocks[0].shape[1]
    copies = []
    for d in range(GROUPS):
        for k in range(3):
            copies.append(
                pltpu.make_async_copy(
                    blocks[3 * d + k],
                    raw.at[:, pl.ds(freqs * d, freqs), pl.ds(cells * k, cells)],
                    in_sems.at[3 * d + k],
                )
            )
    for copy in copies:
        copy.start()
    for copy in copies:
        copy.wait()

    for side in range(2):

        @pl.when(edge_ref[side] == 0)
        def _():
            raw[:, :, pl.ds(2 * cells * side, cells)] = jnp.zeros(
                (2, freqs * GROUPS, cells, ROWS, LANES), jnp.bfloat16
            )

    def widen(p, _):
        for field in range(2):
            for f in range(freqs * GROUPS):
                fields[field, p, f] = raw[field, f, p].astype(jnp.float32)
        return 0

    lax.fori_loop(0, 3 * cells, widen, 0)

    def first_offset(step):
        return jnp.minimum(TH * step, 2 * HMAX + 1 - TH)

    steps = -(-(2 * HMAX + 1) // TH)

    def out_copy(step, slot):
        return pltpu.make_async_copy(stage.at[slot], out_ref.at[:, pl.ds(first_offset(step), TH)], out_sems.at[slot])

    def h_step(step, _):
        slot = lax.rem(step, 2)
        k0 = first_offset(step)

        @pl.when(step >= 2)
        def _():
            out_copy(step - 2, slot).wait()

        def x_step(xt, _):
            x0 = xt * TX
            s0 = x0 + 2 * HMAX - k0 - (TH - 1)
            r0 = x0 + k0
            total = [[None] * TX for _ in range(TH)]
            for f in range(freqs * GROUPS):
                for c in range(2):
                    s = [fields[0, s0 + i, f, 8 * c : 8 * c + 8] for i in range(TX + TH - 1)]
                    r = [fields[1, r0 + i, f, 8 * c : 8 * c + 8] for i in range(TX + TH - 1)]
                    for j in range(TH):
                        for i in range(TX):
                            product = s[i + TH - 1 - j] * r[i + j]
                            total[j][i] = product if total[j][i] is None else total[j][i] + product
            for j in range(TH):
                for i in range(TX):
                    turn[j, pl.ds(i, 8, stride=TX)] = 0.25 * total[j][i]
                for zh in range(2):
                    for y in range(4):
                        row = zh * 4 + y
                        stage[slot, y, j, pl.ds(pl.multiple_of(x0, TX), TX), zh * LANES : (zh + 1) * LANES] = turn[
                            j, row * TX : (row + 1) * TX
                        ]
            return 0

        lax.fori_loop(0, cells // TX, x_step, 0)
        out_copy(step, slot).start()
        return 0

    lax.fori_loop(0, steps, h_step, 0)
    for step in (steps - 2, steps - 1):
        out_copy(step, step % 2).wait()


def image(edge, blocks):
    two, freqs, cells, _, _ = blocks[0].shape
    total_freqs = freqs * GROUPS
    return pl.pallas_call(
        image_kernel,
        in_specs=[pl.BlockSpec(memory_space=pltpu.SMEM)] + [pl.BlockSpec(memory_space=pl.ANY)] * (3 * GROUPS),
        out_specs=pl.BlockSpec(memory_space=pl.ANY),
        out_shape=jax.ShapeDtypeStruct((4, 2 * HMAX + 1, cells, 256), jnp.float32),
        scratch_shapes=[
            pltpu.VMEM((2, total_freqs, 3 * cells, ROWS, LANES), jnp.bfloat16),
            pltpu.VMEM((2, 3 * cells, total_freqs, ROWS, LANES), jnp.float32),
            pltpu.VMEM((TH, 8 * TX, LANES), jnp.float32),
            pltpu.VMEM((2, 4, TH, cells, 256), jnp.float32),
            pltpu.SemaphoreType.DMA((3 * GROUPS,)),
            pltpu.SemaphoreType.DMA((2,)),
        ],
        compiler_params=pltpu.CompilerParams(vmem_limit_bytes=40 << 20),
        cost_estimate=pl.CostEstimate(flops=70_000_000, bytes_accessed=15 << 20, transcendentals=0),
    )(edge, *blocks)


def body(source_field, receiver_field):
    slabs = lax.axis_size("slab")
    forward = [(i, (i + 1) % slabs) for i in range(slabs)]
    backward = [(target, source) for source, target in forward]
    group = lax.axis_index("freq").astype(jnp.int32)
    slab = lax.axis_index("slab")
    edge = jnp.stack([slab > 0, slab < slabs - 1]).astype(jnp.int32)
    parts = regrouped(group[None], source_field, receiver_field)
    blocks = []
    for d in range(GROUPS):
        own = parts[d]
        if d:
            own = lax.ppermute(own, "freq", [(g, g ^ d) for g in range(GROUPS)])
        blocks += [lax.ppermute(own, "slab", forward), own, lax.ppermute(own, "slab", backward)]
    return image(edge, blocks)


def solution(mesh):
    in_specs = (P(None, "freq", "slab", None, None), P(None, "freq", "slab", None, None))
    out_specs = P("freq", None, "slab", None)
    return jax.shard_map(body, mesh=mesh, in_specs=in_specs, out_specs=out_specs, check_vma=False)
```

time: 132 us -> 112 us (0.85)
  other arithmetic: 35.9 us -> 0.07 us
  starting transfers between devices: 12.7 us -> 43.4 us
  blocking collectives: 30.6 us -> 0 us
  Pallas kernels: 0 us -> 22.9 us
  local copies, waits for them, and re-layouts: 6.64 us -> 1.04 us
  waiting for transfers between devices: 44.5 us -> 43.1 us
    ppermute x2 -> x11, starting transfers between devices: 12.7 us -> 43.4 us  [the longest x4 39.6 us: body(): lax.ppermute(own, 'slab', backward)]
    all_to_all x1 -> x0, blocking collectives: 30.6 us -> none  [to_columns(): lax.all_to_all(both_fields, 'freq', split_axis=4, concat_axis=2, tiled=True)]
    reduce_sum x8 -> x0, other arithmetic: 29.2 us -> none  [local_image(): pictures.append(0.25 * jnp.sum(product, axis=(0, 1)))]
    pallas_call x0 -> x2, Pallas kernels: none -> 22.9 us  [the longest x1 18.8 us: image(): pl.pallas_call(image_kernel, in_specs=[pl.BlockSpec(memory_space=pltpu.SM...]
    transpose x1 -> x0, other arithmetic: 5.06 us -> none  [local_image(): reordered = jnp.transpose(padded, (0, 1, 2, 4, 3, 5))]
    unnamed x2, local copies, waits for them, and re-layouts: 3.43 us -> 1.04 us
    another operation x1 -> x0, local copies, waits for them, and re-layouts: 2.26 us -> none  [body(): both_fields = jnp.stack([source_field, receiver_field])]
    ppermute x2 -> x11, waiting for transfers between devices: 44.5 us -> 43.1 us  [the longest x3 20.1 us: body(): own = lax.ppermute(own, 'freq', [(g, g ^ d) for g in range(GROUPS)])]
  transfers between devices with their start and end apart: 2 -> 11, of which waited for: 2 -> 5; matrix products, arithmetic and copies ran while one was open for 0% -> 0% of each run, Pallas kernels for 0% -> 0%
where the time goes in v1:
time: 112 us; the launch traced here: 111 us
  starting transfers between devices  43.4 us (39%)
  waiting for transfers between devices  43.1 us (38%)
  Pallas kernels  22.9 us (20%)
    ppermute x4, starting transfers between devices, body(): lax.ppermute(own, 'slab', backward)  39.6 us
    ppermute x3, waiting for transfers between devices, body(): own = lax.ppermute(own, 'freq', [(g, g ^ d) for g in range(GROUPS)])  20.1 us
    pallas_call x1, Pallas kernels, image(): pl.pallas_call(image_kernel, in_specs=[pl.BlockSpec(memory_space=pltpu.SM...  18.8 us
    ppermute x4, waiting for transfers between devices, body(): lax.ppermute(own, 'slab', forward)  13.4 us
    ppermute x4, waiting for transfers between devices, body(): lax.ppermute(own, 'slab', backward)  9.68 us
    pallas_call x1, Pallas kernels, regrouped(): pl.pallas_call(regroup_kernel, grid=(steps,), in_specs=[pl.BlockSpec(memo...  4.03 us
    ppermute x3, starting transfers between devices, body(): own = lax.ppermute(own, 'freq', [(g, g ^ d) for g in range(GROUPS)])  3.38 us
  transfers between devices with their start and end apart: 11, of which 5 were waited for; matrix products, arithmetic and copies ran while one was open for 0% of the time, Pallas kernels for 0%

profile of v1, /device:TPU:8, one launch (start us, length us, event | category | flops | bytes accessed | tf_op | source)
XLA Modules:
  0.0 110.6 jit_solution(7124795368945923836)
XLA Ops:
  0.0 4.0 %shard_map.28 = (bf16[2,2,32,16,128]{4,3,2,1,0:T(8,128)(2,1)}, bf16[2,2,32,16,128]{4,3,2,1,0:T(8,128)(2,1)}, bf16[2,2,32,16,128]{4,3,2,1,0:T(8,128)(2,1)}, bf16[2,2,32,16,128]{4,3,2,1,0:T(8,128)(2,1)}) custom-call(s32[1]{0:T(128)} %bitcast.2.group_ref, bf16[2,2,32,16,256]{4,3,2,1,0:T(8,128)(2,1)} %source_ref.1, bf16[2,2,32,16,256]{4,3,2,1,0:T(8,128)(2,1)} %receiver_ref.1), custom_call_target="tpu_custom_call" | custom-call | bytes 4194304 | tf_op jit(solution)/shard_map/pallas_call | solution.py:45
  4.0 0.0 collective-permute-start.2
  4.0 2.3 %collective-permute-start.5 = (bf16[2,2,32,16,128]{4,3,2,1,0:T(8,128)(2,1)}, bf16[2,2,32,16,128]{4,3,2,1,0:T(8,128)(2,1)S(1)}, u32[]{:S(2)}, u32[]{:S(2)}) collective-permute-start(bf16[2,2,32,16,128]{4,3,2,1,0:T(8,128)(2,1)} %get-tuple-element.11), channel_id=1, source_target_pairs={{0,2},{1,3},{2,0},{3,1},{4,6},{5,7},{6,4},{7,5},{8,10},{9,11},{10,... | collective-permute-start | bytes 1572872 | tf_op jit(solution)/shard_map/ppermute | solution.py:178
  6.4 1.0 collective-permute-start.8
  7.4 7.9 %collective-permute-start.1 = (bf16[2,2,32,16,128]{4,3,2,1,0:T(8,128)(2,1)}, bf16[2,2,32,16,128]{4,3,2,1,0:T(8,128)(2,1)S(1)}, u32[]{:S(2)}, u32[]{:S(2)}) collective-permute-start(bf16[2,2,32,16,128]{4,3,2,1,0:T(8,128)(2,1)} %get-tuple-element.9.refs_1_), channel_id=1, source_target_pairs={{4,0},{8,4},{12,8},{16,12},{20,16},{24,20},{28,24},{32,28},{36,32}... | collective-permute-start | bytes 1572872 | tf_op jit(solution)/shard_map/ppermute | solution.py:179
  15.4 0.0 collective-permute-start
  15.4 0.0 collective-permute-done.2.refs_4_
  15.4 6.2 %collective-permute-start.4 = (bf16[2,2,32,16,128]{4,3,2,1,0:T(8,128)(2,1)S(1)}, bf16[2,2,32,16,128]{4,3,2,1,0:T(8,128)(2,1)S(1)}, u32[]{:S(2)}, u32[]{:S(2)}) collective-permute-start(bf16[2,2,32,16,128]{4,3,2,1,0:T(8,128)(2,1)S(1)} %collective-permute-done.2.refs_4_), channel_id=1, source_target_pairs={{4,0},{8,4},{12,8},{16,12},{20,16},{24,20},{28,24},{32,28},{36,32}... | collective-permute-start | bytes 1572872 | tf_op jit(solution)/shard_map/ppermute | solution.py:179
  21.6 0.0 collective-permute-done.5.refs_7_
  21.6 0.4 collective-permute-start.3
  22.1 20.1 %collective-permute-done.8.refs_10_ = bf16[2,2,32,16,128]{4,3,2,1,0:T(8,128)(2,1)S(1)} collective-permute-done((bf16[2,2,32,16,128]{4,3,2,1,0:T(8,128)(2,1)}, bf16[2,2,32,16,128]{4,3,2,1,0:T(8,128)(2,1)S(1)}, u32[]{:S(2)}, u32[]{:S(2)}) %collective-permute-start.8) | collective-permute-done | bytes 524320 | tf_op jit(solution)/shard_map/ppermute | solution.py:178
  42.1 19.2 %collective-permute-start.7 = (bf16[2,2,32,16,128]{4,3,2,1,0:T(8,128)(2,1)S(1)}, bf16[2,2,32,16,128]{4,3,2,1,0:T(8,128)(2,1)}, u32[]{:S(2)}, u32[]{:S(2)}) collective-permute-start(bf16[2,2,32,16,128]{4,3,2,1,0:T(8,128)(2,1)S(1)} %collective-permute-done.5.refs_7_), channel_id=1, source_target_pairs={{4,0},{8,4},{12,8},{16,12},{20,16},{24,20},{28,24},{32,28},{36,32}... | collective-permute-start | bytes 1572872 | tf_op jit(solution)/shard_map/ppermute | solution.py:179
  61.3 0.0 collective-permute-done.1.refs_2_
  61.3 0.0 collective-permute-start.6
  61.3 0.0 collective-permute-done.refs_0_
  61.3 6.2 %collective-permute-start.10 = (bf16[2,2,32,16,128]{4,3,2,1,0:T(8,128)(2,1)S(1)}, bf16[2,2,32,16,128]{4,3,2,1,0:T(8,128)(2,1)}, u32[]{:S(2)}, u32[]{:S(2)}) collective-permute-start(bf16[2,2,32,16,128]{4,3,2,1,0:T(8,128)(2,1)S(1)} %collective-permute-done.8.refs_10_), channel_id=1, source_target_pairs={{4,0},{8,4},{12,8},{16,12},{20,16},{24,20},{28,24},{32,28},{36,32}... | collective-permute-start | bytes 1572872 | tf_op jit(solution)/shard_map/ppermute | solution.py:179
  67.5 0.0 collective-permute-done.4.refs_5_
  67.5 0.0 collective-permute-start.9
  67.5 0.1 add_convert_fusion.edge_ref
  67.6 0.0 collective-permute-done.3.refs_3_
  67.6 5.9 %collective-permute-done.7.refs_8_ = bf16[2,2,32,16,128]{4,3,2,1,0:T(8,128)(2,1)} collective-permute-done((bf16[2,2,32,16,128]{4,3,2,1,0:T(8,128)(2,1)S(1)}, bf16[2,2,32,16,128]{4,3,2,1,0:T(8,128)(2,1)}, u32[]{:S(2)}, u32[]{:S(2)}) %collective-permute-start.7) | collective-permute-done | bytes 524320 | tf_op jit(solution)/shard_map/ppermute | solution.py:179
  73.5 6.9 %collective-permute-done.6.refs_6_ = bf16[2,2,32,16,128]{4,3,2,1,0:T(8,128)(2,1)} collective-permute-done((bf16[2,2,32,16,128]{4,3,2,1,0:T(8,128)(2,1)S(1)}, bf16[2,2,32,16,128]{4,3,2,1,0:T(8,128)(2,1)}, u32[]{:S(2)}, u32[]{:S(2)}) %collective-permute-start.6) | collective-permute-done | bytes 524320 | tf_op jit(solution)/shard_map/ppermute | solution.py:179
  80.4 3.8 %collective-permute-done.10.refs_11_ = bf16[2,2,32,16,128]{4,3,2,1,0:T(8,128)(2,1)} collective-permute-done((bf16[2,2,32,16,128]{4,3,2,1,0:T(8,128)(2,1)S(1)}, bf16[2,2,32,16,128]{4,3,2,1,0:T(8,128)(2,1)}, u32[]{:S(2)}, u32[]{:S(2)}) %collective-permute-start.10) | collective-permute-done | bytes 524320 | tf_op jit(solution)/shard_map/ppermute | solution.py:179
  84.2 6.5 %collective-permute-done.9.refs_9_ = bf16[2,2,32,16,128]{4,3,2,1,0:T(8,128)(2,1)} collective-permute-done((bf16[2,2,32,16,128]{4,3,2,1,0:T(8,128)(2,1)S(1)}, bf16[2,2,32,16,128]{4,3,2,1,0:T(8,128)(2,1)}, u32[]{:S(2)}, u32[]{:S(2)}) %collective-permute-start.9) | collective-permute-done | bytes 524320 | tf_op jit(solution)/shard_map/ppermute | solution.py:179
  90.7 0.0 copy-start
  90.7 1.0 copy-done
  91.7 18.8 %shard_map.29 = f32[4,65,32,256]{3,2,1,0:T(8,128)} custom-call(s32[2]{0:T(128)S(1)} %add_convert_fusion.edge_ref, bf16[2,2,32,16,128]{4,3,2,1,0:T(8,128)(2,1)S(1)} %collective-permute-done.refs_0_, bf16[2,2,32,16,128]{4,3,2,1,0:T(8,128)(2,1)S(1)} %copy-done, bf16[2,2,32,16,128]{4,3,2,1,0:T(8,128)(2,1)S(1)} %collective-permute-done.1.refs_2_, ...), custom_call_target="tpu_custom_call" | custom-call | flops 70000000 | bytes 15728640 | tf_op jit(solution)/shard_map/pallas_call | solution.py:148
Async XLA Ops:
  4.0 11.3 %collective-permute-start.2 = (bf16[2,2,32,16,128]{4,3,2,1,0:T(8,128)(2,1)}, bf16[2,2,32,16,128]{4,3,2,1,0:T(8,128)(2,1)S(1)}, u32[]{:S(2)}, u32[]{:S(2)}) collective-permute-start(bf16[2,2,32,16,128]{4,3,2,1,0:T(8,128)(2,1)} %get-tuple-element.10), channel_id=1, source_target_pairs={{0,1},{1,0},{2,3},{3,2},{4,5},{5,4},{6,7},{7,6},{8,9},{9,8},{10,11... | collective-permute-start | bytes 1572872 | tf_op jit(solution)/shard_map/ppermute | solution.py:178
  4.0 17.6 %collective-permute-start.5 = (bf16[2,2,32,16,128]{4,3,2,1,0:T(8,128)(2,1)}, bf16[2,2,32,16,128]{4,3,2,1,0:T(8,128)(2,1)S(1)}, u32[]{:S(2)}, u32[]{:S(2)}) collective-permute-start(bf16[2,2,32,16,128]{4,3,2,1,0:T(8,128)(2,1)} %get-tuple-element.11), channel_id=1, source_target_pairs={{0,2},{1,3},{2,0},{3,1},{4,6},{5,7},{6,4},{7,5},{8,10},{9,11},{10,... | collective-permute-start | bytes 1572872 | tf_op jit(solution)/shard_map/ppermute | solution.py:178
  6.4 35.7 %collective-permute-start.8 = (bf16[2,2,32,16,128]{4,3,2,1,0:T(8,128)(2,1)}, bf16[2,2,32,16,128]{4,3,2,1,0:T(8,128)(2,1)S(1)}, u32[]{:S(2)}, u32[]{:S(2)}) collective-permute-start(bf16[2,2,32,16,128]{4,3,2,1,0:T(8,128)(2,1)} %get-tuple-element.12), channel_id=1, source_target_pairs={{0,3},{1,2},{2,1},{3,0},{4,7},{5,6},{6,5},{7,4},{8,11},{9,10},{10,... | collective-permute-start | bytes 1572872 | tf_op jit(solution)/shard_map/ppermute | solution.py:178
  7.4 53.9 %collective-permute-start.1 = (bf16[2,2,32,16,128]{4,3,2,1,0:T(8,128)(2,1)}, bf16[2,2,32,16,128]{4,3,2,1,0:T(8,128)(2,1)S(1)}, u32[]{:S(2)}, u32[]{:S(2)}) collective-permute-start(bf16[2,2,32,16,128]{4,3,2,1,0:T(8,128)(2,1)} %get-tuple-element.9.refs_1_), channel_id=1, source_target_pairs={{4,0},{8,4},{12,8},{16,12},{20,16},{24,20},{28,24},{32,28},{36,32}... | collective-permute-start | bytes 1572872 | tf_op jit(solution)/shard_map/ppermute | solution.py:179
  15.4 45.9 %collective-permute-start = (bf16[2,2,32,16,128]{4,3,2,1,0:T(8,128)(2,1)}, bf16[2,2,32,16,128]{4,3,2,1,0:T(8,128)(2,1)S(1)}, u32[]{:S(2)}, u32[]{:S(2)}) collective-permute-start(bf16[2,2,32,16,128]{4,3,2,1,0:T(8,128)(2,1)} %get-tuple-element.9.refs_1_), channel_id=1, source_target_pairs={{0,4},{4,8},{8,12},{12,16},{16,20},{20,24},{24,28},{28,32},{32,36}... | collective-permute-start | bytes 1572872 | tf_op jit(solution)/shard_map/ppermute | solution.py:179
  15.4 52.2 %collective-permute-start.4 = (bf16[2,2,32,16,128]{4,3,2,1,0:T(8,128)(2,1)S(1)}, bf16[2,2,32,16,128]{4,3,2,1,0:T(8,128)(2,1)S(1)}, u32[]{:S(2)}, u32[]{:S(2)}) collective-permute-start(bf16[2,2,32,16,128]{4,3,2,1,0:T(8,128)(2,1)S(1)} %collective-permute-done.2.refs_4_), channel_id=1, source_target_pairs={{4,0},{8,4},{12,8},{16,12},{20,16},{24,20},{28,24},{32,28},{36,32}... | collective-permute-start | bytes 1572872 | tf_op jit(solution)/shard_map/ppermute | solution.py:179
  21.6 46.0 %collective-permute-start.3 = (bf16[2,2,32,16,128]{4,3,2,1,0:T(8,128)(2,1)S(1)}, bf16[2,2,32,16,128]{4,3,2,1,0:T(8,128)(2,1)}, u32[]{:S(2)}, u32[]{:S(2)}) collective-permute-start(bf16[2,2,32,16,128]{4,3,2,1,0:T(8,128)(2,1)S(1)} %collective-permute-done.2.refs_4_), channel_id=1, source_target_pairs={{0,4},{4,8},{8,12},{12,16},{16,20},{20,24},{24,28},{28,32},{32,36}... | collective-permute-start | bytes 1572872 | tf_op jit(solution)/shard_map/ppermute | solution.py:179
  42.1 31.4 %collective-permute-start.7 = (bf16[2,2,32,16,128]{4,3,2,1,0:T(8,128)(2,1)S(1)}, bf16[2,2,32,16,128]{4,3,2,1,0:T(8,128)(2,1)}, u32[]{:S(2)}, u32[]{:S(2)}) collective-permute-start(bf16[2,2,32,16,128]{4,3,2,1,0:T(8,128)(2,1)S(1)} %collective-permute-done.5.refs_7_), channel_id=1, source_target_pairs={{4,0},{8,4},{12,8},{16,12},{20,16},{24,20},{28,24},{32,28},{36,32}... | collective-permute-start | bytes 1572872 | tf_op jit(solution)/shard_map/ppermute | solution.py:179
  61.3 19.1 %collective-permute-start.6 = (bf16[2,2,32,16,128]{4,3,2,1,0:T(8,128)(2,1)S(1)}, bf16[2,2,32,16,128]{4,3,2,1,0:T(8,128)(2,1)}, u32[]{:S(2)}, u32[]{:S(2)}) collective-permute-start(bf16[2,2,32,16,128]{4,3,2,1,0:T(8,128)(2,1)S(1)} %collective-permute-done.5.refs_7_), channel_id=1, source_target_pairs={{0,4},{4,8},{8,12},{12,16},{16,20},{20,24},{24,28},{28,32},{32,36}... | collective-permute-start | bytes 1572872 | tf_op jit(solution)/shard_map/ppermute | solution.py:179
  61.3 22.9 %collective-permute-start.10 = (bf16[2,2,32,16,128]{4,3,2,1,0:T(8,128)(2,1)S(1)}, bf16[2,2,32,16,128]{4,3,2,1,0:T(8,128)(2,1)}, u32[]{:S(2)}, u32[]{:S(2)}) collective-permute-start(bf16[2,2,32,16,128]{4,3,2,1,0:T(8,128)(2,1)S(1)} %collective-permute-done.8.refs_10_), channel_id=1, source_target_pairs={{4,0},{8,4},{12,8},{16,12},{20,16},{24,20},{28,24},{32,28},{36,32}... | collective-permute-start | bytes 1572872 | tf_op jit(solution)/shard_map/ppermute | solution.py:179
  67.5 23.1 %collective-permute-start.9 = (bf16[2,2,32,16,128]{4,3,2,1,0:T(8,128)(2,1)S(1)}, bf16[2,2,32,16,128]{4,3,2,1,0:T(8,128)(2,1)}, u32[]{:S(2)}, u32[]{:S(2)}) collective-permute-start(bf16[2,2,32,16,128]{4,3,2,1,0:T(8,128)(2,1)S(1)} %collective-permute-done.8.refs_10_), channel_id=1, source_target_pairs={{0,4},{4,8},{8,12},{12,16},{16,20},{20,24},{24,28},{28,32},{32,36}... | collective-permute-start | bytes 1572872 | tf_op jit(solution)/shard_map/ppermute | solution.py:179
  90.7 1.0 copy-start

commit v2 on v1

v2 whole, which is shorter than its diff:
```python
import functools

import jax
import jax.numpy as jnp
from jax import lax
from jax.experimental import pallas as pl
from jax.experimental.pallas import tpu as pltpu
from jax.sharding import PartitionSpec as P

HMAX = 32
OFFSETS = 2 * HMAX + 1
GROUPS = 4
ROWS = 16
LANES = 128
TX = 8
TH = 5


def regroup_kernel(group_ref, source_ref, receiver_ref, *out_refs):
    freqs, cells = source_ref.shape[1], source_ref.shape[2]

    def regroup(order):
        for field, ref in enumerate((source_ref, receiver_ref)):
            for f in range(freqs):

                def one_cell(x, _):
                    low = lax.broadcasted_iota(jnp.int32, (8, LANES), 0) < 4
                    parts = [[None, None] for _ in range(GROUPS)]
                    for c in range(2):
                        near = ref[c, f, x, :, :LANES].astype(jnp.float32)
                        far = ref[c, f, x, :, LANES:].astype(jnp.float32)
                        for pair in range(2):
                            a = near[8 * pair : 8 * pair + 8]
                            b = far[8 * pair : 8 * pair + 8]
                            parts[2 * pair][c] = jnp.where(low, a, pltpu.roll(b, 4, 0))
                            parts[2 * pair + 1][c] = jnp.where(low, pltpu.roll(a, 4, 0), b)
                    for d in range(GROUPS):
                        out_refs[d][field, f, x] = jnp.concatenate(parts[order ^ d], axis=0).astype(jnp.bfloat16)
                    return 0

                lax.fori_loop(0, cells, one_cell, 0, unroll=4)

    for order in range(GROUPS):
        pl.when(group_ref[0] == order)(functools.partial(regroup, order))


def regrouped(group, source_field, receiver_field):
    two, freqs, cells, _, _ = source_field.shape
    steps = 4
    spec_in = pl.BlockSpec((2, freqs, cells // steps, 16, 256), lambda i: (0, 0, i, 0, 0))
    spec_out = pl.BlockSpec((2, freqs, cells // steps, ROWS, LANES), lambda i: (0, 0, i, 0, 0))
    return pl.pallas_call(
        regroup_kernel,
        grid=(steps,),
        in_specs=[pl.BlockSpec(memory_space=pltpu.SMEM), spec_in, spec_in],
        out_specs=[spec_out] * GROUPS,
        out_shape=[jax.ShapeDtypeStruct((2, freqs, cells, ROWS, LANES), jnp.bfloat16)] * GROUPS,
        cost_estimate=pl.CostEstimate(flops=0, bytes_accessed=4 << 20, transcendentals=0),
    )(group, source_field, receiver_field)


def image_kernel(first, last, groups, *refs):
    blocks = refs[: 3 * groups]
    refs = refs[3 * groups :]
    if not first:
        partial_ref, refs = refs[0], refs[1:]
    out_ref, refs = refs[0], refs[1:]
    raw, fields, stage, in_sems, out_sems = refs[:5]
    refs = refs[5:]
    if last:
        turn, refs = refs[0], refs[1:]
    if not first:
        before, before_sems = refs
    freqs, cells = blocks[0].shape[1], blocks[0].shape[2]
    total_freqs = freqs * groups
    steps = OFFSETS // TH

    def before_copy(step, slot):
        return pltpu.make_async_copy(partial_ref.at[pl.ds(TH * step, TH)], before.at[slot], before_sems.at[slot])

    def out_copy(step, slot):
        if last:
            return pltpu.make_async_copy(stage.at[slot], out_ref.at[:, pl.ds(TH * step, TH)], out_sems.at[slot])
        return pltpu.make_async_copy(stage.at[slot], out_ref.at[pl.ds(TH * step, TH)], out_sems.at[slot])

    copies = []
    for d in range(groups):
        for k in range(3):
            copies.append(
                pltpu.make_async_copy(
                    blocks[3 * d + k],
                    raw.at[:, pl.ds(freqs * d, freqs), pl.ds(cells * k, cells)],
                    in_sems.at[3 * d + k],
                )
            )
    for copy in copies:
        copy.start()
    if not first:
        before_copy(0, 0).start()
    for copy in copies:
        copy.wait()

    def widen(p, _):
        for field in range(2):
            for f in range(total_freqs):
                fields[field, p, f] = raw[field, f, p].astype(jnp.float32)
        return 0

    lax.fori_loop(0, 3 * cells, widen, 0)

    def h_step(step, _):
        slot = lax.rem(step, 2)
        k0 = TH * step

        if not first:

            @pl.when(step + 1 < steps)
            def _():
                before_copy(step + 1, 1 - slot).start()

            before_copy(step, slot).wait()

        @pl.when(step >= 2)
        def _():
            out_copy(step - 2, slot).wait()

        def x_step(xt, _):
            x0 = xt * TX
            s0 = x0 + 2 * HMAX - k0 - (TH - 1)
            r0 = x0 + k0
            total = [[None] * TX for _ in range(TH)]
            if not first:
                total = [[before[slot, j, x0 + i] for i in range(TX)] for j in range(TH)]
            for f in range(total_freqs):
                for c in range(2):
                    s = [fields[0, s0 + i, f, 8 * c : 8 * c + 8] for i in range(TX + TH - 1)]
                    r = [fields[1, r0 + i, f, 8 * c : 8 * c + 8] for i in range(TX + TH - 1)]
                    for j in range(TH):
                        for i in range(TX):
                            product = s[i + TH - 1 - j] * r[i + j]
                            total[j][i] = product if total[j][i] is None else total[j][i] + product
            for j in range(TH):
                if not last:
                    for i in range(TX):
                        stage[slot, j, x0 + i] = total[j][i]
                    continue
                for i in range(TX):
                    turn[j, pl.ds(i, 8, stride=TX)] = 0.25 * total[j][i]
                for zh in range(2):
                    for y in range(4):
                        row = zh * 4 + y
                        stage[slot, y, j, pl.ds(pl.multiple_of(x0, TX), TX), zh * LANES : (zh + 1) * LANES] = turn[
                            j, row * TX : (row + 1) * TX
                        ]
            return 0

        lax.fori_loop(0, cells // TX, x_step, 0)
        out_copy(step, slot).start()
        return 0

    lax.fori_loop(0, steps, h_step, 0)
    for step in (steps - 2, steps - 1):
        out_copy(step, step % 2).wait()


def image(blocks, before, last):
    two, freqs, cells, _, _ = blocks[0].shape
    groups = len(blocks) // 3
    total_freqs = freqs * groups
    first = before is None
    stage_shape = (2, 4, TH, cells, 2 * LANES) if last else (2, TH, cells, 8, LANES)
    out_shape = (4, OFFSETS, cells, 2 * LANES) if last else (OFFSETS, cells, 8, LANES)
    scratch = [
        pltpu.VMEM((2, total_freqs, 3 * cells, ROWS, LANES), jnp.bfloat16),
        pltpu.VMEM((2, 3 * cells, total_freqs, ROWS, LANES), jnp.float32),
        pltpu.VMEM(stage_shape, jnp.float32),
        pltpu.SemaphoreType.DMA((3 * groups,)),
        pltpu.SemaphoreType.DMA((2,)),
    ]
    if last:
        scratch.append(pltpu.VMEM((TH, 8 * TX, LANES), jnp.float32))
    if not first:
        scratch += [pltpu.VMEM((2, TH, cells, 8, LANES), jnp.float32), pltpu.SemaphoreType.DMA((2,))]
    operands = list(blocks) + ([] if first else [before])
    return pl.pallas_call(
        functools.partial(image_kernel, first, last, groups),
        in_specs=[pl.BlockSpec(memory_space=pl.ANY)] * len(operands),
        out_specs=pl.BlockSpec(memory_space=pl.ANY),
        out_shape=jax.ShapeDtypeStruct(out_shape, jnp.float32),
        scratch_shapes=scratch,
        compiler_params=pltpu.CompilerParams(vmem_limit_bytes=60 << 20),
        cost_estimate=pl.CostEstimate(flops=17_000_000 * groups, bytes_accessed=15 << 20, transcendentals=0),
    )(*operands)


def body(source_field, receiver_field):
    slabs = lax.axis_size("slab")
    middle = slabs // 2
    group = lax.axis_index("freq").astype(jnp.int32)
    slab = lax.axis_index("slab")
    parts = list(regrouped(group[None], source_field, receiver_field))
    owned = [parts[0]] + [
        lax.ppermute(parts[d], "freq", [(g, g ^ d) for g in range(GROUPS)]) for d in range(1, GROUPS)
    ]

    def rim(d, step):
        sender = middle - 1 if step > 0 else middle
        direct = d >= 2
        pairs = []
        for s in range(slabs):
            if 0 <= s + step < slabs:
                for g in range(GROUPS):
                    to = g ^ d if direct and s == sender else g
                    pairs.append((s * GROUPS + g, (s + step) * GROUPS + to))
        value = jnp.where(slab == sender, parts[d], owned[d]) if direct else owned[d]
        return lax.ppermute(value, ("slab", "freq"), pairs)

    blocks = []
    for d in range(GROUPS):
        if d >= 2:
            ahead = blocks[d - 2]
            owned[d], parts[d], ahead[0], ahead[2] = lax.optimization_barrier(
                (owned[d], parts[d], ahead[0], ahead[2])
            )
        blocks.append([rim(d, 1), owned[d], rim(d, -1)])
    total = image(blocks[0] + blocks[1], None, False)
    total = image(blocks[2], total, False)
    return image(blocks[3], total, True)


def solution(mesh):
    in_specs = (P(None, "freq", "slab", None, None), P(None, "freq", "slab", None, None))
    out_specs = P("freq", None, "slab", None)
    return jax.shard_map(body, mesh=mesh, in_specs=in_specs, out_specs=out_specs, check_vma=False)
```

time: 112 us -> 108 us (0.964)
  the two profiles are of different devices: /device:TPU:8 before, /device:TPU:239 now
where the time goes in v2:
time: 108 us; the launch traced here: 107 us
  Pallas kernels  42.1 us (39%)
  waiting for transfers between devices  35.9 us (33%)
  starting transfers between devices  23 us (21%)
  other arithmetic  4.74 us (4%)
    pallas_call x3, Pallas kernels, image(): pl.pallas_call(functools.partial(image_kernel, first, last, groups), in_s...  38.1 us
    ppermute x3, waiting for transfers between devices, body(): lax.ppermute(parts[d], 'freq', [(g, g ^ d) for g in range(GROUPS)])  30.7 us
    ppermute x8, starting transfers between devices, rim(): return lax.ppermute(value, ('slab', 'freq'), pairs)  18.5 us
    ppermute x8, waiting for transfers between devices, rim(): return lax.ppermute(value, ('slab', 'freq'), pairs)  5.25 us
    select_n x2, other arithmetic, rim(): jnp.where(slab == sender, parts[d], owned[d])  4.74 us
    ppermute x3, starting transfers between devices, body(): lax.ppermute(parts[d], 'freq', [(g, g ^ d) for g in range(GROUPS)])  4.49 us
    pallas_call x1, Pallas kernels, regrouped(): pl.pallas_call(regroup_kernel, grid=(steps,), in_specs=[pl.BlockSpec(memo...  4 us
  transfers between devices with their start and end apart: 11, of which 3 were waited for; matrix products, arithmetic and copies ran while one was open for 4% of the time, Pallas kernels for 23%

profile of v2, /device:TPU:239, one launch (start us, length us, event | category | flops | bytes accessed | tf_op | source)
XLA Modules:
  0.0 106.7 jit_solution(601345894666495187)
XLA Ops:
  0.0 4.0 %shard_map.28 = (bf16[2,2,32,16,128]{4,3,2,1,0:T(8,128)(2,1)}, bf16[2,2,32,16,128]{4,3,2,1,0:T(8,128)(2,1)}, bf16[2,2,32,16,128]{4,3,2,1,0:T(8,128)(2,1)}, bf16[2,2,32,16,128]{4,3,2,1,0:T(8,128)(2,1)}) custom-call(s32[1]{0:T(128)} %bitcast.group_ref, bf16[2,2,32,16,256]{4,3,2,1,0:T(8,128)(2,1)} %source_ref.1, bf16[2,2,32,16,256]{4,3,2,1,0:T(8,128)(2,1)} %receiver_ref.1), custom_call_target="tpu_custom_call" | custom-call | bytes 4194304 | tf_op jit(solution)/shard_map/pallas_call | solution.py:52
  4.0 0.7 collective-permute-start.1
  4.7 1.3 %collective-permute-start.7 = (bf16[2,2,32,16,128]{4,3,2,1,0:T(8,128)(2,1)}, bf16[2,2,32,16,128]{4,3,2,1,0:T(8,128)(2,1)S(1)}, u32[]{:S(2)}, u32[]{:S(2)}) collective-permute-start(bf16[2,2,32,16,128]{4,3,2,1,0:T(8,128)(2,1)} %get-tuple-element.22.refs_1_), channel_id=1, source_target_pairs={{0,4},{1,5},{2,6},{3,7},{4,8},{5,9},{6,10},{7,11},{8,12},{9,13},{1... | collective-permute-start | bytes 1572872 | tf_op jit(solution)/shard_map/ppermute | solution.py:216
  6.0 4.0 %collective-permute-start.8 = (bf16[2,2,32,16,128]{4,3,2,1,0:T(8,128)(2,1)}, bf16[2,2,32,16,128]{4,3,2,1,0:T(8,128)(2,1)S(1)}, u32[]{:S(2)}, u32[]{:S(2)}) collective-permute-start(bf16[2,2,32,16,128]{4,3,2,1,0:T(8,128)(2,1)} %get-tuple-element.22.refs_1_), channel_id=1, source_target_pairs={{4,0},{5,1},{6,2},{7,3},{8,4},{9,5},{10,6},{11,7},{12,8},{13,9},{1... | collective-permute-start | bytes 1572872 | tf_op jit(solution)/shard_map/ppermute | solution.py:216
  10.0 2.1 %collective-permute-start.6 = (bf16[2,2,32,16,128]{4,3,2,1,0:T(8,128)(2,1)}, bf16[2,2,32,16,128]{4,3,2,1,0:T(8,128)(2,1)S(1)}, u32[]{:S(2)}, u32[]{:S(2)}) collective-permute-start(bf16[2,2,32,16,128]{4,3,2,1,0:T(8,128)(2,1)} %get-tuple-element.23), channel_id=1, source_target_pairs={{0,2},{1,3},{2,0},{3,1},{4,6},{5,7},{6,4},{7,5},{8,10},{9,11},{10,... | collective-permute-start | bytes 1572872 | tf_op jit(solution)/shard_map/ppermute | solution.py:203
  12.1 1.7 %collective-permute-start = (bf16[2,2,32,16,128]{4,3,2,1,0:T(8,128)(2,1)}, bf16[2,2,32,16,128]{4,3,2,1,0:T(8,128)(2,1)S(1)}, u32[]{:S(2)}, u32[]{:S(2)}) collective-permute-start(bf16[2,2,32,16,128]{4,3,2,1,0:T(8,128)(2,1)} %get-tuple-element.19), channel_id=1, source_target_pairs={{0,3},{1,2},{2,1},{3,0},{4,7},{5,6},{6,5},{7,4},{8,11},{9,10},{10,... | collective-permute-start | bytes 1572872 | tf_op jit(solution)/shard_map/ppermute | solution.py:203
  13.8 0.0 collective-permute-done.1.refs_4_
  13.8 0.0 copy-start.2
  13.8 1.3 %collective-permute-start.2 = (bf16[2,2,32,16,128]{4,3,2,1,0:T(8,128)(2,1)S(1)}, bf16[2,2,32,16,128]{4,3,2,1,0:T(8,128)(2,1)S(1)}, u32[]{:S(2)}, u32[]{:S(2)}) collective-permute-start(bf16[2,2,32,16,128]{4,3,2,1,0:T(8,128)(2,1)S(1)} %collective-permute-done.1.refs_4_), channel_id=1, source_target_pairs={{0,4},{1,5},{2,6},{3,7},{4,8},{5,9},{6,10},{7,11},{8,12},{9,13},{1... | collective-permute-start | bytes 1572872 | tf_op jit(solution)/shard_map/ppermute | solution.py:216
  15.1 5.2 %collective-permute-done.7.refs_0_ = bf16[2,2,32,16,128]{4,3,2,1,0:T(8,128)(2,1)S(1)} collective-permute-done((bf16[2,2,32,16,128]{4,3,2,1,0:T(8,128)(2,1)}, bf16[2,2,32,16,128]{4,3,2,1,0:T(8,128)(2,1)S(1)}, u32[]{:S(2)}, u32[]{:S(2)}) %collective-permute-start.7) | collective-permute-done | bytes 524320 | tf_op jit(solution)/shard_map/ppermute | solution.py:216
  20.3 0.0 copy-start.3
  20.3 3.2 %collective-permute-start.3 = (bf16[2,2,32,16,128]{4,3,2,1,0:T(8,128)(2,1)S(1)}, bf16[2,2,32,16,128]{4,3,2,1,0:T(8,128)(2,1)}, u32[]{:S(2)}, u32[]{:S(2)}) collective-permute-start(bf16[2,2,32,16,128]{4,3,2,1,0:T(8,128)(2,1)S(1)} %collective-permute-done.1.refs_4_), channel_id=1, source_target_pairs={{4,0},{5,1},{6,2},{7,3},{8,4},{9,5},{10,6},{11,7},{12,8},{13,9},{1... | collective-permute-start | bytes 1572872 | tf_op jit(solution)/shard_map/ppermute | solution.py:216
  23.6 0.0 collective-permute-done.8.refs_2_
  23.6 0.0 copy-start.4
  23.6 23.6 %collective-permute-done.6.refs_1_ = bf16[2,2,32,16,128]{4,3,2,1,0:T(8,128)(2,1)S(1)} collective-permute-done((bf16[2,2,32,16,128]{4,3,2,1,0:T(8,128)(2,1)}, bf16[2,2,32,16,128]{4,3,2,1,0:T(8,128)(2,1)S(1)}, u32[]{:S(2)}, u32[]{:S(2)}) %collective-permute-start.6) | collective-permute-done | bytes 524320 | tf_op jit(solution)/shard_map/ppermute | solution.py:203
  47.2 0.0 copy-start.1
  47.2 2.3 %broadcast_select_fusion = (bf16[2,2,32,16,128]{4,3,2,1,0:T(8,128)(2,1)}, bf16[2,2,32,16,128]{4,3,2,1,0:T(8,128)(2,1)}) fusion(bf16[2,2,32,16,128]{4,3,2,1,0:T(8,128)(2,1)} %get-tuple-element.23, bf16[2,2,32,16,128]{4,3,2,1,0:T(8,128)(2,1)S(1)} %collective-permute-done.6.refs_1_, pred[]{:T(512)S(6)} %eq.9, pred[]{:T(512)S(6)} %eq.8), kind=kLoop, calls=%fused_computation | loop fusion | flops 524288 | bytes 2097154 | tf_op jit(solution)/shard_map/jit(_where)/select_n | solution.py:215
  49.5 1.3 %collective-permute-start.10 = (bf16[2,2,32,16,128]{4,3,2,1,0:T(8,128)(2,1)}, bf16[2,2,32,16,128]{4,3,2,1,0:T(8,128)(2,1)S(1)}, u32[]{:S(2)}, u32[]{:S(2)}) collective-permute-start(bf16[2,2,32,16,128]{4,3,2,1,0:T(8,128)(2,1)} %get-tuple-element.29), channel_id=1, source_target_pairs={{4,0},{5,1},{6,2},{7,3},{8,4},{9,5},{10,6},{11,7},{12,8},{13,9},{1... | collective-permute-start | bytes 1572872 | tf_op jit(solution)/shard_map/ppermute | solution.py:216
  50.8 1.3 %collective-permute-start.9 = (bf16[2,2,32,16,128]{4,3,2,1,0:T(8,128)(2,1)}, bf16[2,2,32,16,128]{4,3,2,1,0:T(8,128)(2,1)}, u32[]{:S(2)}, u32[]{:S(2)}) collective-permute-start(bf16[2,2,32,16,128]{4,3,2,1,0:T(8,128)(2,1)} %get-tuple-element.30), channel_id=1, source_target_pairs={{0,4},{1,5},{2,6},{3,7},{4,8},{5,9},{6,10},{7,11},{8,12},{9,13},{1... | collective-permute-start | bytes 1572872 | tf_op jit(solution)/shard_map/ppermute | solution.py:216
  52.1 7.1 %collective-permute-done.refs_1_ = bf16[2,2,32,16,128]{4,3,2,1,0:T(8,128)(2,1)S(1)} collective-permute-done((bf16[2,2,32,16,128]{4,3,2,1,0:T(8,128)(2,1)}, bf16[2,2,32,16,128]{4,3,2,1,0:T(8,128)(2,1)S(1)}, u32[]{:S(2)}, u32[]{:S(2)}) %collective-permute-start) | collective-permute-done | bytes 524320 | tf_op jit(solution)/shard_map/ppermute | solution.py:203
  59.2 0.0 copy-start
  59.2 0.0 collective-permute-done.2.refs_3_
  59.2 0.0 copy-start.5
  59.2 0.0 collective-permute-done.3.refs_5_
  59.2 2.5 %broadcast_select_fusion.1 = (bf16[2,2,32,16,128]{4,3,2,1,0:T(8,128)(2,1)}, bf16[2,2,32,16,128]{4,3,2,1,0:T(8,128)(2,1)}) fusion(bf16[2,2,32,16,128]{4,3,2,1,0:T(8,128)(2,1)} %get-tuple-element.19, bf16[2,2,32,16,128]{4,3,2,1,0:T(8,128)(2,1)S(1)} %collective-permute-done.refs_1_, pred[]{:T(512)S(6)} %eq.9, pred[]{:T(512)S(6)} %eq.8), kind=kLoop, calls=%fused_computation.1 | loop fusion | flops 524288 | bytes 2097154 | tf_op jit(solution)/shard_map/jit(_where)/select_n | solution.py:215
  61.6 1.3 %collective-permute-start.4 = (bf16[2,2,32,16,128]{4,3,2,1,0:T(8,128)(2,1)}, bf16[2,2,32,16,128]{4,3,2,1,0:T(8,128)(2,1)}, u32[]{:S(2)}, u32[]{:S(2)}) collective-permute-start(bf16[2,2,32,16,128]{4,3,2,1,0:T(8,128)(2,1)} %get-tuple-element.32), channel_id=1, source_target_pairs={{0,4},{1,5},{2,6},{3,7},{4,8},{5,9},{6,10},{7,11},{8,12},{9,13},{1... | collective-permute-start | bytes 1572872 | tf_op jit(solution)/shard_map/ppermute | solution.py:216
  62.9 4.8 %collective-permute-start.5 = (bf16[2,2,32,16,128]{4,3,2,1,0:T(8,128)(2,1)}, bf16[2,2,32,16,128]{4,3,2,1,0:T(8,128)(2,1)}, u32[]{:S(2)}, u32[]{:S(2)}) collective-permute-start(bf16[2,2,32,16,128]{4,3,2,1,0:T(8,128)(2,1)} %get-tuple-element.31), channel_id=1, source_target_pairs={{4,0},{5,1},{6,2},{7,3},{8,4},{9,5},{10,6},{11,7},{12,8},{13,9},{1... | collective-permute-start | bytes 1572872 | tf_op jit(solution)/shard_map/ppermute | solution.py:216
  67.7 0.0 copy-done.2
  67.7 0.0 copy-done.3
  67.7 0.0 copy-done.4
  67.7 0.0 copy-done.5
  67.7 11.3 %shard_map.29.refs_3_ = f32[65,32,8,128]{3,2,1,0:T(8,128)} custom-call(bf16[2,2,32,16,128]{4,3,2,1,0:T(8,128)(2,1)} %copy-done.3, bf16[2,2,32,16,128]{4,3,2,1,0:T(8,128)(2,1)} %get-tuple-element.22.refs_1_, bf16[2,2,32,16,128]{4,3,2,1,0:T(8,128)(2,1)} %copy-done.4, bf16[2,2,32,16,128]{4,3,2,1,0:T(8,128)(2,1)} %copy-done.5, ...), custom_call_target="tpu_custom_call" | custom-call | flops 34000000 | bytes 15728640 | tf_op jit(solution)/shard_map/pallas_call | solution.py:185
  79.0 0.0 collective-permute-done.10.refs_2_
  79.0 0.0 copy-start.6
  79.0 0.0 collective-permute-done.9.refs_0_
  79.1 0.0 copy-done.1
  79.1 0.8 copy-done.6
  79.8 12.8 %shard_map.30.refs_3_ = f32[65,32,8,128]{3,2,1,0:T(8,128)} custom-call(bf16[2,2,32,16,128]{4,3,2,1,0:T(8,128)(2,1)} %collective-permute-done.9.refs_0_, bf16[2,2,32,16,128]{4,3,2,1,0:T(8,128)(2,1)} %copy-done.1, bf16[2,2,32,16,128]{4,3,2,1,0:T(8,128)(2,1)} %copy-done.6, f32[65,32,8,128]{3,2,1,0:T(8,128)} %shard_map.29.refs_3_), custom_call_target="tpu_custom_call" | custom-call | flops 17000000 | bytes 15728640 | tf_op jit(solution)/shard_map/pallas_call | solution.py:185
  92.6 0.0 copy-done
  92.6 0.0 collective-permute-done.4.refs_0_
  92.7 0.0 collective-permute-done.5.refs_2_
  92.7 14.0 %shard_map.31 = f32[4,65,32,256]{3,2,1,0:T(8,128)} custom-call(bf16[2,2,32,16,128]{4,3,2,1,0:T(8,128)(2,1)} %collective-permute-done.4.refs_0_, bf16[2,2,32,16,128]{4,3,2,1,0:T(8,128)(2,1)} %copy-done, bf16[2,2,32,16,128]{4,3,2,1,0:T(8,128)(2,1)} %collective-permute-done.5.refs_2_, f32[65,32,8,128]{3,2,1,0:T(8,128)} %shard_map.30.refs_3_), custom_call_target="tpu_custom_call" | custom-call | flops 17000000 | bytes 15728640 | tf_op jit(solution)/shard_map/pallas_call | solution.py:185
Async XLA Ops:
  4.0 9.8 %collective-permute-start.1 = (bf16[2,2,32,16,128]{4,3,2,1,0:T(8,128)(2,1)}, bf16[2,2,32,16,128]{4,3,2,1,0:T(8,128)(2,1)S(1)}, u32[]{:S(2)}, u32[]{:S(2)}) collective-permute-start(bf16[2,2,32,16,128]{4,3,2,1,0:T(8,128)(2,1)} %get-tuple-element.18), channel_id=1, source_target_pairs={{0,1},{1,0},{2,3},{3,2},{4,5},{5,4},{6,7},{7,6},{8,9},{9,8},{10,11... | collective-permute-start | bytes 1572872 | tf_op jit(solution)/shard_map/ppermute | solution.py:203
  4.7 15.6 %collective-permute-start.7 = (bf16[2,2,32,16,128]{4,3,2,1,0:T(8,128)(2,1)}, bf16[2,2,32,16,128]{4,3,2,1,0:T(8,128)(2,1)S(1)}, u32[]{:S(2)}, u32[]{:S(2)}) collective-permute-start(bf16[2,2,32,16,128]{4,3,2,1,0:T(8,128)(2,1)} %get-tuple-element.22.refs_1_), channel_id=1, source_target_pairs={{0,4},{1,5},{2,6},{3,7},{4,8},{5,9},{6,10},{7,11},{8,12},{9,13},{1... | collective-permute-start | bytes 1572872 | tf_op jit(solution)/shard_map/ppermute | solution.py:216
  6.0 17.6 %collective-permute-start.8 = (bf16[2,2,32,16,128]{4,3,2,1,0:T(8,128)(2,1)}, bf16[2,2,32,16,128]{4,3,2,1,0:T(8,128)(2,1)S(1)}, u32[]{:S(2)}, u32[]{:S(2)}) collective-permute-start(bf16[2,2,32,16,128]{4,3,2,1,0:T(8,128)(2,1)} %get-tuple-element.22.refs_1_), channel_id=1, source_target_pairs={{4,0},{5,1},{6,2},{7,3},{8,4},{9,5},{10,6},{11,7},{12,8},{13,9},{1... | collective-permute-start | bytes 1572872 | tf_op jit(solution)/shard_map/ppermute | solution.py:216
  10.0 37.2 %collective-permute-start.6 = (bf16[2,2,32,16,128]{4,3,2,1,0:T(8,128)(2,1)}, bf16[2,2,32,16,128]{4,3,2,1,0:T(8,128)(2,1)S(1)}, u32[]{:S(2)}, u32[]{:S(2)}) collective-permute-start(bf16[2,2,32,16,128]{4,3,2,1,0:T(8,128)(2,1)} %get-tuple-element.23), channel_id=1, source_target_pairs={{0,2},{1,3},{2,0},{3,1},{4,6},{5,7},{6,4},{7,5},{8,10},{9,11},{10,... | collective-permute-start | bytes 1572872 | tf_op jit(solution)/shard_map/ppermute | solution.py:203
  12.1 47.1 %collective-permute-start = (bf16[2,2,32,16,128]{4,3,2,1,0:T(8,128)(2,1)}, bf16[2,2,32,16,128]{4,3,2,1,0:T(8,128)(2,1)S(1)}, u32[]{:S(2)}, u32[]{:S(2)}) collective-permute-start(bf16[2,2,32,16,128]{4,3,2,1,0:T(8,128)(2,1)} %get-tuple-element.19), channel_id=1, source_target_pairs={{0,3},{1,2},{2,1},{3,0},{4,7},{5,6},{6,5},{7,4},{8,11},{9,10},{10,... | collective-permute-start | bytes 1572872 | tf_op jit(solution)/shard_map/ppermute | solution.py:203
  13.8 53.9 %copy-start.2 = (bf16[2,2,32,16,128]{4,3,2,1,0:T(8,128)(2,1)}, bf16[2,2,32,16,128]{4,3,2,1,0:T(8,128)(2,1)S(1)}, u32[]{:S(2)}) copy-start(bf16[2,2,32,16,128]{4,3,2,1,0:T(8,128)(2,1)S(1)} %collective-permute-done.1.refs_4_) | copy-start | bytes 1572868
  13.8 45.4 %collective-permute-start.2 = (bf16[2,2,32,16,128]{4,3,2,1,0:T(8,128)(2,1)S(1)}, bf16[2,2,32,16,128]{4,3,2,1,0:T(8,128)(2,1)S(1)}, u32[]{:S(2)}, u32[]{:S(2)}) collective-permute-start(bf16[2,2,32,16,128]{4,3,2,1,0:T(8,128)(2,1)S(1)} %collective-permute-done.1.refs_4_), channel_id=1, source_target_pairs={{0,4},{1,5},{2,6},{3,7},{4,8},{5,9},{6,10},{7,11},{8,12},{9,13},{1... | collective-permute-start | bytes 1572872 | tf_op jit(solution)/shard_map/ppermute | solution.py:216
  20.3 47.4 %copy-start.3 = (bf16[2,2,32,16,128]{4,3,2,1,0:T(8,128)(2,1)}, bf16[2,2,32,16,128]{4,3,2,1,0:T(8,128)(2,1)S(1)}, u32[]{:S(2)}) copy-start(bf16[2,2,32,16,128]{4,3,2,1,0:T(8,128)(2,1)S(1)} %collective-permute-done.7.refs_0_) | copy-start | bytes 1572868
  20.3 38.8 %collective-permute-start.3 = (bf16[2,2,32,16,128]{4,3,2,1,0:T(8,128)(2,1)S(1)}, bf16[2,2,32,16,128]{4,3,2,1,0:T(8,128)(2,1)}, u32[]{:S(2)}, u32[]{:S(2)}) collective-permute-start(bf16[2,2,32,16,128]{4,3,2,1,0:T(8,128)(2,1)S(1)} %collective-permute-done.1.refs_4_), channel_id=1, source_target_pairs={{4,0},{5,1},{6,2},{7,3},{8,4},{9,5},{10,6},{11,7},{12,8},{13,9},{1... | collective-permute-start | bytes 1572872 | tf_op jit(solution)/shard_map/ppermute | solution.py:216
  23.6 44.1 %copy-start.4 = (bf16[2,2,32,16,128]{4,3,2,1,0:T(8,128)(2,1)}, bf16[2,2,32,16,128]{4,3,2,1,0:T(8,128)(2,1)S(1)}, u32[]{:S(2)}) copy-start(bf16[2,2,32,16,128]{4,3,2,1,0:T(8,128)(2,1)S(1)} %collective-permute-done.8.refs_2_) | copy-start | bytes 1572868
  47.2 31.9 %copy-start.1 = (bf16[2,2,32,16,128]{4,3,2,1,0:T(8,128)(2,1)}, bf16[2,2,32,16,128]{4,3,2,1,0:T(8,128)(2,1)S(1)}, u32[]{:S(2)}) copy-start(bf16[2,2,32,16,128]{4,3,2,1,0:T(8,128)(2,1)S(1)} %collective-permute-done.6.refs_1_) | copy-start | bytes 1572868
  49.5 29.6 %collective-permute-start.10 = (bf16[2,2,32,16,128]{4,3,2,1,0:T(8,128)(2,1)}, bf16[2,2,32,16,128]{4,3,2,1,0:T(8,128)(2,1)S(1)}, u32[]{:S(2)}, u32[]{:S(2)}) collective-permute-start(bf16[2,2,32,16,128]{4,3,2,1,0:T(8,128)(2,1)} %get-tuple-element.29), channel_id=1, source_target_pairs={{4,0},{5,1},{6,2},{7,3},{8,4},{9,5},{10,6},{11,7},{12,8},{13,9},{1... | collective-permute-start | bytes 1572872 | tf_op jit(solution)/shard_map/ppermute | solution.py:216
  50.8 28.3 %collective-permute-start.9 = (bf16[2,2,32,16,128]{4,3,2,1,0:T(8,128)(2,1)}, bf16[2,2,32,16,128]{4,3,2,1,0:T(8,128)(2,1)}, u32[]{:S(2)}, u32[]{:S(2)}) collective-permute-start(bf16[2,2,32,16,128]{4,3,2,1,0:T(8,128)(2,1)} %get-tuple-element.30), channel_id=1, source_target_pairs={{0,4},{1,5},{2,6},{3,7},{4,8},{5,9},{6,10},{7,11},{8,12},{9,13},{1... | collective-permute-start | bytes 1572872 | tf_op jit(solution)/shard_map/ppermute | solution.py:216
  59.2 33.5 %copy-start = (bf16[2,2,32,16,128]{4,3,2,1,0:T(8,128)(2,1)}, bf16[2,2,32,16,128]{4,3,2,1,0:T(8,128)(2,1)S(1)}, u32[]{:S(2)}) copy-start(bf16[2,2,32,16,128]{4,3,2,1,0:T(8,128)(2,1)S(1)} %collective-permute-done.refs_1_) | copy-start | bytes 1572868
  59.2 8.6 %copy-start.5 = (bf16[2,2,32,16,128]{4,3,2,1,0:T(8,128)(2,1)}, bf16[2,2,32,16,128]{4,3,2,1,0:T(8,128)(2,1)S(1)}, u32[]{:S(2)}) copy-start(bf16[2,2,32,16,128]{4,3,2,1,0:T(8,128)(2,1)S(1)} %collective-permute-done.2.refs_3_) | copy-start | bytes 1572868
  61.6 31.0 %collective-permute-start.4 = (bf16[2,2,32,16,128]{4,3,2,1,0:T(8,128)(2,1)}, bf16[2,2,32,16,128]{4,3,2,1,0:T(8,128)(2,1)}, u32[]{:S(2)}, u32[]{:S(2)}) collective-permute-start(bf16[2,2,32,16,128]{4,3,2,1,0:T(8,128)(2,1)} %get-tuple-element.32), channel_id=1, source_target_pairs={{0,4},{1,5},{2,6},{3,7},{4,8},{5,9},{6,10},{7,11},{8,12},{9,13},{1... | collective-permute-start | bytes 1572872 | tf_op jit(solution)/shard_map/ppermute | solution.py:216
  62.9 29.7 %collective-permute-start.5 = (bf16[2,2,32,16,128]{4,3,2,1,0:T(8,128)(2,1)}, bf16[2,2,32,16,128]{4,3,2,1,0:T(8,128)(2,1)}, u32[]{:S(2)}, u32[]{:S(2)}) collective-permute-start(bf16[2,2,32,16,128]{4,3,2,1,0:T(8,128)(2,1)} %get-tuple-element.31), channel_id=1, source_target_pairs={{4,0},{5,1},{6,2},{7,3},{8,4},{9,5},{10,6},{11,7},{12,8},{13,9},{1... | collective-permute-start | bytes 1572872 | tf_op jit(solution)/shard_map/ppermute | solution.py:216
  79.0 0.8 copy-start.6

commit v3 on v0

v3 whole, which is shorter than its diff:
```python
import functools

import jax
import jax.numpy as jnp
from jax import lax
from jax.experimental import pallas as pl
from jax.experimental.pallas import tpu as pltpu
from jax.sharding import PartitionSpec as P

HMAX = 32
OFFSETS = 2 * HMAX + 1
GROUPS = 4
ROWS = 16
LANES = 128
TX = 8
TH = 4
SLOTS = 4
CHUNKS = 4
RLIM, SLIM, LLIM = 62, 40, 40


def regroup_kernel(group_ref, source_ref, receiver_ref, *refs):
    out_refs, (held, sems) = refs[:GROUPS], refs[GROUPS:]
    freqs, cells = source_ref.shape[1], source_ref.shape[2]
    share = cells // CHUNKS

    def fetch(field, chunk):
        ref = (source_ref, receiver_ref)[field]
        part = pl.ds(chunk * share, share)
        return pltpu.make_async_copy(ref.at[:, :, part], held.at[field, :, :, part], sems.at[field, chunk])

    for chunk in range(CHUNKS):
        for field in range(2):
            fetch(field, chunk).start()

    def regroup(order):
        low = lax.broadcasted_iota(jnp.int32, (8, LANES), 0) < 4
        for chunk in range(CHUNKS):
            for field in range(2):
                fetch(field, chunk).wait()

                def one_cell(x, _):
                    for f in range(freqs):
                        parts = [[None, None] for _ in range(GROUPS)]
                        for c in range(2):
                            near = held[field, c, f, x, :, :LANES].astype(jnp.float32)
                            far = held[field, c, f, x, :, LANES:].astype(jnp.float32)
                            for pair in range(2):
                                a = near[8 * pair : 8 * pair + 8]
                                b = far[8 * pair : 8 * pair + 8]
                                parts[2 * pair][c] = jnp.where(low, a, pltpu.roll(b, 4, 0))
                                parts[2 * pair + 1][c] = jnp.where(low, pltpu.roll(a, 4, 0), b)
                        for d in range(GROUPS):
                            out_refs[d][field, f, x] = jnp.concatenate(parts[order ^ d], axis=0).astype(jnp.bfloat16)
                    return 0

                lax.fori_loop(chunk * share, (chunk + 1) * share, one_cell, 0, unroll=2)

    for order in range(GROUPS):
        pl.when(group_ref[0] == order)(functools.partial(regroup, order))


def regrouped(group, source_field, receiver_field):
    two, freqs, cells, _, _ = source_field.shape
    return pl.pallas_call(
        regroup_kernel,
        in_specs=[pl.BlockSpec(memory_space=pltpu.SMEM)] + [pl.BlockSpec(memory_space=pltpu.HBM)] * 2,
        out_specs=[pl.BlockSpec(memory_space=pltpu.VMEM)] * GROUPS,
        out_shape=[jax.ShapeDtypeStruct((2, freqs, cells, ROWS, LANES), jnp.bfloat16)] * GROUPS,
        scratch_shapes=[pltpu.VMEM((2, 2, freqs, cells, 16, 2 * LANES), jnp.bfloat16), pltpu.SemaphoreType.DMA((2, CHUNKS))],
        compiler_params=pltpu.CompilerParams(vmem_limit_bytes=RLIM << 20),
        cost_estimate=pl.CostEstimate(flops=0, bytes_accessed=4 << 20, transcendentals=0),
        name="regroup",
    )(group, source_field, receiver_field)


def image_kernel(first, last, counts, side_ref, *refs):
    groups = len(counts)
    blocks = refs[: sum(counts)]
    refs = refs[sum(counts) :]
    if not first:
        before, refs = refs[0], refs[1:]
    out_ref, fields, raw, raw_sems = refs[:4]
    if last:
        turn, stage, sems = refs[4:]
    freqs, cells = blocks[0].shape[1], blocks[0].shape[2]
    total_freqs = freqs * groups

    def fetch(index):
        return pltpu.make_async_copy(blocks[index], raw.at[index], raw_sems.at[index])

    for index in range(sum(counts)):
        fetch(index).start()

    def widen(index, group, part):
        def one_cell(x, _):
            for field in range(2):
                for f in range(freqs):
                    fields[field, cells * part + x, freqs * group + f] = raw[index, field, f, x].astype(jnp.float32)
            return 0

        lax.fori_loop(0, cells, one_cell, 0, unroll=4)

    at = 0
    for group, count in enumerate(counts):
        for index in range(at, at + count):
            fetch(index).wait()
        left, own, right = at, at + 1, at + 2
        widen(own, group, 1)
        if count == 4:
            across = at + 3
            pl.when(side_ref[0] == 1)(functools.partial(widen, across, group, 0))
            pl.when(side_ref[0] == 0)(functools.partial(widen, left, group, 0))
            pl.when(side_ref[1] == 1)(functools.partial(widen, across, group, 2))
            pl.when(side_ref[1] == 0)(functools.partial(widen, right, group, 2))
        else:
            widen(left, group, 0)
            widen(right, group, 2)
        at += count

    def out_copy(k0, rows, slot):
        return pltpu.make_async_copy(stage.at[slot, :, pl.ds(0, rows)], out_ref.at[:, pl.ds(k0, rows)], sems.at[slot])

    def tile(k0, rows, x0, slot):
        s0 = x0 + 2 * HMAX - k0 - (rows - 1)
        r0 = x0 + k0
        if first:
            total = [[None] * TX for _ in range(rows)]
        else:
            total = [[before[k0 + j, x0 + i] for i in range(TX)] for j in range(rows)]
        for f in range(total_freqs):
            for c in range(2):
                s = [fields[0, s0 + i, f, 8 * c : 8 * c + 8] for i in range(TX + rows - 1)]
                r = [fields[1, r0 + i, f, 8 * c : 8 * c + 8] for i in range(TX + rows - 1)]
                for j in range(rows):
                    for i in range(TX):
                        product = s[i + rows - 1 - j] * r[i + j]
                        total[j][i] = product if total[j][i] is None else total[j][i] + product
        for j in range(rows):
            if not last:
                for i in range(TX):
                    out_ref[k0 + j, x0 + i] = total[j][i]
                continue
            for i in range(TX):
                turn[j, pl.ds(i, 8, stride=TX)] = 0.25 * total[j][i]
            for zh in range(2):
                for y in range(4):
                    row = zh * 4 + y
                    stage[slot, y, j, pl.ds(pl.multiple_of(x0, TX), TX), zh * LANES : (zh + 1) * LANES] = turn[
                        j, row * TX : (row + 1) * TX
                    ]

    def band(k0, rows, slot):
        def x_step(xt, _):
            tile(k0, rows, xt * TX, slot)
            return 0

        lax.fori_loop(0, cells // TX, x_step, 0)

    steps = OFFSETS // TH

    def h_step(step, _):
        slot = lax.rem(step, SLOTS)
        if last:

            @pl.when(step >= SLOTS)
            def _():
                out_copy(TH * (step - SLOTS), TH, slot).wait()

        band(TH * step, TH, slot)
        if last:
            out_copy(TH * step, TH, slot).start()
        return 0

    lax.fori_loop(0, steps, h_step, 0)
    rest = OFFSETS - TH * steps
    if last:
        out_copy(TH * (steps - SLOTS), TH, steps % SLOTS).wait()
    band(TH * steps, rest, steps % SLOTS)
    if last:
        out_copy(TH * steps, rest, steps % SLOTS).start()
        for step in range(steps - SLOTS + 1, steps):
            out_copy(TH * step, TH, step % SLOTS).wait()
        out_copy(TH * steps, rest, steps % SLOTS).wait()


def image(side, blocks, before, last):
    two, freqs, cells, _, _ = blocks[0][0].shape
    counts = tuple(len(group) for group in blocks)
    first = before is None
    out_shape = (4, OFFSETS, cells, 2 * LANES) if last else (OFFSETS, cells, 8, LANES)
    scratch = [
        pltpu.VMEM((2, 3 * cells, freqs * len(blocks), ROWS, LANES), jnp.float32),
        pltpu.VMEM((sum(counts), 2, freqs, cells, ROWS, LANES), jnp.bfloat16),
        pltpu.SemaphoreType.DMA((sum(counts),)),
    ]
    if last:
        scratch += [
            pltpu.VMEM((TH, 8 * TX, LANES), jnp.float32),
            pltpu.VMEM((SLOTS, 4, TH, cells, 2 * LANES), jnp.float32),
            pltpu.SemaphoreType.DMA((SLOTS,)),
        ]
    operands = [block for group in blocks for block in group] + ([] if first else [before])
    vmem = pl.BlockSpec(memory_space=pltpu.VMEM)
    hbm = pl.BlockSpec(memory_space=pltpu.HBM)
    return pl.pallas_call(
        functools.partial(image_kernel, first, last, counts),
        in_specs=[pl.BlockSpec(memory_space=pltpu.SMEM)] + [hbm] * sum(counts) + ([] if first else [vmem]),
        out_specs=hbm if last else vmem,
        out_shape=jax.ShapeDtypeStruct(out_shape, jnp.float32),
        scratch_shapes=scratch,
        input_output_aliases={} if first or last else {len(operands): 0},
        compiler_params=pltpu.CompilerParams(vmem_limit_bytes=(LLIM if last else SLIM) << 20),
        cost_estimate=pl.CostEstimate(flops=17_000_000 * len(blocks), bytes_accessed=9 << 20, transcendentals=0),
        name="image_last" if last else "image_sum",
    )(side, *operands)


def body(source_field, receiver_field):
    slabs = lax.axis_size("slab")
    middle = slabs // 2
    group = lax.axis_index("freq").astype(jnp.int32)
    slab = lax.axis_index("slab")
    side = jnp.stack([slab == middle, slab == middle - 1]).astype(jnp.int32)
    parts = list(regrouped(group[None], source_field, receiver_field))
    owned = [parts[0]] + [
        lax.ppermute(parts[d], "freq", [(g, g ^ d) for g in range(GROUPS)]) for d in range(1, GROUPS)
    ]

    def rim(d, step):
        cut = middle - 1 if step > 0 else middle
        pairs = [(s, s + step) for s in range(slabs) if 0 <= s + step < slabs and (d == 0 or s != cut)]
        return lax.ppermute(owned[d], "slab", pairs)

    def across(d):
        value, turn = (parts[d], d) if d >= 2 else (owned[d], 0)
        pairs = []
        for g in range(GROUPS):
            pairs.append(((middle - 1) * GROUPS + g, middle * GROUPS + (g ^ turn)))
            pairs.append((middle * GROUPS + g, (middle - 1) * GROUPS + (g ^ turn)))
        return lax.ppermute(value, ("slab", "freq"), pairs)

    blocks = []
    for d in range(GROUPS):
        if d >= 2:
            ahead = blocks[d - 2]
            owned[d], ahead[0], ahead[2] = lax.optimization_barrier((owned[d], ahead[0], ahead[2]))
        blocks.append([rim(d, 1), owned[d], rim(d, -1)])
        if d:
            blocks[d].append(across(d))
    total = image(side, blocks[:3], None, False)
    return image(side, blocks[3:], total, True)


def solution(mesh):
    in_specs = (P(None, "freq", "slab", None, None), P(None, "freq", "slab", None, None))
    out_specs = P("freq", None, "slab", None)
    return jax.shard_map(body, mesh=mesh, in_specs=in_specs, out_specs=out_specs, check_vma=False)
```

time: 132 us -> 88.4 us (0.67)
  other arithmetic: 35.9 us -> 0.07 us
  starting transfers between devices: 12.7 us -> 43.9 us
  blocking collectives: 30.6 us -> 0 us
  waiting for transfers between devices: 44.5 us -> 14.4 us
  Pallas kernels: 0 us -> 22.8 us
    ppermute x2 -> x14, starting transfers between devices: 12.7 us -> 43.9 us  [the longest x8 28.5 us: rim(): return lax.ppermute(owned[d], 'slab', pairs)]
    all_to_all x1 -> x0, blocking collectives: 30.6 us -> none  [to_columns(): lax.all_to_all(both_fields, 'freq', split_axis=4, concat_axis=2, tiled=True)]
    ppermute x2 -> x14, waiting for transfers between devices: 44.5 us -> 14.4 us  [the longest x3 9.02 us: across(): return lax.ppermute(value, ('slab', 'freq'), pairs)]
    reduce_sum x8 -> x0, other arithmetic: 29.2 us -> none  [local_image(): pictures.append(0.25 * jnp.sum(product, axis=(0, 1)))]
    pallas_call x0 -> x3, Pallas kernels: none -> 22.8 us  [the longest x2 19.8 us: image(): pl.pallas_call(functools.partial(image_kernel, first, last, counts), in_s...]
    transpose x1 -> x0, other arithmetic: 5.06 us -> none  [local_image(): reordered = jnp.transpose(padded, (0, 1, 2, 4, 3, 5))]
    unnamed x2 -> x14, local copies, waits for them, and re-layouts: 3.43 us -> 6.53 us
    another operation x1 -> x0, local copies, waits for them, and re-layouts: 2.26 us -> none  [body(): both_fields = jnp.stack([source_field, receiver_field])]
  transfers between devices with their start and end apart: 2 -> 14, of which waited for: 2 -> 3; matrix products, arithmetic and copies ran while one was open for 0% -> 0% of each run, Pallas kernels for 0% -> 13%
where the time goes in v3:
time: 88.4 us; the launch traced here: 87.8 us
  starting transfers between devices  43.9 us (50%)
  Pallas kernels  22.8 us (26%)
  waiting for transfers between devices  14.4 us (16%)
  local copies, waits for them, and re-layouts  6.53 us (7%)
    ppermute x8, starting transfers between devices, rim(): return lax.ppermute(owned[d], 'slab', pairs)  28.5 us
    pallas_call x2, Pallas kernels, image(): pl.pallas_call(functools.partial(image_kernel, first, last, counts), in_s...  19.8 us
    ppermute x3, starting transfers between devices, across(): return lax.ppermute(value, ('slab', 'freq'), pairs)  12.8 us
    ppermute x3, waiting for transfers between devices, across(): return lax.ppermute(value, ('slab', 'freq'), pairs)  9.02 us
    unnamed x14, local copies, waits for them, and re-layouts  6.53 us
    ppermute x8, waiting for transfers between devices, rim(): return lax.ppermute(owned[d], 'slab', pairs)  5.32 us
    pallas_call x1, Pallas kernels, regrouped(): pl.pallas_call(regroup_kernel, in_specs=[pl.BlockSpec(memory_space=pltpu....  2.98 us
    ppermute x3, starting transfers between devices, body(): lax.ppermute(parts[d], 'freq', [(g, g ^ d) for g in range(GROUPS)])  2.55 us
  transfers between devices with their start and end apart: 14, of which 3 were waited for; matrix products, arithmetic and copies ran while one was open for 0% of the time, Pallas kernels for 13%

profile of v3, /device:TPU:8, one launch (start us, length us, event | category | flops | bytes accessed | tf_op | source)
XLA Modules:
  0.0 87.8 jit_solution(7570041961952251338)
XLA Ops:
  0.0 3.0 %regroup.1 = (bf16[2,2,32,16,128]{4,3,2,1,0:T(8,128)(2,1)}, bf16[2,2,32,16,128]{4,3,2,1,0:T(8,128)(2,1)}, bf16[2,2,32,16,128]{4,3,2,1,0:T(8,128)(2,1)}, bf16[2,2,32,16,128]{4,3,2,1,0:T(8,128)(2,1)}) custom-call(s32[1]{0:T(128)} %bitcast.2.group_ref, bf16[2,2,32,16,256]{4,3,2,1,0:T(8,128)(2,1)} %source_ref.1, bf16[2,2,32,16,256]{4,3,2,1,0:T(8,128)(2,1)} %receiver_ref.1), custom_call_target="tpu_custom_call" | custom-call | bytes 4194304 | tf_op jit(solution)/shard_map/regroup/pallas_call | solution.py:65
  3.0 0.1 collective-permute-start.1
  3.1 2.4 %collective-permute-start.7 = (bf16[2,2,32,16,128]{4,3,2,1,0:T(8,128)(2,1)}, bf16[2,2,32,16,128]{4,3,2,1,0:T(8,128)(2,1)S(1)}, u32[]{:S(2)}, u32[]{:S(2)}) collective-permute-start(bf16[2,2,32,16,128]{4,3,2,1,0:T(8,128)(2,1)} %get-tuple-element.18), channel_id=1, source_target_pairs={{0,2},{1,3},{2,0},{3,1},{4,6},{5,7},{6,4},{7,5},{8,10},{9,11},{10,... | collective-permute-start | bytes 1572872 | tf_op jit(solution)/shard_map/ppermute | solution.py:227
  5.5 10.7 %collective-permute-start.9 = (bf16[2,2,32,16,128]{4,3,2,1,0:T(8,128)(2,1)}, bf16[2,2,32,16,128]{4,3,2,1,0:T(8,128)(2,1)S(1)}, u32[]{:S(2)}, u32[]{:S(2)}) collective-permute-start(bf16[2,2,32,16,128]{4,3,2,1,0:T(8,128)(2,1)} %get-tuple-element.19.refs_1_), channel_id=1, source_target_pairs={{4,0},{8,4},{12,8},{16,12},{20,16},{24,20},{28,24},{32,28},{36,32}... | collective-permute-start | bytes 1572872 | tf_op jit(solution)/shard_map/ppermute | solution.py:233
  16.2 1.9 %collective-permute-start.8 = (bf16[2,2,32,16,128]{4,3,2,1,0:T(8,128)(2,1)}, bf16[2,2,32,16,128]{4,3,2,1,0:T(8,128)(2,1)S(1)}, u32[]{:S(2)}, u32[]{:S(2)}) collective-permute-start(bf16[2,2,32,16,128]{4,3,2,1,0:T(8,128)(2,1)} %get-tuple-element.19.refs_1_), channel_id=1, source_target_pairs={{0,4},{4,8},{8,12},{12,16},{16,20},{20,24},{24,28},{28,32},{32,36}... | collective-permute-start | bytes 1572872 | tf_op jit(solution)/shard_map/ppermute | solution.py:233
  18.1 0.1 collective-permute-start
  18.2 0.0 collective-permute-done.1.refs_4_
  18.2 1.3 %collective-permute-start.3 = (bf16[2,2,32,16,128]{4,3,2,1,0:T(8,128)(2,1)S(1)}, bf16[2,2,32,16,128]{4,3,2,1,0:T(8,128)(2,1)S(1)}, u32[]{:S(2)}, u32[]{:S(2)}) collective-permute-start(bf16[2,2,32,16,128]{4,3,2,1,0:T(8,128)(2,1)S(1)} %collective-permute-done.1.refs_4_), channel_id=1, source_target_pairs={{4,0},{8,4},{12,8},{16,12},{20,16},{24,20},{28,24},{32,28},{36,32}... | collective-permute-start | bytes 1572872 | tf_op jit(solution)/shard_map/ppermute | solution.py:233
  19.5 0.0 collective-permute-done.7.refs_8_
  19.5 4.6 %collective-permute-start.2 = (bf16[2,2,32,16,128]{4,3,2,1,0:T(8,128)(2,1)S(1)}, bf16[2,2,32,16,128]{4,3,2,1,0:T(8,128)(2,1)S(1)}, u32[]{:S(2)}, u32[]{:S(2)}) collective-permute-start(bf16[2,2,32,16,128]{4,3,2,1,0:T(8,128)(2,1)S(1)} %collective-permute-done.1.refs_4_), channel_id=1, source_target_pairs={{0,4},{4,8},{8,12},{12,16},{16,20},{20,24},{24,28},{28,32},{32,36}... | collective-permute-start | bytes 1572872 | tf_op jit(solution)/shard_map/ppermute | solution.py:233
  24.1 3.9 %collective-permute-done.9.refs_2_ = bf16[2,2,32,16,128]{4,3,2,1,0:T(8,128)(2,1)S(1)} collective-permute-done((bf16[2,2,32,16,128]{4,3,2,1,0:T(8,128)(2,1)}, bf16[2,2,32,16,128]{4,3,2,1,0:T(8,128)(2,1)S(1)}, u32[]{:S(2)}, u32[]{:S(2)}) %collective-permute-start.9) | collective-permute-done | bytes 524320 | tf_op jit(solution)/shard_map/ppermute | solution.py:233
  28.0 6.9 %collective-permute-start.13 = (bf16[2,2,32,16,128]{4,3,2,1,0:T(8,128)(2,1)}, bf16[2,2,32,16,128]{4,3,2,1,0:T(8,128)(2,1)S(1)}, u32[]{:S(2)}, u32[]{:S(2)}) collective-permute-start(bf16[2,2,32,16,128]{4,3,2,1,0:T(8,128)(2,1)} %get-tuple-element.18), channel_id=1, source_target_pairs={{124,130},{128,126},{125,131},{129,127},{126,128},{130,124},{127,1... | collective-permute-start | bytes 1572872 | tf_op jit(solution)/shard_map/ppermute | solution.py:241
  34.9 1.5 %collective-permute-done.8.refs_0_ = bf16[2,2,32,16,128]{4,3,2,1,0:T(8,128)(2,1)S(1)} collective-permute-done((bf16[2,2,32,16,128]{4,3,2,1,0:T(8,128)(2,1)}, bf16[2,2,32,16,128]{4,3,2,1,0:T(8,128)(2,1)S(1)}, u32[]{:S(2)}, u32[]{:S(2)}) %collective-permute-start.8) | collective-permute-done | bytes 524320 | tf_op jit(solution)/shard_map/ppermute | solution.py:233
  36.3 2.2 %collective-permute-start.10 = (bf16[2,2,32,16,128]{4,3,2,1,0:T(8,128)(2,1)S(1)}, bf16[2,2,32,16,128]{4,3,2,1,0:T(8,128)(2,1)S(1)}, u32[]{:S(2)}, u32[]{:S(2)}) collective-permute-start(bf16[2,2,32,16,128]{4,3,2,1,0:T(8,128)(2,1)S(1)} %collective-permute-done.1.refs_4_), channel_id=1, source_target_pairs={{124,128},{128,124},{125,129},{129,125},{126,130},{130,126},{127,1... | collective-permute-start | bytes 1572872 | tf_op jit(solution)/shard_map/ppermute | solution.py:241
  38.5 0.0 collective-permute-done.refs_1_
  38.5 1.3 %collective-permute-start.12 = (bf16[2,2,32,16,128]{4,3,2,1,0:T(8,128)(2,1)S(1)}, bf16[2,2,32,16,128]{4,3,2,1,0:T(8,128)(2,1)}, u32[]{:S(2)}, u32[]{:S(2)}) collective-permute-start(bf16[2,2,32,16,128]{4,3,2,1,0:T(8,128)(2,1)S(1)} %collective-permute-done.7.refs_8_), channel_id=1, source_target_pairs={{4,0},{8,4},{12,8},{16,12},{20,16},{24,20},{28,24},{32,28},{36,32}... | collective-permute-start | bytes 1572872 | tf_op jit(solution)/shard_map/ppermute | solution.py:233
  39.8 0.0 collective-permute-done.3.refs_5_
  39.8 5.4 %collective-permute-start.11 = (bf16[2,2,32,16,128]{4,3,2,1,0:T(8,128)(2,1)S(1)}, bf16[2,2,32,16,128]{4,3,2,1,0:T(8,128)(2,1)}, u32[]{:S(2)}, u32[]{:S(2)}) collective-permute-start(bf16[2,2,32,16,128]{4,3,2,1,0:T(8,128)(2,1)S(1)} %collective-permute-done.7.refs_8_), channel_id=1, source_target_pairs={{0,4},{4,8},{8,12},{12,16},{16,20},{20,24},{24,28},{28,32},{32,36}... | collective-permute-start | bytes 1572872 | tf_op jit(solution)/shard_map/ppermute | solution.py:233
  45.2 0.0 collective-permute-done.2.refs_3_
  45.2 0.0 copy-start.1
  45.2 0.8 copy-done.1
  46.0 3.8 %collective-permute-start.6 = (bf16[2,2,32,16,128]{4,3,2,1,0:T(8,128)(2,1)}, bf16[2,2,32,16,128]{4,3,2,1,0:T(8,128)(2,1)}, u32[]{:S(2)}, u32[]{:S(2)}) collective-permute-start(bf16[2,2,32,16,128]{4,3,2,1,0:T(8,128)(2,1)} %get-tuple-element.15), channel_id=1, source_target_pairs={{124,131},{128,127},{125,130},{129,126},{126,129},{130,125},{127,1... | collective-permute-start | bytes 1572872 | tf_op jit(solution)/shard_map/ppermute | solution.py:241
  49.8 0.0 collective-permute-done.13.refs_10_
  49.8 0.0 copy-start.3
  49.8 0.8 copy-done.3
  50.5 1.3 %collective-permute-start.5 = (bf16[2,2,32,16,128]{4,3,2,1,0:T(8,128)(2,1)S(1)}, bf16[2,2,32,16,128]{4,3,2,1,0:T(8,128)(2,1)}, u32[]{:S(2)}, u32[]{:S(2)}) collective-permute-start(bf16[2,2,32,16,128]{4,3,2,1,0:T(8,128)(2,1)S(1)} %collective-permute-done.refs_1_), channel_id=1, source_target_pairs={{4,0},{8,4},{12,8},{16,12},{20,16},{24,20},{28,24},{32,28},{36,32}... | collective-permute-start | bytes 1572872 | tf_op jit(solution)/shard_map/ppermute | solution.py:233
  51.8 9.0 %collective-permute-done.10.refs_6_ = bf16[2,2,32,16,128]{4,3,2,1,0:T(8,128)(2,1)S(1)} collective-permute-done((bf16[2,2,32,16,128]{4,3,2,1,0:T(8,128)(2,1)S(1)}, bf16[2,2,32,16,128]{4,3,2,1,0:T(8,128)(2,1)S(1)}, u32[]{:S(2)}, u32[]{:S(2)}) %collective-permute-start.10) | collective-permute-done | bytes 524320 | tf_op jit(solution)/shard_map/ppermute | solution.py:241
  60.9 0.0 copy-start.5
  60.9 0.8 copy-done.5
  61.7 2.1 %collective-permute-start.4 = (bf16[2,2,32,16,128]{4,3,2,1,0:T(8,128)(2,1)S(1)}, bf16[2,2,32,16,128]{4,3,2,1,0:T(8,128)(2,1)}, u32[]{:S(2)}, u32[]{:S(2)}) collective-permute-start(bf16[2,2,32,16,128]{4,3,2,1,0:T(8,128)(2,1)S(1)} %collective-permute-done.refs_1_), channel_id=1, source_target_pairs={{0,4},{4,8},{8,12},{12,16},{16,20},{20,24},{24,28},{28,32},{32,36}... | collective-permute-start | bytes 1572872 | tf_op jit(solution)/shard_map/ppermute | solution.py:233
  63.7 0.1 add_convert_fusion.side_ref
  63.8 0.0 collective-permute-done.12.refs_9_
  63.8 0.0 collective-permute-done.11.refs_7_
  63.8 0.0 copy-start
  63.8 1.0 %copy-done = bf16[2,2,32,16,128]{4,3,2,1,0:T(8,128)(2,1)S(1)} copy-done((bf16[2,2,32,16,128]{4,3,2,1,0:T(8,128)(2,1)S(1)}, bf16[2,2,32,16,128]{4,3,2,1,0:T(8,128)(2,1)}, u32[]{:S(2)}) %copy-start) | copy-done | bytes 524312
  64.9 0.0 copy-start.2
  64.9 1.0 %copy-done.2 = bf16[2,2,32,16,128]{4,3,2,1,0:T(8,128)(2,1)S(1)} copy-done((bf16[2,2,32,16,128]{4,3,2,1,0:T(8,128)(2,1)S(1)}, bf16[2,2,32,16,128]{4,3,2,1,0:T(8,128)(2,1)}, u32[]{:S(2)}) %copy-start.2) | copy-done | bytes 524312
  65.9 0.0 copy-start.4
  65.9 1.0 %copy-done.4 = bf16[2,2,32,16,128]{4,3,2,1,0:T(8,128)(2,1)S(1)} copy-done((bf16[2,2,32,16,128]{4,3,2,1,0:T(8,128)(2,1)S(1)}, bf16[2,2,32,16,128]{4,3,2,1,0:T(8,128)(2,1)}, u32[]{:S(2)}) %copy-start.4) | copy-done | bytes 524312
  66.9 0.0 copy-start.6
  66.9 1.0 %copy-done.6 = bf16[2,2,32,16,128]{4,3,2,1,0:T(8,128)(2,1)S(1)} copy-done((bf16[2,2,32,16,128]{4,3,2,1,0:T(8,128)(2,1)S(1)}, bf16[2,2,32,16,128]{4,3,2,1,0:T(8,128)(2,1)}, u32[]{:S(2)}) %copy-start.6) | copy-done | bytes 524312
  68.0 11.2 %image_sum.1.refs_4_ = f32[65,32,8,128]{3,2,1,0:T(8,128)S(1)} custom-call(s32[2]{0:T(128)S(1)} %add_convert_fusion.side_ref, bf16[2,2,32,16,128]{4,3,2,1,0:T(8,128)(2,1)S(1)} %collective-permute-done.8.refs_0_, bf16[2,2,32,16,128]{4,3,2,1,0:T(8,128)(2,1)S(1)} %copy-done, bf16[2,2,32,16,128]{4,3,2,1,0:T(8,128)(2,1)S(1)} %collective-permute-done.9.refs_2_, ...), custom_call_target="tpu_custom_call" | custom-call | flops 51000000 | bytes 9437184 | tf_op jit(solution)/shard_map/image_sum/pallas_call | solution.py:206
  79.2 0.0 collective-permute-done.6.refs_3_
  79.2 0.0 collective-permute-done.5.refs_2_
  79.2 0.0 collective-permute-done.4.refs_0_
  79.2 8.6 %image_last.1 = f32[4,65,32,256]{3,2,1,0:T(8,128)} custom-call(s32[2]{0:T(128)S(1)} %add_convert_fusion.side_ref, bf16[2,2,32,16,128]{4,3,2,1,0:T(8,128)(2,1)} %collective-permute-done.4.refs_0_, bf16[2,2,32,16,128]{4,3,2,1,0:T(8,128)(2,1)S(1)} %collective-permute-done.refs_1_, bf16[2,2,32,16,128]{4,3,2,1,0:T(8,128)(2,1)} %collective-permute-done.5.refs_2_, ...), custom_call_target="tpu_custom_call" | custom-call | flops 17000000 | bytes 9437184 | tf_op jit(solution)/shard_map/image_last/pallas_call | solution.py:206
Async XLA Ops:
  3.0 15.2 %collective-permute-start.1 = (bf16[2,2,32,16,128]{4,3,2,1,0:T(8,128)(2,1)}, bf16[2,2,32,16,128]{4,3,2,1,0:T(8,128)(2,1)S(1)}, u32[]{:S(2)}, u32[]{:S(2)}) collective-permute-start(bf16[2,2,32,16,128]{4,3,2,1,0:T(8,128)(2,1)} %get-tuple-element.16), channel_id=1, source_target_pairs={{0,1},{1,0},{2,3},{3,2},{4,5},{5,4},{6,7},{7,6},{8,9},{9,8},{10,11... | collective-permute-start | bytes 1572872 | tf_op jit(solution)/shard_map/ppermute | solution.py:227
  3.1 16.4 %collective-permute-start.7 = (bf16[2,2,32,16,128]{4,3,2,1,0:T(8,128)(2,1)}, bf16[2,2,32,16,128]{4,3,2,1,0:T(8,128)(2,1)S(1)}, u32[]{:S(2)}, u32[]{:S(2)}) collective-permute-start(bf16[2,2,32,16,128]{4,3,2,1,0:T(8,128)(2,1)} %get-tuple-element.18), channel_id=1, source_target_pairs={{0,2},{1,3},{2,0},{3,1},{4,6},{5,7},{6,4},{7,5},{8,10},{9,11},{10,... | collective-permute-start | bytes 1572872 | tf_op jit(solution)/shard_map/ppermute | solution.py:227
  5.5 22.5 %collective-permute-start.9 = (bf16[2,2,32,16,128]{4,3,2,1,0:T(8,128)(2,1)}, bf16[2,2,32,16,128]{4,3,2,1,0:T(8,128)(2,1)S(1)}, u32[]{:S(2)}, u32[]{:S(2)}) collective-permute-start(bf16[2,2,32,16,128]{4,3,2,1,0:T(8,128)(2,1)} %get-tuple-element.19.refs_1_), channel_id=1, source_target_pairs={{4,0},{8,4},{12,8},{16,12},{20,16},{24,20},{28,24},{32,28},{36,32}... | collective-permute-start | bytes 1572872 | tf_op jit(solution)/shard_map/ppermute | solution.py:233
  16.2 20.1 %collective-permute-start.8 = (bf16[2,2,32,16,128]{4,3,2,1,0:T(8,128)(2,1)}, bf16[2,2,32,16,128]{4,3,2,1,0:T(8,128)(2,1)S(1)}, u32[]{:S(2)}, u32[]{:S(2)}) collective-permute-start(bf16[2,2,32,16,128]{4,3,2,1,0:T(8,128)(2,1)} %get-tuple-element.19.refs_1_), channel_id=1, source_target_pairs={{0,4},{4,8},{8,12},{12,16},{16,20},{20,24},{24,28},{28,32},{32,36}... | collective-permute-start | bytes 1572872 | tf_op jit(solution)/shard_map/ppermute | solution.py:233
  18.1 20.4 %collective-permute-start = (bf16[2,2,32,16,128]{4,3,2,1,0:T(8,128)(2,1)}, bf16[2,2,32,16,128]{4,3,2,1,0:T(8,128)(2,1)S(1)}, u32[]{:S(2)}, u32[]{:S(2)}) collective-permute-start(bf16[2,2,32,16,128]{4,3,2,1,0:T(8,128)(2,1)} %get-tuple-element.15), channel_id=1, source_target_pairs={{0,3},{1,2},{2,1},{3,0},{4,7},{5,6},{6,5},{7,4},{8,11},{9,10},{10,... | collective-permute-start | bytes 1572872 | tf_op jit(solution)/shard_map/ppermute | solution.py:227
  18.2 21.6 %collective-permute-start.3 = (bf16[2,2,32,16,128]{4,3,2,1,0:T(8,128)(2,1)S(1)}, bf16[2,2,32,16,128]{4,3,2,1,0:T(8,128)(2,1)S(1)}, u32[]{:S(2)}, u32[]{:S(2)}) collective-permute-start(bf16[2,2,32,16,128]{4,3,2,1,0:T(8,128)(2,1)S(1)} %collective-permute-done.1.refs_4_), channel_id=1, source_target_pairs={{4,0},{8,4},{12,8},{16,12},{20,16},{24,20},{28,24},{32,28},{36,32}... | collective-permute-start | bytes 1572872 | tf_op jit(solution)/shard_map/ppermute | solution.py:233
  19.5 25.7 %collective-permute-start.2 = (bf16[2,2,32,16,128]{4,3,2,1,0:T(8,128)(2,1)S(1)}, bf16[2,2,32,16,128]{4,3,2,1,0:T(8,128)(2,1)S(1)}, u32[]{:S(2)}, u32[]{:S(2)}) collective-permute-start(bf16[2,2,32,16,128]{4,3,2,1,0:T(8,128)(2,1)S(1)} %collective-permute-done.1.refs_4_), channel_id=1, source_target_pairs={{0,4},{4,8},{8,12},{12,16},{16,20},{20,24},{24,28},{28,32},{32,36}... | collective-permute-start | bytes 1572872 | tf_op jit(solution)/shard_map/ppermute | solution.py:233
  28.0 21.8 %collective-permute-start.13 = (bf16[2,2,32,16,128]{4,3,2,1,0:T(8,128)(2,1)}, bf16[2,2,32,16,128]{4,3,2,1,0:T(8,128)(2,1)S(1)}, u32[]{:S(2)}, u32[]{:S(2)}) collective-permute-start(bf16[2,2,32,16,128]{4,3,2,1,0:T(8,128)(2,1)} %get-tuple-element.18), channel_id=1, source_target_pairs={{124,130},{128,126},{125,131},{129,127},{126,128},{130,124},{127,1... | collective-permute-start | bytes 1572872 | tf_op jit(solution)/shard_map/ppermute | solution.py:241
  36.3 24.5 %collective-permute-start.10 = (bf16[2,2,32,16,128]{4,3,2,1,0:T(8,128)(2,1)S(1)}, bf16[2,2,32,16,128]{4,3,2,1,0:T(8,128)(2,1)S(1)}, u32[]{:S(2)}, u32[]{:S(2)}) collective-permute-start(bf16[2,2,32,16,128]{4,3,2,1,0:T(8,128)(2,1)S(1)} %collective-permute-done.1.refs_4_), channel_id=1, source_target_pairs={{124,128},{128,124},{125,129},{129,125},{126,130},{130,126},{127,1... | collective-permute-start | bytes 1572872 | tf_op jit(solution)/shard_map/ppermute | solution.py:241
  38.5 25.3 %collective-permute-start.12 = (bf16[2,2,32,16,128]{4,3,2,1,0:T(8,128)(2,1)S(1)}, bf16[2,2,32,16,128]{4,3,2,1,0:T(8,128)(2,1)}, u32[]{:S(2)}, u32[]{:S(2)}) collective-permute-start(bf16[2,2,32,16,128]{4,3,2,1,0:T(8,128)(2,1)S(1)} %collective-permute-done.7.refs_8_), channel_id=1, source_target_pairs={{4,0},{8,4},{12,8},{16,12},{20,16},{24,20},{28,24},{32,28},{36,32}... | collective-permute-start | bytes 1572872 | tf_op jit(solution)/shard_map/ppermute | solution.py:233
  39.8 24.0 %collective-permute-start.11 = (bf16[2,2,32,16,128]{4,3,2,1,0:T(8,128)(2,1)S(1)}, bf16[2,2,32,16,128]{4,3,2,1,0:T(8,128)(2,1)}, u32[]{:S(2)}, u32[]{:S(2)}) collective-permute-start(bf16[2,2,32,16,128]{4,3,2,1,0:T(8,128)(2,1)S(1)} %collective-permute-done.7.refs_8_), channel_id=1, source_target_pairs={{0,4},{4,8},{8,12},{12,16},{16,20},{20,24},{24,28},{28,32},{32,36}... | collective-permute-start | bytes 1572872 | tf_op jit(solution)/shard_map/ppermute | solution.py:233
  45.2 0.8 copy-start.1
  46.0 33.2 %collective-permute-start.6 = (bf16[2,2,32,16,128]{4,3,2,1,0:T(8,128)(2,1)}, bf16[2,2,32,16,128]{4,3,2,1,0:T(8,128)(2,1)}, u32[]{:S(2)}, u32[]{:S(2)}) collective-permute-start(bf16[2,2,32,16,128]{4,3,2,1,0:T(8,128)(2,1)} %get-tuple-element.15), channel_id=1, source_target_pairs={{124,131},{128,127},{125,130},{129,126},{126,129},{130,125},{127,1... | collective-permute-start | bytes 1572872 | tf_op jit(solution)/shard_map/ppermute | solution.py:241
  49.8 0.8 copy-start.3
  50.5 28.6 %collective-permute-start.5 = (bf16[2,2,32,16,128]{4,3,2,1,0:T(8,128)(2,1)S(1)}, bf16[2,2,32,16,128]{4,3,2,1,0:T(8,128)(2,1)}, u32[]{:S(2)}, u32[]{:S(2)}) collective-permute-start(bf16[2,2,32,16,128]{4,3,2,1,0:T(8,128)(2,1)S(1)} %collective-permute-done.refs_1_), channel_id=1, source_target_pairs={{4,0},{8,4},{12,8},{16,12},{20,16},{24,20},{28,24},{32,28},{36,32}... | collective-permute-start | bytes 1572872 | tf_op jit(solution)/shard_map/ppermute | solution.py:233
  60.9 0.8 copy-start.5
  61.7 17.5 %collective-permute-start.4 = (bf16[2,2,32,16,128]{4,3,2,1,0:T(8,128)(2,1)S(1)}, bf16[2,2,32,16,128]{4,3,2,1,0:T(8,128)(2,1)}, u32[]{:S(2)}, u32[]{:S(2)}) collective-permute-start(bf16[2,2,32,16,128]{4,3,2,1,0:T(8,128)(2,1)S(1)} %collective-permute-done.refs_1_), channel_id=1, source_target_pairs={{0,4},{4,8},{8,12},{12,16},{16,20},{20,24},{24,28},{28,32},{32,36}... | collective-permute-start | bytes 1572872 | tf_op jit(solution)/shard_map/ppermute | solution.py:233
  63.8 1.0 %copy-start = (bf16[2,2,32,16,128]{4,3,2,1,0:T(8,128)(2,1)S(1)}, bf16[2,2,32,16,128]{4,3,2,1,0:T(8,128)(2,1)}, u32[]{:S(2)}) copy-start(bf16[2,2,32,16,128]{4,3,2,1,0:T(8,128)(2,1)} %get-tuple-element.19.refs_1_) | copy-start | bytes 1572868
  64.9 1.0 %copy-start.2 = (bf16[2,2,32,16,128]{4,3,2,1,0:T(8,128)(2,1)S(1)}, bf16[2,2,32,16,128]{4,3,2,1,0:T(8,128)(2,1)}, u32[]{:S(2)}) copy-start(bf16[2,2,32,16,128]{4,3,2,1,0:T(8,128)(2,1)} %copy-done.1) | copy-start | bytes 1572868
  65.9 1.0 %copy-start.4 = (bf16[2,2,32,16,128]{4,3,2,1,0:T(8,128)(2,1)S(1)}, bf16[2,2,32,16,128]{4,3,2,1,0:T(8,128)(2,1)}, u32[]{:S(2)}) copy-start(bf16[2,2,32,16,128]{4,3,2,1,0:T(8,128)(2,1)} %copy-done.3) | copy-start | bytes 1572868
  66.9 1.0 %copy-start.6 = (bf16[2,2,32,16,128]{4,3,2,1,0:T(8,128)(2,1)S(1)}, bf16[2,2,32,16,128]{4,3,2,1,0:T(8,128)(2,1)}, u32[]{:S(2)}) copy-start(bf16[2,2,32,16,128]{4,3,2,1,0:T(8,128)(2,1)} %copy-done.5) | copy-start | bytes 1572868

commit v4 on v3

v4 whole, which is shorter than its diff:
```python
import functools

import jax
import jax.numpy as jnp
from jax import lax
from jax.experimental import pallas as pl
from jax.experimental.pallas import tpu as pltpu
from jax.sharding import PartitionSpec as P

HMAX = 32
OFFSETS = 2 * HMAX + 1
GROUPS = 4
ROWS = 16
LANES = 128
TX = 8
TH = 4
SLOTS = 4
CHUNKS = 4
NEAR = HMAX // 2


def regroup_kernel(group_ref, source_ref, receiver_ref, *refs):
    out_refs, (held, sems) = refs[:GROUPS], refs[GROUPS:]
    freqs, cells = source_ref.shape[1], source_ref.shape[2]
    share = cells // CHUNKS

    def fetch(field, chunk):
        ref = (source_ref, receiver_ref)[field]
        part = pl.ds(chunk * share, share)
        return pltpu.make_async_copy(ref.at[:, :, part], held.at[field, :, :, part], sems.at[field, chunk])

    for chunk in range(CHUNKS):
        for field in range(2):
            fetch(field, chunk).start()

    def regroup(order):
        low = lax.broadcasted_iota(jnp.int32, (8, LANES), 0) < 4
        for chunk in range(CHUNKS):
            for field in range(2):
                fetch(field, chunk).wait()

                def one_cell(x, _):
                    for f in range(freqs):
                        parts = [[None, None] for _ in range(GROUPS)]
                        for c in range(2):
                            near = held[field, c, f, x, :, :LANES].astype(jnp.float32)
                            far = held[field, c, f, x, :, LANES:].astype(jnp.float32)
                            for pair in range(2):
                                a = near[8 * pair : 8 * pair + 8]
                                b = far[8 * pair : 8 * pair + 8]
                                parts[2 * pair][c] = jnp.where(low, a, pltpu.roll(b, 4, 0))
                                parts[2 * pair + 1][c] = jnp.where(low, pltpu.roll(a, 4, 0), b)
                        for d in range(GROUPS):
                            out_refs[d][field, f, x] = jnp.concatenate(parts[order ^ d], axis=0).astype(jnp.bfloat16)
                    return 0

                lax.fori_loop(chunk * share, (chunk + 1) * share, one_cell, 0, unroll=2)

    for order in range(GROUPS):
        pl.when(group_ref[0] == order)(functools.partial(regroup, order))


def regrouped(group, source_field, receiver_field):
    two, freqs, cells, _, _ = source_field.shape
    return pl.pallas_call(
        regroup_kernel,
        in_specs=[pl.BlockSpec(memory_space=pltpu.SMEM)] + [pl.BlockSpec(memory_space=pl.ANY)] * 2,
        out_specs=[pl.BlockSpec(memory_space=pltpu.VMEM)] * GROUPS,
        out_shape=[pltpu.VMEM((2, freqs, cells, ROWS, LANES), jnp.bfloat16)] * GROUPS,
        scratch_shapes=[pltpu.VMEM((2, 2, freqs, cells, 16, 2 * LANES), jnp.bfloat16), pltpu.SemaphoreType.DMA((2, CHUNKS))],
        compiler_params=pltpu.CompilerParams(vmem_limit_bytes=12 << 20),
        cost_estimate=pl.CostEstimate(flops=0, bytes_accessed=4 << 20, transcendentals=0),
        name="regroup",
    )(group, *(pltpu.with_memory_space_constraint(x, pltpu.HBM) for x in (source_field, receiver_field)))


def pack_kernel(copies, refs_in, *refs):
    flags_ref, ins, outs = refs[0], refs[1 : 1 + refs_in], refs[1 + refs_in :]
    for flag, value, source, part, half, out, slot in copies:

        def copy(source=source, part=part, half=half, out=out, slot=slot):
            cells = outs[out].shape[3]

            def one_cell(x, _):
                for field in range(2):
                    for f in range(outs[out].shape[2]):
                        at = (field, f, half * cells + x) if part is None else (part, field, f, half * cells + x)
                        outs[out][slot, field, f, x] = ins[source][at]
                return 0

            lax.fori_loop(0, cells, one_cell, 0, unroll=4)

        if flag is None:
            copy()
        else:
            pl.when(flags_ref[flag] == value)(copy)


def pack(flags, arrays, copies, shapes):
    vmem = pl.BlockSpec(memory_space=pltpu.VMEM)
    return pl.pallas_call(
        functools.partial(pack_kernel, copies, len(arrays)),
        in_specs=[pl.BlockSpec(memory_space=pltpu.SMEM)] + [vmem] * len(arrays),
        out_specs=[vmem] * len(shapes),
        out_shape=[jax.ShapeDtypeStruct(shape, jnp.bfloat16) for shape in shapes],
        compiler_params=pltpu.CompilerParams(vmem_limit_bytes=12 << 20),
        cost_estimate=pl.CostEstimate(flops=0, bytes_accessed=2 << 20, transcendentals=0),
        name="pack",
    )(flags, *arrays)


def sum_kernel(plan, bands, first, last, flags_ref, *refs):
    count = 1 + max(entry[0] for entry in plan)
    blocks, refs = refs[:count], refs[count:]
    befores = ()
    if not first:
        befores, refs = refs[: len(bands)], refs[len(bands) :]
    if last == 2:
        refs = refs[1:]
    outs = refs[: 1 if last else len(bands)]
    fields = refs[len(outs)]
    if last:
        turn, stage, sems = refs[len(outs) + 1 :]
        out_ref = outs[0]
    cells = stage.shape[4 - 1] if last else outs[0].shape[1]
    total_freqs = fields.shape[2]

    def fill(index, part, at, length, to, group):
        def one_cell(x, _):
            for field in range(2):
                for f in range(2):
                    if index is None:
                        value = jnp.zeros((ROWS, LANES), jnp.float32)
                    elif part is None:
                        value = blocks[index][field, f, at + x].astype(jnp.float32)
                    else:
                        value = blocks[index][part, field, f, at + x].astype(jnp.float32)
                    fields[field, to + x, 2 * group + f] = value
            return 0

        lax.fori_loop(0, length, one_cell, 0, unroll=4)

    for index, part, length, to, group, flag, value in plan:
        place = functools.partial(fill, index, part, 0, length, to, group)
        if flag is None:
            place()
        else:
            pl.when(flags_ref[flag] == value)(place)
    for length, to, flag, value in sorted({(e[2], e[3], e[5], 2) for e in plan if e[5] is not None}):
        for group in range(total_freqs // 2):
            pl.when(flags_ref[flag] == value)(functools.partial(fill, None, None, 0, length, to, group))

    def tile(before, out, k0, row0, rows, x0, slot):
        s0 = x0 + 2 * HMAX - k0 - (rows - 1)
        r0 = x0 + k0
        if first:
            total = [[None] * TX for _ in range(rows)]
        else:
            total = [[before[row0 + j, x0 + i] for i in range(TX)] for j in range(rows)]
        for f in range(total_freqs):
            for c in range(2):
                s = [fields[0, s0 + i, f, 8 * c : 8 * c + 8] for i in range(TX + rows - 1)]
                r = [fields[1, r0 + i, f, 8 * c : 8 * c + 8] for i in range(TX + rows - 1)]
                for j in range(rows):
                    for i in range(TX):
                        product = s[i + rows - 1 - j] * r[i + j]
                        total[j][i] = product if total[j][i] is None else total[j][i] + product
        for j in range(rows):
            if not last:
                for i in range(TX):
                    out[row0 + j, x0 + i] = total[j][i]
                continue
            for i in range(TX):
                turn[j, pl.ds(i, 8, stride=TX)] = 0.25 * total[j][i]
            for zh in range(2):
                for y in range(4):
                    row = zh * 4 + y
                    stage[slot, y, j, pl.ds(pl.multiple_of(x0, TX), TX), zh * LANES : (zh + 1) * LANES] = turn[
                        j, row * TX : (row + 1) * TX
                    ]

    def out_copy(k0, rows, slot):
        return pltpu.make_async_copy(stage.at[slot, :, pl.ds(0, rows)], out_ref.at[:, pl.ds(k0, rows)], sems.at[slot])

    for band, (k_first, steps, jump_at, jump, rest) in enumerate(bands):
        before = befores[band] if befores else None
        out = None if last else outs[band]

        def first_row(step):
            k0 = k_first + TH * step
            return k0 if not jump else k0 + jnp.where(step >= jump_at, jump, 0)

        def rows_of(k0, row0, rows, slot):
            def x_step(xt, _):
                tile(before, out, k0, row0, rows, xt * TX, slot)
                return 0

            lax.fori_loop(0, cells // TX, x_step, 0)

        def h_step(step, _):
            slot = lax.rem(step, SLOTS)
            if last:

                @pl.when(step >= SLOTS)
                def _():
                    out_copy(first_row(step - SLOTS), TH, slot).wait()

            rows_of(first_row(step), TH * step, TH, slot)
            if last:
                out_copy(first_row(step), TH, slot).start()
            return 0

        lax.fori_loop(0, steps, h_step, 0)
        if rest:
            slot = steps % SLOTS
            k0 = k_first + TH * steps
            if last:
                out_copy(first_row(steps - SLOTS), TH, slot).wait()
            rows_of(k0, TH * steps, rest, slot)
            if last:
                out_copy(k0, rest, slot).start()
        if last:
            for step in range(steps - SLOTS + (1 if rest else 0), steps):
                out_copy(first_row(step), TH, step % SLOTS).wait()
            if rest:
                out_copy(k_first + TH * steps, rest, steps % SLOTS).wait()


NEAR_BAND = (HMAX - NEAR, 2 * NEAR // TH, 0, 0, 1)
FAR_BAND = (0, 2 * NEAR // TH, NEAR // TH, 2 * NEAR + 1, 0)


def summed(flags, blocks, plan, bands, befores, cells, groups, last, image=None):
    first = befores is None
    heights = [TH * band[1] + band[4] for band in bands]
    scratch = [pltpu.VMEM((2, 3 * cells, 2 * groups, ROWS, LANES), jnp.float32)]
    vmem = pl.BlockSpec(memory_space=pltpu.VMEM)
    hbm = pl.BlockSpec(memory_space=pl.ANY)
    operands = list(blocks) + ([] if first else list(befores))
    in_specs = [pl.BlockSpec(memory_space=pltpu.SMEM)] + [vmem] * len(operands)
    aliases = {}
    if last:
        scratch += [
            pltpu.VMEM((TH, 8 * TX, LANES), jnp.float32),
            pltpu.VMEM((SLOTS, 4, TH, cells, 2 * LANES), jnp.float32),
            pltpu.SemaphoreType.DMA((SLOTS,)),
        ]
        out_shape = jax.ShapeDtypeStruct((4, OFFSETS, cells, 2 * LANES), jnp.float32)
        out_specs = hbm
        if last == 2:
            operands.append(image)
            in_specs.append(hbm)
            aliases = {len(operands): 0}
    else:
        out_shape = [pltpu.VMEM((height, cells, 8, LANES), jnp.float32) for height in heights]
        out_specs = [vmem] * len(heights)
    return pl.pallas_call(
        functools.partial(sum_kernel, plan, bands, first, last),
        in_specs=in_specs,
        out_specs=out_specs,
        out_shape=out_shape,
        scratch_shapes=scratch,
        input_output_aliases=aliases,
        compiler_params=pltpu.CompilerParams(vmem_limit_bytes=24 << 20),
        cost_estimate=pl.CostEstimate(
            flops=260_000 * groups * sum(heights), bytes_accessed=130_000 * sum(heights), transcendentals=0
        ),
        name="image" if last else "partial",
    )(flags, *operands)


def body(source_field, receiver_field):
    slabs = lax.axis_size("slab")
    middle = slabs // 2
    cells, freqs = source_field.shape[2], source_field.shape[1]
    group = lax.axis_index("freq").astype(jnp.int32)
    slab = lax.axis_index("slab")
    left_flag = jnp.where(slab == 0, 2, jnp.where(slab == middle, 1, 0))
    right_flag = jnp.where(slab == slabs - 1, 2, jnp.where(slab == middle - 1, 1, 0))
    flags = jnp.stack([left_flag, right_flag]).astype(jnp.int32)
    edges = jnp.where(flags == 1, 0, flags)
    parts = regrouped(group[None], source_field, receiver_field)

    def swap(part, d):
        return lax.ppermute(part, "freq", [(g, g ^ d) for g in range(GROUPS)])

    two, three, one, other = swap(parts[2], 2), swap(parts[3], 3), swap(parts[1], 1), swap(parts[3], 1)

    whole = (2, 2, freqs, cells, ROWS, LANES)
    (own,) = pack(flags, (parts[0], one), ((None, 0, 0, None, 0, 0, 0), (None, 0, 1, None, 0, 0, 1)), (whole,))
    onward = [(s, s // middle * middle + (s + 1) % middle) for s in range(slabs)]
    left = lax.ppermute(own, "slab", onward)
    right = lax.ppermute(own, "slab", [(t, s) for s, t in onward])
    half = (2, 2, freqs, NEAR, ROWS, LANES)
    copies = []
    for out, flag, side in ((0, 1, 1), (1, 0, 0), (2, 1, 0), (3, 0, 1)):
        for slot in range(2):
            copies += [(flag, value, source, None, side, out, slot) for value, source in ((0, slot), (2, slot), (1, 2 + slot))]
    for slot in range(2):
        copies += [(0, value, source, slot, 0, 4, slot) for value, source in ((0, 5), (1, 5), (2, 4))]
    on_near, back_near, on_far, back_far, across = pack(
        flags, (two, three, parts[2], other, left, right), copies, (half,) * 4 + (whole,)
    )
    across = lax.ppermute(across, "slab", [(0, middle), (slabs - 1, middle - 1)])

    def around(value, step):
        cut = middle - 1 if step > 0 else middle
        pairs = []
        for s in range(slabs):
            for g in range(GROUPS):
                pairs.append((s * GROUPS + g, (s + step) % slabs * GROUPS + (g ^ 2 if s == cut else g)))
        return lax.ppermute(value, ("slab", "freq"), pairs)

    left_near, right_near = around(on_near, 1), around(back_near, -1)
    left_far, right_far = around(on_far, 1), around(back_far, -1)
    plan = []
    for g in range(2):
        plan += [(0, g, cells, cells, g, None, 0)]
        plan += [(1, g, cells, 0, g, 0, 0), (3, g, cells, 0, g, 0, 1)]
        plan += [(2, g, cells, 2 * cells, g, 1, 0), (3, g, cells, 2 * cells, g, 1, 1)]
    blocks = (own, left, right, across)
    befores = summed(flags, blocks, plan, (NEAR_BAND, FAR_BAND), None, cells, 2, 0)
    plan = [(0, None, cells, cells, 0, None, 0), (1, None, cells, cells, 1, None, 0)]
    for g in range(2):
        plan += [(2, g, NEAR, cells - NEAR, g, 0, 0), (3, g, NEAR, 2 * cells, g, 1, 0)]
    image = summed(edges, (two, three, left_near, right_near), plan, (NEAR_BAND,), befores[:1], cells, 2, 1)
    for g in range(2):
        plan += [(4, g, NEAR, cells - 2 * NEAR, g, 0, 0), (5, g, NEAR, 2 * cells + NEAR, g, 1, 0)]
    blocks = (two, three, left_near, right_near, left_far, right_far)
    return summed(edges, blocks, plan, (FAR_BAND,), befores[1:], cells, 2, 2, image)


def solution(mesh):
    in_specs = (P(None, "freq", "slab", None, None), P(None, "freq", "slab", None, None))
    out_specs = P("freq", None, "slab", None)
    return jax.shard_map(body, mesh=mesh, in_specs=in_specs, out_specs=out_specs, check_vma=False)
```

time: 88.4 us -> 86.7 us (0.981)
  waiting for transfers between devices: 14.4 us -> 38.5 us
  starting transfers between devices: 43.9 us -> 25.7 us
  local copies, waits for them, and re-layouts: 6.53 us -> 0 us
    ppermute x14 -> x11, waiting for transfers between devices: 14.4 us -> 38.5 us  [the longest x4 23.4 us: swap(): return lax.ppermute(part, 'freq', [(g, g ^ d) for g in range(GROUPS)])]
    ppermute x14 -> x11, starting transfers between devices: 43.9 us -> 25.7 us  [the longest x4 12.6 us: around(): return lax.ppermute(value, ('slab', 'freq'), pairs)]
    unnamed x14 -> x0, local copies, waits for them, and re-layouts: 6.53 us -> none
    pallas_call x1, Pallas kernels: 2.98 us -> 1.66 us  [regrouped(): pl.pallas_call(regroup_kernel, in_specs=[pl.BlockSpec(memory_space=pltpu....]
    pallas_call x2 -> x5, Pallas kernels: 19.8 us -> 20.5 us  [the longest x3 18.9 us: summed(): pl.pallas_call(functools.partial(sum_kernel, plan, bands, first, last), i...]
  transfers between devices with their start and end apart: 14 -> 11, of which waited for: 3 -> 5; matrix products, arithmetic and copies ran while one was open for 0% -> 0% of each run, Pallas kernels for 13% -> 15%
where the time goes in v4:
time: 86.7 us; the launch traced here: 86.6 us
  waiting for transfers between devices  38.5 us (44%)
  starting transfers between devices  25.7 us (30%)
  Pallas kernels  22.2 us (26%)
    ppermute x4, waiting for transfers between devices, swap(): return lax.ppermute(part, 'freq', [(g, g ^ d) for g in range(GROUPS)])  23.4 us
    pallas_call x3, Pallas kernels, summed(): pl.pallas_call(functools.partial(sum_kernel, plan, bands, first, last), i...  18.9 us
    ppermute x4, starting transfers between devices, around(): return lax.ppermute(value, ('slab', 'freq'), pairs)  12.6 us
    ppermute x1, waiting for transfers between devices, body(): lax.ppermute(across, 'slab', [(0, middle), (slabs - 1, middle - 1)])  12.1 us
    ppermute x1, starting transfers between devices, body(): right = lax.ppermute(own, 'slab', [(t, s) for s, t in onward])  8.13 us
    ppermute x4, starting transfers between devices, swap(): return lax.ppermute(part, 'freq', [(g, g ^ d) for g in range(GROUPS)])  3.74 us
    ppermute x1, waiting for transfers between devices, body(): left = lax.ppermute(own, 'slab', onward)  2.94 us
  transfers between devices with their start and end apart: 11, of which 5 were waited for; matrix products, arithmetic and copies ran while one was open for 0% of the time, Pallas kernels for 15%

profile of v4, /device:TPU:8, one launch (start us, length us, event | category | flops | bytes accessed | tf_op | source)
XLA Modules:
  0.0 86.6 jit_solution(2435876322406577515)
XLA Ops:
  0.0 1.7 %regroup.1 = (bf16[2,2,32,16,128]{4,3,2,1,0:T(8,128)(2,1)S(1)}, bf16[2,2,32,16,128]{4,3,2,1,0:T(8,128)(2,1)S(1)}, bf16[2,2,32,16,128]{4,3,2,1,0:T(8,128)(2,1)S(1)}, bf16[2,2,32,16,128]{4,3,2,1,0:T(8,128)(2,1)S(1)}) custom-call(s32[1]{0:T(128)} %bitcast.2.group_ref, bf16[2,2,32,16,256]{4,3,2,1,0:T(8,128)(2,1)} %source_ref.1, ...), custom_call_target="tpu_custom_call" | custom-call | bytes 4194304 | tf_op jit(solution)/shard_map/regroup/pallas_call | solution.py:65
  1.7 0.1 collective-permute-start.3
  1.8 0.1 compare_select_fusion
  1.9 1.8 %collective-permute-done.3.refs_2_ = bf16[2,2,32,16,128]{4,3,2,1,0:T(8,128)(2,1)S(1)} collective-permute-done((bf16[2,2,32,16,128]{4,3,2,1,0:T(8,128)(2,1)S(1)}, bf16[2,2,32,16,128]{4,3,2,1,0:T(8,128)(2,1)S(1)}, u32[]{:S(2)}, u32[]{:S(2)}) %collective-permute-start.3) | collective-permute-done | bytes 524320 | tf_op jit(solution)/shard_map/ppermute | solution.py:285
  3.7 0.6 pack.2.refs_0_
  4.3 8.1 %collective-permute-start.5 = (bf16[2,2,2,32,16,128]{5,4,3,2,1,0:T(8,128)(2,1)S(1)}, bf16[2,2,2,32,16,128]{5,4,3,2,1,0:T(8,128)(2,1)S(1)}, u32[]{:S(2)}, u32[]{:S(2)}) collective-permute-start(bf16[2,2,2,32,16,128]{5,4,3,2,1,0:T(8,128)(2,1)S(1)} %pack.2.refs_0_), channel_id=1, source_target_pairs={{4,0},{8,4},{12,8},{16,12},{20,16},{24,20},{28,24},{32,28},{36,32}... | collective-permute-start | bytes 3145736 | tf_op jit(solution)/shard_map/ppermute | solution.py:293
  12.4 0.0 collective-permute-start.4
  12.4 2.3 %collective-permute-start = (bf16[2,2,32,16,128]{4,3,2,1,0:T(8,128)(2,1)S(1)}, bf16[2,2,32,16,128]{4,3,2,1,0:T(8,128)(2,1)S(1)}, u32[]{:S(2)}, u32[]{:S(2)}) collective-permute-start(bf16[2,2,32,16,128]{4,3,2,1,0:T(8,128)(2,1)S(1)} %get-tuple-element.16.refs_3_), channel_id=1, source_target_pairs={{0,2},{1,3},{2,0},{3,1},{4,6},{5,7},{6,4},{7,5},{8,10},{9,11},{10,... | collective-permute-start | bytes 1572872 | tf_op jit(solution)/shard_map/ppermute | solution.py:285
  14.7 0.0 collective-permute-start.2
  14.7 1.4 %collective-permute-start.1 = (bf16[2,2,32,16,128]{4,3,2,1,0:T(8,128)(2,1)S(1)}, bf16[2,2,32,16,128]{4,3,2,1,0:T(8,128)(2,1)S(1)}, u32[]{:S(2)}, u32[]{:S(2)}) collective-permute-start(bf16[2,2,32,16,128]{4,3,2,1,0:T(8,128)(2,1)S(1)} %get-tuple-element.17), channel_id=1, source_target_pairs={{0,3},{1,2},{2,1},{3,0},{4,7},{5,6},{6,5},{7,4},{8,11},{9,10},{10,... | collective-permute-start | bytes 1572872 | tf_op jit(solution)/shard_map/ppermute | solution.py:285
  16.1 12.7 %collective-permute-done.refs_1_.refs_0_ = bf16[2,2,32,16,128]{4,3,2,1,0:T(8,128)(2,1)S(1)} collective-permute-done((bf16[2,2,32,16,128]{4,3,2,1,0:T(8,128)(2,1)S(1)}, bf16[2,2,32,16,128]{4,3,2,1,0:T(8,128)(2,1)S(1)}, u32[]{:S(2)}, u32[]{:S(2)}) %collective-permute-start) | collective-permute-done | bytes 524320 | tf_op jit(solution)/shard_map/ppermute | solution.py:285
  28.8 0.0 collective-permute-done.2.refs_4_
  28.8 9.0 %collective-permute-done.1.refs_2_.refs_1_ = bf16[2,2,32,16,128]{4,3,2,1,0:T(8,128)(2,1)S(1)} collective-permute-done((bf16[2,2,32,16,128]{4,3,2,1,0:T(8,128)(2,1)S(1)}, bf16[2,2,32,16,128]{4,3,2,1,0:T(8,128)(2,1)S(1)}, u32[]{:S(2)}, u32[]{:S(2)}) %collective-permute-start.1) | collective-permute-done | bytes 524320 | tf_op jit(solution)/shard_map/ppermute | solution.py:285
  37.7 0.0 collective-permute-done.5.refs_6_.refs_2_
  37.7 2.9 %collective-permute-done.4.refs_5_.refs_1_ = bf16[2,2,2,32,16,128]{5,4,3,2,1,0:T(8,128)(2,1)S(1)} collective-permute-done((bf16[2,2,2,32,16,128]{5,4,3,2,1,0:T(8,128)(2,1)S(1)}, bf16[2,2,2,32,16,128]{5,4,3,2,1,0:T(8,128)(2,1)S(1)}, u32[]{:S(2)}, u32[]{:S(2)}) %collective-permute-start.4) | collective-permute-done | bytes 1048608 | tf_op jit(solution)/shard_map/ppermute | solution.py:292
  40.7 1.0 %pack.3 = (bf16[2,2,2,16,16,128]{5,4,3,2,1,0:T(8,128)(2,1)S(1)}, bf16[2,2,2,16,16,128]{5,4,3,2,1,0:T(8,128)(2,1)S(1)}, bf16[2,2,2,16,16,128]{5,4,3,2,1,0:T(8,128...) custom-call(s32[2]{0:T(128)S(1)} %get-tuple-element.28.refs_0_.flags_ref, ...), custom_call_target="tpu_custom_call" | custom-call | bytes 2097152 | tf_op jit(solution)/shard_map/pack/pallas_call | solution.py:101
  41.7 1.3 %collective-permute-start.10 = (bf16[2,2,2,32,16,128]{5,4,3,2,1,0:T(8,128)(2,1)S(1)}, bf16[2,2,2,32,16,128]{5,4,3,2,1,0:T(8,128)(2,1)S(1)}, u32[]{:S(2)}, u32[]{:S(2)}) collective-permute-start(bf16[2,2,2,32,16,128]{5,4,3,2,1,0:T(8,128)(2,1)S(1)} %get-tuple-element.24), channel_id=1, source_target_pairs={{0,128},{252,124},{1,129},{253,125},{2,130},{254,126},{3,131},{255... | collective-permute-start | bytes 3145736 | tf_op jit(solution)/shard_map/ppermute | solution.py:304
  43.0 0.1 collective-permute-start.6
  43.1 6.2 %collective-permute-start.7 = (bf16[2,2,2,16,16,128]{5,4,3,2,1,0:T(8,128)(2,1)S(1)}, bf16[2,2,2,16,16,128]{5,4,3,2,1,0:T(8,128)(2,1)S(1)}, u32[]{:S(2)}, u32[]{:S(2)}) collective-permute-start(bf16[2,2,2,16,16,128]{5,4,3,2,1,0:T(8,128)(2,1)S(1)} %get-tuple-element.21), channel_id=1, source_target_pairs={{0,252},{1,253},{2,254},{3,255},{4,0},{5,1},{6,2},{7,3},{8,4},{9,5... | collective-permute-start | bytes 1572872 | tf_op jit(solution)/shard_map/ppermute | solution.py:312
  49.4 0.0 collective-permute-start.8
  49.4 6.2 %collective-permute-start.9 = (bf16[2,2,2,16,16,128]{5,4,3,2,1,0:T(8,128)(2,1)S(1)}, bf16[2,2,2,16,16,128]{5,4,3,2,1,0:T(8,128)(2,1)S(1)}, u32[]{:S(2)}, u32[]{:S(2)}) collective-permute-start(bf16[2,2,2,16,16,128]{5,4,3,2,1,0:T(8,128)(2,1)S(1)} %get-tuple-element.23), channel_id=1, source_target_pairs={{0,252},{1,253},{2,254},{3,255},{4,0},{5,1},{6,2},{7,3},{8,4},{9,5... | collective-permute-start | bytes 1572872 | tf_op jit(solution)/shard_map/ppermute | solution.py:312
  55.6 12.1 %collective-permute-done.10.refs_3_ = bf16[2,2,2,32,16,128]{5,4,3,2,1,0:T(8,128)(2,1)S(1)} collective-permute-done((bf16[2,2,2,32,16,128]{5,4,3,2,1,0:T(8,128)(2,1)S(1)}, bf16[2,2,2,32,16,128]{5,4,3,2,1,0:T(8,128)(2,1)S(1)}, u32[]{:S(2)}, u32[]{:S(2)}) %collective-permute-start.10) | collective-permute-done | bytes 1048608 | tf_op jit(solution)/shard_map/ppermute | solution.py:304
  67.7 6.8 %partial.1 = (f32[33,32,8,128]{3,2,1,0:T(8,128)S(1)}, f32[32,32,8,128]{3,2,1,0:T(8,128)S(1)}) custom-call(s32[2]{0:T(128)S(1)} %get-tuple-element.28.refs_0_.flags_ref, bf16[2,2,2,32,16,128]{5,4,3,2,1,0:T(8,128)(2,1)S(1)} %pack.2.refs_0_, bf16[2,2,2,32,16,128]{5,4,3,2,1,0:T(8,128)(2,1)S(1)} %collective-permute-done.4.refs_5_.refs_1_, ...), custom_call_target="tpu_custom_call" | custom-call | flops 33800000 | bytes 8450000 | tf_op jit(solution)/shard_map/partial/pallas_call | solution.py:257
  74.5 0.0 collective-permute-done.6.refs_2_
  74.5 0.0 collective-permute-done.7.refs_3_
  74.5 5.9 %image.2.refs_7_ = f32[4,65,32,256]{3,2,1,0:T(8,128)} custom-call(s32[2]{0:T(128)S(1)} %get-tuple-element.27.flags_ref, bf16[2,2,32,16,128]{4,3,2,1,0:T(8,128)(2,1)S(1)} %collective-permute-done.refs_1_.refs_0_, bf16[2,2,32,16,128]{4,3,2,1,0:T(8,128)(2,1)S(1)} %collective-permute-done.1.refs_2_.refs_1_, ...), custom_call_target="tpu_custom_call" | custom-call | flops 17160000 | bytes 4290000 | tf_op jit(solution)/shard_map/image/pallas_call | solution.py:257
  80.4 0.0 collective-permute-done.8.refs_4_
  80.4 0.0 collective-permute-done.9.refs_5_
  80.5 6.1 %image.3 = f32[4,65,32,256]{3,2,1,0:T(8,128)} custom-call(s32[2]{0:T(128)S(1)} %get-tuple-element.27.flags_ref, bf16[2,2,32,16,128]{4,3,2,1,0:T(8,128)(2,1)S(1)} %collective-permute-done.refs_1_.refs_0_, bf16[2,2,32,16,128]{4,3,2,1,0:T(8,128)(2,1)S(1)} %collective-permute-done.1.refs_2_.refs_1_, ...), custom_call_target="tpu_custom_call", output_to_operand_aliasing={{}: (8, {})} | custom-call | flops 16640000 | bytes 4160000 | tf_op jit(solution)/shard_map/image/pallas_call | solution.py:257
Async XLA Ops:
  1.7 2.0 %collective-permute-start.3 = (bf16[2,2,32,16,128]{4,3,2,1,0:T(8,128)(2,1)S(1)}, bf16[2,2,32,16,128]{4,3,2,1,0:T(8,128)(2,1)S(1)}, u32[]{:S(2)}, u32[]{:S(2)}) collective-permute-start(bf16[2,2,32,16,128]{4,3,2,1,0:T(8,128)(2,1)S(1)} %get-tuple-element.19), channel_id=1, source_target_pairs={{0,1},{1,0},{2,3},{3,2},{4,5},{5,4},{6,7},{7,6},{8,9},{9,8},{10,11... | collective-permute-start | bytes 1572872 | tf_op jit(solution)/shard_map/ppermute | solution.py:285
  4.3 33.4 %collective-permute-start.5 = (bf16[2,2,2,32,16,128]{5,4,3,2,1,0:T(8,128)(2,1)S(1)}, bf16[2,2,2,32,16,128]{5,4,3,2,1,0:T(8,128)(2,1)S(1)}, u32[]{:S(2)}, u32[]{:S(2)}) collective-permute-start(bf16[2,2,2,32,16,128]{5,4,3,2,1,0:T(8,128)(2,1)S(1)} %pack.2.refs_0_), channel_id=1, source_target_pairs={{4,0},{8,4},{12,8},{16,12},{20,16},{24,20},{28,24},{32,28},{36,32}... | collective-permute-start | bytes 3145736 | tf_op jit(solution)/shard_map/ppermute | solution.py:293
  12.4 28.2 %collective-permute-start.4 = (bf16[2,2,2,32,16,128]{5,4,3,2,1,0:T(8,128)(2,1)S(1)}, bf16[2,2,2,32,16,128]{5,4,3,2,1,0:T(8,128)(2,1)S(1)}, u32[]{:S(2)}, u32[]{:S(2)}) collective-permute-start(bf16[2,2,2,32,16,128]{5,4,3,2,1,0:T(8,128)(2,1)S(1)} %pack.2.refs_0_), channel_id=1, source_target_pairs={{0,4},{4,8},{8,12},{12,16},{16,20},{20,24},{24,28},{28,32},{32,36}... | collective-permute-start | bytes 3145736 | tf_op jit(solution)/shard_map/ppermute | solution.py:292
  12.4 16.3 %collective-permute-start = (bf16[2,2,32,16,128]{4,3,2,1,0:T(8,128)(2,1)S(1)}, bf16[2,2,32,16,128]{4,3,2,1,0:T(8,128)(2,1)S(1)}, u32[]{:S(2)}, u32[]{:S(2)}) collective-permute-start(bf16[2,2,32,16,128]{4,3,2,1,0:T(8,128)(2,1)S(1)} %get-tuple-element.16.refs_3_), channel_id=1, source_target_pairs={{0,2},{1,3},{2,0},{3,1},{4,6},{5,7},{6,4},{7,5},{8,10},{9,11},{10,... | collective-permute-start | bytes 1572872 | tf_op jit(solution)/shard_map/ppermute | solution.py:285
  14.7 14.0 %collective-permute-start.2 = (bf16[2,2,32,16,128]{4,3,2,1,0:T(8,128)(2,1)S(1)}, bf16[2,2,32,16,128]{4,3,2,1,0:T(8,128)(2,1)S(1)}, u32[]{:S(2)}, u32[]{:S(2)}) collective-permute-start(bf16[2,2,32,16,128]{4,3,2,1,0:T(8,128)(2,1)S(1)} %get-tuple-element.17), channel_id=1, source_target_pairs={{0,1},{1,0},{2,3},{3,2},{4,5},{5,4},{6,7},{7,6},{8,9},{9,8},{10,11... | collective-permute-start | bytes 1572872 | tf_op jit(solution)/shard_map/ppermute | solution.py:285
  14.7 23.0 %collective-permute-start.1 = (bf16[2,2,32,16,128]{4,3,2,1,0:T(8,128)(2,1)S(1)}, bf16[2,2,32,16,128]{4,3,2,1,0:T(8,128)(2,1)S(1)}, u32[]{:S(2)}, u32[]{:S(2)}) collective-permute-start(bf16[2,2,32,16,128]{4,3,2,1,0:T(8,128)(2,1)S(1)} %get-tuple-element.17), channel_id=1, source_target_pairs={{0,3},{1,2},{2,1},{3,0},{4,7},{5,6},{6,5},{7,4},{8,11},{9,10},{10,... | collective-permute-start | bytes 1572872 | tf_op jit(solution)/shard_map/ppermute | solution.py:285
  41.7 25.9 %collective-permute-start.10 = (bf16[2,2,2,32,16,128]{5,4,3,2,1,0:T(8,128)(2,1)S(1)}, bf16[2,2,2,32,16,128]{5,4,3,2,1,0:T(8,128)(2,1)S(1)}, u32[]{:S(2)}, u32[]{:S(2)}) collective-permute-start(bf16[2,2,2,32,16,128]{5,4,3,2,1,0:T(8,128)(2,1)S(1)} %get-tuple-element.24), channel_id=1, source_target_pairs={{0,128},{252,124},{1,129},{253,125},{2,130},{254,126},{3,131},{255... | collective-permute-start | bytes 3145736 | tf_op jit(solution)/shard_map/ppermute | solution.py:304
  43.0 31.4 %collective-permute-start.6 = (bf16[2,2,2,16,16,128]{5,4,3,2,1,0:T(8,128)(2,1)S(1)}, bf16[2,2,2,16,16,128]{5,4,3,2,1,0:T(8,128)(2,1)S(1)}, u32[]{:S(2)}, u32[]{:S(2)}) collective-permute-start(bf16[2,2,2,16,16,128]{5,4,3,2,1,0:T(8,128)(2,1)S(1)} %get-tuple-element.20), channel_id=1, source_target_pairs={{0,4},{1,5},{2,6},{3,7},{4,8},{5,9},{6,10},{7,11},{8,12},{9,13},{1... | collective-permute-start | bytes 1572872 | tf_op jit(solution)/shard_map/ppermute | solution.py:312
  43.1 31.4 %collective-permute-start.7 = (bf16[2,2,2,16,16,128]{5,4,3,2,1,0:T(8,128)(2,1)S(1)}, bf16[2,2,2,16,16,128]{5,4,3,2,1,0:T(8,128)(2,1)S(1)}, u32[]{:S(2)}, u32[]{:S(2)}) collective-permute-start(bf16[2,2,2,16,16,128]{5,4,3,2,1,0:T(8,128)(2,1)S(1)} %get-tuple-element.21), channel_id=1, source_target_pairs={{0,252},{1,253},{2,254},{3,255},{4,0},{5,1},{6,2},{7,3},{8,4},{9,5... | collective-permute-start | bytes 1572872 | tf_op jit(solution)/shard_map/ppermute | solution.py:312
  49.4 31.1 %collective-permute-start.8 = (bf16[2,2,2,16,16,128]{5,4,3,2,1,0:T(8,128)(2,1)S(1)}, bf16[2,2,2,16,16,128]{5,4,3,2,1,0:T(8,128)(2,1)S(1)}, u32[]{:S(2)}, u32[]{:S(2)}) collective-permute-start(bf16[2,2,2,16,16,128]{5,4,3,2,1,0:T(8,128)(2,1)S(1)} %get-tuple-element.22), channel_id=1, source_target_pairs={{0,4},{1,5},{2,6},{3,7},{4,8},{5,9},{6,10},{7,11},{8,12},{9,13},{1... | collective-permute-start | bytes 1572872 | tf_op jit(solution)/shard_map/ppermute | solution.py:312
  49.4 31.1 %collective-permute-start.9 = (bf16[2,2,2,16,16,128]{5,4,3,2,1,0:T(8,128)(2,1)S(1)}, bf16[2,2,2,16,16,128]{5,4,3,2,1,0:T(8,128)(2,1)S(1)}, u32[]{:S(2)}, u32[]{:S(2)}) collective-permute-start(bf16[2,2,2,16,16,128]{5,4,3,2,1,0:T(8,128)(2,1)S(1)} %get-tuple-element.23), channel_id=1, source_target_pairs={{0,252},{1,253},{2,254},{3,255},{4,0},{5,1},{6,2},{7,3},{8,4},{9,5... | collective-permute-start | bytes 1572872 | tf_op jit(solution)/shard_map/ppermute | solution.py:312

commit v5 on v4

--- a/solution.py
+++ b/solution.py
@@ -74,29 +74,35 @@
     )(group, *(pltpu.with_memory_space_constraint(x, pltpu.HBM) for x in (source_field, receiver_field)))
 
 
+def by_parity(flags_ref, choice):
+    if isinstance(choice, int):
+        return choice
+    return jnp.where(flags_ref[0] == 0, choice[0], choice[1])
+
+
 def pack_kernel(copies, refs_in, *refs):
     flags_ref, ins, outs = refs[0], refs[1 : 1 + refs_in], refs[1 + refs_in :]
-    for flag, value, source, part, half, out, slot in copies:
-
-        def copy(source=source, part=part, half=half, out=out, slot=slot):
-            cells = outs[out].shape[3]
+    for crosses, source, part, at, out, slot in copies:
+
+        def copy(source=source, part=part, at=at, out=out, slot=slot):
+            start = by_parity(flags_ref, at)
 
             def one_cell(x, _):
                 for field in range(2):
                     for f in range(outs[out].shape[2]):
-                        at = (field, f, half * cells + x) if part is None else (part, field, f, half * cells + x)
-                        outs[out][slot, field, f, x] = ins[source][at]
+                        where = (field, f, start + x) if part is None else (part, field, f, start + x)
+                        outs[out][slot, field, f, x] = ins[source][where]
                 return 0
 
-            lax.fori_loop(0, cells, one_cell, 0, unroll=4)
-
-        if flag is None:
+            lax.fori_loop(0, outs[out].shape[3], one_cell, 0, unroll=4)
+
+        if crosses is None:
             copy()
         else:
-            pl.when(flags_ref[flag] == value)(copy)
-
-
-def pack(flags, arrays, copies, shapes):
+            pl.when((flags_ref[1] == 1) == crosses)(copy)
+
+
+def pack(flags, arrays, copies, shapes, weight=1):
     vmem = pl.BlockSpec(memory_space=pltpu.VMEM)
     return pl.pallas_call(
         functools.partial(pack_kernel, copies, len(arrays)),
@@ -104,13 +110,13 @@
         out_specs=[vmem] * len(shapes),
         out_shape=[jax.ShapeDtypeStruct(shape, jnp.bfloat16) for shape in shapes],
         compiler_params=pltpu.CompilerParams(vmem_limit_bytes=12 << 20),
-        cost_estimate=pl.CostEstimate(flops=0, bytes_accessed=2 << 20, transcendentals=0),
+        cost_estimate=pl.CostEstimate(flops=0, bytes_accessed=weight * (2 << 20), transcendentals=0),
         name="pack",
     )(flags, *arrays)
 
 
 def sum_kernel(plan, bands, first, last, flags_ref, *refs):
-    count = 1 + max(entry[0] for entry in plan)
+    count = 1 + max(entry[0] for entry in plan if entry[0] is not None)
     blocks, refs = refs[:count], refs[count:]
     befores = ()
     if not first:
@@ -126,29 +132,28 @@
     total_freqs = fields.shape[2]
 
     def fill(index, part, at, length, to, group):
+        start, to = by_parity(flags_ref, at), by_parity(flags_ref, to)
+
         def one_cell(x, _):
             for field in range(2):
                 for f in range(2):
                     if index is None:
                         value = jnp.zeros((ROWS, LANES), jnp.float32)
                     elif part is None:
-                        value = blocks[index][field, f, at + x].astype(jnp.float32)
+                        value = blocks[index][field, f, start + x].astype(jnp.float32)
                     else:
-                        value = blocks[index][part, field, f, at + x].astype(jnp.float32)
+                        value = blocks[index][part, field, f, start + x].astype(jnp.float32)
                     fields[field, to + x, 2 * group + f] = value
             return 0
 
         lax.fori_loop(0, length, one_cell, 0, unroll=4)
 
-    for index, part, length, to, group, flag, value in plan:
-        place = functools.partial(fill, index, part, 0, length, to, group)
-        if flag is None:
+    for index, part, at, length, to, group, values in plan:
+        place = functools.partial(fill, index, part, at, length, to, group)
+        if values is None:
             place()
         else:
-            pl.when(flags_ref[flag] == value)(place)
-    for length, to, flag, value in sorted({(e[2], e[3], e[5], 2) for e in plan if e[5] is not None}):
-        for group in range(total_freqs // 2):
-            pl.when(flags_ref[flag] == value)(functools.partial(fill, None, None, 0, length, to, group))
+            pl.when(functools.reduce(jnp.logical_or, [flags_ref[1] == value for value in values]))(place)
 
     def tile(before, out, k0, row0, rows, x0, slot):
         s0 = x0 + 2 * HMAX - k0 - (rows - 1)
@@ -275,59 +280,82 @@
     cells, freqs = source_field.shape[2], source_field.shape[1]
     group = lax.axis_index("freq").astype(jnp.int32)
     slab = lax.axis_index("slab")
-    left_flag = jnp.where(slab == 0, 2, jnp.where(slab == middle, 1, 0))
-    right_flag = jnp.where(slab == slabs - 1, 2, jnp.where(slab == middle - 1, 1, 0))
-    flags = jnp.stack([left_flag, right_flag]).astype(jnp.int32)
-    edges = jnp.where(flags == 1, 0, flags)
+    beyond = jnp.where((slab == 0) | (slab == slabs - 1), 2, 0)
+    beyond = jnp.where((slab == middle) | (slab == middle - 1), 1, beyond)
+    flags = jnp.stack([slab % 2, beyond]).astype(jnp.int32)
     parts = regrouped(group[None], source_field, receiver_field)
 
     def swap(part, d):
         return lax.ppermute(part, "freq", [(g, g ^ d) for g in range(GROUPS)])
 
-    two, three, one, other = swap(parts[2], 2), swap(parts[3], 3), swap(parts[1], 1), swap(parts[3], 1)
-
-    whole = (2, 2, freqs, cells, ROWS, LANES)
-    (own,) = pack(flags, (parts[0], one), ((None, 0, 0, None, 0, 0, 0), (None, 0, 1, None, 0, 0, 1)), (whole,))
-    onward = [(s, s // middle * middle + (s + 1) % middle) for s in range(slabs)]
-    left = lax.ppermute(own, "slab", onward)
-    right = lax.ppermute(own, "slab", [(t, s) for s, t in onward])
-    half = (2, 2, freqs, NEAR, ROWS, LANES)
-    copies = []
-    for out, flag, side in ((0, 1, 1), (1, 0, 0), (2, 1, 0), (3, 0, 1)):
-        for slot in range(2):
-            copies += [(flag, value, source, None, side, out, slot) for value, source in ((0, slot), (2, slot), (1, 2 + slot))]
-    for slot in range(2):
-        copies += [(0, value, source, slot, 0, 4, slot) for value, source in ((0, 5), (1, 5), (2, 4))]
-    on_near, back_near, on_far, back_far, across = pack(
-        flags, (two, three, parts[2], other, left, right), copies, (half,) * 4 + (whole,)
-    )
-    across = lax.ppermute(across, "slab", [(0, middle), (slabs - 1, middle - 1)])
-
-    def around(value, step):
-        cut = middle - 1 if step > 0 else middle
+    def trade(value, partner, turned=()):
         pairs = []
         for s in range(slabs):
             for g in range(GROUPS):
-                pairs.append((s * GROUPS + g, (s + step) % slabs * GROUPS + (g ^ 2 if s == cut else g)))
+                pairs.append((s * GROUPS + g, partner(s) * GROUPS + (g ^ 2 if s in turned else g)))
         return lax.ppermute(value, ("slab", "freq"), pairs)
 
-    left_near, right_near = around(on_near, 1), around(back_near, -1)
-    left_far, right_far = around(on_far, 1), around(back_far, -1)
-    plan = []
+    def side_a(s):
+        return s ^ 1
+
+    def side_b(s):
+        return min(max(s + 1 if s % 2 else s - 1, 0), slabs - 1)
+
+    def side_b_of_half(s):
+        return s // middle * middle + (s + 1 if s % 2 else s - 1) % middle
+
+    def over_middle(s):
+        return {0: middle, middle: 0, middle - 1: slabs - 1, slabs - 1: middle - 1}.get(s, s)
+
+    two, three, one, other = swap(parts[2], 2), swap(parts[3], 3), swap(parts[1], 1), swap(parts[3], 1)
+
+    whole, half = [(2, 2, freqs, length, ROWS, LANES) for length in (cells, NEAR)]
+    (own,) = pack(flags, (parts[0], one), ((None, 0, None, 0, 0, 0), (None, 1, None, 0, 0, 1)), (whole,))
+    whole_a, whole_b = trade(own, side_a), trade(own, side_b_of_half)
+
+    rest = cells - NEAR
+    copies = []
+    for slot in range(2):
+        for out, at in ((0, (rest, 0)), (2, (0, rest))):
+            copies.append((None, slot, None, at, out, slot))
+        for out, at in ((1, (0, rest)), (3, (rest, 0))):
+            copies += [(False, slot, None, at, out, slot), (True, 2 + slot, None, at, out, slot)]
+    near_a, near_b, far_a, far_b = pack(flags, (two, three, parts[2], other), copies, (half,) * 4, 1)
+    turned = (middle - 1, middle)
+    near_a, near_b = trade(near_a, side_a), trade(near_b, side_b, turned)
+    whole_a, whole_b, far_a, far_b = lax.optimization_barrier((whole_a, whole_b, far_a, far_b))
+    copies = [(None, 0, slot, at, out, slot) for slot in range(2) for out, at in ((0, (rest, 0)), (1, (0, rest)))]
+    near_over, far_over = pack(flags, (whole_b,), copies, (half,) * 2)
+    near_over = trade(near_over, over_middle)
+    far_a, far_b = trade(far_a, side_a), trade(far_b, side_b, turned)
+    far_over, near_over = lax.optimization_barrier((far_over, near_over))
+    far_over = trade(far_over, over_middle)
+
+    near_at_a, near_at_b = (2 * cells, rest), (rest, 2 * cells)
+    far_at_a, far_at_b = (2 * cells + NEAR, 0), (0, 2 * cells + NEAR)
+    plan, far_plan = [], []
     for g in range(2):
-        plan += [(0, g, cells, cells, g, None, 0)]
-        plan += [(1, g, cells, 0, g, 0, 0), (3, g, cells, 0, g, 0, 1)]
-        plan += [(2, g, cells, 2 * cells, g, 1, 0), (3, g, cells, 2 * cells, g, 1, 1)]
-    blocks = (own, left, right, across)
-    befores = summed(flags, blocks, plan, (NEAR_BAND, FAR_BAND), None, cells, 2, 0)
-    plan = [(0, None, cells, cells, 0, None, 0), (1, None, cells, cells, 1, None, 0)]
+        plan += [(0, g, 0, cells, cells, g, None), (1, g, (0, rest), NEAR, near_at_a, g, None)]
+        plan += [(2, g, (rest, 0), NEAR, near_at_b, g, (0,)), (3, g, 0, NEAR, near_at_b, g, (1,))]
+        plan += [(None, g, 0, NEAR, near_at_b, g, (2,))]
+        far_plan += [(1, g, (rest, 0), NEAR, far_at_a, g, None)]
+        far_plan += [(2, g, (0, rest), NEAR, far_at_b, g, (0,)), (4, g, 0, NEAR, far_at_b, g, (1,))]
+        far_plan += [(None, g, 0, NEAR, far_at_b, g, (2,))]
+    blocks = (own, whole_a, whole_b, near_over)
+    befores = summed(flags, blocks, plan, (NEAR_BAND,), None, cells, 2, 0)
+    far_sums = (flags, plan + far_plan, blocks)
+    plan = [(0, None, 0, cells, cells, 0, None), (1, None, 0, cells, cells, 1, None)]
+    far_plan = []
     for g in range(2):
-        plan += [(2, g, NEAR, cells - NEAR, g, 0, 0), (3, g, NEAR, 2 * cells, g, 1, 0)]
-    image = summed(edges, (two, three, left_near, right_near), plan, (NEAR_BAND,), befores[:1], cells, 2, 1)
-    for g in range(2):
-        plan += [(4, g, NEAR, cells - 2 * NEAR, g, 0, 0), (5, g, NEAR, 2 * cells + NEAR, g, 1, 0)]
-    blocks = (two, three, left_near, right_near, left_far, right_far)
-    return summed(edges, blocks, plan, (FAR_BAND,), befores[1:], cells, 2, 2, image)
+        plan += [(2, g, 0, NEAR, near_at_a, g, None)]
+        plan += [(3, g, 0, NEAR, near_at_b, g, (0, 1)), (None, g, 0, NEAR, near_at_b, g, (2,))]
+        far_plan += [(4, g, 0, NEAR, far_at_a, g, None)]
+        far_plan += [(5, g, 0, NEAR, far_at_b, g, (0, 1)), (None, g, 0, NEAR, far_at_b, g, (2,))]
+    image = summed(flags, (two, three, near_a, near_b), plan, (NEAR_BAND,), befores, cells, 2, 1)
+    image, far_over = lax.optimization_barrier((image, far_over))
+    befores = summed(flags, far_sums[2] + (far_over,), far_sums[1], (FAR_BAND,), None, cells, 2, 0)
+    blocks = (two, three, near_a, near_b, far_a, far_b)
+    return summed(flags, blocks, plan + far_plan, (FAR_BAND,), befores, cells, 2, 2, image)
 
 
 def solution(mesh):

time: 86.7 us -> 86 us (level)
  the two profiles are of different devices: /device:TPU:8 before, /device:TPU:24 now
where the time goes in v5:
time: 86 us; the launch traced here: 85.8 us
  waiting for transfers between devices  36 us (42%)
  starting transfers between devices  25.9 us (30%)
  Pallas kernels  23.6 us (27%)
    ppermute x4, waiting for transfers between devices, swap(): return lax.ppermute(part, 'freq', [(g, g ^ d) for g in range(GROUPS)])  23.4 us
    ppermute x8, starting transfers between devices, trade(): return lax.ppermute(value, ('slab', 'freq'), pairs)  22.2 us
    pallas_call x4, Pallas kernels, summed(): pl.pallas_call(functools.partial(sum_kernel, plan, bands, first, last), i...  19.8 us
    ppermute x8, waiting for transfers between devices, trade(): return lax.ppermute(value, ('slab', 'freq'), pairs)  12.6 us
    ppermute x4, starting transfers between devices, swap(): return lax.ppermute(part, 'freq', [(g, g ^ d) for g in range(GROUPS)])  3.74 us
    pallas_call x3, Pallas kernels, pack(): pl.pallas_call(functools.partial(pack_kernel, copies, len(arrays)), in_sp...  2.14 us
  transfers between devices with their start and end apart: 12, of which 5 were waited for; matrix products, arithmetic and copies ran while one was open for 0% of the time, Pallas kernels for 17%

profile of v5, /device:TPU:24, one launch (start us, length us, event | category | flops | bytes accessed | tf_op | source)
XLA Modules:
  0.0 85.8 jit_solution(13718459830341323)
XLA Ops:
  0.0 1.6 %regroup.1 = (bf16[2,2,32,16,128]{4,3,2,1,0:T(8,128)(2,1)S(1)}, bf16[2,2,32,16,128]{4,3,2,1,0:T(8,128)(2,1)S(1)}, bf16[2,2,32,16,128]{4,3,2,1,0:T(8,128)(2,1)S(1)}, bf16[2,2,32,16,128]{4,3,2,1,0:T(8,128)(2,1)S(1)}) custom-call(s32[1]{0:T(128)} %bitcast.2.group_ref, bf16[2,2,32,16,256]{4,3,2,1,0:T(8,128)(2,1)} %source_ref.1, ...), custom_call_target="tpu_custom_call" | custom-call | bytes 4194304 | tf_op jit(solution)/shard_map/regroup/pallas_call | solution.py:65
  1.7 0.1 collective-permute-start.5
  1.8 0.1 pad_add_fusion.refs_0_.flags_ref
  1.9 1.8 %collective-permute-done.5.refs_2_ = bf16[2,2,32,16,128]{4,3,2,1,0:T(8,128)(2,1)S(1)} collective-permute-done((bf16[2,2,32,16,128]{4,3,2,1,0:T(8,128)(2,1)S(1)}, bf16[2,2,32,16,128]{4,3,2,1,0:T(8,128)(2,1)S(1)}, u32[]{:S(2)}, u32[]{:S(2)}) %collective-permute-start.5) | collective-permute-done | bytes 524320 | tf_op jit(solution)/shard_map/ppermute | solution.py:289
  3.6 0.6 pack.4.refs_0_
  4.3 8.1 %collective-permute-start.7 = (bf16[2,2,2,32,16,128]{5,4,3,2,1,0:T(8,128)(2,1)S(1)}, bf16[2,2,2,32,16,128]{5,4,3,2,1,0:T(8,128)(2,1)S(1)}, u32[]{:S(2)}, u32[]{:S(2)}) collective-permute-start(bf16[2,2,2,32,16,128]{5,4,3,2,1,0:T(8,128)(2,1)S(1)} %pack.4.refs_0_), channel_id=1, source_target_pairs={{0,124},{1,125},{2,126},{3,127},{4,8},{5,9},{6,10},{7,11},{8,4},{9... | collective-permute-start | bytes 3145736 | tf_op jit(solution)/shard_map/ppermute | solution.py:296
  12.4 0.0 collective-permute-start.6
  12.4 1.3 %collective-permute-start = (bf16[2,2,32,16,128]{4,3,2,1,0:T(8,128)(2,1)S(1)}, bf16[2,2,32,16,128]{4,3,2,1,0:T(8,128)(2,1)S(1)}, u32[]{:S(2)}, u32[]{:S(2)}) collective-permute-start(bf16[2,2,32,16,128]{4,3,2,1,0:T(8,128)(2,1)S(1)} %get-tuple-element.23.refs_3_), channel_id=1, source_target_pairs={{0,2},{1,3},{2,0},{3,1},{4,6},{5,7},{6,4},{7,5},{8,10},{9,11},{10,... | collective-permute-start | bytes 1572872 | tf_op jit(solution)/shard_map/ppermute | solution.py:289
  13.7 0.0 collective-permute-start.2
  13.7 2.4 %collective-permute-start.1 = (bf16[2,2,32,16,128]{4,3,2,1,0:T(8,128)(2,1)S(1)}, bf16[2,2,32,16,128]{4,3,2,1,0:T(8,128)(2,1)S(1)}, u32[]{:S(2)}, u32[]{:S(2)}) collective-permute-start(bf16[2,2,32,16,128]{4,3,2,1,0:T(8,128)(2,1)S(1)} %get-tuple-element.24), channel_id=1, source_target_pairs={{0,3},{1,2},{2,1},{3,0},{4,7},{5,6},{6,5},{7,4},{8,11},{9,10},{10,... | collective-permute-start | bytes 1572872 | tf_op jit(solution)/shard_map/ppermute | solution.py:289
  16.1 12.7 %collective-permute-done.refs_1_.refs_0_ = bf16[2,2,32,16,128]{4,3,2,1,0:T(8,128)(2,1)S(1)} collective-permute-done((bf16[2,2,32,16,128]{4,3,2,1,0:T(8,128)(2,1)S(1)}, bf16[2,2,32,16,128]{4,3,2,1,0:T(8,128)(2,1)S(1)}, u32[]{:S(2)}, u32[]{:S(2)}) %collective-permute-start) | collective-permute-done | bytes 524320 | tf_op jit(solution)/shard_map/ppermute | solution.py:289
  28.8 0.0 collective-permute-done.2.refs_4_
  28.8 9.0 %collective-permute-done.1.refs_2_.refs_1_ = bf16[2,2,32,16,128]{4,3,2,1,0:T(8,128)(2,1)S(1)} collective-permute-done((bf16[2,2,32,16,128]{4,3,2,1,0:T(8,128)(2,1)S(1)}, bf16[2,2,32,16,128]{4,3,2,1,0:T(8,128)(2,1)S(1)}, u32[]{:S(2)}, u32[]{:S(2)}) %collective-permute-start.1) | collective-permute-done | bytes 524320 | tf_op jit(solution)/shard_map/ppermute | solution.py:289
  37.7 0.8 pack.3
  38.6 0.0 collective-permute-done.7.refs_1_.refs_2_
  38.6 0.0 collective-permute-done.6.refs_1_
  38.6 0.7 pack.5
  39.3 2.7 %collective-permute-start.10 = (bf16[2,2,2,16,16,128]{5,4,3,2,1,0:T(8,128)(2,1)S(1)}, bf16[2,2,2,16,16,128]{5,4,3,2,1,0:T(8,128)(2,1)S(1)}, u32[]{:S(2)}, u32[]{:S(2)}) collective-permute-start(bf16[2,2,2,16,16,128]{5,4,3,2,1,0:T(8,128)(2,1)S(1)} %get-tuple-element.36), channel_id=1, source_target_pairs={{0,128},{1,129},{2,130},{3,131},{4,4},{5,5},{6,6},{7,7},{8,8},{9,9... | collective-permute-start | bytes 1572872 | tf_op jit(solution)/shard_map/ppermute | solution.py:296
  41.9 0.1 collective-permute-start.3
  42.0 4.8 %collective-permute-start.4 = (bf16[2,2,2,16,16,128]{5,4,3,2,1,0:T(8,128)(2,1)S(1)}, bf16[2,2,2,16,16,128]{5,4,3,2,1,0:T(8,128)(2,1)S(1)}, u32[]{:S(2)}, u32[]{:S(2)}) collective-permute-start(bf16[2,2,2,16,16,128]{5,4,3,2,1,0:T(8,128)(2,1)S(1)} %get-tuple-element.26), channel_id=1, source_target_pairs={{0,0},{1,1},{2,2},{3,3},{4,8},{5,9},{6,10},{7,11},{8,4},{9,5},{10,... | collective-permute-start | bytes 1572872 | tf_op jit(solution)/shard_map/ppermute | solution.py:296
  46.8 9.1 %collective-permute-done.10.refs_3_ = bf16[2,2,2,16,16,128]{5,4,3,2,1,0:T(8,128)(2,1)S(1)} collective-permute-done((bf16[2,2,2,16,16,128]{5,4,3,2,1,0:T(8,128)(2,1)S(1)}, bf16[2,2,2,16,16,128]{5,4,3,2,1,0:T(8,128)(2,1)S(1)}, u32[]{:S(2)}, u32[]{:S(2)}) %collective-permute-start.10) | collective-permute-done | bytes 524320 | tf_op jit(solution)/shard_map/ppermute | solution.py:296
  55.9 2.6 %collective-permute-start.11 = (bf16[2,2,2,16,16,128]{5,4,3,2,1,0:T(8,128)(2,1)S(1)}, bf16[2,2,2,16,16,128]{5,4,3,2,1,0:T(8,128)(2,1)S(1)}, u32[]{:S(2)}, u32[]{:S(2)}) collective-permute-start(bf16[2,2,2,16,16,128]{5,4,3,2,1,0:T(8,128)(2,1)S(1)} %get-tuple-element.38), channel_id=1, source_target_pairs={{0,128},{1,129},{2,130},{3,131},{4,4},{5,5},{6,6},{7,7},{8,8},{9,9... | collective-permute-start | bytes 1572872 | tf_op jit(solution)/shard_map/ppermute | solution.py:296
  58.6 0.1 collective-permute-start.8
  58.7 3.8 %collective-permute-start.9 = (bf16[2,2,2,16,16,128]{5,4,3,2,1,0:T(8,128)(2,1)S(1)}, bf16[2,2,2,16,16,128]{5,4,3,2,1,0:T(8,128)(2,1)S(1)}, u32[]{:S(2)}, u32[]{:S(2)}) collective-permute-start(bf16[2,2,2,16,16,128]{5,4,3,2,1,0:T(8,128)(2,1)S(1)} %get-tuple-element.32), channel_id=1, source_target_pairs={{0,0},{1,1},{2,2},{3,3},{4,8},{5,9},{6,10},{7,11},{8,4},{9,5},{10,... | collective-permute-start | bytes 1572872 | tf_op jit(solution)/shard_map/ppermute | solution.py:296
  62.5 3.8 %partial.2.refs_4_ = f32[33,32,8,128]{3,2,1,0:T(8,128)S(1)} custom-call(s32[2]{0:T(128)S(1)} %pad_add_fusion.refs_0_.flags_ref, bf16[2,2,2,32,16,128]{5,4,3,2,1,0:T(8,128)(2,1)S(1)} %pack.4.refs_0_, bf16[2,2,2,32,16,128]{5,4,3,2,1,0:T(8,128)(2,1)S(1)} %collective-permute-done.6.refs_1_, ...), custom_call_target="tpu_custom_call" | custom-call | flops 17160000 | bytes 4290000 | tf_op jit(solution)/shard_map/partial/pallas_call | solution.py:262
  66.3 0.0 collective-permute-done.3.refs_2_
  66.3 0.0 collective-permute-done.4.refs_3_
  66.3 5.9 %image.2.refs_7_ = f32[4,65,32,256]{3,2,1,0:T(8,128)} custom-call(s32[2]{0:T(128)S(1)} %pad_add_fusion.refs_0_.flags_ref, bf16[2,2,32,16,128]{4,3,2,1,0:T(8,128)(2,1)S(1)} %collective-permute-done.refs_1_.refs_0_, bf16[2,2,32,16,128]{4,3,2,1,0:T(8,128)(2,1)S(1)} %collective-permute-done.1.refs_2_.refs_1_, ...), custom_call_target="tpu_custom_call" | custom-call | flops 17160000 | bytes 4290000 | tf_op jit(solution)/shard_map/image/pallas_call | solution.py:262
  72.3 0.0 collective-permute-done.11.refs_4_
  72.3 4.0 %partial.3.refs_6_ = f32[32,32,8,128]{3,2,1,0:T(8,128)S(1)} custom-call(s32[2]{0:T(128)S(1)} %pad_add_fusion.refs_0_.flags_ref, bf16[2,2,2,32,16,128]{5,4,3,2,1,0:T(8,128)(2,1)S(1)} %pack.4.refs_0_, bf16[2,2,2,32,16,128]{5,4,3,2,1,0:T(8,128)(2,1)S(1)} %collective-permute-done.6.refs_1_, ...), custom_call_target="tpu_custom_call" | custom-call | flops 16640000 | bytes 4160000 | tf_op jit(solution)/shard_map/partial/pallas_call | solution.py:262
  76.2 0.0 collective-permute-done.8.refs_4_
  76.3 3.4 %collective-permute-done.9.refs_5_ = bf16[2,2,2,16,16,128]{5,4,3,2,1,0:T(8,128)(2,1)S(1)} collective-permute-done((bf16[2,2,2,16,16,128]{5,4,3,2,1,0:T(8,128)(2,1)S(1)}, bf16[2,2,2,16,16,128]{5,4,3,2,1,0:T(8,128)(2,1)S(1)}, u32[]{:S(2)}, u32[]{:S(2)}) %collective-permute-start.9) | collective-permute-done | bytes 524320 | tf_op jit(solution)/shard_map/ppermute | solution.py:296
  79.7 6.1 %image.3 = f32[4,65,32,256]{3,2,1,0:T(8,128)} custom-call(s32[2]{0:T(128)S(1)} %pad_add_fusion.refs_0_.flags_ref, bf16[2,2,32,16,128]{4,3,2,1,0:T(8,128)(2,1)S(1)} %collective-permute-done.refs_1_.refs_0_, bf16[2,2,32,16,128]{4,3,2,1,0:T(8,128)(2,1)S(1)} %collective-permute-done.1.refs_2_.refs_1_, ...), custom_call_target="tpu_custom_call", output_to_operand_aliasing={{}: (8, {})} | custom-call | flops 16640000 | bytes 4160000 | tf_op jit(solution)/shard_map/image/pallas_call | solution.py:262
Async XLA Ops:
  1.7 2.0 %collective-permute-start.5 = (bf16[2,2,32,16,128]{4,3,2,1,0:T(8,128)(2,1)S(1)}, bf16[2,2,32,16,128]{4,3,2,1,0:T(8,128)(2,1)S(1)}, u32[]{:S(2)}, u32[]{:S(2)}) collective-permute-start(bf16[2,2,32,16,128]{4,3,2,1,0:T(8,128)(2,1)S(1)} %get-tuple-element.28), channel_id=1, source_target_pairs={{0,1},{1,0},{2,3},{3,2},{4,5},{5,4},{6,7},{7,6},{8,9},{9,8},{10,11... | collective-permute-start | bytes 1572872 | tf_op jit(solution)/shard_map/ppermute | solution.py:289
  4.3 34.3 %collective-permute-start.7 = (bf16[2,2,2,32,16,128]{5,4,3,2,1,0:T(8,128)(2,1)S(1)}, bf16[2,2,2,32,16,128]{5,4,3,2,1,0:T(8,128)(2,1)S(1)}, u32[]{:S(2)}, u32[]{:S(2)}) collective-permute-start(bf16[2,2,2,32,16,128]{5,4,3,2,1,0:T(8,128)(2,1)S(1)} %pack.4.refs_0_), channel_id=1, source_target_pairs={{0,124},{1,125},{2,126},{3,127},{4,8},{5,9},{6,10},{7,11},{8,4},{9... | collective-permute-start | bytes 3145736 | tf_op jit(solution)/shard_map/ppermute | solution.py:296
  12.4 26.2 %collective-permute-start.6 = (bf16[2,2,2,32,16,128]{5,4,3,2,1,0:T(8,128)(2,1)S(1)}, bf16[2,2,2,32,16,128]{5,4,3,2,1,0:T(8,128)(2,1)S(1)}, u32[]{:S(2)}, u32[]{:S(2)}) collective-permute-start(bf16[2,2,2,32,16,128]{5,4,3,2,1,0:T(8,128)(2,1)S(1)} %pack.4.refs_0_), channel_id=1, source_target_pairs={{0,4},{1,5},{2,6},{3,7},{4,0},{5,1},{6,2},{7,3},{8,12},{9,13},{10,... | collective-permute-start | bytes 3145736 | tf_op jit(solution)/shard_map/ppermute | solution.py:296
  12.4 16.3 %collective-permute-start = (bf16[2,2,32,16,128]{4,3,2,1,0:T(8,128)(2,1)S(1)}, bf16[2,2,32,16,128]{4,3,2,1,0:T(8,128)(2,1)S(1)}, u32[]{:S(2)}, u32[]{:S(2)}) collective-permute-start(bf16[2,2,32,16,128]{4,3,2,1,0:T(8,128)(2,1)S(1)} %get-tuple-element.23.refs_3_), channel_id=1, source_target_pairs={{0,2},{1,3},{2,0},{3,1},{4,6},{5,7},{6,4},{7,5},{8,10},{9,11},{10,... | collective-permute-start | bytes 1572872 | tf_op jit(solution)/shard_map/ppermute | solution.py:289
  13.7 15.1 %collective-permute-start.2 = (bf16[2,2,32,16,128]{4,3,2,1,0:T(8,128)(2,1)S(1)}, bf16[2,2,32,16,128]{4,3,2,1,0:T(8,128)(2,1)S(1)}, u32[]{:S(2)}, u32[]{:S(2)}) collective-permute-start(bf16[2,2,32,16,128]{4,3,2,1,0:T(8,128)(2,1)S(1)} %get-tuple-element.24), channel_id=1, source_target_pairs={{0,1},{1,0},{2,3},{3,2},{4,5},{5,4},{6,7},{7,6},{8,9},{9,8},{10,11... | collective-permute-start | bytes 1572872 | tf_op jit(solution)/shard_map/ppermute | solution.py:289
  13.7 24.0 %collective-permute-start.1 = (bf16[2,2,32,16,128]{4,3,2,1,0:T(8,128)(2,1)S(1)}, bf16[2,2,32,16,128]{4,3,2,1,0:T(8,128)(2,1)S(1)}, u32[]{:S(2)}, u32[]{:S(2)}) collective-permute-start(bf16[2,2,32,16,128]{4,3,2,1,0:T(8,128)(2,1)S(1)} %get-tuple-element.24), channel_id=1, source_target_pairs={{0,3},{1,2},{2,1},{3,0},{4,7},{5,6},{6,5},{7,4},{8,11},{9,10},{10,... | collective-permute-start | bytes 1572872 | tf_op jit(solution)/shard_map/ppermute | solution.py:289
  39.3 16.7 %collective-permute-start.10 = (bf16[2,2,2,16,16,128]{5,4,3,2,1,0:T(8,128)(2,1)S(1)}, bf16[2,2,2,16,16,128]{5,4,3,2,1,0:T(8,128)(2,1)S(1)}, u32[]{:S(2)}, u32[]{:S(2)}) collective-permute-start(bf16[2,2,2,16,16,128]{5,4,3,2,1,0:T(8,128)(2,1)S(1)} %get-tuple-element.36), channel_id=1, source_target_pairs={{0,128},{1,129},{2,130},{3,131},{4,4},{5,5},{6,6},{7,7},{8,8},{9,9... | collective-permute-start | bytes 1572872 | tf_op jit(solution)/shard_map/ppermute | solution.py:296
  41.9 24.4 %collective-permute-start.3 = (bf16[2,2,2,16,16,128]{5,4,3,2,1,0:T(8,128)(2,1)S(1)}, bf16[2,2,2,16,16,128]{5,4,3,2,1,0:T(8,128)(2,1)S(1)}, u32[]{:S(2)}, u32[]{:S(2)}) collective-permute-start(bf16[2,2,2,16,16,128]{5,4,3,2,1,0:T(8,128)(2,1)S(1)} %get-tuple-element.25), channel_id=1, source_target_pairs={{0,4},{1,5},{2,6},{3,7},{4,0},{5,1},{6,2},{7,3},{8,12},{9,13},{10,... | collective-permute-start | bytes 1572872 | tf_op jit(solution)/shard_map/ppermute | solution.py:296
  42.0 24.3 %collective-permute-start.4 = (bf16[2,2,2,16,16,128]{5,4,3,2,1,0:T(8,128)(2,1)S(1)}, bf16[2,2,2,16,16,128]{5,4,3,2,1,0:T(8,128)(2,1)S(1)}, u32[]{:S(2)}, u32[]{:S(2)}) collective-permute-start(bf16[2,2,2,16,16,128]{5,4,3,2,1,0:T(8,128)(2,1)S(1)} %get-tuple-element.26), channel_id=1, source_target_pairs={{0,0},{1,1},{2,2},{3,3},{4,8},{5,9},{6,10},{7,11},{8,4},{9,5},{10,... | collective-permute-start | bytes 1572872 | tf_op jit(solution)/shard_map/ppermute | solution.py:296
  55.9 16.3 %collective-permute-start.11 = (bf16[2,2,2,16,16,128]{5,4,3,2,1,0:T(8,128)(2,1)S(1)}, bf16[2,2,2,16,16,128]{5,4,3,2,1,0:T(8,128)(2,1)S(1)}, u32[]{:S(2)}, u32[]{:S(2)}) collective-permute-start(bf16[2,2,2,16,16,128]{5,4,3,2,1,0:T(8,128)(2,1)S(1)} %get-tuple-element.38), channel_id=1, source_target_pairs={{0,128},{1,129},{2,130},{3,131},{4,4},{5,5},{6,6},{7,7},{8,8},{9,9... | collective-permute-start | bytes 1572872 | tf_op jit(solution)/shard_map/ppermute | solution.py:296
  58.6 17.7 %collective-permute-start.8 = (bf16[2,2,2,16,16,128]{5,4,3,2,1,0:T(8,128)(2,1)S(1)}, bf16[2,2,2,16,16,128]{5,4,3,2,1,0:T(8,128)(2,1)S(1)}, u32[]{:S(2)}, u32[]{:S(2)}) collective-permute-start(bf16[2,2,2,16,16,128]{5,4,3,2,1,0:T(8,128)(2,1)S(1)} %get-tuple-element.31), channel_id=1, source_target_pairs={{0,4},{1,5},{2,6},{3,7},{4,0},{5,1},{6,2},{7,3},{8,12},{9,13},{10,... | collective-permute-start | bytes 1572872 | tf_op jit(solution)/shard_map/ppermute | solution.py:296
  58.7 21.0 %collective-permute-start.9 = (bf16[2,2,2,16,16,128]{5,4,3,2,1,0:T(8,128)(2,1)S(1)}, bf16[2,2,2,16,16,128]{5,4,3,2,1,0:T(8,128)(2,1)S(1)}, u32[]{:S(2)}, u32[]{:S(2)}) collective-permute-start(bf16[2,2,2,16,16,128]{5,4,3,2,1,0:T(8,128)(2,1)S(1)} %get-tuple-element.32), channel_id=1, source_target_pairs={{0,0},{1,1},{2,2},{3,3},{4,8},{5,9},{6,10},{7,11},{8,4},{9,5},{10,... | collective-permute-start | bytes 1572872 | tf_op jit(solution)/shard_map/ppermute | solution.py:296

commit v6 on v5

--- a/solution.py
+++ b/solution.py
@@ -102,7 +102,7 @@
             pl.when((flags_ref[1] == 1) == crosses)(copy)
 
 
-def pack(flags, arrays, copies, shapes, weight=1):
+def pack(flags, arrays, copies, shapes):
     vmem = pl.BlockSpec(memory_space=pltpu.VMEM)
     return pl.pallas_call(
         functools.partial(pack_kernel, copies, len(arrays)),
@@ -110,7 +110,7 @@
         out_specs=[vmem] * len(shapes),
         out_shape=[jax.ShapeDtypeStruct(shape, jnp.bfloat16) for shape in shapes],
         compiler_params=pltpu.CompilerParams(vmem_limit_bytes=12 << 20),
-        cost_estimate=pl.CostEstimate(flops=0, bytes_accessed=weight * (2 << 20), transcendentals=0),
+        cost_estimate=pl.CostEstimate(flops=0, bytes_accessed=2 << 20, transcendentals=0),
         name="pack",
     )(flags, *arrays)
 
@@ -310,38 +310,41 @@
     two, three, one, other = swap(parts[2], 2), swap(parts[3], 3), swap(parts[1], 1), swap(parts[3], 1)
 
     whole, half = [(2, 2, freqs, length, ROWS, LANES) for length in (cells, NEAR)]
-    (own,) = pack(flags, (parts[0], one), ((None, 0, None, 0, 0, 0), (None, 1, None, 0, 0, 1)), (whole,))
-    whole_a, whole_b = trade(own, side_a), trade(own, side_b_of_half)
-
     rest = cells - NEAR
+    copies = []
+    for slot in range(2):
+        copies += [(None, slot, None, 0, 0, slot), (None, 2 + slot, None, 0, 1, slot)]
+        copies += [(None, slot, None, (0, rest), 2, slot), (None, slot, None, (rest, 0), 3, slot)]
+    own, turned_own, near_b, far_b = pack(flags, (parts[0], one, parts[2], other), copies, (whole,) * 2 + (half,) * 2)
+    whole_a = trade(own, side_a)
+    first_near_b, first_far_b = trade(near_b, side_b_of_half), trade(far_b, side_b_of_half)
+    near_over, far_over = trade(first_near_b, over_middle), trade(first_far_b, over_middle)
+
     copies = []
     for slot in range(2):
         for out, at in ((0, (rest, 0)), (2, (0, rest))):
             copies.append((None, slot, None, at, out, slot))
         for out, at in ((1, (0, rest)), (3, (rest, 0))):
-            copies += [(False, slot, None, at, out, slot), (True, 2 + slot, None, at, out, slot)]
-    near_a, near_b, far_a, far_b = pack(flags, (two, three, parts[2], other), copies, (half,) * 4, 1)
+            copies += [(False, slot, None, at, out, slot), (True, 2, slot, at, out, slot)]
+    near_a, near_b, far_a, far_b = pack(flags, (two, three, turned_own), copies, (half,) * 4)
     turned = (middle - 1, middle)
     near_a, near_b = trade(near_a, side_a), trade(near_b, side_b, turned)
-    whole_a, whole_b, far_a, far_b = lax.optimization_barrier((whole_a, whole_b, far_a, far_b))
-    copies = [(None, 0, slot, at, out, slot) for slot in range(2) for out, at in ((0, (rest, 0)), (1, (0, rest)))]
-    near_over, far_over = pack(flags, (whole_b,), copies, (half,) * 2)
-    near_over = trade(near_over, over_middle)
+    whole_a, first_near_b, first_far_b, far_a, far_b = lax.optimization_barrier(
+        (whole_a, first_near_b, first_far_b, far_a, far_b)
+    )
     far_a, far_b = trade(far_a, side_a), trade(far_b, side_b, turned)
-    far_over, near_over = lax.optimization_barrier((far_over, near_over))
-    far_over = trade(far_over, over_middle)
 
     near_at_a, near_at_b = (2 * cells, rest), (rest, 2 * cells)
     far_at_a, far_at_b = (2 * cells + NEAR, 0), (0, 2 * cells + NEAR)
     plan, far_plan = [], []
     for g in range(2):
         plan += [(0, g, 0, cells, cells, g, None), (1, g, (0, rest), NEAR, near_at_a, g, None)]
-        plan += [(2, g, (rest, 0), NEAR, near_at_b, g, (0,)), (3, g, 0, NEAR, near_at_b, g, (1,))]
+        plan += [(2, g, 0, NEAR, near_at_b, g, (0,)), (3, g, 0, NEAR, near_at_b, g, (1,))]
         plan += [(None, g, 0, NEAR, near_at_b, g, (2,))]
         far_plan += [(1, g, (rest, 0), NEAR, far_at_a, g, None)]
-        far_plan += [(2, g, (0, rest), NEAR, far_at_b, g, (0,)), (4, g, 0, NEAR, far_at_b, g, (1,))]
+        far_plan += [(4, g, 0, NEAR, far_at_b, g, (0,)), (5, g, 0, NEAR, far_at_b, g, (1,))]
         far_plan += [(None, g, 0, NEAR, far_at_b, g, (2,))]
-    blocks = (own, whole_a, whole_b, near_over)
+    blocks = (own, whole_a, first_near_b, near_over)
     befores = summed(flags, blocks, plan, (NEAR_BAND,), None, cells, 2, 0)
     far_sums = (flags, plan + far_plan, blocks)
     plan = [(0, None, 0, cells, cells, 0, None), (1, None, 0, cells, cells, 1, None)]
@@ -353,7 +356,7 @@
         far_plan += [(5, g, 0, NEAR, far_at_b, g, (0, 1)), (None, g, 0, NEAR, far_at_b, g, (2,))]
     image = summed(flags, (two, three, near_a, near_b), plan, (NEAR_BAND,), befores, cells, 2, 1)
     image, far_over = lax.optimization_barrier((image, far_over))
-    befores = summed(flags, far_sums[2] + (far_over,), far_sums[1], (FAR_BAND,), None, cells, 2, 0)
+    befores = summed(flags, far_sums[2] + (first_far_b, far_over), far_sums[1], (FAR_BAND,), None, cells, 2, 0)
     blocks = (two, three, near_a, near_b, far_a, far_b)
     return summed(flags, blocks, plan + far_plan, (FAR_BAND,), befores, cells, 2, 2, image)
 

time: 86 us -> 79.7 us (0.927)
  the two profiles are of different devices: /device:TPU:24 before, /device:TPU:8 now
where the time goes in v6:
time: 79.7 us; the launch traced here: 79.3 us
  waiting for transfers between devices  33.8 us (42%)
  Pallas kernels  23.2 us (29%)
  starting transfers between devices  22.1 us (28%)
    ppermute x9, waiting for transfers between devices, trade(): return lax.ppermute(value, ('slab', 'freq'), pairs)  21 us
    pallas_call x4, Pallas kernels, summed(): pl.pallas_call(functools.partial(sum_kernel, plan, bands, first, last), i...  19.8 us
    ppermute x9, starting transfers between devices, trade(): return lax.ppermute(value, ('slab', 'freq'), pairs)  19.1 us
    ppermute x4, waiting for transfers between devices, swap(): return lax.ppermute(part, 'freq', [(g, g ^ d) for g in range(GROUPS)])  12.9 us
    ppermute x4, starting transfers between devices, swap(): return lax.ppermute(part, 'freq', [(g, g ^ d) for g in range(GROUPS)])  3.02 us
    pallas_call x2, Pallas kernels, pack(): pl.pallas_call(functools.partial(pack_kernel, copies, len(arrays)), in_sp...  1.7 us
    pallas_call x1, Pallas kernels, regrouped(): pl.pallas_call(regroup_kernel, in_specs=[pl.BlockSpec(memory_space=pltpu....  1.66 us
  transfers between devices with their start and end apart: 13, of which 8 were waited for; matrix products, arithmetic and copies ran while one was open for 0% of the time, Pallas kernels for 18%

profile of v6, /device:TPU:8, one launch (start us, length us, event | category | flops | bytes accessed | tf_op | source)
XLA Modules:
  0.0 79.3 jit_solution(10463732892842279596)
XLA Ops:
  0.0 1.7 %regroup.1 = (bf16[2,2,32,16,128]{4,3,2,1,0:T(8,128)(2,1)S(1)}, bf16[2,2,32,16,128]{4,3,2,1,0:T(8,128)(2,1)S(1)}, bf16[2,2,32,16,128]{4,3,2,1,0:T(8,128)(2,1)S(1)}, bf16[2,2,32,16,128]{4,3,2,1,0:T(8,128)(2,1)S(1)}) custom-call(s32[1]{0:T(128)} %bitcast.2.group_ref, bf16[2,2,32,16,256]{4,3,2,1,0:T(8,128)(2,1)} %source_ref.1, ...), custom_call_target="tpu_custom_call" | custom-call | bytes 4194304 | tf_op jit(solution)/shard_map/regroup/pallas_call | solution.py:65
  1.7 0.1 collective-permute-start.2
  1.8 0.5 collective-permute-start.3
  2.3 0.1 pad_add_fusion.refs_0_.flags_ref
  2.3 1.3 %collective-permute-done.2.refs_2_ = bf16[2,2,32,16,128]{4,3,2,1,0:T(8,128)(2,1)S(1)} collective-permute-done((bf16[2,2,32,16,128]{4,3,2,1,0:T(8,128)(2,1)S(1)}, bf16[2,2,32,16,128]{4,3,2,1,0:T(8,128)(2,1)S(1)}, u32[]{:S(2)}, u32[]{:S(2)}) %collective-permute-start.2) | collective-permute-done | bytes 524320 | tf_op jit(solution)/shard_map/ppermute | solution.py:289
  3.7 0.7 collective-permute-done.3.refs_4_
  4.4 0.9 %pack.2 = (bf16[2,2,2,32,16,128]{5,4,3,2,1,0:T(8,128)(2,1)S(1)}, bf16[2,2,2,32,16,128]{5,4,3,2,1,0:T(8,128)(2,1)S(1)}, bf16[2,2,2,16,16,128]{5,4,3,2,1,0:T(8,128)(2,1)S(1)}, bf16[2,2,2,16,16,128]{5,4,3,2,1,0:T(8,128)(2,1)S(1)}) custom-call(s32[2]{0:T(128)S(1)} %pad_add_fusion.refs_0_.flags_ref, bf16[2,2,32,16,128]{4,3,2,1,0:T(8,128)(2,1)S(1)} %get-tuple-element.26.refs_1_, ...), custom_call_target="tpu_custom_call" | custom-call | bytes 2097152 | tf_op jit(solution)/shard_map/pack/pallas_call | solution.py:107
  5.3 1.6 %collective-permute-start.6 = (bf16[2,2,2,32,16,128]{5,4,3,2,1,0:T(8,128)(2,1)S(1)}, bf16[2,2,2,32,16,128]{5,4,3,2,1,0:T(8,128)(2,1)S(1)}, u32[]{:S(2)}, u32[]{:S(2)}) collective-permute-start(bf16[2,2,2,32,16,128]{5,4,3,2,1,0:T(8,128)(2,1)S(1)} %get-tuple-element.31.refs_0_), channel_id=1, source_target_pairs={{0,4},{1,5},{2,6},{3,7},{4,0},{5,1},{6,2},{7,3},{8,12},{9,13},{10,... | collective-permute-start | bytes 3145736 | tf_op jit(solution)/shard_map/ppermute | solution.py:296
  6.9 7.4 %collective-permute-start.7 = (bf16[2,2,2,16,16,128]{5,4,3,2,1,0:T(8,128)(2,1)S(1)}, bf16[2,2,2,16,16,128]{5,4,3,2,1,0:T(8,128)(2,1)S(1)}, u32[]{:S(2)}, u32[]{:S(2)}) collective-permute-start(bf16[2,2,2,16,16,128]{5,4,3,2,1,0:T(8,128)(2,1)S(1)} %get-tuple-element.32), channel_id=1, source_target_pairs={{0,124},{1,125},{2,126},{3,127},{4,8},{5,9},{6,10},{7,11},{8,4},{9... | collective-permute-start | bytes 1572872 | tf_op jit(solution)/shard_map/ppermute | solution.py:296
  14.3 2.3 %collective-permute-start = (bf16[2,2,32,16,128]{4,3,2,1,0:T(8,128)(2,1)S(1)}, bf16[2,2,32,16,128]{4,3,2,1,0:T(8,128)(2,1)S(1)}, u32[]{:S(2)}, u32[]{:S(2)}) collective-permute-start(bf16[2,2,32,16,128]{4,3,2,1,0:T(8,128)(2,1)S(1)} %get-tuple-element.24.refs_3_), channel_id=1, source_target_pairs={{0,2},{1,3},{2,0},{3,1},{4,6},{5,7},{6,4},{7,5},{8,10},{9,11},{10,... | collective-permute-start | bytes 1572872 | tf_op jit(solution)/shard_map/ppermute | solution.py:289
  16.5 0.2 collective-permute-start.1
  16.7 0.3 collective-permute-start.8
  17.0 10.0 %collective-permute-done.7.refs_2_ = bf16[2,2,2,16,16,128]{5,4,3,2,1,0:T(8,128)(2,1)S(1)} collective-permute-done((bf16[2,2,2,16,16,128]{5,4,3,2,1,0:T(8,128)(2,1)S(1)}, bf16[2,2,2,16,16,128]{5,4,3,2,1,0:T(8,128)(2,1)S(1)}, u32[]{:S(2)}, u32[]{:S(2)}) %collective-permute-start.7) | collective-permute-done | bytes 524320 | tf_op jit(solution)/shard_map/ppermute | solution.py:296
  27.0 2.3 %collective-permute-start.11 = (bf16[2,2,2,16,16,128]{5,4,3,2,1,0:T(8,128)(2,1)S(1)}, bf16[2,2,2,16,16,128]{5,4,3,2,1,0:T(8,128)(2,1)S(1)}, u32[]{:S(2)}, u32[]{:S(2)}) collective-permute-start(bf16[2,2,2,16,16,128]{5,4,3,2,1,0:T(8,128)(2,1)S(1)} %collective-permute-done.7.refs_2_), channel_id=1, source_target_pairs={{0,128},{1,129},{2,130},{3,131},{4,4},{5,5},{6,6},{7,7},{8,8},{9,9... | collective-permute-start | bytes 1572872 | tf_op jit(solution)/shard_map/ppermute | solution.py:296
  29.3 1.3 %collective-permute-done.refs_1_.refs_0_ = bf16[2,2,32,16,128]{4,3,2,1,0:T(8,128)(2,1)S(1)} collective-permute-done((bf16[2,2,32,16,128]{4,3,2,1,0:T(8,128)(2,1)S(1)}, bf16[2,2,32,16,128]{4,3,2,1,0:T(8,128)(2,1)S(1)}, u32[]{:S(2)}, u32[]{:S(2)}) %collective-permute-start) | collective-permute-done | bytes 524320 | tf_op jit(solution)/shard_map/ppermute | solution.py:289
  30.6 9.5 %collective-permute-done.1.refs_2_.refs_1_ = bf16[2,2,32,16,128]{4,3,2,1,0:T(8,128)(2,1)S(1)} collective-permute-done((bf16[2,2,32,16,128]{4,3,2,1,0:T(8,128)(2,1)S(1)}, bf16[2,2,32,16,128]{4,3,2,1,0:T(8,128)(2,1)S(1)}, u32[]{:S(2)}, u32[]{:S(2)}) %collective-permute-start.1) | collective-permute-done | bytes 524320 | tf_op jit(solution)/shard_map/ppermute | solution.py:289
  40.1 0.8 %pack.3 = (bf16[2,2,2,16,16,128]{5,4,3,2,1,0:T(8,128)(2,1)S(1)}, bf16[2,2,2,16,16,128]{5,4,3,2,1,0:T(8,128)(2,1)S(1)}, bf16[2,2,2,16,16,128]{5,4,3,2,1,0:T(8,128)(2,1)S(1)}, bf16[2,2,2,16,16,128]{5,4,3,2,1,0:T(8,128)(2,1)S(1)}) custom-call(s32[2]{0:T(128)S(1)} %pad_add_fusion.refs_0_.flags_ref, ...), custom_call_target="tpu_custom_call" | custom-call | bytes 2097152 | tf_op jit(solution)/shard_map/pack/pallas_call | solution.py:107
  41.0 0.1 collective-permute-start.4
  41.1 3.5 %collective-permute-start.5 = (bf16[2,2,2,16,16,128]{5,4,3,2,1,0:T(8,128)(2,1)S(1)}, bf16[2,2,2,16,16,128]{5,4,3,2,1,0:T(8,128)(2,1)S(1)}, u32[]{:S(2)}, u32[]{:S(2)}) collective-permute-start(bf16[2,2,2,16,16,128]{5,4,3,2,1,0:T(8,128)(2,1)S(1)} %get-tuple-element.30), channel_id=1, source_target_pairs={{0,0},{1,1},{2,2},{3,3},{4,8},{5,9},{6,10},{7,11},{8,4},{9,5},{10,... | collective-permute-start | bytes 1572872 | tf_op jit(solution)/shard_map/ppermute | solution.py:296
  44.6 0.0 collective-permute-done.8.refs_4_
  44.6 1.9 %collective-permute-start.12 = (bf16[2,2,2,16,16,128]{5,4,3,2,1,0:T(8,128)(2,1)S(1)}, bf16[2,2,2,16,16,128]{5,4,3,2,1,0:T(8,128)(2,1)S(1)}, u32[]{:S(2)}, u32[]{:S(2)}) collective-permute-start(bf16[2,2,2,16,16,128]{5,4,3,2,1,0:T(8,128)(2,1)S(1)} %collective-permute-done.8.refs_4_), channel_id=1, source_target_pairs={{0,128},{1,129},{2,130},{3,131},{4,4},{5,5},{6,6},{7,7},{8,8},{9,9... | collective-permute-start | bytes 1572872 | tf_op jit(solution)/shard_map/ppermute | solution.py:296
  46.5 0.0 collective-permute-done.6.refs_1_
  46.5 0.1 collective-permute-start.9
  46.6 6.5 %collective-permute-done.11.refs_3_ = bf16[2,2,2,16,16,128]{5,4,3,2,1,0:T(8,128)(2,1)S(1)} collective-permute-done((bf16[2,2,2,16,16,128]{5,4,3,2,1,0:T(8,128)(2,1)S(1)}, bf16[2,2,2,16,16,128]{5,4,3,2,1,0:T(8,128)(2,1)S(1)}, u32[]{:S(2)}, u32[]{:S(2)}) %collective-permute-start.11) | collective-permute-done | bytes 524320 | tf_op jit(solution)/shard_map/ppermute | solution.py:296
  53.2 1.9 %collective-permute-start.10 = (bf16[2,2,2,16,16,128]{5,4,3,2,1,0:T(8,128)(2,1)S(1)}, bf16[2,2,2,16,16,128]{5,4,3,2,1,0:T(8,128)(2,1)S(1)}, u32[]{:S(2)}, u32[]{:S(2)}) collective-permute-start(bf16[2,2,2,16,16,128]{5,4,3,2,1,0:T(8,128)(2,1)S(1)} %get-tuple-element.37), channel_id=1, source_target_pairs={{0,0},{1,1},{2,2},{3,3},{4,8},{5,9},{6,10},{7,11},{8,4},{9,5},{10,... | collective-permute-start | bytes 1572872 | tf_op jit(solution)/shard_map/ppermute | solution.py:296
  55.1 3.8 %partial.2.refs_4_ = f32[33,32,8,128]{3,2,1,0:T(8,128)S(1)} custom-call(s32[2]{0:T(128)S(1)} %pad_add_fusion.refs_0_.flags_ref, bf16[2,2,2,32,16,128]{5,4,3,2,1,0:T(8,128)(2,1)S(1)} %get-tuple-element.31.refs_0_, bf16[2,2,2,32,16,128]{5,4,3,2,1,0:T(8,128)(2,1)S(1)} %collective-permute-done.6.refs_1_, ...), custom_call_target="tpu_custom_call" | custom-call | flops 17160000 | bytes 4290000 | tf_op jit(solution)/shard_map/partial/pallas_call | solution.py:262
  58.9 0.0 collective-permute-done.4.refs_2_
  58.9 2.6 %collective-permute-done.5.refs_3_ = bf16[2,2,2,16,16,128]{5,4,3,2,1,0:T(8,128)(2,1)S(1)} collective-permute-done((bf16[2,2,2,16,16,128]{5,4,3,2,1,0:T(8,128)(2,1)S(1)}, bf16[2,2,2,16,16,128]{5,4,3,2,1,0:T(8,128)(2,1)S(1)}, u32[]{:S(2)}, u32[]{:S(2)}) %collective-permute-start.5) | collective-permute-done | bytes 524320 | tf_op jit(solution)/shard_map/ppermute | solution.py:296
  61.5 5.9 %image.2.refs_7_ = f32[4,65,32,256]{3,2,1,0:T(8,128)} custom-call(s32[2]{0:T(128)S(1)} %pad_add_fusion.refs_0_.flags_ref, bf16[2,2,32,16,128]{4,3,2,1,0:T(8,128)(2,1)S(1)} %collective-permute-done.refs_1_.refs_0_, bf16[2,2,32,16,128]{4,3,2,1,0:T(8,128)(2,1)S(1)} %collective-permute-done.1.refs_2_.refs_1_, ...), custom_call_target="tpu_custom_call" | custom-call | flops 17160000 | bytes 4290000 | tf_op jit(solution)/shard_map/image/pallas_call | solution.py:262
  67.4 0.0 collective-permute-done.12.refs_5_
  67.4 4.0 %partial.3.refs_6_ = f32[32,32,8,128]{3,2,1,0:T(8,128)S(1)} custom-call(s32[2]{0:T(128)S(1)} %pad_add_fusion.refs_0_.flags_ref, bf16[2,2,2,32,16,128]{5,4,3,2,1,0:T(8,128)(2,1)S(1)} %get-tuple-element.31.refs_0_, bf16[2,2,2,32,16,128]{5,4,3,2,1,0:T(8,128)(2,1)S(1)} %collective-permute-done.6.refs_1_, ...), custom_call_target="tpu_custom_call" | custom-call | flops 16640000 | bytes 4160000 | tf_op jit(solution)/shard_map/partial/pallas_call | solution.py:262
  71.4 0.0 collective-permute-done.9.refs_4_
  71.4 1.8 %collective-permute-done.10.refs_5_ = bf16[2,2,2,16,16,128]{5,4,3,2,1,0:T(8,128)(2,1)S(1)} collective-permute-done((bf16[2,2,2,16,16,128]{5,4,3,2,1,0:T(8,128)(2,1)S(1)}, bf16[2,2,2,16,16,128]{5,4,3,2,1,0:T(8,128)(2,1)S(1)}, u32[]{:S(2)}, u32[]{:S(2)}) %collective-permute-start.10) | collective-permute-done | bytes 524320 | tf_op jit(solution)/shard_map/ppermute | solution.py:296
  73.2 6.1 %image.3 = f32[4,65,32,256]{3,2,1,0:T(8,128)} custom-call(s32[2]{0:T(128)S(1)} %pad_add_fusion.refs_0_.flags_ref, bf16[2,2,32,16,128]{4,3,2,1,0:T(8,128)(2,1)S(1)} %collective-permute-done.refs_1_.refs_0_, bf16[2,2,32,16,128]{4,3,2,1,0:T(8,128)(2,1)S(1)} %collective-permute-done.1.refs_2_.refs_1_, ...), custom_call_target="tpu_custom_call", output_to_operand_aliasing={{}: (8, {})} | custom-call | flops 16640000 | bytes 4160000 | tf_op jit(solution)/shard_map/image/pallas_call | solution.py:262
Async XLA Ops:
  1.7 2.0 %collective-permute-start.2 = (bf16[2,2,32,16,128]{4,3,2,1,0:T(8,128)(2,1)S(1)}, bf16[2,2,32,16,128]{4,3,2,1,0:T(8,128)(2,1)S(1)}, u32[]{:S(2)}, u32[]{:S(2)}) collective-permute-start(bf16[2,2,32,16,128]{4,3,2,1,0:T(8,128)(2,1)S(1)} %get-tuple-element.27), channel_id=1, source_target_pairs={{0,1},{1,0},{2,3},{3,2},{4,5},{5,4},{6,7},{7,6},{8,9},{9,8},{10,11... | collective-permute-start | bytes 1572872 | tf_op jit(solution)/shard_map/ppermute | solution.py:289
  1.8 2.6 %collective-permute-start.3 = (bf16[2,2,32,16,128]{4,3,2,1,0:T(8,128)(2,1)S(1)}, bf16[2,2,32,16,128]{4,3,2,1,0:T(8,128)(2,1)S(1)}, u32[]{:S(2)}, u32[]{:S(2)}) collective-permute-start(bf16[2,2,32,16,128]{4,3,2,1,0:T(8,128)(2,1)S(1)} %get-tuple-element.25), channel_id=1, source_target_pairs={{0,1},{1,0},{2,3},{3,2},{4,5},{5,4},{6,7},{7,6},{8,9},{9,8},{10,11... | collective-permute-start | bytes 1572872 | tf_op jit(solution)/shard_map/ppermute | solution.py:289
  5.3 41.2 %collective-permute-start.6 = (bf16[2,2,2,32,16,128]{5,4,3,2,1,0:T(8,128)(2,1)S(1)}, bf16[2,2,2,32,16,128]{5,4,3,2,1,0:T(8,128)(2,1)S(1)}, u32[]{:S(2)}, u32[]{:S(2)}) collective-permute-start(bf16[2,2,2,32,16,128]{5,4,3,2,1,0:T(8,128)(2,1)S(1)} %get-tuple-element.31.refs_0_), channel_id=1, source_target_pairs={{0,4},{1,5},{2,6},{3,7},{4,0},{5,1},{6,2},{7,3},{8,12},{9,13},{10,... | collective-permute-start | bytes 3145736 | tf_op jit(solution)/shard_map/ppermute | solution.py:296
  6.9 20.1 %collective-permute-start.7 = (bf16[2,2,2,16,16,128]{5,4,3,2,1,0:T(8,128)(2,1)S(1)}, bf16[2,2,2,16,16,128]{5,4,3,2,1,0:T(8,128)(2,1)S(1)}, u32[]{:S(2)}, u32[]{:S(2)}) collective-permute-start(bf16[2,2,2,16,16,128]{5,4,3,2,1,0:T(8,128)(2,1)S(1)} %get-tuple-element.32), channel_id=1, source_target_pairs={{0,124},{1,125},{2,126},{3,127},{4,8},{5,9},{6,10},{7,11},{8,4},{9... | collective-permute-start | bytes 1572872 | tf_op jit(solution)/shard_map/ppermute | solution.py:296
  14.3 16.4 %collective-permute-start = (bf16[2,2,32,16,128]{4,3,2,1,0:T(8,128)(2,1)S(1)}, bf16[2,2,32,16,128]{4,3,2,1,0:T(8,128)(2,1)S(1)}, u32[]{:S(2)}, u32[]{:S(2)}) collective-permute-start(bf16[2,2,32,16,128]{4,3,2,1,0:T(8,128)(2,1)S(1)} %get-tuple-element.24.refs_3_), channel_id=1, source_target_pairs={{0,2},{1,3},{2,0},{3,1},{4,6},{5,7},{6,4},{7,5},{8,10},{9,11},{10,... | collective-permute-start | bytes 1572872 | tf_op jit(solution)/shard_map/ppermute | solution.py:289
  16.5 23.6 %collective-permute-start.1 = (bf16[2,2,32,16,128]{4,3,2,1,0:T(8,128)(2,1)S(1)}, bf16[2,2,32,16,128]{4,3,2,1,0:T(8,128)(2,1)S(1)}, u32[]{:S(2)}, u32[]{:S(2)}) collective-permute-start(bf16[2,2,32,16,128]{4,3,2,1,0:T(8,128)(2,1)S(1)} %get-tuple-element.25), channel_id=1, source_target_pairs={{0,3},{1,2},{2,1},{3,0},{4,7},{5,6},{6,5},{7,4},{8,11},{9,10},{10,... | collective-permute-start | bytes 1572872 | tf_op jit(solution)/shard_map/ppermute | solution.py:289
  16.7 27.9 %collective-permute-start.8 = (bf16[2,2,2,16,16,128]{5,4,3,2,1,0:T(8,128)(2,1)S(1)}, bf16[2,2,2,16,16,128]{5,4,3,2,1,0:T(8,128)(2,1)S(1)}, u32[]{:S(2)}, u32[]{:S(2)}) collective-permute-start(bf16[2,2,2,16,16,128]{5,4,3,2,1,0:T(8,128)(2,1)S(1)} %get-tuple-element.33), channel_id=1, source_target_pairs={{0,124},{1,125},{2,126},{3,127},{4,8},{5,9},{6,10},{7,11},{8,4},{9... | collective-permute-start | bytes 1572872 | tf_op jit(solution)/shard_map/ppermute | solution.py:296
  27.0 26.2 %collective-permute-start.11 = (bf16[2,2,2,16,16,128]{5,4,3,2,1,0:T(8,128)(2,1)S(1)}, bf16[2,2,2,16,16,128]{5,4,3,2,1,0:T(8,128)(2,1)S(1)}, u32[]{:S(2)}, u32[]{:S(2)}) collective-permute-start(bf16[2,2,2,16,16,128]{5,4,3,2,1,0:T(8,128)(2,1)S(1)} %collective-permute-done.7.refs_2_), channel_id=1, source_target_pairs={{0,128},{1,129},{2,130},{3,131},{4,4},{5,5},{6,6},{7,7},{8,8},{9,9... | collective-permute-start | bytes 1572872 | tf_op jit(solution)/shard_map/ppermute | solution.py:296
  41.0 17.9 %collective-permute-start.4 = (bf16[2,2,2,16,16,128]{5,4,3,2,1,0:T(8,128)(2,1)S(1)}, bf16[2,2,2,16,16,128]{5,4,3,2,1,0:T(8,128)(2,1)S(1)}, u32[]{:S(2)}, u32[]{:S(2)}) collective-permute-start(bf16[2,2,2,16,16,128]{5,4,3,2,1,0:T(8,128)(2,1)S(1)} %get-tuple-element.29), channel_id=1, source_target_pairs={{0,4},{1,5},{2,6},{3,7},{4,0},{5,1},{6,2},{7,3},{8,12},{9,13},{10,... | collective-permute-start | bytes 1572872 | tf_op jit(solution)/shard_map/ppermute | solution.py:296
  41.1 20.4 %collective-permute-start.5 = (bf16[2,2,2,16,16,128]{5,4,3,2,1,0:T(8,128)(2,1)S(1)}, bf16[2,2,2,16,16,128]{5,4,3,2,1,0:T(8,128)(2,1)S(1)}, u32[]{:S(2)}, u32[]{:S(2)}) collective-permute-start(bf16[2,2,2,16,16,128]{5,4,3,2,1,0:T(8,128)(2,1)S(1)} %get-tuple-element.30), channel_id=1, source_target_pairs={{0,0},{1,1},{2,2},{3,3},{4,8},{5,9},{6,10},{7,11},{8,4},{9,5},{10,... | collective-permute-start | bytes 1572872 | tf_op jit(solution)/shard_map/ppermute | solution.py:296
  44.6 22.8 %collective-permute-start.12 = (bf16[2,2,2,16,16,128]{5,4,3,2,1,0:T(8,128)(2,1)S(1)}, bf16[2,2,2,16,16,128]{5,4,3,2,1,0:T(8,128)(2,1)S(1)}, u32[]{:S(2)}, u32[]{:S(2)}) collective-permute-start(bf16[2,2,2,16,16,128]{5,4,3,2,1,0:T(8,128)(2,1)S(1)} %collective-permute-done.8.refs_4_), channel_id=1, source_target_pairs={{0,128},{1,129},{2,130},{3,131},{4,4},{5,5},{6,6},{7,7},{8,8},{9,9... | collective-permute-start | bytes 1572872 | tf_op jit(solution)/shard_map/ppermute | solution.py:296
  46.5 24.9 %collective-permute-start.9 = (bf16[2,2,2,16,16,128]{5,4,3,2,1,0:T(8,128)(2,1)S(1)}, bf16[2,2,2,16,16,128]{5,4,3,2,1,0:T(8,128)(2,1)S(1)}, u32[]{:S(2)}, u32[]{:S(2)}) collective-permute-start(bf16[2,2,2,16,16,128]{5,4,3,2,1,0:T(8,128)(2,1)S(1)} %get-tuple-element.36), channel_id=1, source_target_pairs={{0,4},{1,5},{2,6},{3,7},{4,0},{5,1},{6,2},{7,3},{8,12},{9,13},{10,... | collective-permute-start | bytes 1572872 | tf_op jit(solution)/shard_map/ppermute | solution.py:296
  53.2 20.1 %collective-permute-start.10 = (bf16[2,2,2,16,16,128]{5,4,3,2,1,0:T(8,128)(2,1)S(1)}, bf16[2,2,2,16,16,128]{5,4,3,2,1,0:T(8,128)(2,1)S(1)}, u32[]{:S(2)}, u32[]{:S(2)}) collective-permute-start(bf16[2,2,2,16,16,128]{5,4,3,2,1,0:T(8,128)(2,1)S(1)} %get-tuple-element.37), channel_id=1, source_target_pairs={{0,0},{1,1},{2,2},{3,3},{4,8},{5,9},{6,10},{7,11},{8,4},{9,5},{10,... | collective-permute-start | bytes 1572872 | tf_op jit(solution)/shard_map/ppermute | solution.py:296

commit v7 on v6

--- a/solution.py
+++ b/solution.py
@@ -304,10 +304,7 @@
     def side_b_of_half(s):
         return s // middle * middle + (s + 1 if s % 2 else s - 1) % middle
 
-    def over_middle(s):
-        return {0: middle, middle: 0, middle - 1: slabs - 1, slabs - 1: middle - 1}.get(s, s)
-
-    two, three, one, other = swap(parts[2], 2), swap(parts[3], 3), swap(parts[1], 1), swap(parts[3], 1)
+    one, other = swap(parts[1], 1), swap(parts[3], 1)
 
     whole, half = [(2, 2, freqs, length, ROWS, LANES) for length in (cells, NEAR)]
     rest = cells - NEAR
@@ -316,17 +313,19 @@
         copies += [(None, slot, None, 0, 0, slot), (None, 2 + slot, None, 0, 1, slot)]
         copies += [(None, slot, None, (0, rest), 2, slot), (None, slot, None, (rest, 0), 3, slot)]
     own, turned_own, near_b, far_b = pack(flags, (parts[0], one, parts[2], other), copies, (whole,) * 2 + (half,) * 2)
+    far_own = swap(turned_own, 2)
     whole_a = trade(own, side_a)
     first_near_b, first_far_b = trade(near_b, side_b_of_half), trade(far_b, side_b_of_half)
-    near_over, far_over = trade(first_near_b, over_middle), trade(first_far_b, over_middle)
+    over_middle = [(0, middle), (slabs - 1, middle - 1)]
+    near_over, far_over = [lax.ppermute(value, "slab", over_middle) for value in (first_near_b, first_far_b)]
 
     copies = []
     for slot in range(2):
         for out, at in ((0, (rest, 0)), (2, (0, rest))):
-            copies.append((None, slot, None, at, out, slot))
+            copies.append((None, 0, slot, at, out, slot))
         for out, at in ((1, (0, rest)), (3, (rest, 0))):
-            copies += [(False, slot, None, at, out, slot), (True, 2, slot, at, out, slot)]
-    near_a, near_b, far_a, far_b = pack(flags, (two, three, turned_own), copies, (half,) * 4)
+            copies += [(False, 0, slot, at, out, slot), (True, 1, slot, at, out, slot)]
+    near_a, near_b, far_a, far_b = pack(flags, (far_own, turned_own), copies, (half,) * 4)
     turned = (middle - 1, middle)
     near_a, near_b = trade(near_a, side_a), trade(near_b, side_b, turned)
     whole_a, first_near_b, first_far_b, far_a, far_b = lax.optimization_barrier(
@@ -347,17 +346,16 @@
     blocks = (own, whole_a, first_near_b, near_over)
     befores = summed(flags, blocks, plan, (NEAR_BAND,), None, cells, 2, 0)
     far_sums = (flags, plan + far_plan, blocks)
-    plan = [(0, None, 0, cells, cells, 0, None), (1, None, 0, cells, cells, 1, None)]
-    far_plan = []
+    plan, far_plan = [], []
     for g in range(2):
-        plan += [(2, g, 0, NEAR, near_at_a, g, None)]
-        plan += [(3, g, 0, NEAR, near_at_b, g, (0, 1)), (None, g, 0, NEAR, near_at_b, g, (2,))]
-        far_plan += [(4, g, 0, NEAR, far_at_a, g, None)]
-        far_plan += [(5, g, 0, NEAR, far_at_b, g, (0, 1)), (None, g, 0, NEAR, far_at_b, g, (2,))]
-    image = summed(flags, (two, three, near_a, near_b), plan, (NEAR_BAND,), befores, cells, 2, 1)
+        plan += [(0, g, 0, cells, cells, g, None), (1, g, 0, NEAR, near_at_a, g, None)]
+        plan += [(2, g, 0, NEAR, near_at_b, g, (0, 1)), (None, g, 0, NEAR, near_at_b, g, (2,))]
+        far_plan += [(3, g, 0, NEAR, far_at_a, g, None)]
+        far_plan += [(4, g, 0, NEAR, far_at_b, g, (0, 1)), (None, g, 0, NEAR, far_at_b, g, (2,))]
+    image = summed(flags, (far_own, near_a, near_b), plan, (NEAR_BAND,), befores, cells, 2, 1)
     image, far_over = lax.optimization_barrier((image, far_over))
     befores = summed(flags, far_sums[2] + (first_far_b, far_over), far_sums[1], (FAR_BAND,), None, cells, 2, 0)
-    blocks = (two, three, near_a, near_b, far_a, far_b)
+    blocks = (far_own, near_a, near_b, far_a, far_b)
     return summed(flags, blocks, plan + far_plan, (FAR_BAND,), befores, cells, 2, 2, image)
 
 

time: 79.7 us -> 74.1 us (0.930)
  waiting for transfers between devices: 33.8 us -> 16.3 us
  starting transfers between devices: 22.1 us -> 34.2 us
    ppermute x9 -> x7, starting transfers between devices: 19.1 us -> 28.7 us  [trade(): return lax.ppermute(value, ('slab', 'freq'), pairs)]
    ppermute x4 -> x3, waiting for transfers between devices: 12.9 us -> 3.54 us  [swap(): return lax.ppermute(part, 'freq', [(g, g ^ d) for g in range(GROUPS)])]
    ppermute x9 -> x7, waiting for transfers between devices: 21 us -> 12.8 us  [trade(): return lax.ppermute(value, ('slab', 'freq'), pairs)]
    ppermute x0 -> x2, starting transfers between devices: none -> 2.57 us  [body(): lax.ppermute(value, 'slab', over_middle)]
    ppermute x4 -> x3, starting transfers between devices: 3.02 us -> 2.96 us  [swap(): return lax.ppermute(part, 'freq', [(g, g ^ d) for g in range(GROUPS)])]
  transfers between devices with their start and end apart: 13 -> 12, of which waited for: 8 -> 4; matrix products, arithmetic and copies ran while one was open for 0% -> 0% of each run, Pallas kernels for 18% -> 20%
where the time goes in v7:
time: 74.1 us; the launch traced here: 73.9 us
  starting transfers between devices  34.2 us (46%)
  Pallas kernels  23.2 us (31%)
  waiting for transfers between devices  16.3 us (22%)
    ppermute x7, starting transfers between devices, trade(): return lax.ppermute(value, ('slab', 'freq'), pairs)  28.7 us
    pallas_call x4, Pallas kernels, summed(): pl.pallas_call(functools.partial(sum_kernel, plan, bands, first, last), i...  19.8 us
    ppermute x7, waiting for transfers between devices, trade(): return lax.ppermute(value, ('slab', 'freq'), pairs)  12.8 us
    ppermute x3, waiting for transfers between devices, swap(): return lax.ppermute(part, 'freq', [(g, g ^ d) for g in range(GROUPS)])  3.54 us
    ppermute x3, starting transfers between devices, swap(): return lax.ppermute(part, 'freq', [(g, g ^ d) for g in range(GROUPS)])  2.96 us
    ppermute x2, starting transfers between devices, body(): lax.ppermute(value, 'slab', over_middle)  2.57 us
    pallas_call x2, Pallas kernels, pack(): pl.pallas_call(functools.partial(pack_kernel, copies, len(arrays)), in_sp...  1.7 us
    pallas_call x1, Pallas kernels, regrouped(): pl.pallas_call(regroup_kernel, in_specs=[pl.BlockSpec(memory_space=pltpu....  1.66 us
  transfers between devices with their start and end apart: 12, of which 4 were waited for; matrix products, arithmetic and copies ran while one was open for 0% of the time, Pallas kernels for 20%

profile of v7, /device:TPU:8, one launch (start us, length us, event | category | flops | bytes accessed | tf_op | source)
XLA Modules:
  0.0 73.9 jit_solution(10959871397310929409)
XLA Ops:
  0.0 1.7 %regroup.1 = (bf16[2,2,32,16,128]{4,3,2,1,0:T(8,128)(2,1)S(1)}, bf16[2,2,32,16,128]{4,3,2,1,0:T(8,128)(2,1)S(1)}, bf16[2,2,32,16,128]{4,3,2,1,0:T(8,128)(2,1)S(1)}, bf16[2,2,32,16,128]{4,3,2,1,0:T(8,128)(2,1)S(1)}) custom-call(s32[1]{0:T(128)} %bitcast.2.group_ref, bf16[2,2,32,16,256]{4,3,2,1,0:T(8,128)(2,1)} %source_ref.1, ...), custom_call_target="tpu_custom_call" | custom-call | bytes 4194304 | tf_op jit(solution)/shard_map/regroup/pallas_call | solution.py:65
  1.7 0.1 collective-permute-start
  1.8 0.5 collective-permute-start.1
  2.3 0.1 pad_add_fusion.refs_0_.flags_ref
  2.3 1.3 %collective-permute-done.refs_2_ = bf16[2,2,32,16,128]{4,3,2,1,0:T(8,128)(2,1)S(1)} collective-permute-done((bf16[2,2,32,16,128]{4,3,2,1,0:T(8,128)(2,1)S(1)}, bf16[2,2,32,16,128]{4,3,2,1,0:T(8,128)(2,1)S(1)}, u32[]{:S(2)}, u32[]{:S(2)}) %collective-permute-start) | collective-permute-done | bytes 524320 | tf_op jit(solution)/shard_map/ppermute | solution.py:289
  3.7 0.7 %collective-permute-done.1.refs_4_ = bf16[2,2,32,16,128]{4,3,2,1,0:T(8,128)(2,1)S(1)} collective-permute-done((bf16[2,2,32,16,128]{4,3,2,1,0:T(8,128)(2,1)S(1)}, bf16[2,2,32,16,128]{4,3,2,1,0:T(8,128)(2,1)S(1)}, u32[]{:S(2)}, u32[]{:S(2)}) %collective-permute-start.1) | collective-permute-done | bytes 524320 | tf_op jit(solution)/shard_map/ppermute | solution.py:289
  4.4 0.9 %pack.2 = (bf16[2,2,2,32,16,128]{5,4,3,2,1,0:T(8,128)(2,1)S(1)}, bf16[2,2,2,32,16,128]{5,4,3,2,1,0:T(8,128)(2,1)S(1)}, bf16[2,2,2,16,16,128]{5,4,3,2,1,0:T(8,128)(2,1)S(1)}, bf16[2,2,2,16,16,128]{5,4,3,2,1,0:T(8,128)(2,1)S(1)}) custom-call(s32[2]{0:T(128)S(1)} %pad_add_fusion.refs_0_.flags_ref, bf16[2,2,32,16,128]{4,3,2,1,0:T(8,128)(2,1)S(1)} %get-tuple-element.24.refs_1_, ...), custom_call_target="tpu_custom_call" | custom-call | bytes 2097152 | tf_op jit(solution)/shard_map/pack/pallas_call | solution.py:107
  5.3 2.4 %collective-permute-start.2 = (bf16[2,2,2,32,16,128]{5,4,3,2,1,0:T(8,128)(2,1)S(1)}, bf16[2,2,2,32,16,128]{5,4,3,2,1,0:T(8,128)(2,1)S(1)}, u32[]{:S(2)}, u32[]{:S(2)}) collective-permute-start(bf16[2,2,2,32,16,128]{5,4,3,2,1,0:T(8,128)(2,1)S(1)} %get-tuple-element.28.refs_2_), channel_id=1, source_target_pairs={{0,2},{1,3},{2,0},{3,1},{4,6},{5,7},{6,4},{7,5},{8,10},{9,11},{10,... | collective-permute-start | bytes 3145736 | tf_op jit(solution)/shard_map/ppermute | solution.py:289
  7.7 1.5 %collective-permute-start.5 = (bf16[2,2,2,32,16,128]{5,4,3,2,1,0:T(8,128)(2,1)S(1)}, bf16[2,2,2,32,16,128]{5,4,3,2,1,0:T(8,128)(2,1)S(1)}, u32[]{:S(2)}, u32[]{:S(2)}) collective-permute-start(bf16[2,2,2,32,16,128]{5,4,3,2,1,0:T(8,128)(2,1)S(1)} %get-tuple-element.31.refs_0_), channel_id=1, source_target_pairs={{0,4},{1,5},{2,6},{3,7},{4,0},{5,1},{6,2},{7,3},{8,12},{9,13},{10,... | collective-permute-start | bytes 3145736 | tf_op jit(solution)/shard_map/ppermute | solution.py:296
  9.1 7.4 %collective-permute-start.6 = (bf16[2,2,2,16,16,128]{5,4,3,2,1,0:T(8,128)(2,1)S(1)}, bf16[2,2,2,16,16,128]{5,4,3,2,1,0:T(8,128)(2,1)S(1)}, u32[]{:S(2)}, u32[]{:S(2)}) collective-permute-start(bf16[2,2,2,16,16,128]{5,4,3,2,1,0:T(8,128)(2,1)S(1)} %get-tuple-element.32), channel_id=1, source_target_pairs={{0,124},{1,125},{2,126},{3,127},{4,8},{5,9},{6,10},{7,11},{8,4},{9... | collective-permute-start | bytes 1572872 | tf_op jit(solution)/shard_map/ppermute | solution.py:296
  16.5 0.0 collective-permute-start.7
  16.6 12.8 %collective-permute-done.6.refs_2_ = bf16[2,2,2,16,16,128]{5,4,3,2,1,0:T(8,128)(2,1)S(1)} collective-permute-done((bf16[2,2,2,16,16,128]{5,4,3,2,1,0:T(8,128)(2,1)S(1)}, bf16[2,2,2,16,16,128]{5,4,3,2,1,0:T(8,128)(2,1)S(1)}, u32[]{:S(2)}, u32[]{:S(2)}) %collective-permute-start.6) | collective-permute-done | bytes 524320 | tf_op jit(solution)/shard_map/ppermute | solution.py:296
  29.3 1.3 %collective-permute-start.10 = (bf16[2,2,2,16,16,128]{5,4,3,2,1,0:T(8,128)(2,1)S(1)}, bf16[2,2,2,16,16,128]{5,4,3,2,1,0:T(8,128)(2,1)S(1)}, u32[]{:S(2)}, u32[]{:S(2)}) collective-permute-start(bf16[2,2,2,16,16,128]{5,4,3,2,1,0:T(8,128)(2,1)S(1)} %collective-permute-done.6.refs_2_), channel_id=1, source_target_pairs={{0,128},{252,124},{1,129},{253,125},{2,130},{254,126},{3,131},{255... | collective-permute-start | bytes 1572872 | tf_op jit(solution)/shard_map/ppermute | solution.py:320
  30.6 1.5 %collective-permute-done.2.refs_1_.refs_0_ = bf16[2,2,2,32,16,128]{5,4,3,2,1,0:T(8,128)(2,1)S(1)} collective-permute-done((bf16[2,2,2,32,16,128]{5,4,3,2,1,0:T(8,128)(2,1)S(1)}, bf16[2,2,2,32,16,128]{5,4,3,2,1,0:T(8,128)(2,1)S(1)}, u32[]{:S(2)}, u32[]{:S(2)}) %collective-permute-start.2) | collective-permute-done | bytes 1048608 | tf_op jit(solution)/shard_map/ppermute | solution.py:289
  32.1 0.8 %pack.3 = (bf16[2,2,2,16,16,128]{5,4,3,2,1,0:T(8,128)(2,1)S(1)}, bf16[2,2,2,16,16,128]{5,4,3,2,1,0:T(8,128)(2,1)S(1)}, bf16[2,2,2,16,16,128]{5,4,3,2,1,0:T(8,128)(2,1)S(1)}, bf16[2,2,2,16,16,128]{5,4,3,2,1,0:T(8,128)(2,1)S(1)}) custom-call(s32[2]{0:T(128)S(1)} %pad_add_fusion.refs_0_.flags_ref, ...), custom_call_target="tpu_custom_call" | custom-call | bytes 2097152 | tf_op jit(solution)/shard_map/pack/pallas_call | solution.py:107
  32.9 1.6 %collective-permute-start.3 = (bf16[2,2,2,16,16,128]{5,4,3,2,1,0:T(8,128)(2,1)S(1)}, bf16[2,2,2,16,16,128]{5,4,3,2,1,0:T(8,128)(2,1)S(1)}, u32[]{:S(2)}, u32[]{:S(2)}) collective-permute-start(bf16[2,2,2,16,16,128]{5,4,3,2,1,0:T(8,128)(2,1)S(1)} %get-tuple-element.29), channel_id=1, source_target_pairs={{0,4},{1,5},{2,6},{3,7},{4,0},{5,1},{6,2},{7,3},{8,12},{9,13},{10,... | collective-permute-start | bytes 1572872 | tf_op jit(solution)/shard_map/ppermute | solution.py:296
  34.5 10.3 %collective-permute-start.4 = (bf16[2,2,2,16,16,128]{5,4,3,2,1,0:T(8,128)(2,1)S(1)}, bf16[2,2,2,16,16,128]{5,4,3,2,1,0:T(8,128)(2,1)S(1)}, u32[]{:S(2)}, u32[]{:S(2)}) collective-permute-start(bf16[2,2,2,16,16,128]{5,4,3,2,1,0:T(8,128)(2,1)S(1)} %get-tuple-element.30), channel_id=1, source_target_pairs={{0,0},{1,1},{2,2},{3,3},{4,8},{5,9},{6,10},{7,11},{8,4},{9,5},{10,... | collective-permute-start | bytes 1572872 | tf_op jit(solution)/shard_map/ppermute | solution.py:296
  44.8 0.0 collective-permute-done.7.refs_4_
  44.8 1.3 %collective-permute-start.11 = (bf16[2,2,2,16,16,128]{5,4,3,2,1,0:T(8,128)(2,1)S(1)}, bf16[2,2,2,16,16,128]{5,4,3,2,1,0:T(8,128)(2,1)S(1)}, u32[]{:S(2)}, u32[]{:S(2)}) collective-permute-start(bf16[2,2,2,16,16,128]{5,4,3,2,1,0:T(8,128)(2,1)S(1)} %collective-permute-done.7.refs_4_), channel_id=1, source_target_pairs={{0,128},{252,124},{1,129},{253,125},{2,130},{254,126},{3,131},{255... | collective-permute-start | bytes 1572872 | tf_op jit(solution)/shard_map/ppermute | solution.py:320
  46.1 0.0 collective-permute-done.5.refs_1_
  46.1 0.1 collective-permute-start.8
  46.2 0.0 collective-permute-done.10.refs_3_
  46.2 7.8 %collective-permute-start.9 = (bf16[2,2,2,16,16,128]{5,4,3,2,1,0:T(8,128)(2,1)S(1)}, bf16[2,2,2,16,16,128]{5,4,3,2,1,0:T(8,128)(2,1)S(1)}, u32[]{:S(2)}, u32[]{:S(2)}) collective-permute-start(bf16[2,2,2,16,16,128]{5,4,3,2,1,0:T(8,128)(2,1)S(1)} %get-tuple-element.37), channel_id=1, source_target_pairs={{0,0},{1,1},{2,2},{3,3},{4,8},{5,9},{6,10},{7,11},{8,4},{9,5},{10,... | collective-permute-start | bytes 1572872 | tf_op jit(solution)/shard_map/ppermute | solution.py:296
  54.1 3.8 %partial.2.refs_3_ = f32[33,32,8,128]{3,2,1,0:T(8,128)S(1)} custom-call(s32[2]{0:T(128)S(1)} %pad_add_fusion.refs_0_.flags_ref, bf16[2,2,2,32,16,128]{5,4,3,2,1,0:T(8,128)(2,1)S(1)} %get-tuple-element.31.refs_0_, bf16[2,2,2,32,16,128]{5,4,3,2,1,0:T(8,128)(2,1)S(1)} %collective-permute-done.5.refs_1_, ...), custom_call_target="tpu_custom_call" | custom-call | flops 17160000 | bytes 4290000 | tf_op jit(solution)/shard_map/partial/pallas_call | solution.py:262
  57.9 0.0 collective-permute-done.3.refs_1_
  57.9 0.0 collective-permute-done.4.refs_2_
  57.9 5.9 %image.2.refs_6_ = f32[4,65,32,256]{3,2,1,0:T(8,128)} custom-call(s32[2]{0:T(128)S(1)} %pad_add_fusion.refs_0_.flags_ref, bf16[2,2,2,32,16,128]{5,4,3,2,1,0:T(8,128)(2,1)S(1)} %collective-permute-done.2.refs_1_.refs_0_, bf16[2,2,2,16,16,128]{5,4,3,2,1,0:T(8,128)(2,1)S(1)} %collective-permute-done.3.refs_1_, ...), custom_call_target="tpu_custom_call" | custom-call | flops 17160000 | bytes 4290000 | tf_op jit(solution)/shard_map/image/pallas_call | solution.py:262
  63.8 0.0 collective-permute-done.11.refs_5_
  63.9 4.0 %partial.3.refs_5_ = f32[32,32,8,128]{3,2,1,0:T(8,128)S(1)} custom-call(s32[2]{0:T(128)S(1)} %pad_add_fusion.refs_0_.flags_ref, bf16[2,2,2,32,16,128]{5,4,3,2,1,0:T(8,128)(2,1)S(1)} %get-tuple-element.31.refs_0_, bf16[2,2,2,32,16,128]{5,4,3,2,1,0:T(8,128)(2,1)S(1)} %collective-permute-done.5.refs_1_, ...), custom_call_target="tpu_custom_call" | custom-call | flops 16640000 | bytes 4160000 | tf_op jit(solution)/shard_map/partial/pallas_call | solution.py:262
  67.8 0.0 collective-permute-done.8.refs_3_
  67.8 0.0 collective-permute-done.9.refs_4_
  67.8 6.1 %image.3 = f32[4,65,32,256]{3,2,1,0:T(8,128)} custom-call(s32[2]{0:T(128)S(1)} %pad_add_fusion.refs_0_.flags_ref, bf16[2,2,2,32,16,128]{5,4,3,2,1,0:T(8,128)(2,1)S(1)} %collective-permute-done.2.refs_1_.refs_0_, bf16[2,2,2,16,16,128]{5,4,3,2,1,0:T(8,128)(2,1)S(1)} %collective-permute-done.3.refs_1_, ...), custom_call_target="tpu_custom_call", output_to_operand_aliasing={{}: (7, {})} | custom-call | flops 16640000 | bytes 4160000 | tf_op jit(solution)/shard_map/image/pallas_call | solution.py:262
Async XLA Ops:
  1.7 2.0 %collective-permute-start = (bf16[2,2,32,16,128]{4,3,2,1,0:T(8,128)(2,1)S(1)}, bf16[2,2,32,16,128]{4,3,2,1,0:T(8,128)(2,1)S(1)}, u32[]{:S(2)}, u32[]{:S(2)}) collective-permute-start(bf16[2,2,32,16,128]{4,3,2,1,0:T(8,128)(2,1)S(1)} %get-tuple-element.25), channel_id=1, source_target_pairs={{0,1},{1,0},{2,3},{3,2},{4,5},{5,4},{6,7},{7,6},{8,9},{9,8},{10,11... | collective-permute-start | bytes 1572872 | tf_op jit(solution)/shard_map/ppermute | solution.py:289
  1.8 2.6 %collective-permute-start.1 = (bf16[2,2,32,16,128]{4,3,2,1,0:T(8,128)(2,1)S(1)}, bf16[2,2,32,16,128]{4,3,2,1,0:T(8,128)(2,1)S(1)}, u32[]{:S(2)}, u32[]{:S(2)}) collective-permute-start(bf16[2,2,32,16,128]{4,3,2,1,0:T(8,128)(2,1)S(1)} %get-tuple-element.27), channel_id=1, source_target_pairs={{0,1},{1,0},{2,3},{3,2},{4,5},{5,4},{6,7},{7,6},{8,9},{9,8},{10,11... | collective-permute-start | bytes 1572872 | tf_op jit(solution)/shard_map/ppermute | solution.py:289
  5.3 26.8 %collective-permute-start.2 = (bf16[2,2,2,32,16,128]{5,4,3,2,1,0:T(8,128)(2,1)S(1)}, bf16[2,2,2,32,16,128]{5,4,3,2,1,0:T(8,128)(2,1)S(1)}, u32[]{:S(2)}, u32[]{:S(2)}) collective-permute-start(bf16[2,2,2,32,16,128]{5,4,3,2,1,0:T(8,128)(2,1)S(1)} %get-tuple-element.28.refs_2_), channel_id=1, source_target_pairs={{0,2},{1,3},{2,0},{3,1},{4,6},{5,7},{6,4},{7,5},{8,10},{9,11},{10,... | collective-permute-start | bytes 3145736 | tf_op jit(solution)/shard_map/ppermute | solution.py:289
  7.7 38.5 %collective-permute-start.5 = (bf16[2,2,2,32,16,128]{5,4,3,2,1,0:T(8,128)(2,1)S(1)}, bf16[2,2,2,32,16,128]{5,4,3,2,1,0:T(8,128)(2,1)S(1)}, u32[]{:S(2)}, u32[]{:S(2)}) collective-permute-start(bf16[2,2,2,32,16,128]{5,4,3,2,1,0:T(8,128)(2,1)S(1)} %get-tuple-element.31.refs_0_), channel_id=1, source_target_pairs={{0,4},{1,5},{2,6},{3,7},{4,0},{5,1},{6,2},{7,3},{8,12},{9,13},{10,... | collective-permute-start | bytes 3145736 | tf_op jit(solution)/shard_map/ppermute | solution.py:296
  9.1 20.2 %collective-permute-start.6 = (bf16[2,2,2,16,16,128]{5,4,3,2,1,0:T(8,128)(2,1)S(1)}, bf16[2,2,2,16,16,128]{5,4,3,2,1,0:T(8,128)(2,1)S(1)}, u32[]{:S(2)}, u32[]{:S(2)}) collective-permute-start(bf16[2,2,2,16,16,128]{5,4,3,2,1,0:T(8,128)(2,1)S(1)} %get-tuple-element.32), channel_id=1, source_target_pairs={{0,124},{1,125},{2,126},{3,127},{4,8},{5,9},{6,10},{7,11},{8,4},{9... | collective-permute-start | bytes 1572872 | tf_op jit(solution)/shard_map/ppermute | solution.py:296
  16.5 28.3 %collective-permute-start.7 = (bf16[2,2,2,16,16,128]{5,4,3,2,1,0:T(8,128)(2,1)S(1)}, bf16[2,2,2,16,16,128]{5,4,3,2,1,0:T(8,128)(2,1)S(1)}, u32[]{:S(2)}, u32[]{:S(2)}) collective-permute-start(bf16[2,2,2,16,16,128]{5,4,3,2,1,0:T(8,128)(2,1)S(1)} %get-tuple-element.33), channel_id=1, source_target_pairs={{0,124},{1,125},{2,126},{3,127},{4,8},{5,9},{6,10},{7,11},{8,4},{9... | collective-permute-start | bytes 1572872 | tf_op jit(solution)/shard_map/ppermute | solution.py:296
  29.3 16.9 %collective-permute-start.10 = (bf16[2,2,2,16,16,128]{5,4,3,2,1,0:T(8,128)(2,1)S(1)}, bf16[2,2,2,16,16,128]{5,4,3,2,1,0:T(8,128)(2,1)S(1)}, u32[]{:S(2)}, u32[]{:S(2)}) collective-permute-start(bf16[2,2,2,16,16,128]{5,4,3,2,1,0:T(8,128)(2,1)S(1)} %collective-permute-done.6.refs_2_), channel_id=1, source_target_pairs={{0,128},{252,124},{1,129},{253,125},{2,130},{254,126},{3,131},{255... | collective-permute-start | bytes 1572872 | tf_op jit(solution)/shard_map/ppermute | solution.py:320
  32.9 25.0 %collective-permute-start.3 = (bf16[2,2,2,16,16,128]{5,4,3,2,1,0:T(8,128)(2,1)S(1)}, bf16[2,2,2,16,16,128]{5,4,3,2,1,0:T(8,128)(2,1)S(1)}, u32[]{:S(2)}, u32[]{:S(2)}) collective-permute-start(bf16[2,2,2,16,16,128]{5,4,3,2,1,0:T(8,128)(2,1)S(1)} %get-tuple-element.29), channel_id=1, source_target_pairs={{0,4},{1,5},{2,6},{3,7},{4,0},{5,1},{6,2},{7,3},{8,12},{9,13},{10,... | collective-permute-start | bytes 1572872 | tf_op jit(solution)/shard_map/ppermute | solution.py:296
  34.5 23.4 %collective-permute-start.4 = (bf16[2,2,2,16,16,128]{5,4,3,2,1,0:T(8,128)(2,1)S(1)}, bf16[2,2,2,16,16,128]{5,4,3,2,1,0:T(8,128)(2,1)S(1)}, u32[]{:S(2)}, u32[]{:S(2)}) collective-permute-start(bf16[2,2,2,16,16,128]{5,4,3,2,1,0:T(8,128)(2,1)S(1)} %get-tuple-element.30), channel_id=1, source_target_pairs={{0,0},{1,1},{2,2},{3,3},{4,8},{5,9},{6,10},{7,11},{8,4},{9,5},{10,... | collective-permute-start | bytes 1572872 | tf_op jit(solution)/shard_map/ppermute | solution.py:296
  44.8 19.0 %collective-permute-start.11 = (bf16[2,2,2,16,16,128]{5,4,3,2,1,0:T(8,128)(2,1)S(1)}, bf16[2,2,2,16,16,128]{5,4,3,2,1,0:T(8,128)(2,1)S(1)}, u32[]{:S(2)}, u32[]{:S(2)}) collective-permute-start(bf16[2,2,2,16,16,128]{5,4,3,2,1,0:T(8,128)(2,1)S(1)} %collective-permute-done.7.refs_4_), channel_id=1, source_target_pairs={{0,128},{252,124},{1,129},{253,125},{2,130},{254,126},{3,131},{255... | collective-permute-start | bytes 1572872 | tf_op jit(solution)/shard_map/ppermute | solution.py:320
  46.1 21.7 %collective-permute-start.8 = (bf16[2,2,2,16,16,128]{5,4,3,2,1,0:T(8,128)(2,1)S(1)}, bf16[2,2,2,16,16,128]{5,4,3,2,1,0:T(8,128)(2,1)S(1)}, u32[]{:S(2)}, u32[]{:S(2)}) collective-permute-start(bf16[2,2,2,16,16,128]{5,4,3,2,1,0:T(8,128)(2,1)S(1)} %get-tuple-element.36), channel_id=1, source_target_pairs={{0,4},{1,5},{2,6},{3,7},{4,0},{5,1},{6,2},{7,3},{8,12},{9,13},{10,... | collective-permute-start | bytes 1572872 | tf_op jit(solution)/shard_map/ppermute | solution.py:296
  46.2 21.6 %collective-permute-start.9 = (bf16[2,2,2,16,16,128]{5,4,3,2,1,0:T(8,128)(2,1)S(1)}, bf16[2,2,2,16,16,128]{5,4,3,2,1,0:T(8,128)(2,1)S(1)}, u32[]{:S(2)}, u32[]{:S(2)}) collective-permute-start(bf16[2,2,2,16,16,128]{5,4,3,2,1,0:T(8,128)(2,1)S(1)} %get-tuple-element.37), channel_id=1, source_target_pairs={{0,0},{1,1},{2,2},{3,3},{4,8},{5,9},{6,10},{7,11},{8,4},{9,5},{10,... | collective-permute-start | bytes 1572872 | tf_op jit(solution)/shard_map/ppermute | solution.py:296

commit v8 on v7

--- a/solution.py
+++ b/solution.py
@@ -345,6 +345,7 @@
         far_plan += [(None, g, 0, NEAR, far_at_b, g, (2,))]
     blocks = (own, whole_a, first_near_b, near_over)
     befores = summed(flags, blocks, plan, (NEAR_BAND,), None, cells, 2, 0)
+    far_over, *befores = lax.optimization_barrier((far_over, *befores))
     far_sums = (flags, plan + far_plan, blocks)
     plan, far_plan = [], []
     for g in range(2):
@@ -352,11 +353,10 @@
         plan += [(2, g, 0, NEAR, near_at_b, g, (0, 1)), (None, g, 0, NEAR, near_at_b, g, (2,))]
         far_plan += [(3, g, 0, NEAR, far_at_a, g, None)]
         far_plan += [(4, g, 0, NEAR, far_at_b, g, (0, 1)), (None, g, 0, NEAR, far_at_b, g, (2,))]
+    far_befores = summed(flags, far_sums[2] + (first_far_b, far_over), far_sums[1], (FAR_BAND,), None, cells, 2, 0)
     image = summed(flags, (far_own, near_a, near_b), plan, (NEAR_BAND,), befores, cells, 2, 1)
-    image, far_over = lax.optimization_barrier((image, far_over))
-    befores = summed(flags, far_sums[2] + (first_far_b, far_over), far_sums[1], (FAR_BAND,), None, cells, 2, 0)
     blocks = (far_own, near_a, near_b, far_a, far_b)
-    return summed(flags, blocks, plan + far_plan, (FAR_BAND,), befores, cells, 2, 2, image)
+    return summed(flags, blocks, plan + far_plan, (FAR_BAND,), far_befores, cells, 2, 2, image)
 
 
 def solution(mesh):

time: 74.1 us -> 78.3 us (1.057)
  waiting for transfers between devices: 16.3 us -> 27.7 us
  starting transfers between devices: 34.2 us -> 26.9 us
    ppermute x7, waiting for transfers between devices: 12.8 us -> 25.6 us  [trade(): return lax.ppermute(value, ('slab', 'freq'), pairs)]
    ppermute x7, starting transfers between devices: 28.7 us -> 21.4 us  [trade(): return lax.ppermute(value, ('slab', 'freq'), pairs)]
    ppermute x3, waiting for transfers between devices: 3.54 us -> 2.08 us  [swap(): return lax.ppermute(part, 'freq', [(g, g ^ d) for g in range(GROUPS)])]
  transfers between devices with their start and end apart: 12 -> 12, of which waited for: 4 -> 6; matrix products, arithmetic and copies ran while one was open for 0% -> 0% of each run, Pallas kernels for 20% -> 19%
where the time goes in v8:
time: 78.3 us; the launch traced here: 77.9 us
  waiting for transfers between devices  27.7 us (35%)
  starting transfers between devices  26.9 us (34%)
  Pallas kernels  23.1 us (30%)
    ppermute x7, waiting for transfers between devices, trade(): return lax.ppermute(value, ('slab', 'freq'), pairs)  25.6 us
    ppermute x7, starting transfers between devices, trade(): return lax.ppermute(value, ('slab', 'freq'), pairs)  21.4 us
    pallas_call x4, Pallas kernels, summed(): pl.pallas_call(functools.partial(sum_kernel, plan, bands, first, last), i...  19.8 us
    ppermute x3, starting transfers between devices, swap(): return lax.ppermute(part, 'freq', [(g, g ^ d) for g in range(GROUPS)])  2.96 us
    ppermute x2, starting transfers between devices, body(): lax.ppermute(value, 'slab', over_middle)  2.56 us
    ppermute x3, waiting for transfers between devices, swap(): return lax.ppermute(part, 'freq', [(g, g ^ d) for g in range(GROUPS)])  2.08 us
    pallas_call x2, Pallas kernels, pack(): pl.pallas_call(functools.partial(pack_kernel, copies, len(arrays)), in_sp...  1.7 us
    pallas_call x1, Pallas kernels, regrouped(): pl.pallas_call(regroup_kernel, in_specs=[pl.BlockSpec(memory_space=pltpu....  1.66 us
  transfers between devices with their start and end apart: 12, of which 6 were waited for; matrix products, arithmetic and copies ran while one was open for 0% of the time, Pallas kernels for 19%

profile of v8, /device:TPU:8, one launch (start us, length us, event | category | flops | bytes accessed | tf_op | source)
XLA Modules:
  0.0 77.9 jit_solution(8137075056472829283)
XLA Ops:
  0.0 1.7 %regroup.1 = (bf16[2,2,32,16,128]{4,3,2,1,0:T(8,128)(2,1)S(1)}, bf16[2,2,32,16,128]{4,3,2,1,0:T(8,128)(2,1)S(1)}, bf16[2,2,32,16,128]{4,3,2,1,0:T(8,128)(2,1)S(1)}, bf16[2,2,32,16,128]{4,3,2,1,0:T(8,128)(2,1)S(1)}) custom-call(s32[1]{0:T(128)} %bitcast.2.group_ref, bf16[2,2,32,16,256]{4,3,2,1,0:T(8,128)(2,1)} %source_ref.1, ...), custom_call_target="tpu_custom_call" | custom-call | bytes 4194304 | tf_op jit(solution)/shard_map/regroup/pallas_call | solution.py:65
  1.7 0.1 collective-permute-start
  1.8 0.5 collective-permute-start.1
  2.3 0.1 pad_add_fusion.refs_0_.flags_ref
  2.3 1.3 %collective-permute-done.refs_2_ = bf16[2,2,32,16,128]{4,3,2,1,0:T(8,128)(2,1)S(1)} collective-permute-done((bf16[2,2,32,16,128]{4,3,2,1,0:T(8,128)(2,1)S(1)}, bf16[2,2,32,16,128]{4,3,2,1,0:T(8,128)(2,1)S(1)}, u32[]{:S(2)}, u32[]{:S(2)}) %collective-permute-start) | collective-permute-done | bytes 524320 | tf_op jit(solution)/shard_map/ppermute | solution.py:289
  3.7 0.7 collective-permute-done.1.refs_4_
  4.4 0.9 %pack.2 = (bf16[2,2,2,32,16,128]{5,4,3,2,1,0:T(8,128)(2,1)S(1)}, bf16[2,2,2,32,16,128]{5,4,3,2,1,0:T(8,128)(2,1)S(1)}, bf16[2,2,2,16,16,128]{5,4,3,2,1,0:T(8,128)(2,1)S(1)}, bf16[2,2,2,16,16,128]{5,4,3,2,1,0:T(8,128)(2,1)S(1)}) custom-call(s32[2]{0:T(128)S(1)} %pad_add_fusion.refs_0_.flags_ref, bf16[2,2,32,16,128]{4,3,2,1,0:T(8,128)(2,1)S(1)} %get-tuple-element.24.refs_1_, ...), custom_call_target="tpu_custom_call" | custom-call | bytes 2097152 | tf_op jit(solution)/shard_map/pack/pallas_call | solution.py:107
  5.3 2.4 %collective-permute-start.2 = (bf16[2,2,2,32,16,128]{5,4,3,2,1,0:T(8,128)(2,1)S(1)}, bf16[2,2,2,32,16,128]{5,4,3,2,1,0:T(8,128)(2,1)S(1)}, u32[]{:S(2)}, u32[]{:S(2)}) collective-permute-start(bf16[2,2,2,32,16,128]{5,4,3,2,1,0:T(8,128)(2,1)S(1)} %get-tuple-element.28.refs_2_), channel_id=1, source_target_pairs={{0,2},{1,3},{2,0},{3,1},{4,6},{5,7},{6,4},{7,5},{8,10},{9,11},{10,... | collective-permute-start | bytes 3145736 | tf_op jit(solution)/shard_map/ppermute | solution.py:289
  7.7 1.5 %collective-permute-start.5 = (bf16[2,2,2,32,16,128]{5,4,3,2,1,0:T(8,128)(2,1)S(1)}, bf16[2,2,2,32,16,128]{5,4,3,2,1,0:T(8,128)(2,1)S(1)}, u32[]{:S(2)}, u32[]{:S(2)}) collective-permute-start(bf16[2,2,2,32,16,128]{5,4,3,2,1,0:T(8,128)(2,1)S(1)} %get-tuple-element.31.refs_0_), channel_id=1, source_target_pairs={{0,4},{1,5},{2,6},{3,7},{4,0},{5,1},{6,2},{7,3},{8,12},{9,13},{10,... | collective-permute-start | bytes 3145736 | tf_op jit(solution)/shard_map/ppermute | solution.py:296
  9.1 7.4 %collective-permute-start.6 = (bf16[2,2,2,16,16,128]{5,4,3,2,1,0:T(8,128)(2,1)S(1)}, bf16[2,2,2,16,16,128]{5,4,3,2,1,0:T(8,128)(2,1)S(1)}, u32[]{:S(2)}, u32[]{:S(2)}) collective-permute-start(bf16[2,2,2,16,16,128]{5,4,3,2,1,0:T(8,128)(2,1)S(1)} %get-tuple-element.32), channel_id=1, source_target_pairs={{0,124},{1,125},{2,126},{3,127},{4,8},{5,9},{6,10},{7,11},{8,4},{9... | collective-permute-start | bytes 1572872 | tf_op jit(solution)/shard_map/ppermute | solution.py:296
  16.5 0.0 collective-permute-start.7
  16.6 12.8 %collective-permute-done.6.refs_2_ = bf16[2,2,2,16,16,128]{5,4,3,2,1,0:T(8,128)(2,1)S(1)} collective-permute-done((bf16[2,2,2,16,16,128]{5,4,3,2,1,0:T(8,128)(2,1)S(1)}, bf16[2,2,2,16,16,128]{5,4,3,2,1,0:T(8,128)(2,1)S(1)}, u32[]{:S(2)}, u32[]{:S(2)}) %collective-permute-start.6) | collective-permute-done | bytes 524320 | tf_op jit(solution)/shard_map/ppermute | solution.py:296
  29.3 1.3 %collective-permute-start.10 = (bf16[2,2,2,16,16,128]{5,4,3,2,1,0:T(8,128)(2,1)S(1)}, bf16[2,2,2,16,16,128]{5,4,3,2,1,0:T(8,128)(2,1)S(1)}, u32[]{:S(2)}, u32[]{:S(2)}) collective-permute-start(bf16[2,2,2,16,16,128]{5,4,3,2,1,0:T(8,128)(2,1)S(1)} %collective-permute-done.6.refs_2_), channel_id=1, source_target_pairs={{0,128},{252,124},{1,129},{253,125},{2,130},{254,126},{3,131},{255... | collective-permute-start | bytes 1572872 | tf_op jit(solution)/shard_map/ppermute | solution.py:320
  30.6 8.8 %collective-permute-done.7.refs_4_ = bf16[2,2,2,16,16,128]{5,4,3,2,1,0:T(8,128)(2,1)S(1)} collective-permute-done((bf16[2,2,2,16,16,128]{5,4,3,2,1,0:T(8,128)(2,1)S(1)}, bf16[2,2,2,16,16,128]{5,4,3,2,1,0:T(8,128)(2,1)S(1)}, u32[]{:S(2)}, u32[]{:S(2)}) %collective-permute-start.7) | collective-permute-done | bytes 524320 | tf_op jit(solution)/shard_map/ppermute | solution.py:296
  39.4 1.3 %collective-permute-start.11 = (bf16[2,2,2,16,16,128]{5,4,3,2,1,0:T(8,128)(2,1)S(1)}, bf16[2,2,2,16,16,128]{5,4,3,2,1,0:T(8,128)(2,1)S(1)}, u32[]{:S(2)}, u32[]{:S(2)}) collective-permute-start(bf16[2,2,2,16,16,128]{5,4,3,2,1,0:T(8,128)(2,1)S(1)} %collective-permute-done.7.refs_4_), channel_id=1, source_target_pairs={{0,128},{252,124},{1,129},{253,125},{2,130},{254,126},{3,131},{255... | collective-permute-start | bytes 1572872 | tf_op jit(solution)/shard_map/ppermute | solution.py:320
  40.7 0.0 collective-permute-done.2.refs_1_.refs_0_
  40.7 0.8 %pack.3 = (bf16[2,2,2,16,16,128]{5,4,3,2,1,0:T(8,128)(2,1)S(1)}, bf16[2,2,2,16,16,128]{5,4,3,2,1,0:T(8,128)(2,1)S(1)}, bf16[2,2,2,16,16,128]{5,4,3,2,1,0:T(8,128)(2,1)S(1)}, bf16[2,2,2,16,16,128]{5,4,3,2,1,0:T(8,128)(2,1)S(1)}) custom-call(s32[2]{0:T(128)S(1)} %pad_add_fusion.refs_0_.flags_ref, ...), custom_call_target="tpu_custom_call" | custom-call | bytes 2097152 | tf_op jit(solution)/shard_map/pack/pallas_call | solution.py:107
  41.6 0.1 collective-permute-start.3
  41.7 6.1 %collective-permute-start.4 = (bf16[2,2,2,16,16,128]{5,4,3,2,1,0:T(8,128)(2,1)S(1)}, bf16[2,2,2,16,16,128]{5,4,3,2,1,0:T(8,128)(2,1)S(1)}, u32[]{:S(2)}, u32[]{:S(2)}) collective-permute-start(bf16[2,2,2,16,16,128]{5,4,3,2,1,0:T(8,128)(2,1)S(1)} %get-tuple-element.30), channel_id=1, source_target_pairs={{0,0},{1,1},{2,2},{3,3},{4,8},{5,9},{6,10},{7,11},{8,4},{9,5},{10,... | collective-permute-start | bytes 1572872 | tf_op jit(solution)/shard_map/ppermute | solution.py:296
  47.8 0.0 collective-permute-done.5.refs_1_
  47.8 0.1 collective-permute-start.8
  47.9 0.0 collective-permute-done.10.refs_3_
  47.9 6.2 %collective-permute-start.9 = (bf16[2,2,2,16,16,128]{5,4,3,2,1,0:T(8,128)(2,1)S(1)}, bf16[2,2,2,16,16,128]{5,4,3,2,1,0:T(8,128)(2,1)S(1)}, u32[]{:S(2)}, u32[]{:S(2)}) collective-permute-start(bf16[2,2,2,16,16,128]{5,4,3,2,1,0:T(8,128)(2,1)S(1)} %get-tuple-element.37), channel_id=1, source_target_pairs={{0,0},{1,1},{2,2},{3,3},{4,8},{5,9},{6,10},{7,11},{8,4},{9,5},{10,... | collective-permute-start | bytes 1572872 | tf_op jit(solution)/shard_map/ppermute | solution.py:296
  54.1 3.8 %partial.2.refs_3_ = f32[33,32,8,128]{3,2,1,0:T(8,128)S(1)} custom-call(s32[2]{0:T(128)S(1)} %pad_add_fusion.refs_0_.flags_ref, bf16[2,2,2,32,16,128]{5,4,3,2,1,0:T(8,128)(2,1)S(1)} %get-tuple-element.31.refs_0_, bf16[2,2,2,32,16,128]{5,4,3,2,1,0:T(8,128)(2,1)S(1)} %collective-permute-done.5.refs_1_, ...), custom_call_target="tpu_custom_call" | custom-call | flops 17160000 | bytes 4290000 | tf_op jit(solution)/shard_map/partial/pallas_call | solution.py:262
  57.9 0.0 collective-permute-done.11.refs_5_
  57.9 4.0 %partial.3.refs_5_ = f32[32,32,8,128]{3,2,1,0:T(8,128)S(1)} custom-call(s32[2]{0:T(128)S(1)} %pad_add_fusion.refs_0_.flags_ref, bf16[2,2,2,32,16,128]{5,4,3,2,1,0:T(8,128)(2,1)S(1)} %get-tuple-element.31.refs_0_, bf16[2,2,2,32,16,128]{5,4,3,2,1,0:T(8,128)(2,1)S(1)} %collective-permute-done.5.refs_1_, ...), custom_call_target="tpu_custom_call" | custom-call | flops 16640000 | bytes 4160000 | tf_op jit(solution)/shard_map/partial/pallas_call | solution.py:262
  61.9 0.0 collective-permute-done.3.refs_1_
  61.9 0.8 collective-permute-done.4.refs_2_
  62.6 5.9 %image.2.refs_6_ = f32[4,65,32,256]{3,2,1,0:T(8,128)} custom-call(s32[2]{0:T(128)S(1)} %pad_add_fusion.refs_0_.flags_ref, bf16[2,2,2,32,16,128]{5,4,3,2,1,0:T(8,128)(2,1)S(1)} %collective-permute-done.2.refs_1_.refs_0_, bf16[2,2,2,16,16,128]{5,4,3,2,1,0:T(8,128)(2,1)S(1)} %collective-permute-done.3.refs_1_, ...), custom_call_target="tpu_custom_call" | custom-call | flops 17160000 | bytes 4290000 | tf_op jit(solution)/shard_map/image/pallas_call | solution.py:262
  68.6 0.0 collective-permute-done.8.refs_3_
  68.6 3.3 %collective-permute-done.9.refs_4_ = bf16[2,2,2,16,16,128]{5,4,3,2,1,0:T(8,128)(2,1)S(1)} collective-permute-done((bf16[2,2,2,16,16,128]{5,4,3,2,1,0:T(8,128)(2,1)S(1)}, bf16[2,2,2,16,16,128]{5,4,3,2,1,0:T(8,128)(2,1)S(1)}, u32[]{:S(2)}, u32[]{:S(2)}) %collective-permute-start.9) | collective-permute-done | bytes 524320 | tf_op jit(solution)/shard_map/ppermute | solution.py:296
  71.8 6.1 %image.3 = f32[4,65,32,256]{3,2,1,0:T(8,128)} custom-call(s32[2]{0:T(128)S(1)} %pad_add_fusion.refs_0_.flags_ref, bf16[2,2,2,32,16,128]{5,4,3,2,1,0:T(8,128)(2,1)S(1)} %collective-permute-done.2.refs_1_.refs_0_, bf16[2,2,2,16,16,128]{5,4,3,2,1,0:T(8,128)(2,1)S(1)} %collective-permute-done.3.refs_1_, ...), custom_call_target="tpu_custom_call", output_to_operand_aliasing={{}: (7, {})} | custom-call | flops 16640000 | bytes 4160000 | tf_op jit(solution)/shard_map/image/pallas_call | solution.py:262
Async XLA Ops:
  1.7 2.0 %collective-permute-start = (bf16[2,2,32,16,128]{4,3,2,1,0:T(8,128)(2,1)S(1)}, bf16[2,2,32,16,128]{4,3,2,1,0:T(8,128)(2,1)S(1)}, u32[]{:S(2)}, u32[]{:S(2)}) collective-permute-start(bf16[2,2,32,16,128]{4,3,2,1,0:T(8,128)(2,1)S(1)} %get-tuple-element.25), channel_id=1, source_target_pairs={{0,1},{1,0},{2,3},{3,2},{4,5},{5,4},{6,7},{7,6},{8,9},{9,8},{10,11... | collective-permute-start | bytes 1572872 | tf_op jit(solution)/shard_map/ppermute | solution.py:289
  1.8 2.6 %collective-permute-start.1 = (bf16[2,2,32,16,128]{4,3,2,1,0:T(8,128)(2,1)S(1)}, bf16[2,2,32,16,128]{4,3,2,1,0:T(8,128)(2,1)S(1)}, u32[]{:S(2)}, u32[]{:S(2)}) collective-permute-start(bf16[2,2,32,16,128]{4,3,2,1,0:T(8,128)(2,1)S(1)} %get-tuple-element.27), channel_id=1, source_target_pairs={{0,1},{1,0},{2,3},{3,2},{4,5},{5,4},{6,7},{7,6},{8,9},{9,8},{10,11... | collective-permute-start | bytes 1572872 | tf_op jit(solution)/shard_map/ppermute | solution.py:289
  5.3 35.4 %collective-permute-start.2 = (bf16[2,2,2,32,16,128]{5,4,3,2,1,0:T(8,128)(2,1)S(1)}, bf16[2,2,2,32,16,128]{5,4,3,2,1,0:T(8,128)(2,1)S(1)}, u32[]{:S(2)}, u32[]{:S(2)}) collective-permute-start(bf16[2,2,2,32,16,128]{5,4,3,2,1,0:T(8,128)(2,1)S(1)} %get-tuple-element.28.refs_2_), channel_id=1, source_target_pairs={{0,2},{1,3},{2,0},{3,1},{4,6},{5,7},{6,4},{7,5},{8,10},{9,11},{10,... | collective-permute-start | bytes 3145736 | tf_op jit(solution)/shard_map/ppermute | solution.py:289
  7.7 40.1 %collective-permute-start.5 = (bf16[2,2,2,32,16,128]{5,4,3,2,1,0:T(8,128)(2,1)S(1)}, bf16[2,2,2,32,16,128]{5,4,3,2,1,0:T(8,128)(2,1)S(1)}, u32[]{:S(2)}, u32[]{:S(2)}) collective-permute-start(bf16[2,2,2,32,16,128]{5,4,3,2,1,0:T(8,128)(2,1)S(1)} %get-tuple-element.31.refs_0_), channel_id=1, source_target_pairs={{0,4},{1,5},{2,6},{3,7},{4,0},{5,1},{6,2},{7,3},{8,12},{9,13},{10,... | collective-permute-start | bytes 3145736 | tf_op jit(solution)/shard_map/ppermute | solution.py:296
  9.1 20.2 %collective-permute-start.6 = (bf16[2,2,2,16,16,128]{5,4,3,2,1,0:T(8,128)(2,1)S(1)}, bf16[2,2,2,16,16,128]{5,4,3,2,1,0:T(8,128)(2,1)S(1)}, u32[]{:S(2)}, u32[]{:S(2)}) collective-permute-start(bf16[2,2,2,16,16,128]{5,4,3,2,1,0:T(8,128)(2,1)S(1)} %get-tuple-element.32), channel_id=1, source_target_pairs={{0,124},{1,125},{2,126},{3,127},{4,8},{5,9},{6,10},{7,11},{8,4},{9... | collective-permute-start | bytes 1572872 | tf_op jit(solution)/shard_map/ppermute | solution.py:296
  16.5 22.9 %collective-permute-start.7 = (bf16[2,2,2,16,16,128]{5,4,3,2,1,0:T(8,128)(2,1)S(1)}, bf16[2,2,2,16,16,128]{5,4,3,2,1,0:T(8,128)(2,1)S(1)}, u32[]{:S(2)}, u32[]{:S(2)}) collective-permute-start(bf16[2,2,2,16,16,128]{5,4,3,2,1,0:T(8,128)(2,1)S(1)} %get-tuple-element.33), channel_id=1, source_target_pairs={{0,124},{1,125},{2,126},{3,127},{4,8},{5,9},{6,10},{7,11},{8,4},{9... | collective-permute-start | bytes 1572872 | tf_op jit(solution)/shard_map/ppermute | solution.py:296
  29.3 18.5 %collective-permute-start.10 = (bf16[2,2,2,16,16,128]{5,4,3,2,1,0:T(8,128)(2,1)S(1)}, bf16[2,2,2,16,16,128]{5,4,3,2,1,0:T(8,128)(2,1)S(1)}, u32[]{:S(2)}, u32[]{:S(2)}) collective-permute-start(bf16[2,2,2,16,16,128]{5,4,3,2,1,0:T(8,128)(2,1)S(1)} %collective-permute-done.6.refs_2_), channel_id=1, source_target_pairs={{0,128},{252,124},{1,129},{253,125},{2,130},{254,126},{3,131},{255... | collective-permute-start | bytes 1572872 | tf_op jit(solution)/shard_map/ppermute | solution.py:320
  39.4 18.5 %collective-permute-start.11 = (bf16[2,2,2,16,16,128]{5,4,3,2,1,0:T(8,128)(2,1)S(1)}, bf16[2,2,2,16,16,128]{5,4,3,2,1,0:T(8,128)(2,1)S(1)}, u32[]{:S(2)}, u32[]{:S(2)}) collective-permute-start(bf16[2,2,2,16,16,128]{5,4,3,2,1,0:T(8,128)(2,1)S(1)} %collective-permute-done.7.refs_4_), channel_id=1, source_target_pairs={{0,128},{252,124},{1,129},{253,125},{2,130},{254,126},{3,131},{255... | collective-permute-start | bytes 1572872 | tf_op jit(solution)/shard_map/ppermute | solution.py:320
  41.6 20.3 %collective-permute-start.3 = (bf16[2,2,2,16,16,128]{5,4,3,2,1,0:T(8,128)(2,1)S(1)}, bf16[2,2,2,16,16,128]{5,4,3,2,1,0:T(8,128)(2,1)S(1)}, u32[]{:S(2)}, u32[]{:S(2)}) collective-permute-start(bf16[2,2,2,16,16,128]{5,4,3,2,1,0:T(8,128)(2,1)S(1)} %get-tuple-element.29), channel_id=1, source_target_pairs={{0,4},{1,5},{2,6},{3,7},{4,0},{5,1},{6,2},{7,3},{8,12},{9,13},{10,... | collective-permute-start | bytes 1572872 | tf_op jit(solution)/shard_map/ppermute | solution.py:296
  41.7 21.0 %collective-permute-start.4 = (bf16[2,2,2,16,16,128]{5,4,3,2,1,0:T(8,128)(2,1)S(1)}, bf16[2,2,2,16,16,128]{5,4,3,2,1,0:T(8,128)(2,1)S(1)}, u32[]{:S(2)}, u32[]{:S(2)}) collective-permute-start(bf16[2,2,2,16,16,128]{5,4,3,2,1,0:T(8,128)(2,1)S(1)} %get-tuple-element.30), channel_id=1, source_target_pairs={{0,0},{1,1},{2,2},{3,3},{4,8},{5,9},{6,10},{7,11},{8,4},{9,5},{10,... | collective-permute-start | bytes 1572872 | tf_op jit(solution)/shard_map/ppermute | solution.py:296
  47.8 20.8 %collective-permute-start.8 = (bf16[2,2,2,16,16,128]{5,4,3,2,1,0:T(8,128)(2,1)S(1)}, bf16[2,2,2,16,16,128]{5,4,3,2,1,0:T(8,128)(2,1)S(1)}, u32[]{:S(2)}, u32[]{:S(2)}) collective-permute-start(bf16[2,2,2,16,16,128]{5,4,3,2,1,0:T(8,128)(2,1)S(1)} %get-tuple-element.36), channel_id=1, source_target_pairs={{0,4},{1,5},{2,6},{3,7},{4,0},{5,1},{6,2},{7,3},{8,12},{9,13},{10,... | collective-permute-start | bytes 1572872 | tf_op jit(solution)/shard_map/ppermute | solution.py:296
  47.9 24.0 %collective-permute-start.9 = (bf16[2,2,2,16,16,128]{5,4,3,2,1,0:T(8,128)(2,1)S(1)}, bf16[2,2,2,16,16,128]{5,4,3,2,1,0:T(8,128)(2,1)S(1)}, u32[]{:S(2)}, u32[]{:S(2)}) collective-permute-start(bf16[2,2,2,16,16,128]{5,4,3,2,1,0:T(8,128)(2,1)S(1)} %get-tuple-element.37), channel_id=1, source_target_pairs={{0,0},{1,1},{2,2},{3,3},{4,8},{5,9},{6,10},{7,11},{8,4},{9,5},{10,... | collective-permute-start | bytes 1572872 | tf_op jit(solution)/shard_map/ppermute | solution.py:296

commit v9 on v8

--- a/solution.py
+++ b/solution.py
@@ -15,8 +15,8 @@
 TX = 8
 TH = 4
 SLOTS = 4
+ORDER = (0, 2, 1, 3)
 CHUNKS = 4
-NEAR = HMAX // 2
 
 
 def regroup_kernel(group_ref, source_ref, receiver_ref, *refs):
@@ -80,39 +80,33 @@
     return jnp.where(flags_ref[0] == 0, choice[0], choice[1])
 
 
-def pack_kernel(copies, refs_in, *refs):
-    flags_ref, ins, outs = refs[0], refs[1 : 1 + refs_in], refs[1 + refs_in :]
-    for crosses, source, part, at, out, slot in copies:
-
-        def copy(source=source, part=part, at=at, out=out, slot=slot):
-            start = by_parity(flags_ref, at)
-
-            def one_cell(x, _):
-                for field in range(2):
-                    for f in range(outs[out].shape[2]):
-                        where = (field, f, start + x) if part is None else (part, field, f, start + x)
-                        outs[out][slot, field, f, x] = ins[source][where]
-                return 0
-
-            lax.fori_loop(0, outs[out].shape[3], one_cell, 0, unroll=4)
-
-        if crosses is None:
-            copy()
-        else:
-            pl.when((flags_ref[1] == 1) == crosses)(copy)
-
-
-def pack(flags, arrays, copies, shapes):
+def choose_kernel(flags_ref, usual_ref, crossing_ref, out_ref):
+    cells = out_ref.shape[2]
+
+    def copy(ref):
+        def one_cell(x, _):
+            for field in range(2):
+                for f in range(out_ref.shape[1]):
+                    out_ref[field, f, x] = ref[field, f, x]
+            return 0
+
+        lax.fori_loop(0, cells, one_cell, 0, unroll=4)
+
+    pl.when(flags_ref[1] != 1)(functools.partial(copy, usual_ref))
+    pl.when(flags_ref[1] == 1)(functools.partial(copy, crossing_ref))
+
+
+def choose(flags, usual, crossing):
     vmem = pl.BlockSpec(memory_space=pltpu.VMEM)
     return pl.pallas_call(
-        functools.partial(pack_kernel, copies, len(arrays)),
-        in_specs=[pl.BlockSpec(memory_space=pltpu.SMEM)] + [vmem] * len(arrays),
-        out_specs=[vmem] * len(shapes),
-        out_shape=[jax.ShapeDtypeStruct(shape, jnp.bfloat16) for shape in shapes],
+        choose_kernel,
+        in_specs=[pl.BlockSpec(memory_space=pltpu.SMEM), vmem, vmem],
+        out_specs=vmem,
+        out_shape=jax.ShapeDtypeStruct(usual.shape, jnp.bfloat16),
         compiler_params=pltpu.CompilerParams(vmem_limit_bytes=12 << 20),
-        cost_estimate=pl.CostEstimate(flops=0, bytes_accessed=2 << 20, transcendentals=0),
-        name="pack",
-    )(flags, *arrays)
+        cost_estimate=pl.CostEstimate(flops=0, bytes_accessed=1 << 20, transcendentals=0),
+        name="choose",
+    )(flags, usual, crossing)
 
 
 def sum_kernel(plan, bands, first, last, flags_ref, *refs):
@@ -121,8 +115,6 @@
     befores = ()
     if not first:
         befores, refs = refs[: len(bands)], refs[len(bands) :]
-    if last == 2:
-        refs = refs[1:]
     outs = refs[: 1 if last else len(bands)]
     fields = refs[len(outs)]
     if last:
@@ -231,12 +223,12 @@
                 out_copy(k_first + TH * steps, rest, steps % SLOTS).wait()
 
 
-NEAR_BAND = (HMAX - NEAR, 2 * NEAR // TH, 0, 0, 1)
-FAR_BAND = (0, 2 * NEAR // TH, NEAR // TH, 2 * NEAR + 1, 0)
-
-
-def summed(flags, blocks, plan, bands, befores, cells, groups, last, image=None):
-    first = befores is None
+ALL_ROWS = (0, OFFSETS // TH, 0, 0, OFFSETS % TH)
+
+
+def summed(flags, blocks, plan, before, cells, groups, last):
+    first = before is None
+    bands, befores = (ALL_ROWS,), None if first else (before,)
     heights = [TH * band[1] + band[4] for band in bands]
     scratch = [pltpu.VMEM((2, 3 * cells, 2 * groups, ROWS, LANES), jnp.float32)]
     vmem = pl.BlockSpec(memory_space=pltpu.VMEM)
@@ -252,14 +244,11 @@
         ]
         out_shape = jax.ShapeDtypeStruct((4, OFFSETS, cells, 2 * LANES), jnp.float32)
         out_specs = hbm
-        if last == 2:
-            operands.append(image)
-            in_specs.append(hbm)
-            aliases = {len(operands): 0}
     else:
         out_shape = [pltpu.VMEM((height, cells, 8, LANES), jnp.float32) for height in heights]
         out_specs = [vmem] * len(heights)
-    return pl.pallas_call(
+        aliases = {} if first else {len(operands): 0}
+    result = pl.pallas_call(
         functools.partial(sum_kernel, plan, bands, first, last),
         in_specs=in_specs,
         out_specs=out_specs,
@@ -272,12 +261,13 @@
         ),
         name="image" if last else "partial",
     )(flags, *operands)
+    return result if last else result[0]
 
 
 def body(source_field, receiver_field):
     slabs = lax.axis_size("slab")
     middle = slabs // 2
-    cells, freqs = source_field.shape[2], source_field.shape[1]
+    cells = source_field.shape[2]
     group = lax.axis_index("freq").astype(jnp.int32)
     slab = lax.axis_index("slab")
     beyond = jnp.where((slab == 0) | (slab == slabs - 1), 2, 0)
@@ -288,11 +278,12 @@
     def swap(part, d):
         return lax.ppermute(part, "freq", [(g, g ^ d) for g in range(GROUPS)])
 
-    def trade(value, partner, turned=()):
+    def trade(value, partner, turn=0):
         pairs = []
         for s in range(slabs):
             for g in range(GROUPS):
-                pairs.append((s * GROUPS + g, partner(s) * GROUPS + (g ^ 2 if s in turned else g)))
+                to = g ^ turn if s in (middle - 1, middle) else g
+                pairs.append((s * GROUPS + g, partner(s) * GROUPS + to))
         return lax.ppermute(value, ("slab", "freq"), pairs)
 
     def side_a(s):
@@ -304,59 +295,27 @@
     def side_b_of_half(s):
         return s // middle * middle + (s + 1 if s % 2 else s - 1) % middle
 
-    one, other = swap(parts[1], 1), swap(parts[3], 1)
-
-    whole, half = [(2, 2, freqs, length, ROWS, LANES) for length in (cells, NEAR)]
-    rest = cells - NEAR
-    copies = []
-    for slot in range(2):
-        copies += [(None, slot, None, 0, 0, slot), (None, 2 + slot, None, 0, 1, slot)]
-        copies += [(None, slot, None, (0, rest), 2, slot), (None, slot, None, (rest, 0), 3, slot)]
-    own, turned_own, near_b, far_b = pack(flags, (parts[0], one, parts[2], other), copies, (whole,) * 2 + (half,) * 2)
-    far_own = swap(turned_own, 2)
-    whole_a = trade(own, side_a)
-    first_near_b, first_far_b = trade(near_b, side_b_of_half), trade(far_b, side_b_of_half)
+    owned = [parts[0]] + [swap(parts[d], d) for d in range(1, GROUPS)]
     over_middle = [(0, middle), (slabs - 1, middle - 1)]
-    near_over, far_over = [lax.ppermute(value, "slab", over_middle) for value in (first_near_b, first_far_b)]
-
-    copies = []
-    for slot in range(2):
-        for out, at in ((0, (rest, 0)), (2, (0, rest))):
-            copies.append((None, 0, slot, at, out, slot))
-        for out, at in ((1, (0, rest)), (3, (rest, 0))):
-            copies += [(False, 0, slot, at, out, slot), (True, 1, slot, at, out, slot)]
-    near_a, near_b, far_a, far_b = pack(flags, (far_own, turned_own), copies, (half,) * 4)
-    turned = (middle - 1, middle)
-    near_a, near_b = trade(near_a, side_a), trade(near_b, side_b, turned)
-    whole_a, first_near_b, first_far_b, far_a, far_b = lax.optimization_barrier(
-        (whole_a, first_near_b, first_far_b, far_a, far_b)
-    )
-    far_a, far_b = trade(far_a, side_a), trade(far_b, side_b, turned)
-
-    near_at_a, near_at_b = (2 * cells, rest), (rest, 2 * cells)
-    far_at_a, far_at_b = (2 * cells + NEAR, 0), (0, 2 * cells + NEAR)
-    plan, far_plan = [], []
-    for g in range(2):
-        plan += [(0, g, 0, cells, cells, g, None), (1, g, (0, rest), NEAR, near_at_a, g, None)]
-        plan += [(2, g, 0, NEAR, near_at_b, g, (0,)), (3, g, 0, NEAR, near_at_b, g, (1,))]
-        plan += [(None, g, 0, NEAR, near_at_b, g, (2,))]
-        far_plan += [(1, g, (rest, 0), NEAR, far_at_a, g, None)]
-        far_plan += [(4, g, 0, NEAR, far_at_b, g, (0,)), (5, g, 0, NEAR, far_at_b, g, (1,))]
-        far_plan += [(None, g, 0, NEAR, far_at_b, g, (2,))]
-    blocks = (own, whole_a, first_near_b, near_over)
-    befores = summed(flags, blocks, plan, (NEAR_BAND,), None, cells, 2, 0)
-    far_over, *befores = lax.optimization_barrier((far_over, *befores))
-    far_sums = (flags, plan + far_plan, blocks)
-    plan, far_plan = [], []
-    for g in range(2):
-        plan += [(0, g, 0, cells, cells, g, None), (1, g, 0, NEAR, near_at_a, g, None)]
-        plan += [(2, g, 0, NEAR, near_at_b, g, (0, 1)), (None, g, 0, NEAR, near_at_b, g, (2,))]
-        far_plan += [(3, g, 0, NEAR, far_at_a, g, None)]
-        far_plan += [(4, g, 0, NEAR, far_at_b, g, (0, 1)), (None, g, 0, NEAR, far_at_b, g, (2,))]
-    far_befores = summed(flags, far_sums[2] + (first_far_b, far_over), far_sums[1], (FAR_BAND,), None, cells, 2, 0)
-    image = summed(flags, (far_own, near_a, near_b), plan, (NEAR_BAND,), befores, cells, 2, 1)
-    blocks = (far_own, near_a, near_b, far_a, far_b)
-    return summed(flags, blocks, plan + far_plan, (FAR_BAND,), far_befores, cells, 2, 2, image)
+    at_a, at_b = (2 * cells, 0), (0, 2 * cells)
+    traded = []
+    for d in range(GROUPS):
+        if d >= 2:
+            sent_b = choose(flags, owned[d], parts[d])
+            traded.append([trade(owned[d], side_a), trade(sent_b, side_b, d)])
+        else:
+            traded.append([trade(owned[d], side_a), trade(owned[d], side_b_of_half)])
+            traded[d].append(lax.ppermute(traded[d][1], "slab", over_middle))
+    total = None
+    for d in ORDER:
+        plan = [(0, None, 0, cells, cells, 0, None), (1, None, 0, cells, at_a, 0, None)]
+        if d >= 2:
+            plan += [(2, None, 0, cells, at_b, 0, (0, 1))]
+        else:
+            plan += [(2, None, 0, cells, at_b, 0, (0,)), (3, None, 0, cells, at_b, 0, (1,))]
+        plan += [(None, None, 0, cells, at_b, 0, (2,))]
+        total = summed(flags, (owned[d], *traded[d]), plan, total, cells, 1, d == ORDER[-1])
+    return total
 
 
 def solution(mesh):

time: 78.3 us -> 76.4 us (0.976)
  starting transfers between devices: 26.9 us -> 23.1 us
  waiting for transfers between devices: 27.7 us -> 29.9 us
    ppermute x7 -> x8, waiting for transfers between devices: 25.6 us -> 13.8 us  [trade(): return lax.ppermute(value, ('slab', 'freq'), pairs)]
    ppermute x2, waiting for transfers between devices: 0.01 us -> 9.73 us  [body(): traded[d].append(lax.ppermute(traded[d][1], 'slab', over_middle))]
    ppermute x3, waiting for transfers between devices: 2.08 us -> 6.33 us  [swap(): return lax.ppermute(part, 'freq', [(g, g ^ d) for g in range(GROUPS)])]
    ppermute x7 -> x8, starting transfers between devices: 21.4 us -> 17.4 us  [trade(): return lax.ppermute(value, ('slab', 'freq'), pairs)]
    pallas_call x1, Pallas kernels: 1.66 us -> 2.45 us  [regrouped(): pl.pallas_call(regroup_kernel, in_specs=[pl.BlockSpec(memory_space=pltpu....]
  transfers between devices with their start and end apart: 12 -> 13, of which waited for: 6 -> 8; matrix products, arithmetic and copies ran while one was open for 0% -> 0% of each run, Pallas kernels for 19% -> 18%
where the time goes in v9:
time: 76.4 us; the launch traced here: 76.2 us
  waiting for transfers between devices  29.9 us (39%)
  starting transfers between devices  23.1 us (30%)
  Pallas kernels  23 us (30%)
    pallas_call x4, Pallas kernels, summed(): pl.pallas_call(functools.partial(sum_kernel, plan, bands, first, last), i...  19.3 us
    ppermute x8, starting transfers between devices, trade(): return lax.ppermute(value, ('slab', 'freq'), pairs)  17.4 us
    ppermute x8, waiting for transfers between devices, trade(): return lax.ppermute(value, ('slab', 'freq'), pairs)  13.8 us
    ppermute x2, waiting for transfers between devices, body(): traded[d].append(lax.ppermute(traded[d][1], 'slab', over_middle))  9.73 us
    ppermute x3, waiting for transfers between devices, swap(): return lax.ppermute(part, 'freq', [(g, g ^ d) for g in range(GROUPS)])  6.33 us
    ppermute x3, starting transfers between devices, swap(): return lax.ppermute(part, 'freq', [(g, g ^ d) for g in range(GROUPS)])  3.1 us
    ppermute x2, starting transfers between devices, body(): traded[d].append(lax.ppermute(traded[d][1], 'slab', over_middle))  2.56 us
    pallas_call x1, Pallas kernels, regrouped(): pl.pallas_call(regroup_kernel, in_specs=[pl.BlockSpec(memory_space=pltpu....  2.45 us
  transfers between devices with their start and end apart: 13, of which 8 were waited for; matrix products, arithmetic and copies ran while one was open for 0% of the time, Pallas kernels for 18%

profile of v9, /device:TPU:8, one launch (start us, length us, event | category | flops | bytes accessed | tf_op | source)
XLA Modules:
  0.0 76.2 jit_solution(17803960504117479195)
XLA Ops:
  0.0 2.5 %regroup.1 = (bf16[2,2,32,16,128]{4,3,2,1,0:T(8,128)(2,1)S(1)}, bf16[2,2,32,16,128]{4,3,2,1,0:T(8,128)(2,1)}, bf16[2,2,32,16,128]{4,3,2,1,0:T(8,128)(2,1)S(1)}, bf16[2,2,32,16,128]{4,3,2,1,0:T(8,128)(2,1)S(1)}) custom-call(s32[1]{0:T(128)} %bitcast.2.group_ref, bf16[2,2,32,16,256]{4,3,2,1,0:T(8,128)(2,1)} %source_ref.1, bf16[2,2,32,16,256]{4,3,2,1,0:T(8,128)(2,1)} %receiver_ref.1), custom_call_target="tpu_custom_call" | custom-call | bytes 4194304 | tf_op jit(solution)/shard_map/regroup/pallas_call | solution.py:65
  2.5 0.1 collective-permute-start.3
  2.6 8.1 %collective-permute-start.11 = (bf16[2,2,32,16,128]{4,3,2,1,0:T(8,128)(2,1)S(1)}, bf16[2,2,32,16,128]{4,3,2,1,0:T(8,128)(2,1)}, u32[]{:S(2)}, u32[]{:S(2)}) collective-permute-start(bf16[2,2,32,16,128]{4,3,2,1,0:T(8,128)(2,1)S(1)} %get-tuple-element.12.refs_0_), channel_id=1, source_target_pairs={{0,124},{1,125},{2,126},{3,127},{4,8},{5,9},{6,10},{7,11},{8,4},{9... | collective-permute-start | bytes 1572872 | tf_op jit(solution)/shard_map/ppermute | solution.py:287
  10.7 2.3 %collective-permute-start.7 = (bf16[2,2,32,16,128]{4,3,2,1,0:T(8,128)(2,1)S(1)}, bf16[2,2,32,16,128]{4,3,2,1,0:T(8,128)(2,1)S(1)}, u32[]{:S(2)}, u32[]{:S(2)}) collective-permute-start(bf16[2,2,32,16,128]{4,3,2,1,0:T(8,128)(2,1)S(1)} %get-tuple-element.11.crossing_ref), channel_id=1, source_target_pairs={{0,2},{1,3},{2,0},{3,1},{4,6},{5,7},{6,4},{7,5},{8,10},{9,11},{10,... | collective-permute-start | bytes 1572872 | tf_op jit(solution)/shard_map/ppermute | solution.py:279
  13.0 0.0 collective-permute-start.10
  13.0 0.7 collective-permute-start
  13.7 0.0 collective-permute-done.3.refs_0_
  13.7 1.1 %collective-permute-start.5 = (bf16[2,2,32,16,128]{4,3,2,1,0:T(8,128)(2,1)S(1)}, bf16[2,2,32,16,128]{4,3,2,1,0:T(8,128)(2,1)S(1)}, u32[]{:S(2)}, u32[]{:S(2)}) collective-permute-start(bf16[2,2,32,16,128]{4,3,2,1,0:T(8,128)(2,1)S(1)} %collective-permute-done.3.refs_0_), channel_id=1, source_target_pairs={{0,124},{1,125},{2,126},{3,127},{4,8},{5,9},{6,10},{7,11},{8,4},{9... | collective-permute-start | bytes 1572872 | tf_op jit(solution)/shard_map/ppermute | solution.py:287
  14.8 0.1 pad_add_fusion.flags_ref
  14.9 8.7 %collective-permute-done.11.refs_2_ = bf16[2,2,32,16,128]{4,3,2,1,0:T(8,128)(2,1)} collective-permute-done((bf16[2,2,32,16,128]{4,3,2,1,0:T(8,128)(2,1)S(1)}, bf16[2,2,32,16,128]{4,3,2,1,0:T(8,128)(2,1)}, u32[]{:S(2)}, u32[]{:S(2)}) %collective-permute-start.11) | collective-permute-done | bytes 524320 | tf_op jit(solution)/shard_map/ppermute | solution.py:287
  23.6 1.3 %collective-permute-start.12 = (bf16[2,2,32,16,128]{4,3,2,1,0:T(8,128)(2,1)}, bf16[2,2,32,16,128]{4,3,2,1,0:T(8,128)(2,1)S(1)}, u32[]{:S(2)}, u32[]{:S(2)}) collective-permute-start(bf16[2,2,32,16,128]{4,3,2,1,0:T(8,128)(2,1)} %collective-permute-done.11.refs_2_), channel_id=1, source_target_pairs={{0,128},{252,124},{1,129},{253,125},{2,130},{254,126},{3,131},{255... | collective-permute-start | bytes 1572872 | tf_op jit(solution)/shard_map/ppermute | solution.py:308
  24.9 2.1 %collective-permute-done.7.usual_ref.refs_0_ = bf16[2,2,32,16,128]{4,3,2,1,0:T(8,128)(2,1)S(1)} collective-permute-done((bf16[2,2,32,16,128]{4,3,2,1,0:T(8,128)(2,1)S(1)}, bf16[2,2,32,16,128]{4,3,2,1,0:T(8,128)(2,1)S(1)}, u32[]{:S(2)}, u32[]{:S(2)}) %collective-permute-start.7) | collective-permute-done | bytes 524320 | tf_op jit(solution)/shard_map/ppermute | solution.py:279
  27.0 0.6 choose.3
  27.6 6.1 %collective-permute-start.9 = (bf16[2,2,32,16,128]{4,3,2,1,0:T(8,128)(2,1)S(1)}, bf16[2,2,32,16,128]{4,3,2,1,0:T(8,128)(2,1)S(1)}, u32[]{:S(2)}, u32[]{:S(2)}) collective-permute-start(bf16[2,2,32,16,128]{4,3,2,1,0:T(8,128)(2,1)S(1)} %choose.3), channel_id=1, source_target_pairs={{0,0},{1,1},{2,2},{3,3},{4,8},{5,9},{6,10},{7,11},{8,4},{9,5},{10,... | collective-permute-start | bytes 1572872 | tf_op jit(solution)/shard_map/ppermute | solution.py:287
  33.7 0.0 collective-permute-done.10.refs_1_
  33.7 0.1 collective-permute-start.8
  33.8 4.2 %collective-permute-done.usual_ref.refs_0_ = bf16[2,2,32,16,128]{4,3,2,1,0:T(8,128)(2,1)S(1)} collective-permute-done((bf16[2,2,32,16,128]{4,3,2,1,0:T(8,128)(2,1)S(1)}, bf16[2,2,32,16,128]{4,3,2,1,0:T(8,128)(2,1)S(1)}, u32[]{:S(2)}, u32[]{:S(2)}) %collective-permute-start) | collective-permute-done | bytes 524320 | tf_op jit(solution)/shard_map/ppermute | solution.py:279
  38.0 0.0 collective-permute-start.4
  38.0 0.0 collective-permute-done.5.refs_2_
  38.0 1.3 %collective-permute-start.6 = (bf16[2,2,32,16,128]{4,3,2,1,0:T(8,128)(2,1)S(1)}, bf16[2,2,32,16,128]{4,3,2,1,0:T(8,128)(2,1)S(1)}, u32[]{:S(2)}, u32[]{:S(2)}) collective-permute-start(bf16[2,2,32,16,128]{4,3,2,1,0:T(8,128)(2,1)S(1)} %collective-permute-done.5.refs_2_), channel_id=1, source_target_pairs={{0,128},{252,124},{1,129},{253,125},{2,130},{254,126},{3,131},{255... | collective-permute-start | bytes 1572872 | tf_op jit(solution)/shard_map/ppermute | solution.py:308
  39.3 0.6 choose.2
  39.9 9.6 %collective-permute-done.12.refs_3_ = bf16[2,2,32,16,128]{4,3,2,1,0:T(8,128)(2,1)S(1)} collective-permute-done((bf16[2,2,32,16,128]{4,3,2,1,0:T(8,128)(2,1)}, bf16[2,2,32,16,128]{4,3,2,1,0:T(8,128)(2,1)S(1)}, u32[]{:S(2)}, u32[]{:S(2)}) %collective-permute-start.12) | collective-permute-done | bytes 524320 | tf_op jit(solution)/shard_map/ppermute | solution.py:308
  49.5 1.9 %collective-permute-start.2 = (bf16[2,2,32,16,128]{4,3,2,1,0:T(8,128)(2,1)S(1)}, bf16[2,2,32,16,128]{4,3,2,1,0:T(8,128)(2,1)S(1)}, u32[]{:S(2)}, u32[]{:S(2)}) collective-permute-start(bf16[2,2,32,16,128]{4,3,2,1,0:T(8,128)(2,1)S(1)} %choose.2), channel_id=1, source_target_pairs={{0,0},{1,1},{2,2},{3,3},{4,8},{5,9},{6,10},{7,11},{8,4},{9,5},{10,... | collective-permute-start | bytes 1572872 | tf_op jit(solution)/shard_map/ppermute | solution.py:287
  51.5 0.0 collective-permute-done.9.refs_2_
  51.5 0.1 collective-permute-start.1
  51.6 4.2 %partial.3.refs_3_ = f32[65,32,8,128]{3,2,1,0:T(8,128)S(1)} custom-call(s32[2]{0:T(128)S(1)} %pad_add_fusion.flags_ref, bf16[2,2,32,16,128]{4,3,2,1,0:T(8,128)(2,1)S(1)} %get-tuple-element.12.refs_0_, bf16[2,2,32,16,128]{4,3,2,1,0:T(8,128)(2,1)} %collective-permute-done.10.refs_1_, bf16[2,2,32,16,128]{4,3,2,1,0:T(8,128)(2,1)} %collective-permute-done.11.refs_2_, ...), custom_call_target="tpu_custom_call" | custom-call | flops 16900000 | bytes 8450000 | tf_op jit(solution)/shard_map/partial/pallas_call | solution.py:251
  55.7 0.0 collective-permute-done.8.refs_1_
  55.8 4.0 %partial.4.refs_4_ = f32[65,32,8,128]{3,2,1,0:T(8,128)S(1)} custom-call(s32[2]{0:T(128)S(1)} %pad_add_fusion.flags_ref, bf16[2,2,32,16,128]{4,3,2,1,0:T(8,128)(2,1)S(1)} %collective-permute-done.7.usual_ref.refs_0_, bf16[2,2,32,16,128]{4,3,2,1,0:T(8,128)(2,1)S(1)} %collective-permute-done.8.refs_1_, ...), custom_call_target="tpu_custom_call", output_to_operand_aliasing={{}: (4, {})} | custom-call | flops 16900000 | bytes 8450000 | tf_op jit(solution)/shard_map/partial/pallas_call | solution.py:251
  59.7 0.1 collective-permute-done.4.refs_1_
  59.9 0.1 collective-permute-done.6.refs_3_
  60.0 4.0 %partial.5.refs_3_ = f32[65,32,8,128]{3,2,1,0:T(8,128)S(1)} custom-call(s32[2]{0:T(128)S(1)} %pad_add_fusion.flags_ref, bf16[2,2,32,16,128]{4,3,2,1,0:T(8,128)(2,1)S(1)} %collective-permute-done.3.refs_0_, bf16[2,2,32,16,128]{4,3,2,1,0:T(8,128)(2,1)S(1)} %collective-permute-done.4.refs_1_, ...), custom_call_target="tpu_custom_call", output_to_operand_aliasing={{}: (5, {})} | custom-call | flops 16900000 | bytes 8450000 | tf_op jit(solution)/shard_map/partial/pallas_call | solution.py:251
  64.0 4.6 %collective-permute-done.2.refs_2_ = bf16[2,2,32,16,128]{4,3,2,1,0:T(8,128)(2,1)S(1)} collective-permute-done((bf16[2,2,32,16,128]{4,3,2,1,0:T(8,128)(2,1)S(1)}, bf16[2,2,32,16,128]{4,3,2,1,0:T(8,128)(2,1)S(1)}, u32[]{:S(2)}, u32[]{:S(2)}) %collective-permute-start.2) | collective-permute-done | bytes 524320 | tf_op jit(solution)/shard_map/ppermute | solution.py:287
  68.6 0.4 collective-permute-done.1.refs_1_
  69.0 7.2 %image.1 = f32[4,65,32,256]{3,2,1,0:T(8,128)} custom-call(s32[2]{0:T(128)S(1)} %pad_add_fusion.flags_ref, bf16[2,2,32,16,128]{4,3,2,1,0:T(8,128)(2,1)S(1)} %collective-permute-done.usual_ref.refs_0_, bf16[2,2,32,16,128]{4,3,2,1,0:T(8,128)(2,1)S(1)} %collective-permute-done.1.refs_1_, bf16[2,2,32,16,128]{4,3,2,1,0:T(8,128)(2,1)S(1)} %collective-permute-done.2.refs_2_, ...), custom_call_target="tpu_custom_call" | custom-call | flops 16900000 | bytes 8450000 | tf_op jit(solution)/shard_map/image/pallas_call | solution.py:251
Async XLA Ops:
  2.5 11.2 %collective-permute-start.3 = (bf16[2,2,32,16,128]{4,3,2,1,0:T(8,128)(2,1)}, bf16[2,2,32,16,128]{4,3,2,1,0:T(8,128)(2,1)S(1)}, u32[]{:S(2)}, u32[]{:S(2)}) collective-permute-start(bf16[2,2,32,16,128]{4,3,2,1,0:T(8,128)(2,1)} %get-tuple-element.10), channel_id=1, source_target_pairs={{0,1},{1,0},{2,3},{3,2},{4,5},{5,4},{6,7},{7,6},{8,9},{9,8},{10,11... | collective-permute-start | bytes 1572872 | tf_op jit(solution)/shard_map/ppermute | solution.py:279
  2.6 21.0 %collective-permute-start.11 = (bf16[2,2,32,16,128]{4,3,2,1,0:T(8,128)(2,1)S(1)}, bf16[2,2,32,16,128]{4,3,2,1,0:T(8,128)(2,1)}, u32[]{:S(2)}, u32[]{:S(2)}) collective-permute-start(bf16[2,2,32,16,128]{4,3,2,1,0:T(8,128)(2,1)S(1)} %get-tuple-element.12.refs_0_), channel_id=1, source_target_pairs={{0,124},{1,125},{2,126},{3,127},{4,8},{5,9},{6,10},{7,11},{8,4},{9... | collective-permute-start | bytes 1572872 | tf_op jit(solution)/shard_map/ppermute | solution.py:287
  10.7 16.3 %collective-permute-start.7 = (bf16[2,2,32,16,128]{4,3,2,1,0:T(8,128)(2,1)S(1)}, bf16[2,2,32,16,128]{4,3,2,1,0:T(8,128)(2,1)S(1)}, u32[]{:S(2)}, u32[]{:S(2)}) collective-permute-start(bf16[2,2,32,16,128]{4,3,2,1,0:T(8,128)(2,1)S(1)} %get-tuple-element.11.crossing_ref), channel_id=1, source_target_pairs={{0,2},{1,3},{2,0},{3,1},{4,6},{5,7},{6,4},{7,5},{8,10},{9,11},{10,... | collective-permute-start | bytes 1572872 | tf_op jit(solution)/shard_map/ppermute | solution.py:279
  13.0 20.7 %collective-permute-start.10 = (bf16[2,2,32,16,128]{4,3,2,1,0:T(8,128)(2,1)S(1)}, bf16[2,2,32,16,128]{4,3,2,1,0:T(8,128)(2,1)}, u32[]{:S(2)}, u32[]{:S(2)}) collective-permute-start(bf16[2,2,32,16,128]{4,3,2,1,0:T(8,128)(2,1)S(1)} %get-tuple-element.12.refs_0_), channel_id=1, source_target_pairs={{0,4},{1,5},{2,6},{3,7},{4,0},{5,1},{6,2},{7,3},{8,12},{9,13},{10,... | collective-permute-start | bytes 1572872 | tf_op jit(solution)/shard_map/ppermute | solution.py:287
  13.0 25.0 %collective-permute-start = (bf16[2,2,32,16,128]{4,3,2,1,0:T(8,128)(2,1)S(1)}, bf16[2,2,32,16,128]{4,3,2,1,0:T(8,128)(2,1)S(1)}, u32[]{:S(2)}, u32[]{:S(2)}) collective-permute-start(bf16[2,2,32,16,128]{4,3,2,1,0:T(8,128)(2,1)S(1)} %get-tuple-element.9.crossing_ref), channel_id=1, source_target_pairs={{0,3},{1,2},{2,1},{3,0},{4,7},{5,6},{6,5},{7,4},{8,11},{9,10},{10,... | collective-permute-start | bytes 1572872 | tf_op jit(solution)/shard_map/ppermute | solution.py:279
  13.7 24.3 %collective-permute-start.5 = (bf16[2,2,32,16,128]{4,3,2,1,0:T(8,128)(2,1)S(1)}, bf16[2,2,32,16,128]{4,3,2,1,0:T(8,128)(2,1)S(1)}, u32[]{:S(2)}, u32[]{:S(2)}) collective-permute-start(bf16[2,2,32,16,128]{4,3,2,1,0:T(8,128)(2,1)S(1)} %collective-permute-done.3.refs_0_), channel_id=1, source_target_pairs={{0,124},{1,125},{2,126},{3,127},{4,8},{5,9},{6,10},{7,11},{8,4},{9... | collective-permute-start | bytes 1572872 | tf_op jit(solution)/shard_map/ppermute | solution.py:287
  23.6 26.0 %collective-permute-start.12 = (bf16[2,2,32,16,128]{4,3,2,1,0:T(8,128)(2,1)}, bf16[2,2,32,16,128]{4,3,2,1,0:T(8,128)(2,1)S(1)}, u32[]{:S(2)}, u32[]{:S(2)}) collective-permute-start(bf16[2,2,32,16,128]{4,3,2,1,0:T(8,128)(2,1)} %collective-permute-done.11.refs_2_), channel_id=1, source_target_pairs={{0,128},{252,124},{1,129},{253,125},{2,130},{254,126},{3,131},{255... | collective-permute-start | bytes 1572872 | tf_op jit(solution)/shard_map/ppermute | solution.py:308
  27.6 23.9 %collective-permute-start.9 = (bf16[2,2,32,16,128]{4,3,2,1,0:T(8,128)(2,1)S(1)}, bf16[2,2,32,16,128]{4,3,2,1,0:T(8,128)(2,1)S(1)}, u32[]{:S(2)}, u32[]{:S(2)}) collective-permute-start(bf16[2,2,32,16,128]{4,3,2,1,0:T(8,128)(2,1)S(1)} %choose.3), channel_id=1, source_target_pairs={{0,0},{1,1},{2,2},{3,3},{4,8},{5,9},{6,10},{7,11},{8,4},{9,5},{10,... | collective-permute-start | bytes 1572872 | tf_op jit(solution)/shard_map/ppermute | solution.py:287
  33.7 22.1 %collective-permute-start.8 = (bf16[2,2,32,16,128]{4,3,2,1,0:T(8,128)(2,1)S(1)}, bf16[2,2,32,16,128]{4,3,2,1,0:T(8,128)(2,1)S(1)}, u32[]{:S(2)}, u32[]{:S(2)}) collective-permute-start(bf16[2,2,32,16,128]{4,3,2,1,0:T(8,128)(2,1)S(1)} %collective-permute-done.7.usual_ref.refs_0_), channel_id=1, source_target_pairs={{0,4},{1,5},{2,6},{3,7},{4,0},{5,1},{6,2},{7,3},{8,12},{9,13},{10,... | collective-permute-start | bytes 1572872 | tf_op jit(solution)/shard_map/ppermute | solution.py:287
  38.0 21.9 %collective-permute-start.4 = (bf16[2,2,32,16,128]{4,3,2,1,0:T(8,128)(2,1)S(1)}, bf16[2,2,32,16,128]{4,3,2,1,0:T(8,128)(2,1)S(1)}, u32[]{:S(2)}, u32[]{:S(2)}) collective-permute-start(bf16[2,2,32,16,128]{4,3,2,1,0:T(8,128)(2,1)S(1)} %collective-permute-done.3.refs_0_), channel_id=1, source_target_pairs={{0,4},{1,5},{2,6},{3,7},{4,0},{5,1},{6,2},{7,3},{8,12},{9,13},{10,... | collective-permute-start | bytes 1572872 | tf_op jit(solution)/shard_map/ppermute | solution.py:287
  38.0 22.0 %collective-permute-start.6 = (bf16[2,2,32,16,128]{4,3,2,1,0:T(8,128)(2,1)S(1)}, bf16[2,2,32,16,128]{4,3,2,1,0:T(8,128)(2,1)S(1)}, u32[]{:S(2)}, u32[]{:S(2)}) collective-permute-start(bf16[2,2,32,16,128]{4,3,2,1,0:T(8,128)(2,1)S(1)} %collective-permute-done.5.refs_2_), channel_id=1, source_target_pairs={{0,128},{252,124},{1,129},{253,125},{2,130},{254,126},{3,131},{255... | collective-permute-start | bytes 1572872 | tf_op jit(solution)/shard_map/ppermute | solution.py:308
  49.5 19.0 %collective-permute-start.2 = (bf16[2,2,32,16,128]{4,3,2,1,0:T(8,128)(2,1)S(1)}, bf16[2,2,32,16,128]{4,3,2,1,0:T(8,128)(2,1)S(1)}, u32[]{:S(2)}, u32[]{:S(2)}) collective-permute-start(bf16[2,2,32,16,128]{4,3,2,1,0:T(8,128)(2,1)S(1)} %choose.2), channel_id=1, source_target_pairs={{0,0},{1,1},{2,2},{3,3},{4,8},{5,9},{6,10},{7,11},{8,4},{9,5},{10,... | collective-permute-start | bytes 1572872 | tf_op jit(solution)/shard_map/ppermute | solution.py:287
  51.5 17.5 %collective-permute-start.1 = (bf16[2,2,32,16,128]{4,3,2,1,0:T(8,128)(2,1)S(1)}, bf16[2,2,32,16,128]{4,3,2,1,0:T(8,128)(2,1)S(1)}, u32[]{:S(2)}, u32[]{:S(2)}) collective-permute-start(bf16[2,2,32,16,128]{4,3,2,1,0:T(8,128)(2,1)S(1)} %collective-permute-done.usual_ref.refs_0_), channel_id=1, source_target_pairs={{0,4},{1,5},{2,6},{3,7},{4,0},{5,1},{6,2},{7,3},{8,12},{9,13},{10,... | collective-permute-start | bytes 1572872 | tf_op jit(solution)/shard_map/ppermute | solution.py:287

commit v10 on v9

--- a/solution.py
+++ b/solution.py
@@ -15,7 +15,7 @@
 TX = 8
 TH = 4
 SLOTS = 4
-ORDER = (0, 2, 1, 3)
+ORDER = (2, 0, 1, 3)
 CHUNKS = 4
 
 
@@ -300,12 +300,17 @@
     at_a, at_b = (2 * cells, 0), (0, 2 * cells)
     traded = []
     for d in range(GROUPS):
-        if d >= 2:
-            sent_b = choose(flags, owned[d], parts[d])
-            traded.append([trade(owned[d], side_a), trade(sent_b, side_b, d)])
-        else:
+        if d < 2:
             traded.append([trade(owned[d], side_a), trade(owned[d], side_b_of_half)])
-            traded[d].append(lax.ppermute(traded[d][1], "slab", over_middle))
+            continue
+        sent_a, sent_b = owned[d], choose(flags, owned[d], parts[d])
+        sent_a, traded[d - 2][0] = lax.optimization_barrier((sent_a, traded[d - 2][0]))
+        sent_b, traded[d - 2][1] = lax.optimization_barrier((sent_b, traded[d - 2][1]))
+        traded.append([trade(sent_a, side_a), trade(sent_b, side_b, d)])
+    over_0, owned[3], *traded[1] = lax.optimization_barrier((traded[0][1], owned[3], *traded[1]))
+    over_1, *traded[2] = lax.optimization_barrier((traded[1][1], *traded[2]))
+    for d, value in enumerate((over_0, over_1)):
+        traded[d].append(lax.ppermute(value, "slab", over_middle))
     total = None
     for d in ORDER:
         plan = [(0, None, 0, cells, cells, 0, None), (1, None, 0, cells, at_a, 0, None)]

time: 76.4 us -> 78.9 us (1.033)
  starting transfers between devices: 23.1 us -> 28.1 us
  waiting for transfers between devices: 29.9 us -> 25.9 us
    ppermute x2, waiting for transfers between devices: 9.73 us -> 0.48 us  [body(): traded[d].append(lax.ppermute(value, 'slab', over_middle))]
    ppermute x8, waiting for transfers between devices: 13.8 us -> 21.2 us  [trade(): return lax.ppermute(value, ('slab', 'freq'), pairs)]
    ppermute x8, starting transfers between devices: 17.4 us -> 22.4 us  [trade(): return lax.ppermute(value, ('slab', 'freq'), pairs)]
    ppermute x3, waiting for transfers between devices: 6.33 us -> 4.31 us  [swap(): return lax.ppermute(part, 'freq', [(g, g ^ d) for g in range(GROUPS)])]
    pallas_call x2, Pallas kernels: 1.2 us -> 2.22 us  [choose(): pl.pallas_call(choose_kernel, in_specs=[pl.BlockSpec(memory_space=pltpu.S...]
  transfers between devices with their start and end apart: 13 -> 13, of which waited for: 8 -> 9; matrix products, arithmetic and copies ran while one was open for 0% -> 0% of each run, Pallas kernels for 18% -> 18%
where the time goes in v10:
time: 78.9 us; the launch traced here: 78 us
  starting transfers between devices  28.1 us (36%)
  waiting for transfers between devices  25.9 us (33%)
  Pallas kernels  23.7 us (30%)
    ppermute x8, starting transfers between devices, trade(): return lax.ppermute(value, ('slab', 'freq'), pairs)  22.4 us
    ppermute x8, waiting for transfers between devices, trade(): return lax.ppermute(value, ('slab', 'freq'), pairs)  21.2 us
    pallas_call x4, Pallas kernels, summed(): pl.pallas_call(functools.partial(sum_kernel, plan, bands, first, last), i...  18.7 us
    ppermute x3, waiting for transfers between devices, swap(): return lax.ppermute(part, 'freq', [(g, g ^ d) for g in range(GROUPS)])  4.31 us
    ppermute x3, starting transfers between devices, swap(): return lax.ppermute(part, 'freq', [(g, g ^ d) for g in range(GROUPS)])  3.18 us
    pallas_call x1, Pallas kernels, regrouped(): pl.pallas_call(regroup_kernel, in_specs=[pl.BlockSpec(memory_space=pltpu....  2.8 us
    ppermute x2, starting transfers between devices, body(): traded[d].append(lax.ppermute(value, 'slab', over_middle))  2.56 us
    pallas_call x2, Pallas kernels, choose(): pl.pallas_call(choose_kernel, in_specs=[pl.BlockSpec(memory_space=pltpu.S...  2.22 us
  transfers between devices with their start and end apart: 13, of which 9 were waited for; matrix products, arithmetic and copies ran while one was open for 0% of the time, Pallas kernels for 18%

profile of v10, /device:TPU:8, one launch (start us, length us, event | category | flops | bytes accessed | tf_op | source)
XLA Modules:
  0.0 78.0 jit_solution(8458884898133250528)
XLA Ops:
  0.0 2.8 %regroup.1 = (bf16[2,2,32,16,128]{4,3,2,1,0:T(8,128)(2,1)S(1)}, bf16[2,2,32,16,128]{4,3,2,1,0:T(8,128)(2,1)}, bf16[2,2,32,16,128]{4,3,2,1,0:T(8,128)(2,1)}, bf16[2,2,32,16,128]{4,3,2,1,0:T(8,128)(2,1)}) custom-call(s32[1]{0:T(128)} %bitcast.2.group_ref, bf16[2,2,32,16,256]{4,3,2,1,0:T(8,128)(2,1)} %source_ref.1, bf16[2,2,32,16,256]{4,3,2,1,0:T(8,128)(2,1)} %receiver_ref.1), custom_call_target="tpu_custom_call" | custom-call | bytes 4194304 | tf_op jit(solution)/shard_map/regroup/pallas_call | solution.py:65
  2.8 0.1 collective-permute-start.3
  2.9 2.4 %collective-permute-start = (bf16[2,2,32,16,128]{4,3,2,1,0:T(8,128)(2,1)}, bf16[2,2,32,16,128]{4,3,2,1,0:T(8,128)(2,1)S(1)}, u32[]{:S(2)}, u32[]{:S(2)}) collective-permute-start(bf16[2,2,32,16,128]{4,3,2,1,0:T(8,128)(2,1)} %get-tuple-element.24.crossing_ref), channel_id=1, source_target_pairs={{0,2},{1,3},{2,0},{3,1},{4,6},{5,7},{6,4},{7,5},{8,10},{9,11},{10,... | collective-permute-start | bytes 1572872 | tf_op jit(solution)/shard_map/ppermute | solution.py:279
  5.3 8.1 %collective-permute-start.1 = (bf16[2,2,32,16,128]{4,3,2,1,0:T(8,128)(2,1)S(1)}, bf16[2,2,32,16,128]{4,3,2,1,0:T(8,128)(2,1)S(1)}, u32[]{:S(2)}, u32[]{:S(2)}) collective-permute-start(bf16[2,2,32,16,128]{4,3,2,1,0:T(8,128)(2,1)S(1)} %get-tuple-element.25.refs_0_), channel_id=1, source_target_pairs={{0,124},{1,125},{2,126},{3,127},{4,8},{5,9},{6,10},{7,11},{8,4},{9... | collective-permute-start | bytes 1572872 | tf_op jit(solution)/shard_map/ppermute | solution.py:287
  13.3 0.0 collective-permute-start.8
  13.3 0.7 collective-permute-start.2
  14.0 0.0 collective-permute-done.3.refs_0_
  14.1 1.1 %collective-permute-start.5 = (bf16[2,2,32,16,128]{4,3,2,1,0:T(8,128)(2,1)S(1)}, bf16[2,2,32,16,128]{4,3,2,1,0:T(8,128)(2,1)S(1)}, u32[]{:S(2)}, u32[]{:S(2)}) collective-permute-start(bf16[2,2,32,16,128]{4,3,2,1,0:T(8,128)(2,1)S(1)} %collective-permute-done.3.refs_0_), channel_id=1, source_target_pairs={{0,124},{1,125},{2,126},{3,127},{4,8},{5,9},{6,10},{7,11},{8,4},{9... | collective-permute-start | bytes 1572872 | tf_op jit(solution)/shard_map/ppermute | solution.py:287
  15.1 4.3 %collective-permute-done.usual_ref.refs_0_ = bf16[2,2,32,16,128]{4,3,2,1,0:T(8,128)(2,1)S(1)} collective-permute-done((bf16[2,2,32,16,128]{4,3,2,1,0:T(8,128)(2,1)}, bf16[2,2,32,16,128]{4,3,2,1,0:T(8,128)(2,1)S(1)}, u32[]{:S(2)}, u32[]{:S(2)}) %collective-permute-start) | collective-permute-done | bytes 524320 | tf_op jit(solution)/shard_map/ppermute | solution.py:279
  19.4 1.4 %collective-permute-start.4 = (bf16[2,2,32,16,128]{4,3,2,1,0:T(8,128)(2,1)S(1)}, bf16[2,2,32,16,128]{4,3,2,1,0:T(8,128)(2,1)S(1)}, u32[]{:S(2)}, u32[]{:S(2)}) collective-permute-start(bf16[2,2,32,16,128]{4,3,2,1,0:T(8,128)(2,1)S(1)} %collective-permute-done.3.refs_0_), channel_id=1, source_target_pairs={{0,4},{1,5},{2,6},{3,7},{4,0},{5,1},{6,2},{7,3},{8,12},{9,13},{10,... | collective-permute-start | bytes 1572872 | tf_op jit(solution)/shard_map/ppermute | solution.py:287
  20.8 0.1 pad_add_fusion.flags_ref
  20.9 1.1 %choose.2 = bf16[2,2,32,16,128]{4,3,2,1,0:T(8,128)(2,1)S(1)} custom-call(s32[2]{0:T(128)S(1)} %pad_add_fusion.flags_ref, bf16[2,2,32,16,128]{4,3,2,1,0:T(8,128)(2,1)S(1)} %collective-permute-done.usual_ref.refs_0_, bf16[2,2,32,16,128]{4,3,2,1,0:T(8,128)(2,1)} %get-tuple-element.24.crossing_ref), custom_call_target="tpu_custom_call" | custom-call | bytes 1048576 | tf_op jit(solution)/shard_map/choose/pallas_call | solution.py:101
  22.0 4.0 %collective-permute-done.1.refs_2_ = bf16[2,2,32,16,128]{4,3,2,1,0:T(8,128)(2,1)S(1)} collective-permute-done((bf16[2,2,32,16,128]{4,3,2,1,0:T(8,128)(2,1)S(1)}, bf16[2,2,32,16,128]{4,3,2,1,0:T(8,128)(2,1)S(1)}, u32[]{:S(2)}, u32[]{:S(2)}) %collective-permute-start.1) | collective-permute-done | bytes 524320 | tf_op jit(solution)/shard_map/ppermute | solution.py:287
  26.0 6.4 %collective-permute-start.10 = (bf16[2,2,32,16,128]{4,3,2,1,0:T(8,128)(2,1)S(1)}, bf16[2,2,32,16,128]{4,3,2,1,0:T(8,128)(2,1)S(1)}, u32[]{:S(2)}, u32[]{:S(2)}) collective-permute-start(bf16[2,2,32,16,128]{4,3,2,1,0:T(8,128)(2,1)S(1)} %choose.2), channel_id=1, source_target_pairs={{0,0},{1,1},{2,2},{3,3},{4,8},{5,9},{6,10},{7,11},{8,4},{9,5},{10,... | collective-permute-start | bytes 1572872 | tf_op jit(solution)/shard_map/ppermute | solution.py:287
  32.4 0.0 collective-permute-done.8.refs_1_
  32.4 0.1 collective-permute-start.9
  32.5 0.0 collective-permute-done.2.usual_ref.refs_0_
  32.6 1.1 %choose.3 = bf16[2,2,32,16,128]{4,3,2,1,0:T(8,128)(2,1)S(1)} custom-call(s32[2]{0:T(128)S(1)} %pad_add_fusion.flags_ref, bf16[2,2,32,16,128]{4,3,2,1,0:T(8,128)(2,1)S(1)} %collective-permute-done.2.usual_ref.refs_0_, bf16[2,2,32,16,128]{4,3,2,1,0:T(8,128)(2,1)} %get-tuple-element.27.crossing_ref), custom_call_target="tpu_custom_call" | custom-call | bytes 1048576 | tf_op jit(solution)/shard_map/choose/pallas_call | solution.py:101
  33.7 3.2 %collective-permute-done.5.refs_2_ = bf16[2,2,32,16,128]{4,3,2,1,0:T(8,128)(2,1)S(1)} collective-permute-done((bf16[2,2,32,16,128]{4,3,2,1,0:T(8,128)(2,1)S(1)}, bf16[2,2,32,16,128]{4,3,2,1,0:T(8,128)(2,1)S(1)}, u32[]{:S(2)}, u32[]{:S(2)}) %collective-permute-start.5) | collective-permute-done | bytes 524320 | tf_op jit(solution)/shard_map/ppermute | solution.py:287
  36.8 2.5 %collective-permute-done.4.refs_1_ = bf16[2,2,32,16,128]{4,3,2,1,0:T(8,128)(2,1)S(1)} collective-permute-done((bf16[2,2,32,16,128]{4,3,2,1,0:T(8,128)(2,1)S(1)}, bf16[2,2,32,16,128]{4,3,2,1,0:T(8,128)(2,1)S(1)}, u32[]{:S(2)}, u32[]{:S(2)}) %collective-permute-start.4) | collective-permute-done | bytes 524320 | tf_op jit(solution)/shard_map/ppermute | solution.py:287
  39.4 1.3 %collective-permute-start.12 = (bf16[2,2,32,16,128]{4,3,2,1,0:T(8,128)(2,1)S(1)}, bf16[2,2,32,16,128]{4,3,2,1,0:T(8,128)(2,1)S(1)}, u32[]{:S(2)}, u32[]{:S(2)}) collective-permute-start(bf16[2,2,32,16,128]{4,3,2,1,0:T(8,128)(2,1)S(1)} %collective-permute-done.1.refs_2_), channel_id=1, source_target_pairs={{0,128},{252,124},{1,129},{253,125},{2,130},{254,126},{3,131},{255... | collective-permute-start | bytes 1572872 | tf_op jit(solution)/shard_map/ppermute | solution.py:313
  40.7 6.6 %collective-permute-done.10.refs_2_ = bf16[2,2,32,16,128]{4,3,2,1,0:T(8,128)(2,1)S(1)} collective-permute-done((bf16[2,2,32,16,128]{4,3,2,1,0:T(8,128)(2,1)S(1)}, bf16[2,2,32,16,128]{4,3,2,1,0:T(8,128)(2,1)S(1)}, u32[]{:S(2)}, u32[]{:S(2)}) %collective-permute-start.10) | collective-permute-done | bytes 524320 | tf_op jit(solution)/shard_map/ppermute | solution.py:287
  47.3 2.2 %collective-permute-done.9.refs_1_ = bf16[2,2,32,16,128]{4,3,2,1,0:T(8,128)(2,1)S(1)} collective-permute-done((bf16[2,2,32,16,128]{4,3,2,1,0:T(8,128)(2,1)S(1)}, bf16[2,2,32,16,128]{4,3,2,1,0:T(8,128)(2,1)S(1)}, u32[]{:S(2)}, u32[]{:S(2)}) %collective-permute-start.9) | collective-permute-done | bytes 524320 | tf_op jit(solution)/shard_map/ppermute | solution.py:287
  49.5 1.3 %collective-permute-start.11 = (bf16[2,2,32,16,128]{4,3,2,1,0:T(8,128)(2,1)S(1)}, bf16[2,2,32,16,128]{4,3,2,1,0:T(8,128)(2,1)S(1)}, u32[]{:S(2)}, u32[]{:S(2)}) collective-permute-start(bf16[2,2,32,16,128]{4,3,2,1,0:T(8,128)(2,1)S(1)} %collective-permute-done.5.refs_2_), channel_id=1, source_target_pairs={{0,128},{252,124},{1,129},{253,125},{2,130},{254,126},{3,131},{255... | collective-permute-start | bytes 1572872 | tf_op jit(solution)/shard_map/ppermute | solution.py:313
  50.8 5.3 %collective-permute-start.7 = (bf16[2,2,32,16,128]{4,3,2,1,0:T(8,128)(2,1)S(1)}, bf16[2,2,32,16,128]{4,3,2,1,0:T(8,128)(2,1)S(1)}, u32[]{:S(2)}, u32[]{:S(2)}) collective-permute-start(bf16[2,2,32,16,128]{4,3,2,1,0:T(8,128)(2,1)S(1)} %choose.3), channel_id=1, source_target_pairs={{0,0},{1,1},{2,2},{3,3},{4,8},{5,9},{6,10},{7,11},{8,4},{9,5},{10,... | collective-permute-start | bytes 1572872 | tf_op jit(solution)/shard_map/ppermute | solution.py:287
  56.1 0.1 collective-permute-start.6
  56.2 3.5 %partial.3.refs_4_ = f32[65,32,8,128]{3,2,1,0:T(8,128)S(1)} custom-call(s32[2]{0:T(128)S(1)} %pad_add_fusion.flags_ref, bf16[2,2,32,16,128]{4,3,2,1,0:T(8,128)(2,1)S(1)} %collective-permute-done.usual_ref.refs_0_, bf16[2,2,32,16,128]{4,3,2,1,0:T(8,128)(2,1)S(1)} %collective-permute-done.9.refs_1_, ...), custom_call_target="tpu_custom_call" | custom-call | flops 16900000 | bytes 8450000 | tf_op jit(solution)/shard_map/partial/pallas_call | solution.py:251
  59.7 0.0 collective-permute-done.12.refs_3_
  59.7 4.0 %partial.4.refs_4_ = f32[65,32,8,128]{3,2,1,0:T(8,128)S(1)} custom-call(s32[2]{0:T(128)S(1)} %pad_add_fusion.flags_ref, bf16[2,2,32,16,128]{4,3,2,1,0:T(8,128)(2,1)S(1)} %get-tuple-element.25.refs_0_, bf16[2,2,32,16,128]{4,3,2,1,0:T(8,128)(2,1)S(1)} %collective-permute-done.8.refs_1_, ...), custom_call_target="tpu_custom_call", output_to_operand_aliasing={{}: (5, {})} | custom-call | flops 16900000 | bytes 8450000 | tf_op jit(solution)/shard_map/partial/pallas_call | solution.py:251
  63.7 0.5 collective-permute-done.11.refs_3_
  64.2 4.0 %partial.5.refs_3_ = f32[65,32,8,128]{3,2,1,0:T(8,128)S(1)} custom-call(s32[2]{0:T(128)S(1)} %pad_add_fusion.flags_ref, bf16[2,2,32,16,128]{4,3,2,1,0:T(8,128)(2,1)S(1)} %collective-permute-done.3.refs_0_, bf16[2,2,32,16,128]{4,3,2,1,0:T(8,128)(2,1)S(1)} %collective-permute-done.4.refs_1_, ...), custom_call_target="tpu_custom_call", output_to_operand_aliasing={{}: (5, {})} | custom-call | flops 16900000 | bytes 8450000 | tf_op jit(solution)/shard_map/partial/pallas_call | solution.py:251
  68.2 2.1 %collective-permute-done.7.refs_2_ = bf16[2,2,32,16,128]{4,3,2,1,0:T(8,128)(2,1)S(1)} collective-permute-done((bf16[2,2,32,16,128]{4,3,2,1,0:T(8,128)(2,1)S(1)}, bf16[2,2,32,16,128]{4,3,2,1,0:T(8,128)(2,1)S(1)}, u32[]{:S(2)}, u32[]{:S(2)}) %collective-permute-start.7) | collective-permute-done | bytes 524320 | tf_op jit(solution)/shard_map/ppermute | solution.py:287
  70.3 0.5 collective-permute-done.6.refs_1_
  70.8 7.2 %image.1 = f32[4,65,32,256]{3,2,1,0:T(8,128)} custom-call(s32[2]{0:T(128)S(1)} %pad_add_fusion.flags_ref, bf16[2,2,32,16,128]{4,3,2,1,0:T(8,128)(2,1)S(1)} %collective-permute-done.2.usual_ref.refs_0_, bf16[2,2,32,16,128]{4,3,2,1,0:T(8,128)(2,1)S(1)} %collective-permute-done.6.refs_1_, bf16[2,2,32,16,128]{4,3,2,1,0:T(8,128)(2,1)S(1)} %collective-permute-done.7.refs_2_, ...), custom_call_target="tpu_custom_call" | custom-call | flops 16900000 | bytes 8450000 | tf_op jit(solution)/shard_map/image/pallas_call | solution.py:251
Async XLA Ops:
  2.8 11.2 %collective-permute-start.3 = (bf16[2,2,32,16,128]{4,3,2,1,0:T(8,128)(2,1)}, bf16[2,2,32,16,128]{4,3,2,1,0:T(8,128)(2,1)S(1)}, u32[]{:S(2)}, u32[]{:S(2)}) collective-permute-start(bf16[2,2,32,16,128]{4,3,2,1,0:T(8,128)(2,1)} %get-tuple-element.28), channel_id=1, source_target_pairs={{0,1},{1,0},{2,3},{3,2},{4,5},{5,4},{6,7},{7,6},{8,9},{9,8},{10,11... | collective-permute-start | bytes 1572872 | tf_op jit(solution)/shard_map/ppermute | solution.py:279
  2.9 16.5 %collective-permute-start = (bf16[2,2,32,16,128]{4,3,2,1,0:T(8,128)(2,1)}, bf16[2,2,32,16,128]{4,3,2,1,0:T(8,128)(2,1)S(1)}, u32[]{:S(2)}, u32[]{:S(2)}) collective-permute-start(bf16[2,2,32,16,128]{4,3,2,1,0:T(8,128)(2,1)} %get-tuple-element.24.crossing_ref), channel_id=1, source_target_pairs={{0,2},{1,3},{2,0},{3,1},{4,6},{5,7},{6,4},{7,5},{8,10},{9,11},{10,... | collective-permute-start | bytes 1572872 | tf_op jit(solution)/shard_map/ppermute | solution.py:279
  5.3 20.8 %collective-permute-start.1 = (bf16[2,2,32,16,128]{4,3,2,1,0:T(8,128)(2,1)S(1)}, bf16[2,2,32,16,128]{4,3,2,1,0:T(8,128)(2,1)S(1)}, u32[]{:S(2)}, u32[]{:S(2)}) collective-permute-start(bf16[2,2,32,16,128]{4,3,2,1,0:T(8,128)(2,1)S(1)} %get-tuple-element.25.refs_0_), channel_id=1, source_target_pairs={{0,124},{1,125},{2,126},{3,127},{4,8},{5,9},{6,10},{7,11},{8,4},{9... | collective-permute-start | bytes 1572872 | tf_op jit(solution)/shard_map/ppermute | solution.py:287
  13.3 19.1 %collective-permute-start.8 = (bf16[2,2,32,16,128]{4,3,2,1,0:T(8,128)(2,1)S(1)}, bf16[2,2,32,16,128]{4,3,2,1,0:T(8,128)(2,1)S(1)}, u32[]{:S(2)}, u32[]{:S(2)}) collective-permute-start(bf16[2,2,32,16,128]{4,3,2,1,0:T(8,128)(2,1)S(1)} %get-tuple-element.25.refs_0_), channel_id=1, source_target_pairs={{0,4},{1,5},{2,6},{3,7},{4,0},{5,1},{6,2},{7,3},{8,12},{9,13},{10,... | collective-permute-start | bytes 1572872 | tf_op jit(solution)/shard_map/ppermute | solution.py:287
  13.3 19.2 %collective-permute-start.2 = (bf16[2,2,32,16,128]{4,3,2,1,0:T(8,128)(2,1)}, bf16[2,2,32,16,128]{4,3,2,1,0:T(8,128)(2,1)S(1)}, u32[]{:S(2)}, u32[]{:S(2)}) collective-permute-start(bf16[2,2,32,16,128]{4,3,2,1,0:T(8,128)(2,1)} %get-tuple-element.27.crossing_ref), channel_id=1, source_target_pairs={{0,3},{1,2},{2,1},{3,0},{4,7},{5,6},{6,5},{7,4},{8,11},{9,10},{10,... | collective-permute-start | bytes 1572872 | tf_op jit(solution)/shard_map/ppermute | solution.py:279
  14.1 22.8 %collective-permute-start.5 = (bf16[2,2,32,16,128]{4,3,2,1,0:T(8,128)(2,1)S(1)}, bf16[2,2,32,16,128]{4,3,2,1,0:T(8,128)(2,1)S(1)}, u32[]{:S(2)}, u32[]{:S(2)}) collective-permute-start(bf16[2,2,32,16,128]{4,3,2,1,0:T(8,128)(2,1)S(1)} %collective-permute-done.3.refs_0_), channel_id=1, source_target_pairs={{0,124},{1,125},{2,126},{3,127},{4,8},{5,9},{6,10},{7,11},{8,4},{9... | collective-permute-start | bytes 1572872 | tf_op jit(solution)/shard_map/ppermute | solution.py:287
  19.4 19.9 %collective-permute-start.4 = (bf16[2,2,32,16,128]{4,3,2,1,0:T(8,128)(2,1)S(1)}, bf16[2,2,32,16,128]{4,3,2,1,0:T(8,128)(2,1)S(1)}, u32[]{:S(2)}, u32[]{:S(2)}) collective-permute-start(bf16[2,2,32,16,128]{4,3,2,1,0:T(8,128)(2,1)S(1)} %collective-permute-done.3.refs_0_), channel_id=1, source_target_pairs={{0,4},{1,5},{2,6},{3,7},{4,0},{5,1},{6,2},{7,3},{8,12},{9,13},{10,... | collective-permute-start | bytes 1572872 | tf_op jit(solution)/shard_map/ppermute | solution.py:287
  26.0 21.3 %collective-permute-start.10 = (bf16[2,2,32,16,128]{4,3,2,1,0:T(8,128)(2,1)S(1)}, bf16[2,2,32,16,128]{4,3,2,1,0:T(8,128)(2,1)S(1)}, u32[]{:S(2)}, u32[]{:S(2)}) collective-permute-start(bf16[2,2,32,16,128]{4,3,2,1,0:T(8,128)(2,1)S(1)} %choose.2), channel_id=1, source_target_pairs={{0,0},{1,1},{2,2},{3,3},{4,8},{5,9},{6,10},{7,11},{8,4},{9,5},{10,... | collective-permute-start | bytes 1572872 | tf_op jit(solution)/shard_map/ppermute | solution.py:287
  32.4 17.0 %collective-permute-start.9 = (bf16[2,2,32,16,128]{4,3,2,1,0:T(8,128)(2,1)S(1)}, bf16[2,2,32,16,128]{4,3,2,1,0:T(8,128)(2,1)S(1)}, u32[]{:S(2)}, u32[]{:S(2)}) collective-permute-start(bf16[2,2,32,16,128]{4,3,2,1,0:T(8,128)(2,1)S(1)} %collective-permute-done.usual_ref.refs_0_), channel_id=1, source_target_pairs={{0,4},{1,5},{2,6},{3,7},{4,0},{5,1},{6,2},{7,3},{8,12},{9,13},{10,... | collective-permute-start | bytes 1572872 | tf_op jit(solution)/shard_map/ppermute | solution.py:287
  39.4 20.4 %collective-permute-start.12 = (bf16[2,2,32,16,128]{4,3,2,1,0:T(8,128)(2,1)S(1)}, bf16[2,2,32,16,128]{4,3,2,1,0:T(8,128)(2,1)S(1)}, u32[]{:S(2)}, u32[]{:S(2)}) collective-permute-start(bf16[2,2,32,16,128]{4,3,2,1,0:T(8,128)(2,1)S(1)} %collective-permute-done.1.refs_2_), channel_id=1, source_target_pairs={{0,128},{252,124},{1,129},{253,125},{2,130},{254,126},{3,131},{255... | collective-permute-start | bytes 1572872 | tf_op jit(solution)/shard_map/ppermute | solution.py:313
  49.5 14.7 %collective-permute-start.11 = (bf16[2,2,32,16,128]{4,3,2,1,0:T(8,128)(2,1)S(1)}, bf16[2,2,32,16,128]{4,3,2,1,0:T(8,128)(2,1)S(1)}, u32[]{:S(2)}, u32[]{:S(2)}) collective-permute-start(bf16[2,2,32,16,128]{4,3,2,1,0:T(8,128)(2,1)S(1)} %collective-permute-done.5.refs_2_), channel_id=1, source_target_pairs={{0,128},{252,124},{1,129},{253,125},{2,130},{254,126},{3,131},{255... | collective-permute-start | bytes 1572872 | tf_op jit(solution)/shard_map/ppermute | solution.py:313
  50.8 19.5 %collective-permute-start.7 = (bf16[2,2,32,16,128]{4,3,2,1,0:T(8,128)(2,1)S(1)}, bf16[2,2,32,16,128]{4,3,2,1,0:T(8,128)(2,1)S(1)}, u32[]{:S(2)}, u32[]{:S(2)}) collective-permute-start(bf16[2,2,32,16,128]{4,3,2,1,0:T(8,128)(2,1)S(1)} %choose.3), channel_id=1, source_target_pairs={{0,0},{1,1},{2,2},{3,3},{4,8},{5,9},{6,10},{7,11},{8,4},{9,5},{10,... | collective-permute-start | bytes 1572872 | tf_op jit(solution)/shard_map/ppermute | solution.py:287
  56.1 14.7 %collective-permute-start.6 = (bf16[2,2,32,16,128]{4,3,2,1,0:T(8,128)(2,1)S(1)}, bf16[2,2,32,16,128]{4,3,2,1,0:T(8,128)(2,1)S(1)}, u32[]{:S(2)}, u32[]{:S(2)}) collective-permute-start(bf16[2,2,32,16,128]{4,3,2,1,0:T(8,128)(2,1)S(1)} %collective-permute-done.2.usual_ref.refs_0_), channel_id=1, source_target_pairs={{0,4},{1,5},{2,6},{3,7},{4,0},{5,1},{6,2},{7,3},{8,12},{9,13},{10,... | collective-permute-start | bytes 1572872 | tf_op jit(solution)/shard_map/ppermute | solution.py:287

commit v11 on v7

--- a/solution.py
+++ b/solution.py
@@ -115,14 +115,22 @@
     )(flags, *arrays)
 
 
-def sum_kernel(plan, bands, first, last, flags_ref, *refs):
+def sum_kernel(plan, bands, first, last, crosses, flags_ref, *refs):
+    if crosses is None:
+        sum_body(plan, bands, first, last, flags_ref, *refs)
+    else:
+        pl.when((flags_ref[1] == 1) == crosses)(functools.partial(sum_body, plan, bands, first, last, flags_ref, *refs))
+
+
+def sum_body(plan, bands, first, last, flags_ref, *refs):
     count = 1 + max(entry[0] for entry in plan if entry[0] is not None)
     blocks, refs = refs[:count], refs[count:]
     befores = ()
     if not first:
         befores, refs = refs[: len(bands)], refs[len(bands) :]
-    if last == 2:
+    if last in (2, 3):
         refs = refs[1:]
+    last = 0 if last == 3 else last
     outs = refs[: 1 if last else len(bands)]
     fields = refs[len(outs)]
     if last:
@@ -235,7 +243,7 @@
 FAR_BAND = (0, 2 * NEAR // TH, NEAR // TH, 2 * NEAR + 1, 0)
 
 
-def summed(flags, blocks, plan, bands, befores, cells, groups, last, image=None):
+def summed(flags, blocks, plan, bands, befores, cells, groups, last, image=None, crosses=None):
     first = befores is None
     heights = [TH * band[1] + band[4] for band in bands]
     scratch = [pltpu.VMEM((2, 3 * cells, 2 * groups, ROWS, LANES), jnp.float32)]
@@ -259,8 +267,12 @@
     else:
         out_shape = [pltpu.VMEM((height, cells, 8, LANES), jnp.float32) for height in heights]
         out_specs = [vmem] * len(heights)
+        if image is not None:
+            operands.append(image)
+            in_specs.append(vmem)
+            aliases = {len(operands): 0}
     return pl.pallas_call(
-        functools.partial(sum_kernel, plan, bands, first, last),
+        functools.partial(sum_kernel, plan, bands, first, last or (0 if image is None else 3), crosses),
         in_specs=in_specs,
         out_specs=out_specs,
         out_shape=out_shape,
@@ -331,7 +343,6 @@
     whole_a, first_near_b, first_far_b, far_a, far_b = lax.optimization_barrier(
         (whole_a, first_near_b, first_far_b, far_a, far_b)
     )
-    far_a, far_b = trade(far_a, side_a), trade(far_b, side_b, turned)
 
     near_at_a, near_at_b = (2 * cells, rest), (rest, 2 * cells)
     far_at_a, far_at_b = (2 * cells + NEAR, 0), (0, 2 * cells + NEAR)
@@ -345,7 +356,13 @@
         far_plan += [(None, g, 0, NEAR, far_at_b, g, (2,))]
     blocks = (own, whole_a, first_near_b, near_over)
     befores = summed(flags, blocks, plan, (NEAR_BAND,), None, cells, 2, 0)
-    far_sums = (flags, plan + far_plan, blocks)
+    far_b, *befores = lax.optimization_barrier((far_b, *befores))
+    far_a, far_b = trade(far_a, side_a), trade(far_b, side_b, turned)
+    usual = [entry for entry in plan + far_plan if entry[-1] != (1,) and entry[0] != 3]
+    usual = [(3 if entry[0] == 4 else entry[0], *entry[1:]) for entry in usual]
+    far_blocks, far_plan = blocks + (first_far_b, far_over), plan + far_plan
+    far_befores = summed(flags, blocks[:3] + (first_far_b,), usual, (FAR_BAND,), None, cells, 2, 0, None, False)
+    crossing = (far_blocks, far_plan)
     plan, far_plan = [], []
     for g in range(2):
         plan += [(0, g, 0, cells, cells, g, None), (1, g, 0, NEAR, near_at_a, g, None)]
@@ -354,7 +371,8 @@
         far_plan += [(4, g, 0, NEAR, far_at_b, g, (0, 1)), (None, g, 0, NEAR, far_at_b, g, (2,))]
     image = summed(flags, (far_own, near_a, near_b), plan, (NEAR_BAND,), befores, cells, 2, 1)
     image, far_over = lax.optimization_barrier((image, far_over))
-    befores = summed(flags, far_sums[2] + (first_far_b, far_over), far_sums[1], (FAR_BAND,), None, cells, 2, 0)
+    far_blocks = crossing[0][:-1] + (far_over,)
+    befores = summed(flags, far_blocks, crossing[1], (FAR_BAND,), None, cells, 2, 0, far_befores[0], True)
     blocks = (far_own, near_a, near_b, far_a, far_b)
     return summed(flags, blocks, plan + far_plan, (FAR_BAND,), befores, cells, 2, 2, image)
 

time: 74.1 us -> 75 us (1.012)
    pallas_call x4 -> x5, Pallas kernels: 19.8 us -> 20.3 us  [summed(): pl.pallas_call(functools.partial(sum_kernel, plan, bands, first, last or...]
  transfers between devices with their start and end apart: 12 -> 12, of which waited for: 4 -> 5; matrix products, arithmetic and copies ran while one was open for 0% -> 0% of each run, Pallas kernels for 20% -> 20%
where the time goes in v11:
time: 75 us; the launch traced here: 74.8 us
  starting transfers between devices  34.2 us (46%)
  Pallas kernels  23.7 us (32%)
  waiting for transfers between devices  16.7 us (22%)
    ppermute x7, starting transfers between devices, trade(): return lax.ppermute(value, ('slab', 'freq'), pairs)  28.7 us
    pallas_call x5, Pallas kernels, summed(): pl.pallas_call(functools.partial(sum_kernel, plan, bands, first, last or...  20.3 us
    ppermute x7, waiting for transfers between devices, trade(): return lax.ppermute(value, ('slab', 'freq'), pairs)  13.1 us
    ppermute x3, waiting for transfers between devices, swap(): return lax.ppermute(part, 'freq', [(g, g ^ d) for g in range(GROUPS)])  3.54 us
    ppermute x3, starting transfers between devices, swap(): return lax.ppermute(part, 'freq', [(g, g ^ d) for g in range(GROUPS)])  2.96 us
    ppermute x2, starting transfers between devices, body(): lax.ppermute(value, 'slab', over_middle)  2.57 us
    pallas_call x2, Pallas kernels, pack(): pl.pallas_call(functools.partial(pack_kernel, copies, len(arrays)), in_sp...  1.7 us
    pallas_call x1, Pallas kernels, regrouped(): pl.pallas_call(regroup_kernel, in_specs=[pl.BlockSpec(memory_space=pltpu....  1.66 us
  transfers between devices with their start and end apart: 12, of which 5 were waited for; matrix products, arithmetic and copies ran while one was open for 0% of the time, Pallas kernels for 20%

profile of v11, /device:TPU:8, one launch (start us, length us, event | category | flops | bytes accessed | tf_op | source)
XLA Modules:
  0.0 74.8 jit_solution(10354900387257266914)
XLA Ops:
  0.0 1.7 %regroup.1 = (bf16[2,2,32,16,128]{4,3,2,1,0:T(8,128)(2,1)S(1)}, bf16[2,2,32,16,128]{4,3,2,1,0:T(8,128)(2,1)S(1)}, bf16[2,2,32,16,128]{4,3,2,1,0:T(8,128)(2,1)S(1)}, bf16[2,2,32,16,128]{4,3,2,1,0:T(8,128)(2,1)S(1)}) custom-call(s32[1]{0:T(128)} %bitcast.2.group_ref, bf16[2,2,32,16,256]{4,3,2,1,0:T(8,128)(2,1)} %source_ref.1, ...), custom_call_target="tpu_custom_call" | custom-call | bytes 4194304 | tf_op jit(solution)/shard_map/regroup/pallas_call | solution.py:65
  1.7 0.1 collective-permute-start
  1.8 0.5 collective-permute-start.1
  2.3 0.1 pad_add_fusion.refs_0_.flags_ref
  2.3 1.3 %collective-permute-done.refs_2_ = bf16[2,2,32,16,128]{4,3,2,1,0:T(8,128)(2,1)S(1)} collective-permute-done((bf16[2,2,32,16,128]{4,3,2,1,0:T(8,128)(2,1)S(1)}, bf16[2,2,32,16,128]{4,3,2,1,0:T(8,128)(2,1)S(1)}, u32[]{:S(2)}, u32[]{:S(2)}) %collective-permute-start) | collective-permute-done | bytes 524320 | tf_op jit(solution)/shard_map/ppermute | solution.py:301
  3.7 0.7 %collective-permute-done.1.refs_4_ = bf16[2,2,32,16,128]{4,3,2,1,0:T(8,128)(2,1)S(1)} collective-permute-done((bf16[2,2,32,16,128]{4,3,2,1,0:T(8,128)(2,1)S(1)}, bf16[2,2,32,16,128]{4,3,2,1,0:T(8,128)(2,1)S(1)}, u32[]{:S(2)}, u32[]{:S(2)}) %collective-permute-start.1) | collective-permute-done | bytes 524320 | tf_op jit(solution)/shard_map/ppermute | solution.py:301
  4.4 0.9 %pack.2 = (bf16[2,2,2,32,16,128]{5,4,3,2,1,0:T(8,128)(2,1)S(1)}, bf16[2,2,2,32,16,128]{5,4,3,2,1,0:T(8,128)(2,1)S(1)}, bf16[2,2,2,16,16,128]{5,4,3,2,1,0:T(8,128)(2,1)S(1)}, bf16[2,2,2,16,16,128]{5,4,3,2,1,0:T(8,128)(2,1)S(1)}) custom-call(s32[2]{0:T(128)S(1)} %pad_add_fusion.refs_0_.flags_ref, bf16[2,2,32,16,128]{4,3,2,1,0:T(8,128)(2,1)S(1)} %get-tuple-element.26.refs_1_, ...), custom_call_target="tpu_custom_call" | custom-call | bytes 2097152 | tf_op jit(solution)/shard_map/pack/pallas_call | solution.py:107
  5.3 2.4 %collective-permute-start.2 = (bf16[2,2,2,32,16,128]{5,4,3,2,1,0:T(8,128)(2,1)S(1)}, bf16[2,2,2,32,16,128]{5,4,3,2,1,0:T(8,128)(2,1)S(1)}, u32[]{:S(2)}, u32[]{:S(2)}) collective-permute-start(bf16[2,2,2,32,16,128]{5,4,3,2,1,0:T(8,128)(2,1)S(1)} %get-tuple-element.30.refs_2_), channel_id=1, source_target_pairs={{0,2},{1,3},{2,0},{3,1},{4,6},{5,7},{6,4},{7,5},{8,10},{9,11},{10,... | collective-permute-start | bytes 3145736 | tf_op jit(solution)/shard_map/ppermute | solution.py:301
  7.7 1.5 %collective-permute-start.5 = (bf16[2,2,2,32,16,128]{5,4,3,2,1,0:T(8,128)(2,1)S(1)}, bf16[2,2,2,32,16,128]{5,4,3,2,1,0:T(8,128)(2,1)S(1)}, u32[]{:S(2)}, u32[]{:S(2)}) collective-permute-start(bf16[2,2,2,32,16,128]{5,4,3,2,1,0:T(8,128)(2,1)S(1)} %get-tuple-element.33.refs_0_), channel_id=1, source_target_pairs={{0,4},{1,5},{2,6},{3,7},{4,0},{5,1},{6,2},{7,3},{8,12},{9,13},{10,... | collective-permute-start | bytes 3145736 | tf_op jit(solution)/shard_map/ppermute | solution.py:308
  9.1 7.4 %collective-permute-start.6 = (bf16[2,2,2,16,16,128]{5,4,3,2,1,0:T(8,128)(2,1)S(1)}, bf16[2,2,2,16,16,128]{5,4,3,2,1,0:T(8,128)(2,1)S(1)}, u32[]{:S(2)}, u32[]{:S(2)}) collective-permute-start(bf16[2,2,2,16,16,128]{5,4,3,2,1,0:T(8,128)(2,1)S(1)} %get-tuple-element.34), channel_id=1, source_target_pairs={{0,124},{1,125},{2,126},{3,127},{4,8},{5,9},{6,10},{7,11},{8,4},{9... | collective-permute-start | bytes 1572872 | tf_op jit(solution)/shard_map/ppermute | solution.py:308
  16.5 0.0 collective-permute-start.7
  16.6 12.8 %collective-permute-done.6.refs_2_ = bf16[2,2,2,16,16,128]{5,4,3,2,1,0:T(8,128)(2,1)S(1)} collective-permute-done((bf16[2,2,2,16,16,128]{5,4,3,2,1,0:T(8,128)(2,1)S(1)}, bf16[2,2,2,16,16,128]{5,4,3,2,1,0:T(8,128)(2,1)S(1)}, u32[]{:S(2)}, u32[]{:S(2)}) %collective-permute-start.6) | collective-permute-done | bytes 524320 | tf_op jit(solution)/shard_map/ppermute | solution.py:308
  29.3 1.3 %collective-permute-start.9 = (bf16[2,2,2,16,16,128]{5,4,3,2,1,0:T(8,128)(2,1)S(1)}, bf16[2,2,2,16,16,128]{5,4,3,2,1,0:T(8,128)(2,1)S(1)}, u32[]{:S(2)}, u32[]{:S(2)}) collective-permute-start(bf16[2,2,2,16,16,128]{5,4,3,2,1,0:T(8,128)(2,1)S(1)} %collective-permute-done.6.refs_2_), channel_id=1, source_target_pairs={{0,128},{252,124},{1,129},{253,125},{2,130},{254,126},{3,131},{255... | collective-permute-start | bytes 1572872 | tf_op jit(solution)/shard_map/ppermute | solution.py:332
  30.6 1.5 %collective-permute-done.2.refs_1_.refs_0_ = bf16[2,2,2,32,16,128]{5,4,3,2,1,0:T(8,128)(2,1)S(1)} collective-permute-done((bf16[2,2,2,32,16,128]{5,4,3,2,1,0:T(8,128)(2,1)S(1)}, bf16[2,2,2,32,16,128]{5,4,3,2,1,0:T(8,128)(2,1)S(1)}, u32[]{:S(2)}, u32[]{:S(2)}) %collective-permute-start.2) | collective-permute-done | bytes 1048608 | tf_op jit(solution)/shard_map/ppermute | solution.py:301
  32.1 0.8 %pack.3 = (bf16[2,2,2,16,16,128]{5,4,3,2,1,0:T(8,128)(2,1)S(1)}, bf16[2,2,2,16,16,128]{5,4,3,2,1,0:T(8,128)(2,1)S(1)}, bf16[2,2,2,16,16,128]{5,4,3,2,1,0:T(8,128)(2,1)S(1)}, bf16[2,2,2,16,16,128]{5,4,3,2,1,0:T(8,128)(2,1)S(1)}) custom-call(s32[2]{0:T(128)S(1)} %pad_add_fusion.refs_0_.flags_ref, ...), custom_call_target="tpu_custom_call" | custom-call | bytes 2097152 | tf_op jit(solution)/shard_map/pack/pallas_call | solution.py:107
  32.9 1.6 %collective-permute-start.3 = (bf16[2,2,2,16,16,128]{5,4,3,2,1,0:T(8,128)(2,1)S(1)}, bf16[2,2,2,16,16,128]{5,4,3,2,1,0:T(8,128)(2,1)S(1)}, u32[]{:S(2)}, u32[]{:S(2)}) collective-permute-start(bf16[2,2,2,16,16,128]{5,4,3,2,1,0:T(8,128)(2,1)S(1)} %get-tuple-element.31), channel_id=1, source_target_pairs={{0,4},{1,5},{2,6},{3,7},{4,0},{5,1},{6,2},{7,3},{8,12},{9,13},{10,... | collective-permute-start | bytes 1572872 | tf_op jit(solution)/shard_map/ppermute | solution.py:308
  34.5 10.3 %collective-permute-start.4 = (bf16[2,2,2,16,16,128]{5,4,3,2,1,0:T(8,128)(2,1)S(1)}, bf16[2,2,2,16,16,128]{5,4,3,2,1,0:T(8,128)(2,1)S(1)}, u32[]{:S(2)}, u32[]{:S(2)}) collective-permute-start(bf16[2,2,2,16,16,128]{5,4,3,2,1,0:T(8,128)(2,1)S(1)} %get-tuple-element.32), channel_id=1, source_target_pairs={{0,0},{1,1},{2,2},{3,3},{4,8},{5,9},{6,10},{7,11},{8,4},{9,5},{10,... | collective-permute-start | bytes 1572872 | tf_op jit(solution)/shard_map/ppermute | solution.py:308
  44.8 0.0 collective-permute-done.7.refs_3_.refs_4_
  44.8 1.3 %collective-permute-start.11 = (bf16[2,2,2,16,16,128]{5,4,3,2,1,0:T(8,128)(2,1)S(1)}, bf16[2,2,2,16,16,128]{5,4,3,2,1,0:T(8,128)(2,1)S(1)}, u32[]{:S(2)}, u32[]{:S(2)}) collective-permute-start(bf16[2,2,2,16,16,128]{5,4,3,2,1,0:T(8,128)(2,1)S(1)} %collective-permute-done.7.refs_3_.refs_4_), channel_id=1, source_target_pairs={{0,128},{252,124},{1,129},{253,125},{2,130},{254,126},{3,131},{255... | collective-permute-start | bytes 1572872 | tf_op jit(solution)/shard_map/ppermute | solution.py:332
  46.1 0.0 collective-permute-done.5.refs_1_
  46.1 0.1 collective-permute-start.8
  46.2 0.0 collective-permute-done.9.refs_3_
  46.2 3.8 %partial.3.refs_3_ = f32[33,32,8,128]{3,2,1,0:T(8,128)S(1)} custom-call(s32[2]{0:T(128)S(1)} %pad_add_fusion.refs_0_.flags_ref, bf16[2,2,2,32,16,128]{5,4,3,2,1,0:T(8,128)(2,1)S(1)} %get-tuple-element.33.refs_0_, bf16[2,2,2,32,16,128]{5,4,3,2,1,0:T(8,128)(2,1)S(1)} %collective-permute-done.5.refs_1_, ...), custom_call_target="tpu_custom_call" | custom-call | flops 17160000 | bytes 4290000 | tf_op jit(solution)/shard_map/partial/pallas_call | solution.py:274
  50.1 7.8 %collective-permute-start.10 = (bf16[2,2,2,16,16,128]{5,4,3,2,1,0:T(8,128)(2,1)S(1)}, bf16[2,2,2,16,16,128]{5,4,3,2,1,0:T(8,128)(2,1)S(1)}, u32[]{:S(2)}, u32[]{:S(2)}) collective-permute-start(bf16[2,2,2,16,16,128]{5,4,3,2,1,0:T(8,128)(2,1)S(1)} %get-tuple-element.42), channel_id=1, source_target_pairs={{0,0},{1,1},{2,2},{3,3},{4,8},{5,9},{6,10},{7,11},{8,4},{9,5},{10,... | collective-permute-start | bytes 1572872 | tf_op jit(solution)/shard_map/ppermute | solution.py:308
  57.9 0.6 partial.4.refs_6_
  58.5 0.0 collective-permute-done.3.refs_1_
  58.5 0.0 collective-permute-done.4.refs_2_
  58.5 5.9 %image.2.refs_6_ = f32[4,65,32,256]{3,2,1,0:T(8,128)} custom-call(s32[2]{0:T(128)S(1)} %pad_add_fusion.refs_0_.flags_ref, bf16[2,2,2,32,16,128]{5,4,3,2,1,0:T(8,128)(2,1)S(1)} %collective-permute-done.2.refs_1_.refs_0_, bf16[2,2,2,16,16,128]{5,4,3,2,1,0:T(8,128)(2,1)S(1)} %collective-permute-done.3.refs_1_, ...), custom_call_target="tpu_custom_call" | custom-call | flops 17160000 | bytes 4290000 | tf_op jit(solution)/shard_map/image/pallas_call | solution.py:274
  64.4 0.0 collective-permute-done.11.refs_5_
  64.4 4.0 %partial.5.refs_5_ = f32[32,32,8,128]{3,2,1,0:T(8,128)S(1)} custom-call(s32[2]{0:T(128)S(1)} %pad_add_fusion.refs_0_.flags_ref, bf16[2,2,2,32,16,128]{5,4,3,2,1,0:T(8,128)(2,1)S(1)} %get-tuple-element.33.refs_0_, bf16[2,2,2,32,16,128]{5,4,3,2,1,0:T(8,128)(2,1)S(1)} %collective-permute-done.5.refs_1_, ...), custom_call_target="tpu_custom_call", output_to_operand_aliasing={{}: (7, {})} | custom-call | flops 16640000 | bytes 4160000 | tf_op jit(solution)/shard_map/partial/pallas_call | solution.py:274
  68.4 0.0 collective-permute-done.8.refs_3_
  68.4 0.3 collective-permute-done.10.refs_4_
  68.7 6.1 %image.3 = f32[4,65,32,256]{3,2,1,0:T(8,128)} custom-call(s32[2]{0:T(128)S(1)} %pad_add_fusion.refs_0_.flags_ref, bf16[2,2,2,32,16,128]{5,4,3,2,1,0:T(8,128)(2,1)S(1)} %collective-permute-done.2.refs_1_.refs_0_, bf16[2,2,2,16,16,128]{5,4,3,2,1,0:T(8,128)(2,1)S(1)} %collective-permute-done.3.refs_1_, ...), custom_call_target="tpu_custom_call", output_to_operand_aliasing={{}: (7, {})} | custom-call | flops 16640000 | bytes 4160000 | tf_op jit(solution)/shard_map/image/pallas_call | solution.py:274
Async XLA Ops:
  1.7 2.0 %collective-permute-start = (bf16[2,2,32,16,128]{4,3,2,1,0:T(8,128)(2,1)S(1)}, bf16[2,2,32,16,128]{4,3,2,1,0:T(8,128)(2,1)S(1)}, u32[]{:S(2)}, u32[]{:S(2)}) collective-permute-start(bf16[2,2,32,16,128]{4,3,2,1,0:T(8,128)(2,1)S(1)} %get-tuple-element.27), channel_id=1, source_target_pairs={{0,1},{1,0},{2,3},{3,2},{4,5},{5,4},{6,7},{7,6},{8,9},{9,8},{10,11... | collective-permute-start | bytes 1572872 | tf_op jit(solution)/shard_map/ppermute | solution.py:301
  1.8 2.6 %collective-permute-start.1 = (bf16[2,2,32,16,128]{4,3,2,1,0:T(8,128)(2,1)S(1)}, bf16[2,2,32,16,128]{4,3,2,1,0:T(8,128)(2,1)S(1)}, u32[]{:S(2)}, u32[]{:S(2)}) collective-permute-start(bf16[2,2,32,16,128]{4,3,2,1,0:T(8,128)(2,1)S(1)} %get-tuple-element.29), channel_id=1, source_target_pairs={{0,1},{1,0},{2,3},{3,2},{4,5},{5,4},{6,7},{7,6},{8,9},{9,8},{10,11... | collective-permute-start | bytes 1572872 | tf_op jit(solution)/shard_map/ppermute | solution.py:301
  5.3 26.8 %collective-permute-start.2 = (bf16[2,2,2,32,16,128]{5,4,3,2,1,0:T(8,128)(2,1)S(1)}, bf16[2,2,2,32,16,128]{5,4,3,2,1,0:T(8,128)(2,1)S(1)}, u32[]{:S(2)}, u32[]{:S(2)}) collective-permute-start(bf16[2,2,2,32,16,128]{5,4,3,2,1,0:T(8,128)(2,1)S(1)} %get-tuple-element.30.refs_2_), channel_id=1, source_target_pairs={{0,2},{1,3},{2,0},{3,1},{4,6},{5,7},{6,4},{7,5},{8,10},{9,11},{10,... | collective-permute-start | bytes 3145736 | tf_op jit(solution)/shard_map/ppermute | solution.py:301
  7.7 38.5 %collective-permute-start.5 = (bf16[2,2,2,32,16,128]{5,4,3,2,1,0:T(8,128)(2,1)S(1)}, bf16[2,2,2,32,16,128]{5,4,3,2,1,0:T(8,128)(2,1)S(1)}, u32[]{:S(2)}, u32[]{:S(2)}) collective-permute-start(bf16[2,2,2,32,16,128]{5,4,3,2,1,0:T(8,128)(2,1)S(1)} %get-tuple-element.33.refs_0_), channel_id=1, source_target_pairs={{0,4},{1,5},{2,6},{3,7},{4,0},{5,1},{6,2},{7,3},{8,12},{9,13},{10,... | collective-permute-start | bytes 3145736 | tf_op jit(solution)/shard_map/ppermute | solution.py:308
  9.1 20.2 %collective-permute-start.6 = (bf16[2,2,2,16,16,128]{5,4,3,2,1,0:T(8,128)(2,1)S(1)}, bf16[2,2,2,16,16,128]{5,4,3,2,1,0:T(8,128)(2,1)S(1)}, u32[]{:S(2)}, u32[]{:S(2)}) collective-permute-start(bf16[2,2,2,16,16,128]{5,4,3,2,1,0:T(8,128)(2,1)S(1)} %get-tuple-element.34), channel_id=1, source_target_pairs={{0,124},{1,125},{2,126},{3,127},{4,8},{5,9},{6,10},{7,11},{8,4},{9... | collective-permute-start | bytes 1572872 | tf_op jit(solution)/shard_map/ppermute | solution.py:308
  16.5 28.3 %collective-permute-start.7 = (bf16[2,2,2,16,16,128]{5,4,3,2,1,0:T(8,128)(2,1)S(1)}, bf16[2,2,2,16,16,128]{5,4,3,2,1,0:T(8,128)(2,1)S(1)}, u32[]{:S(2)}, u32[]{:S(2)}) collective-permute-start(bf16[2,2,2,16,16,128]{5,4,3,2,1,0:T(8,128)(2,1)S(1)} %get-tuple-element.35), channel_id=1, source_target_pairs={{0,124},{1,125},{2,126},{3,127},{4,8},{5,9},{6,10},{7,11},{8,4},{9... | collective-permute-start | bytes 1572872 | tf_op jit(solution)/shard_map/ppermute | solution.py:308
  29.3 16.9 %collective-permute-start.9 = (bf16[2,2,2,16,16,128]{5,4,3,2,1,0:T(8,128)(2,1)S(1)}, bf16[2,2,2,16,16,128]{5,4,3,2,1,0:T(8,128)(2,1)S(1)}, u32[]{:S(2)}, u32[]{:S(2)}) collective-permute-start(bf16[2,2,2,16,16,128]{5,4,3,2,1,0:T(8,128)(2,1)S(1)} %collective-permute-done.6.refs_2_), channel_id=1, source_target_pairs={{0,128},{252,124},{1,129},{253,125},{2,130},{254,126},{3,131},{255... | collective-permute-start | bytes 1572872 | tf_op jit(solution)/shard_map/ppermute | solution.py:332
  32.9 25.5 %collective-permute-start.3 = (bf16[2,2,2,16,16,128]{5,4,3,2,1,0:T(8,128)(2,1)S(1)}, bf16[2,2,2,16,16,128]{5,4,3,2,1,0:T(8,128)(2,1)S(1)}, u32[]{:S(2)}, u32[]{:S(2)}) collective-permute-start(bf16[2,2,2,16,16,128]{5,4,3,2,1,0:T(8,128)(2,1)S(1)} %get-tuple-element.31), channel_id=1, source_target_pairs={{0,4},{1,5},{2,6},{3,7},{4,0},{5,1},{6,2},{7,3},{8,12},{9,13},{10,... | collective-permute-start | bytes 1572872 | tf_op jit(solution)/shard_map/ppermute | solution.py:308
  34.5 24.0 %collective-permute-start.4 = (bf16[2,2,2,16,16,128]{5,4,3,2,1,0:T(8,128)(2,1)S(1)}, bf16[2,2,2,16,16,128]{5,4,3,2,1,0:T(8,128)(2,1)S(1)}, u32[]{:S(2)}, u32[]{:S(2)}) collective-permute-start(bf16[2,2,2,16,16,128]{5,4,3,2,1,0:T(8,128)(2,1)S(1)} %get-tuple-element.32), channel_id=1, source_target_pairs={{0,0},{1,1},{2,2},{3,3},{4,8},{5,9},{6,10},{7,11},{8,4},{9,5},{10,... | collective-permute-start | bytes 1572872 | tf_op jit(solution)/shard_map/ppermute | solution.py:308
  44.8 19.6 %collective-permute-start.11 = (bf16[2,2,2,16,16,128]{5,4,3,2,1,0:T(8,128)(2,1)S(1)}, bf16[2,2,2,16,16,128]{5,4,3,2,1,0:T(8,128)(2,1)S(1)}, u32[]{:S(2)}, u32[]{:S(2)}) collective-permute-start(bf16[2,2,2,16,16,128]{5,4,3,2,1,0:T(8,128)(2,1)S(1)} %collective-permute-done.7.refs_3_.refs_4_), channel_id=1, source_target_pairs={{0,128},{252,124},{1,129},{253,125},{2,130},{254,126},{3,131},{255... | collective-permute-start | bytes 1572872 | tf_op jit(solution)/shard_map/ppermute | solution.py:332
  46.1 22.3 %collective-permute-start.8 = (bf16[2,2,2,16,16,128]{5,4,3,2,1,0:T(8,128)(2,1)S(1)}, bf16[2,2,2,16,16,128]{5,4,3,2,1,0:T(8,128)(2,1)S(1)}, u32[]{:S(2)}, u32[]{:S(2)}) collective-permute-start(bf16[2,2,2,16,16,128]{5,4,3,2,1,0:T(8,128)(2,1)S(1)} %get-tuple-element.38), channel_id=1, source_target_pairs={{0,4},{1,5},{2,6},{3,7},{4,0},{5,1},{6,2},{7,3},{8,12},{9,13},{10,... | collective-permute-start | bytes 1572872 | tf_op jit(solution)/shard_map/ppermute | solution.py:308
  50.1 18.7 %collective-permute-start.10 = (bf16[2,2,2,16,16,128]{5,4,3,2,1,0:T(8,128)(2,1)S(1)}, bf16[2,2,2,16,16,128]{5,4,3,2,1,0:T(8,128)(2,1)S(1)}, u32[]{:S(2)}, u32[]{:S(2)}) collective-permute-start(bf16[2,2,2,16,16,128]{5,4,3,2,1,0:T(8,128)(2,1)S(1)} %get-tuple-element.42), channel_id=1, source_target_pairs={{0,0},{1,1},{2,2},{3,3},{4,8},{5,9},{6,10},{7,11},{8,4},{9,5},{10,... | collective-permute-start | bytes 1572872 | tf_op jit(solution)/shard_map/ppermute | solution.py:308

commit v12 on v8

--- a/solution.py
+++ b/solution.py
@@ -315,9 +315,8 @@
     own, turned_own, near_b, far_b = pack(flags, (parts[0], one, parts[2], other), copies, (whole,) * 2 + (half,) * 2)
     far_own = swap(turned_own, 2)
     whole_a = trade(own, side_a)
-    first_near_b, first_far_b = trade(near_b, side_b_of_half), trade(far_b, side_b_of_half)
-    over_middle = [(0, middle), (slabs - 1, middle - 1)]
-    near_over, far_over = [lax.ppermute(value, "slab", over_middle) for value in (first_near_b, first_far_b)]
+    first_near_b, first_far_b = trade(near_b, side_b_of_half), trade(far_b, side_b)
+    near_over = lax.ppermute(first_near_b, "slab", [(0, middle), (slabs - 1, middle - 1)])
 
     copies = []
     for slot in range(2):
@@ -341,11 +340,9 @@
         plan += [(2, g, 0, NEAR, near_at_b, g, (0,)), (3, g, 0, NEAR, near_at_b, g, (1,))]
         plan += [(None, g, 0, NEAR, near_at_b, g, (2,))]
         far_plan += [(1, g, (rest, 0), NEAR, far_at_a, g, None)]
-        far_plan += [(4, g, 0, NEAR, far_at_b, g, (0,)), (5, g, 0, NEAR, far_at_b, g, (1,))]
-        far_plan += [(None, g, 0, NEAR, far_at_b, g, (2,))]
+        far_plan += [(4, g, 0, NEAR, far_at_b, g, (0, 1)), (None, g, 0, NEAR, far_at_b, g, (2,))]
     blocks = (own, whole_a, first_near_b, near_over)
     befores = summed(flags, blocks, plan, (NEAR_BAND,), None, cells, 2, 0)
-    far_over, *befores = lax.optimization_barrier((far_over, *befores))
     far_sums = (flags, plan + far_plan, blocks)
     plan, far_plan = [], []
     for g in range(2):
@@ -353,7 +350,7 @@
         plan += [(2, g, 0, NEAR, near_at_b, g, (0, 1)), (None, g, 0, NEAR, near_at_b, g, (2,))]
         far_plan += [(3, g, 0, NEAR, far_at_a, g, None)]
         far_plan += [(4, g, 0, NEAR, far_at_b, g, (0, 1)), (None, g, 0, NEAR, far_at_b, g, (2,))]
-    far_befores = summed(flags, far_sums[2] + (first_far_b, far_over), far_sums[1], (FAR_BAND,), None, cells, 2, 0)
+    far_befores = summed(flags, far_sums[2] + (first_far_b,), far_sums[1], (FAR_BAND,), None, cells, 2, 0)
     image = summed(flags, (far_own, near_a, near_b), plan, (NEAR_BAND,), befores, cells, 2, 1)
     blocks = (far_own, near_a, near_b, far_a, far_b)
     return summed(flags, blocks, plan + far_plan, (FAR_BAND,), far_befores, cells, 2, 2, image)

time: 78.3 us -> 78.8 us (level)
  the two profiles are of different devices: /device:TPU:8 before, /device:TPU:2 now
where the time goes in v12:
time: 78.8 us; the launch traced here: 78.6 us
  starting transfers between devices  29.5 us (37%)
  waiting for transfers between devices  25.8 us (33%)
  Pallas kernels  23.1 us (29%)
    ppermute x7, starting transfers between devices, trade(): return lax.ppermute(value, ('slab', 'freq'), pairs)  24.9 us
    pallas_call x4, Pallas kernels, summed(): pl.pallas_call(functools.partial(sum_kernel, plan, bands, first, last), i...  19.8 us
    ppermute x7, waiting for transfers between devices, trade(): return lax.ppermute(value, ('slab', 'freq'), pairs)  16.4 us
    ppermute x3, waiting for transfers between devices, swap(): return lax.ppermute(part, 'freq', [(g, g ^ d) for g in range(GROUPS)])  9.43 us
    ppermute x3, starting transfers between devices, swap(): return lax.ppermute(part, 'freq', [(g, g ^ d) for g in range(GROUPS)])  3.85 us
    pallas_call x2, Pallas kernels, pack(): pl.pallas_call(functools.partial(pack_kernel, copies, len(arrays)), in_sp...  1.7 us
    pallas_call x1, Pallas kernels, regrouped(): pl.pallas_call(regroup_kernel, in_specs=[pl.BlockSpec(memory_space=pltpu....  1.66 us
  transfers between devices with their start and end apart: 11, of which 6 were waited for; matrix products, arithmetic and copies ran while one was open for 0% of the time, Pallas kernels for 18%

profile of v12, /device:TPU:2, one launch (start us, length us, event | category | flops | bytes accessed | tf_op | source)
XLA Modules:
  0.0 78.6 jit_solution(15017452074941295773)
XLA Ops:
  0.0 1.7 %regroup.1 = (bf16[2,2,32,16,128]{4,3,2,1,0:T(8,128)(2,1)S(1)}, bf16[2,2,32,16,128]{4,3,2,1,0:T(8,128)(2,1)S(1)}, bf16[2,2,32,16,128]{4,3,2,1,0:T(8,128)(2,1)S(1)}, bf16[2,2,32,16,128]{4,3,2,1,0:T(8,128)(2,1)S(1)}) custom-call(s32[1]{0:T(128)} %bitcast.2.group_ref, bf16[2,2,32,16,256]{4,3,2,1,0:T(8,128)(2,1)} %source_ref.1, ...), custom_call_target="tpu_custom_call" | custom-call | bytes 4194304 | tf_op jit(solution)/shard_map/regroup/pallas_call | solution.py:65
  1.7 0.1 collective-permute-start
  1.8 0.5 collective-permute-start.1
  2.3 0.1 pad_add_fusion.refs_0_.flags_ref
  2.3 1.3 %collective-permute-done.refs_2_ = bf16[2,2,32,16,128]{4,3,2,1,0:T(8,128)(2,1)S(1)} collective-permute-done((bf16[2,2,32,16,128]{4,3,2,1,0:T(8,128)(2,1)S(1)}, bf16[2,2,32,16,128]{4,3,2,1,0:T(8,128)(2,1)S(1)}, u32[]{:S(2)}, u32[]{:S(2)}) %collective-permute-start) | collective-permute-done | bytes 524320 | tf_op jit(solution)/shard_map/ppermute | solution.py:289
  3.7 0.7 collective-permute-done.1.refs_4_
  4.4 0.9 %pack.2 = (bf16[2,2,2,32,16,128]{5,4,3,2,1,0:T(8,128)(2,1)S(1)}, bf16[2,2,2,32,16,128]{5,4,3,2,1,0:T(8,128)(2,1)S(1)}, bf16[2,2,2,16,16,128]{5,4,3,2,1,0:T(8,128)(2,1)S(1)}, bf16[2,2,2,16,16,128]{5,4,3,2,1,0:T(8,128)(2,1)S(1)}) custom-call(s32[2]{0:T(128)S(1)} %pad_add_fusion.refs_0_.flags_ref, bf16[2,2,32,16,128]{4,3,2,1,0:T(8,128)(2,1)S(1)} %get-tuple-element.22.refs_1_, ...), custom_call_target="tpu_custom_call" | custom-call | bytes 2097152 | tf_op jit(solution)/shard_map/pack/pallas_call | solution.py:107
  5.3 3.3 %collective-permute-start.2 = (bf16[2,2,2,32,16,128]{5,4,3,2,1,0:T(8,128)(2,1)S(1)}, bf16[2,2,2,32,16,128]{5,4,3,2,1,0:T(8,128)(2,1)S(1)}, u32[]{:S(2)}, u32[]{:S(2)}) collective-permute-start(bf16[2,2,2,32,16,128]{5,4,3,2,1,0:T(8,128)(2,1)S(1)} %get-tuple-element.26.refs_2_), channel_id=1, source_target_pairs={{0,2},{1,3},{2,0},{3,1},{4,6},{5,7},{6,4},{7,5},{8,10},{9,11},{10,... | collective-permute-start | bytes 3145736 | tf_op jit(solution)/shard_map/ppermute | solution.py:289
  8.6 0.5 collective-permute-start.5
  9.1 2.2 %collective-permute-start.6 = (bf16[2,2,2,16,16,128]{5,4,3,2,1,0:T(8,128)(2,1)S(1)}, bf16[2,2,2,16,16,128]{5,4,3,2,1,0:T(8,128)(2,1)S(1)}, u32[]{:S(2)}, u32[]{:S(2)}) collective-permute-start(bf16[2,2,2,16,16,128]{5,4,3,2,1,0:T(8,128)(2,1)S(1)} %get-tuple-element.30), channel_id=1, source_target_pairs={{0,124},{1,125},{2,126},{3,127},{4,8},{5,9},{6,10},{7,11},{8,4},{9... | collective-permute-start | bytes 1572872 | tf_op jit(solution)/shard_map/ppermute | solution.py:296
  11.2 1.9 %collective-permute-start.7 = (bf16[2,2,2,16,16,128]{5,4,3,2,1,0:T(8,128)(2,1)S(1)}, bf16[2,2,2,16,16,128]{5,4,3,2,1,0:T(8,128)(2,1)S(1)}, u32[]{:S(2)}, u32[]{:S(2)}) collective-permute-start(bf16[2,2,2,16,16,128]{5,4,3,2,1,0:T(8,128)(2,1)S(1)} %get-tuple-element.31), channel_id=1, source_target_pairs={{0,0},{1,1},{2,2},{3,3},{4,8},{5,9},{6,10},{7,11},{8,4},{9,5},{10,... | collective-permute-start | bytes 1572872 | tf_op jit(solution)/shard_map/ppermute | solution.py:296
  13.2 10.9 %collective-permute-done.6.refs_2_ = bf16[2,2,2,16,16,128]{5,4,3,2,1,0:T(8,128)(2,1)S(1)} collective-permute-done((bf16[2,2,2,16,16,128]{5,4,3,2,1,0:T(8,128)(2,1)S(1)}, bf16[2,2,2,16,16,128]{5,4,3,2,1,0:T(8,128)(2,1)S(1)}, u32[]{:S(2)}, u32[]{:S(2)}) %collective-permute-start.6) | collective-permute-done | bytes 524320 | tf_op jit(solution)/shard_map/ppermute | solution.py:296
  24.0 0.7 collective-permute-start.10
  24.7 7.4 %collective-permute-done.2.refs_1_.refs_0_ = bf16[2,2,2,32,16,128]{5,4,3,2,1,0:T(8,128)(2,1)S(1)} collective-permute-done((bf16[2,2,2,32,16,128]{5,4,3,2,1,0:T(8,128)(2,1)S(1)}, bf16[2,2,2,32,16,128]{5,4,3,2,1,0:T(8,128)(2,1)S(1)}, u32[]{:S(2)}, u32[]{:S(2)}) %collective-permute-start.2) | collective-permute-done | bytes 1048608 | tf_op jit(solution)/shard_map/ppermute | solution.py:289
  32.1 0.8 %pack.3 = (bf16[2,2,2,16,16,128]{5,4,3,2,1,0:T(8,128)(2,1)S(1)}, bf16[2,2,2,16,16,128]{5,4,3,2,1,0:T(8,128)(2,1)S(1)}, bf16[2,2,2,16,16,128]{5,4,3,2,1,0:T(8,128)(2,1)S(1)}, bf16[2,2,2,16,16,128]{5,4,3,2,1,0:T(8,128)(2,1)S(1)}) custom-call(s32[2]{0:T(128)S(1)} %pad_add_fusion.refs_0_.flags_ref, ...), custom_call_target="tpu_custom_call" | custom-call | bytes 2097152 | tf_op jit(solution)/shard_map/pack/pallas_call | solution.py:107
  32.9 14.4 %collective-permute-start.3 = (bf16[2,2,2,16,16,128]{5,4,3,2,1,0:T(8,128)(2,1)S(1)}, bf16[2,2,2,16,16,128]{5,4,3,2,1,0:T(8,128)(2,1)S(1)}, u32[]{:S(2)}, u32[]{:S(2)}) collective-permute-start(bf16[2,2,2,16,16,128]{5,4,3,2,1,0:T(8,128)(2,1)S(1)} %get-tuple-element.27), channel_id=1, source_target_pairs={{0,4},{1,5},{2,6},{3,7},{4,0},{5,1},{6,2},{7,3},{8,12},{9,13},{10,... | collective-permute-start | bytes 1572872 | tf_op jit(solution)/shard_map/ppermute | solution.py:296
  47.3 1.9 %collective-permute-start.4 = (bf16[2,2,2,16,16,128]{5,4,3,2,1,0:T(8,128)(2,1)S(1)}, bf16[2,2,2,16,16,128]{5,4,3,2,1,0:T(8,128)(2,1)S(1)}, u32[]{:S(2)}, u32[]{:S(2)}) collective-permute-start(bf16[2,2,2,16,16,128]{5,4,3,2,1,0:T(8,128)(2,1)S(1)} %get-tuple-element.28), channel_id=1, source_target_pairs={{0,0},{1,1},{2,2},{3,3},{4,8},{5,9},{6,10},{7,11},{8,4},{9,5},{10,... | collective-permute-start | bytes 1572872 | tf_op jit(solution)/shard_map/ppermute | solution.py:296
  49.2 0.0 collective-permute-done.7.refs_4_
  49.2 0.0 collective-permute-done.5.refs_1_
  49.3 0.1 collective-permute-start.8
  49.4 3.9 %collective-permute-start.9 = (bf16[2,2,2,16,16,128]{5,4,3,2,1,0:T(8,128)(2,1)S(1)}, bf16[2,2,2,16,16,128]{5,4,3,2,1,0:T(8,128)(2,1)S(1)}, u32[]{:S(2)}, u32[]{:S(2)}) collective-permute-start(bf16[2,2,2,16,16,128]{5,4,3,2,1,0:T(8,128)(2,1)S(1)} %get-tuple-element.35), channel_id=1, source_target_pairs={{0,0},{1,1},{2,2},{3,3},{4,8},{5,9},{6,10},{7,11},{8,4},{9,5},{10,... | collective-permute-start | bytes 1572872 | tf_op jit(solution)/shard_map/ppermute | solution.py:296
  53.3 0.0 collective-permute-done.10.refs_3_
  53.3 3.9 %partial.2.refs_5_ = f32[32,32,8,128]{3,2,1,0:T(8,128)S(1)} custom-call(s32[2]{0:T(128)S(1)} %pad_add_fusion.refs_0_.flags_ref, bf16[2,2,2,32,16,128]{5,4,3,2,1,0:T(8,128)(2,1)S(1)} %get-tuple-element.29.refs_0_, bf16[2,2,2,32,16,128]{5,4,3,2,1,0:T(8,128)(2,1)S(1)} %collective-permute-done.5.refs_1_, ...), custom_call_target="tpu_custom_call" | custom-call | flops 16640000 | bytes 4160000 | tf_op jit(solution)/shard_map/partial/pallas_call | solution.py:262
  57.2 3.8 %partial.3.refs_3_ = f32[33,32,8,128]{3,2,1,0:T(8,128)S(1)} custom-call(s32[2]{0:T(128)S(1)} %pad_add_fusion.refs_0_.flags_ref, bf16[2,2,2,32,16,128]{5,4,3,2,1,0:T(8,128)(2,1)S(1)} %get-tuple-element.29.refs_0_, bf16[2,2,2,32,16,128]{5,4,3,2,1,0:T(8,128)(2,1)S(1)} %collective-permute-done.5.refs_1_, ...), custom_call_target="tpu_custom_call" | custom-call | flops 17160000 | bytes 4290000 | tf_op jit(solution)/shard_map/partial/pallas_call | solution.py:262
  61.1 0.0 collective-permute-done.3.refs_1_
  61.1 3.0 %collective-permute-done.4.refs_2_ = bf16[2,2,2,16,16,128]{5,4,3,2,1,0:T(8,128)(2,1)S(1)} collective-permute-done((bf16[2,2,2,16,16,128]{5,4,3,2,1,0:T(8,128)(2,1)S(1)}, bf16[2,2,2,16,16,128]{5,4,3,2,1,0:T(8,128)(2,1)S(1)}, u32[]{:S(2)}, u32[]{:S(2)}) %collective-permute-start.4) | collective-permute-done | bytes 524320 | tf_op jit(solution)/shard_map/ppermute | solution.py:296
  64.1 5.9 %image.2.refs_6_ = f32[4,65,32,256]{3,2,1,0:T(8,128)} custom-call(s32[2]{0:T(128)S(1)} %pad_add_fusion.refs_0_.flags_ref, bf16[2,2,2,32,16,128]{5,4,3,2,1,0:T(8,128)(2,1)S(1)} %collective-permute-done.2.refs_1_.refs_0_, bf16[2,2,2,16,16,128]{5,4,3,2,1,0:T(8,128)(2,1)S(1)} %collective-permute-done.3.refs_1_, ...), custom_call_target="tpu_custom_call" | custom-call | flops 17160000 | bytes 4290000 | tf_op jit(solution)/shard_map/image/pallas_call | solution.py:262
  70.0 0.0 collective-permute-done.8.refs_3_
  70.0 2.5 %collective-permute-done.9.refs_4_ = bf16[2,2,2,16,16,128]{5,4,3,2,1,0:T(8,128)(2,1)S(1)} collective-permute-done((bf16[2,2,2,16,16,128]{5,4,3,2,1,0:T(8,128)(2,1)S(1)}, bf16[2,2,2,16,16,128]{5,4,3,2,1,0:T(8,128)(2,1)S(1)}, u32[]{:S(2)}, u32[]{:S(2)}) %collective-permute-start.9) | collective-permute-done | bytes 524320 | tf_op jit(solution)/shard_map/ppermute | solution.py:296
  72.5 6.1 %image.3 = f32[4,65,32,256]{3,2,1,0:T(8,128)} custom-call(s32[2]{0:T(128)S(1)} %pad_add_fusion.refs_0_.flags_ref, bf16[2,2,2,32,16,128]{5,4,3,2,1,0:T(8,128)(2,1)S(1)} %collective-permute-done.2.refs_1_.refs_0_, bf16[2,2,2,16,16,128]{5,4,3,2,1,0:T(8,128)(2,1)S(1)} %collective-permute-done.3.refs_1_, ...), custom_call_target="tpu_custom_call", output_to_operand_aliasing={{}: (7, {})} | custom-call | flops 16640000 | bytes 4160000 | tf_op jit(solution)/shard_map/image/pallas_call | solution.py:262
Async XLA Ops:
  1.7 2.0 %collective-permute-start = (bf16[2,2,32,16,128]{4,3,2,1,0:T(8,128)(2,1)S(1)}, bf16[2,2,32,16,128]{4,3,2,1,0:T(8,128)(2,1)S(1)}, u32[]{:S(2)}, u32[]{:S(2)}) collective-permute-start(bf16[2,2,32,16,128]{4,3,2,1,0:T(8,128)(2,1)S(1)} %get-tuple-element.23), channel_id=1, source_target_pairs={{0,1},{1,0},{2,3},{3,2},{4,5},{5,4},{6,7},{7,6},{8,9},{9,8},{10,11... | collective-permute-start | bytes 1572872 | tf_op jit(solution)/shard_map/ppermute | solution.py:289
  1.8 2.6 %collective-permute-start.1 = (bf16[2,2,32,16,128]{4,3,2,1,0:T(8,128)(2,1)S(1)}, bf16[2,2,32,16,128]{4,3,2,1,0:T(8,128)(2,1)S(1)}, u32[]{:S(2)}, u32[]{:S(2)}) collective-permute-start(bf16[2,2,32,16,128]{4,3,2,1,0:T(8,128)(2,1)S(1)} %get-tuple-element.25), channel_id=1, source_target_pairs={{0,1},{1,0},{2,3},{3,2},{4,5},{5,4},{6,7},{7,6},{8,9},{9,8},{10,11... | collective-permute-start | bytes 1572872 | tf_op jit(solution)/shard_map/ppermute | solution.py:289
  5.3 26.8 %collective-permute-start.2 = (bf16[2,2,2,32,16,128]{5,4,3,2,1,0:T(8,128)(2,1)S(1)}, bf16[2,2,2,32,16,128]{5,4,3,2,1,0:T(8,128)(2,1)S(1)}, u32[]{:S(2)}, u32[]{:S(2)}) collective-permute-start(bf16[2,2,2,32,16,128]{5,4,3,2,1,0:T(8,128)(2,1)S(1)} %get-tuple-element.26.refs_2_), channel_id=1, source_target_pairs={{0,2},{1,3},{2,0},{3,1},{4,6},{5,7},{6,4},{7,5},{8,10},{9,11},{10,... | collective-permute-start | bytes 3145736 | tf_op jit(solution)/shard_map/ppermute | solution.py:289
  8.6 40.7 %collective-permute-start.5 = (bf16[2,2,2,32,16,128]{5,4,3,2,1,0:T(8,128)(2,1)S(1)}, bf16[2,2,2,32,16,128]{5,4,3,2,1,0:T(8,128)(2,1)S(1)}, u32[]{:S(2)}, u32[]{:S(2)}) collective-permute-start(bf16[2,2,2,32,16,128]{5,4,3,2,1,0:T(8,128)(2,1)S(1)} %get-tuple-element.29.refs_0_), channel_id=1, source_target_pairs={{0,4},{1,5},{2,6},{3,7},{4,0},{5,1},{6,2},{7,3},{8,12},{9,13},{10,... | collective-permute-start | bytes 3145736 | tf_op jit(solution)/shard_map/ppermute | solution.py:296
  9.1 14.9 %collective-permute-start.6 = (bf16[2,2,2,16,16,128]{5,4,3,2,1,0:T(8,128)(2,1)S(1)}, bf16[2,2,2,16,16,128]{5,4,3,2,1,0:T(8,128)(2,1)S(1)}, u32[]{:S(2)}, u32[]{:S(2)}) collective-permute-start(bf16[2,2,2,16,16,128]{5,4,3,2,1,0:T(8,128)(2,1)S(1)} %get-tuple-element.30), channel_id=1, source_target_pairs={{0,124},{1,125},{2,126},{3,127},{4,8},{5,9},{6,10},{7,11},{8,4},{9... | collective-permute-start | bytes 1572872 | tf_op jit(solution)/shard_map/ppermute | solution.py:296
  11.2 38.0 %collective-permute-start.7 = (bf16[2,2,2,16,16,128]{5,4,3,2,1,0:T(8,128)(2,1)S(1)}, bf16[2,2,2,16,16,128]{5,4,3,2,1,0:T(8,128)(2,1)S(1)}, u32[]{:S(2)}, u32[]{:S(2)}) collective-permute-start(bf16[2,2,2,16,16,128]{5,4,3,2,1,0:T(8,128)(2,1)S(1)} %get-tuple-element.31), channel_id=1, source_target_pairs={{0,0},{1,1},{2,2},{3,3},{4,8},{5,9},{6,10},{7,11},{8,4},{9,5},{10,... | collective-permute-start | bytes 1572872 | tf_op jit(solution)/shard_map/ppermute | solution.py:296
  24.0 29.3 %collective-permute-start.10 = (bf16[2,2,2,16,16,128]{5,4,3,2,1,0:T(8,128)(2,1)S(1)}, bf16[2,2,2,16,16,128]{5,4,3,2,1,0:T(8,128)(2,1)S(1)}, u32[]{:S(2)}, u32[]{:S(2)}) collective-permute-start(bf16[2,2,2,16,16,128]{5,4,3,2,1,0:T(8,128)(2,1)S(1)} %collective-permute-done.6.refs_2_), channel_id=1, source_target_pairs={{0,128},{252,124},{1,129},{253,125},{2,130},{254,126},{3,131},{255... | collective-permute-start | bytes 1572872 | tf_op jit(solution)/shard_map/ppermute | solution.py:319
  32.9 28.2 %collective-permute-start.3 = (bf16[2,2,2,16,16,128]{5,4,3,2,1,0:T(8,128)(2,1)S(1)}, bf16[2,2,2,16,16,128]{5,4,3,2,1,0:T(8,128)(2,1)S(1)}, u32[]{:S(2)}, u32[]{:S(2)}) collective-permute-start(bf16[2,2,2,16,16,128]{5,4,3,2,1,0:T(8,128)(2,1)S(1)} %get-tuple-element.27), channel_id=1, source_target_pairs={{0,4},{1,5},{2,6},{3,7},{4,0},{5,1},{6,2},{7,3},{8,12},{9,13},{10,... | collective-permute-start | bytes 1572872 | tf_op jit(solution)/shard_map/ppermute | solution.py:296
  47.3 16.7 %collective-permute-start.4 = (bf16[2,2,2,16,16,128]{5,4,3,2,1,0:T(8,128)(2,1)S(1)}, bf16[2,2,2,16,16,128]{5,4,3,2,1,0:T(8,128)(2,1)S(1)}, u32[]{:S(2)}, u32[]{:S(2)}) collective-permute-start(bf16[2,2,2,16,16,128]{5,4,3,2,1,0:T(8,128)(2,1)S(1)} %get-tuple-element.28), channel_id=1, source_target_pairs={{0,0},{1,1},{2,2},{3,3},{4,8},{5,9},{6,10},{7,11},{8,4},{9,5},{10,... | collective-permute-start | bytes 1572872 | tf_op jit(solution)/shard_map/ppermute | solution.py:296
  49.3 20.7 %collective-permute-start.8 = (bf16[2,2,2,16,16,128]{5,4,3,2,1,0:T(8,128)(2,1)S(1)}, bf16[2,2,2,16,16,128]{5,4,3,2,1,0:T(8,128)(2,1)S(1)}, u32[]{:S(2)}, u32[]{:S(2)}) collective-permute-start(bf16[2,2,2,16,16,128]{5,4,3,2,1,0:T(8,128)(2,1)S(1)} %get-tuple-element.34), channel_id=1, source_target_pairs={{0,4},{1,5},{2,6},{3,7},{4,0},{5,1},{6,2},{7,3},{8,12},{9,13},{10,... | collective-permute-start | bytes 1572872 | tf_op jit(solution)/shard_map/ppermute | solution.py:296
  49.4 23.1 %collective-permute-start.9 = (bf16[2,2,2,16,16,128]{5,4,3,2,1,0:T(8,128)(2,1)S(1)}, bf16[2,2,2,16,16,128]{5,4,3,2,1,0:T(8,128)(2,1)S(1)}, u32[]{:S(2)}, u32[]{:S(2)}) collective-permute-start(bf16[2,2,2,16,16,128]{5,4,3,2,1,0:T(8,128)(2,1)S(1)} %get-tuple-element.35), channel_id=1, source_target_pairs={{0,0},{1,1},{2,2},{3,3},{4,8},{5,9},{6,10},{7,11},{8,4},{9,5},{10,... | collective-permute-start | bytes 1572872 | tf_op jit(solution)/shard_map/ppermute | solution.py:296

commit v13 on v8

--- a/solution.py
+++ b/solution.py
@@ -115,11 +115,19 @@
     )(flags, *arrays)
 
 
-def sum_kernel(plan, bands, first, last, flags_ref, *refs):
-    count = 1 + max(entry[0] for entry in plan if entry[0] is not None)
+def sum_kernel(variants, count, bands, last, flags_ref, *refs):
+    for crosses, plan, first, groups in variants:
+        run = functools.partial(sum_body, plan, count, groups, bands, first, last, flags_ref, *refs)
+        if crosses is None:
+            run()
+        else:
+            pl.when((flags_ref[1] == 1) == crosses)(run)
+
+
+def sum_body(plan, count, groups, bands, first, last, flags_ref, *refs):
     blocks, refs = refs[:count], refs[count:]
     befores = ()
-    if not first:
+    if last:
         befores, refs = refs[: len(bands)], refs[len(bands) :]
     if last == 2:
         refs = refs[1:]
@@ -129,7 +137,7 @@
         turn, stage, sems = refs[len(outs) + 1 :]
         out_ref = outs[0]
     cells = stage.shape[4 - 1] if last else outs[0].shape[1]
-    total_freqs = fields.shape[2]
+    total_freqs = 2 * groups
 
     def fill(index, part, at, length, to, group):
         start, to = by_parity(flags_ref, at), by_parity(flags_ref, to)
@@ -235,13 +243,13 @@
 FAR_BAND = (0, 2 * NEAR // TH, NEAR // TH, 2 * NEAR + 1, 0)
 
 
-def summed(flags, blocks, plan, bands, befores, cells, groups, last, image=None):
-    first = befores is None
+def summed(flags, blocks, variants, bands, befores, cells, last, image=None):
     heights = [TH * band[1] + band[4] for band in bands]
+    groups = max(variant[-1] for variant in variants)
     scratch = [pltpu.VMEM((2, 3 * cells, 2 * groups, ROWS, LANES), jnp.float32)]
     vmem = pl.BlockSpec(memory_space=pltpu.VMEM)
     hbm = pl.BlockSpec(memory_space=pl.ANY)
-    operands = list(blocks) + ([] if first else list(befores))
+    operands = list(blocks) + list(befores)
     in_specs = [pl.BlockSpec(memory_space=pltpu.SMEM)] + [vmem] * len(operands)
     aliases = {}
     if last:
@@ -260,15 +268,15 @@
         out_shape = [pltpu.VMEM((height, cells, 8, LANES), jnp.float32) for height in heights]
         out_specs = [vmem] * len(heights)
     return pl.pallas_call(
-        functools.partial(sum_kernel, plan, bands, first, last),
+        functools.partial(sum_kernel, variants, len(blocks), bands, last),
         in_specs=in_specs,
         out_specs=out_specs,
         out_shape=out_shape,
         scratch_shapes=scratch,
         input_output_aliases=aliases,
-        compiler_params=pltpu.CompilerParams(vmem_limit_bytes=24 << 20),
+        compiler_params=pltpu.CompilerParams(vmem_limit_bytes=32 << 20),
         cost_estimate=pl.CostEstimate(
-            flops=260_000 * groups * sum(heights), bytes_accessed=130_000 * sum(heights), transcendentals=0
+            flops=520_000 * sum(heights), bytes_accessed=130_000 * sum(heights), transcendentals=0
         ),
         name="image" if last else "partial",
     )(flags, *operands)
@@ -308,16 +316,18 @@
 
     whole, half = [(2, 2, freqs, length, ROWS, LANES) for length in (cells, NEAR)]
     rest = cells - NEAR
+    copies = [(None, slot, None, 0, 0, slot) for slot in range(2)]
+    (turned_own,) = pack(flags, (parts[2], other), copies, (whole,))
+    far_own = swap(turned_own, 2)
     copies = []
     for slot in range(2):
-        copies += [(None, slot, None, 0, 0, slot), (None, 2 + slot, None, 0, 1, slot)]
-        copies += [(None, slot, None, (0, rest), 2, slot), (None, slot, None, (rest, 0), 3, slot)]
-    own, turned_own, near_b, far_b = pack(flags, (parts[0], one, parts[2], other), copies, (whole,) * 2 + (half,) * 2)
-    far_own = swap(turned_own, 2)
+        for out, at in ((0, 0), (1, (0, rest)), (2, (rest, 0))):
+            copies.append((None, slot, None, at, out, slot))
+    own, near_b, far_b = pack(flags, (parts[0], one), copies, (whole,) + (half,) * 2)
     whole_a = trade(own, side_a)
     first_near_b, first_far_b = trade(near_b, side_b_of_half), trade(far_b, side_b_of_half)
     over_middle = [(0, middle), (slabs - 1, middle - 1)]
-    near_over, far_over = [lax.ppermute(value, "slab", over_middle) for value in (first_near_b, first_far_b)]
+    near_over = lax.ppermute(first_near_b, "slab", over_middle)
 
     copies = []
     for slot in range(2):
@@ -328,35 +338,52 @@
     near_a, near_b, far_a, far_b = pack(flags, (far_own, turned_own), copies, (half,) * 4)
     turned = (middle - 1, middle)
     near_a, near_b = trade(near_a, side_a), trade(near_b, side_b, turned)
-    whole_a, first_near_b, first_far_b, far_a, far_b = lax.optimization_barrier(
-        (whole_a, first_near_b, first_far_b, far_a, far_b)
-    )
     far_a, far_b = trade(far_a, side_a), trade(far_b, side_b, turned)
 
     near_at_a, near_at_b = (2 * cells, rest), (rest, 2 * cells)
     far_at_a, far_at_b = (2 * cells + NEAR, 0), (0, 2 * cells + NEAR)
-    plan, far_plan = [], []
-    for g in range(2):
-        plan += [(0, g, 0, cells, cells, g, None), (1, g, (0, rest), NEAR, near_at_a, g, None)]
-        plan += [(2, g, 0, NEAR, near_at_b, g, (0,)), (3, g, 0, NEAR, near_at_b, g, (1,))]
-        plan += [(None, g, 0, NEAR, near_at_b, g, (2,))]
-        far_plan += [(1, g, (rest, 0), NEAR, far_at_a, g, None)]
-        far_plan += [(4, g, 0, NEAR, far_at_b, g, (0,)), (5, g, 0, NEAR, far_at_b, g, (1,))]
-        far_plan += [(None, g, 0, NEAR, far_at_b, g, (2,))]
-    blocks = (own, whole_a, first_near_b, near_over)
-    befores = summed(flags, blocks, plan, (NEAR_BAND,), None, cells, 2, 0)
-    far_over, *befores = lax.optimization_barrier((far_over, *befores))
-    far_sums = (flags, plan + far_plan, blocks)
-    plan, far_plan = [], []
-    for g in range(2):
-        plan += [(0, g, 0, cells, cells, g, None), (1, g, 0, NEAR, near_at_a, g, None)]
-        plan += [(2, g, 0, NEAR, near_at_b, g, (0, 1)), (None, g, 0, NEAR, near_at_b, g, (2,))]
-        far_plan += [(3, g, 0, NEAR, far_at_a, g, None)]
-        far_plan += [(4, g, 0, NEAR, far_at_b, g, (0, 1)), (None, g, 0, NEAR, far_at_b, g, (2,))]
-    far_befores = summed(flags, far_sums[2] + (first_far_b, far_over), far_sums[1], (FAR_BAND,), None, cells, 2, 0)
-    image = summed(flags, (far_own, near_a, near_b), plan, (NEAR_BAND,), befores, cells, 2, 1)
-    blocks = (far_own, near_a, near_b, far_a, far_b)
-    return summed(flags, blocks, plan + far_plan, (FAR_BAND,), far_befores, cells, 2, 2, image)
+    zero = (None, 0, 0, NEAR)
+
+    def first_groups(own, whole_a, near_b, far_b, near_over, far_over, to, far):
+        plan = []
+        for g in range(2):
+            plan += [(own, g, 0, cells, cells, to + g, None), (whole_a, g, (0, rest), NEAR, near_at_a, to + g, None)]
+            plan += [(near_b, g, 0, NEAR, near_at_b, to + g, (0,)), (*zero, near_at_b, to + g, (2,))]
+            if near_over is not None:
+                plan += [(near_over, g, 0, NEAR, near_at_b, to + g, (1,))]
+            if far:
+                plan += [(whole_a, g, (rest, 0), NEAR, far_at_a, to + g, None)]
+                plan += [(far_b, g, 0, NEAR, far_at_b, to + g, (0,)), (*zero, far_at_b, to + g, (2,))]
+                if far_over is not None:
+                    plan += [(far_over, g, 0, NEAR, far_at_b, to + g, (1,))]
+        return plan
+
+    def last_groups(own, near_a, near_b, far_a, far_b, far):
+        plan = []
+        for g in range(2):
+            plan += [(own, g, 0, cells, cells, g, None), (near_a, g, 0, NEAR, near_at_a, g, None)]
+            plan += [(near_b, g, 0, NEAR, near_at_b, g, (0, 1)), (*zero, near_at_b, g, (2,))]
+            if far:
+                plan += [(far_a, g, 0, NEAR, far_at_a, g, None)]
+                plan += [(far_b, g, 0, NEAR, far_at_b, g, (0, 1)), (*zero, far_at_b, g, (2,))]
+        return plan
+
+    plan = first_groups(0, 1, 2, None, 3, None, 0, False)
+    near_sums = summed(flags, (own, whole_a, first_near_b, near_over), ((None, plan, True, 2),), (NEAR_BAND,), (), cells, 0)
+    plan = first_groups(0, 1, 2, 3, None, None, 0, True)
+    blocks = (own, whole_a, first_near_b, first_far_b)
+    far_sums = summed(flags, blocks, ((False, plan, True, 2),), (FAR_BAND,), (), cells, 0)
+    far_over, *far_sums = lax.optimization_barrier((first_far_b, *far_sums))
+    far_over = lax.ppermute(far_over, "slab", over_middle)
+    plan = last_groups(0, 1, 2, None, None, False)
+    image = summed(flags, (far_own, near_a, near_b), ((None, plan, False, 2),), (NEAR_BAND,), near_sums, cells, 1)
+    plan = last_groups(0, 1, 2, 3, 4, True)
+    crossing = plan + first_groups(5, 6, None, None, 7, 8, 2, True)
+    crossing = [entry for entry in crossing if entry[0] is not None or entry[5] < 2]
+    crossing = [entry for entry in crossing if entry[-1] != (0,)]
+    blocks = (far_own, near_a, near_b, far_a, far_b, own, whole_a, near_over, far_over)
+    variants = ((False, plan, False, 2), (True, crossing, True, 4))
+    return summed(flags, blocks, variants, (FAR_BAND,), far_sums, cells, 2, image)
 
 
 def solution(mesh):

time: 78.3 us -> 75.1 us (0.959)
  waiting for transfers between devices: 27.7 us -> 22.2 us
  starting transfers between devices: 26.9 us -> 29.6 us
    ppermute x7, waiting for transfers between devices: 25.6 us -> 20.2 us  [trade(): return lax.ppermute(value, ('slab', 'freq'), pairs)]
    ppermute x7, starting transfers between devices: 21.4 us -> 24 us  [trade(): return lax.ppermute(value, ('slab', 'freq'), pairs)]
    pallas_call x2 -> x3, Pallas kernels: 1.7 us -> 2.24 us  [pack(): pl.pallas_call(functools.partial(pack_kernel, copies, len(arrays)), in_sp...]
  transfers between devices with their start and end apart: 12 -> 12, of which waited for: 6 -> 5; matrix products, arithmetic and copies ran while one was open for 0% -> 0% of each run, Pallas kernels for 19% -> 17%
where the time goes in v13:
time: 75.1 us; the launch traced here: 74.9 us
  starting transfers between devices  29.6 us (39%)
  Pallas kernels  22.9 us (30%)
  waiting for transfers between devices  22.2 us (30%)
    ppermute x7, starting transfers between devices, trade(): return lax.ppermute(value, ('slab', 'freq'), pairs)  24 us
    ppermute x7, waiting for transfers between devices, trade(): return lax.ppermute(value, ('slab', 'freq'), pairs)  20.2 us
    pallas_call x4, Pallas kernels, summed(): pl.pallas_call(functools.partial(sum_kernel, variants, len(blocks), bands...  19 us
    ppermute x3, starting transfers between devices, swap(): return lax.ppermute(part, 'freq', [(g, g ^ d) for g in range(GROUPS)])  2.96 us
    pallas_call x3, Pallas kernels, pack(): pl.pallas_call(functools.partial(pack_kernel, copies, len(arrays)), in_sp...  2.24 us
    ppermute x3, waiting for transfers between devices, swap(): return lax.ppermute(part, 'freq', [(g, g ^ d) for g in range(GROUPS)])  1.94 us
    pallas_call x1, Pallas kernels, regrouped(): pl.pallas_call(regroup_kernel, in_specs=[pl.BlockSpec(memory_space=pltpu....  1.66 us
  transfers between devices with their start and end apart: 12, of which 5 were waited for; matrix products, arithmetic and copies ran while one was open for 0% of the time, Pallas kernels for 17%

profile of v13, /device:TPU:8, one launch (start us, length us, event | category | flops | bytes accessed | tf_op | source)
XLA Modules:
  0.0 74.9 jit_solution(18288221323995854867)
XLA Ops:
  0.0 1.7 %regroup.1 = (bf16[2,2,32,16,128]{4,3,2,1,0:T(8,128)(2,1)S(1)}, bf16[2,2,32,16,128]{4,3,2,1,0:T(8,128)(2,1)S(1)}, bf16[2,2,32,16,128]{4,3,2,1,0:T(8,128)(2,1)S(1)}, bf16[2,2,32,16,128]{4,3,2,1,0:T(8,128)(2,1)S(1)}) custom-call(s32[1]{0:T(128)} %bitcast.2.group_ref, bf16[2,2,32,16,256]{4,3,2,1,0:T(8,128)(2,1)} %source_ref.1, ...), custom_call_target="tpu_custom_call" | custom-call | bytes 4194304 | tf_op jit(solution)/shard_map/regroup/pallas_call | solution.py:65
  1.7 0.1 collective-permute-start
  1.8 0.5 collective-permute-start.6
  2.3 0.1 pad_add_fusion.refs_0_.flags_ref
  2.3 1.3 %collective-permute-done.refs_2_ = bf16[2,2,32,16,128]{4,3,2,1,0:T(8,128)(2,1)S(1)} collective-permute-done((bf16[2,2,32,16,128]{4,3,2,1,0:T(8,128)(2,1)S(1)}, bf16[2,2,32,16,128]{4,3,2,1,0:T(8,128)(2,1)S(1)}, u32[]{:S(2)}, u32[]{:S(2)}) %collective-permute-start) | collective-permute-done | bytes 524320 | tf_op jit(solution)/shard_map/ppermute | solution.py:297
  3.7 0.6 pack.3.refs_2_
  4.3 2.4 %collective-permute-start.1 = (bf16[2,2,2,32,16,128]{5,4,3,2,1,0:T(8,128)(2,1)S(1)}, bf16[2,2,2,32,16,128]{5,4,3,2,1,0:T(8,128)(2,1)S(1)}, u32[]{:S(2)}, u32[]{:S(2)}) collective-permute-start(bf16[2,2,2,32,16,128]{5,4,3,2,1,0:T(8,128)(2,1)S(1)} %pack.3.refs_2_), channel_id=1, source_target_pairs={{0,2},{1,3},{2,0},{3,1},{4,6},{5,7},{6,4},{7,5},{8,10},{9,11},{10,... | collective-permute-start | bytes 3145736 | tf_op jit(solution)/shard_map/ppermute | solution.py:297
  6.7 0.0 collective-permute-done.6.refs_2_
  6.7 0.8 %pack.5 = (bf16[2,2,2,32,16,128]{5,4,3,2,1,0:T(8,128)(2,1)S(1)}, bf16[2,2,2,16,16,128]{5,4,3,2,1,0:T(8,128)(2,1)S(1)}, bf16[2,2,2,16,16,128]{5,4,3,2,1,0:T(8,128)(2,1)S(1)}) custom-call(s32[2]{0:T(128)S(1)} %pad_add_fusion.refs_0_.flags_ref, bf16[2,2,32,16,128]{4,3,2,1,0:T(8,128)(2,1)S(1)} %get-tuple-element.24.refs_1_, ...), custom_call_target="tpu_custom_call" | custom-call | bytes 2097152 | tf_op jit(solution)/shard_map/pack/pallas_call | solution.py:107
  7.4 1.6 %collective-permute-start.7 = (bf16[2,2,2,32,16,128]{5,4,3,2,1,0:T(8,128)(2,1)S(1)}, bf16[2,2,2,32,16,128]{5,4,3,2,1,0:T(8,128)(2,1)S(1)}, u32[]{:S(2)}, u32[]{:S(2)}) collective-permute-start(bf16[2,2,2,32,16,128]{5,4,3,2,1,0:T(8,128)(2,1)S(1)} %get-tuple-element.26.refs_0_.refs_5_), channel_id=1, source_target_pairs={{0,4},{1,5},{2,6},{3,7},{4,0},{5,1},{6,2},{7,3},{8,12},{9,13},{10,... | collective-permute-start | bytes 3145736 | tf_op jit(solution)/shard_map/ppermute | solution.py:304
  9.0 7.4 %collective-permute-start.8 = (bf16[2,2,2,16,16,128]{5,4,3,2,1,0:T(8,128)(2,1)S(1)}, bf16[2,2,2,16,16,128]{5,4,3,2,1,0:T(8,128)(2,1)S(1)}, u32[]{:S(2)}, u32[]{:S(2)}) collective-permute-start(bf16[2,2,2,16,16,128]{5,4,3,2,1,0:T(8,128)(2,1)S(1)} %get-tuple-element.27), channel_id=1, source_target_pairs={{0,124},{1,125},{2,126},{3,127},{4,8},{5,9},{6,10},{7,11},{8,4},{9... | collective-permute-start | bytes 1572872 | tf_op jit(solution)/shard_map/ppermute | solution.py:304
  16.4 0.0 collective-permute-start.10
  16.4 12.8 %collective-permute-done.8.refs_2_ = bf16[2,2,2,16,16,128]{5,4,3,2,1,0:T(8,128)(2,1)S(1)} collective-permute-done((bf16[2,2,2,16,16,128]{5,4,3,2,1,0:T(8,128)(2,1)S(1)}, bf16[2,2,2,16,16,128]{5,4,3,2,1,0:T(8,128)(2,1)S(1)}, u32[]{:S(2)}, u32[]{:S(2)}) %collective-permute-start.8) | collective-permute-done | bytes 524320 | tf_op jit(solution)/shard_map/ppermute | solution.py:304
  29.2 1.3 %collective-permute-start.9 = (bf16[2,2,2,16,16,128]{5,4,3,2,1,0:T(8,128)(2,1)S(1)}, bf16[2,2,2,16,16,128]{5,4,3,2,1,0:T(8,128)(2,1)S(1)}, u32[]{:S(2)}, u32[]{:S(2)}) collective-permute-start(bf16[2,2,2,16,16,128]{5,4,3,2,1,0:T(8,128)(2,1)S(1)} %collective-permute-done.8.refs_2_), channel_id=1, source_target_pairs={{0,128},{252,124},{1,129},{253,125},{2,130},{254,126},{3,131},{255... | collective-permute-start | bytes 1572872 | tf_op jit(solution)/shard_map/ppermute | solution.py:330
  30.5 0.6 collective-permute-done.1.refs_1_.refs_0_
  31.1 0.8 %pack.4 = (bf16[2,2,2,16,16,128]{5,4,3,2,1,0:T(8,128)(2,1)S(1)}, bf16[2,2,2,16,16,128]{5,4,3,2,1,0:T(8,128)(2,1)S(1)}, bf16[2,2,2,16,16,128]{5,4,3,2,1,0:T(8,128)(2,1)S(1)}, bf16[2,2,2,16,16,128]{5,4,3,2,1,0:T(8,128)(2,1)S(1)}) custom-call(s32[2]{0:T(128)S(1)} %pad_add_fusion.refs_0_.flags_ref, ...), custom_call_target="tpu_custom_call" | custom-call | bytes 2097152 | tf_op jit(solution)/shard_map/pack/pallas_call | solution.py:107
  31.9 1.6 %collective-permute-start.2 = (bf16[2,2,2,16,16,128]{5,4,3,2,1,0:T(8,128)(2,1)S(1)}, bf16[2,2,2,16,16,128]{5,4,3,2,1,0:T(8,128)(2,1)S(1)}, u32[]{:S(2)}, u32[]{:S(2)}) collective-permute-start(bf16[2,2,2,16,16,128]{5,4,3,2,1,0:T(8,128)(2,1)S(1)} %get-tuple-element.20), channel_id=1, source_target_pairs={{0,4},{1,5},{2,6},{3,7},{4,0},{5,1},{6,2},{7,3},{8,12},{9,13},{10,... | collective-permute-start | bytes 1572872 | tf_op jit(solution)/shard_map/ppermute | solution.py:304
  33.5 10.3 %collective-permute-start.3 = (bf16[2,2,2,16,16,128]{5,4,3,2,1,0:T(8,128)(2,1)S(1)}, bf16[2,2,2,16,16,128]{5,4,3,2,1,0:T(8,128)(2,1)S(1)}, u32[]{:S(2)}, u32[]{:S(2)}) collective-permute-start(bf16[2,2,2,16,16,128]{5,4,3,2,1,0:T(8,128)(2,1)S(1)} %get-tuple-element.21), channel_id=1, source_target_pairs={{0,0},{1,1},{2,2},{3,3},{4,8},{5,9},{6,10},{7,11},{8,4},{9,5},{10,... | collective-permute-start | bytes 1572872 | tf_op jit(solution)/shard_map/ppermute | solution.py:304
  43.8 0.0 collective-permute-done.10.refs_3_
  43.8 0.1 collective-permute-start.4
  43.9 0.0 collective-permute-done.7.refs_1_.refs_6_
  43.9 3.1 %collective-permute-start.5 = (bf16[2,2,2,16,16,128]{5,4,3,2,1,0:T(8,128)(2,1)S(1)}, bf16[2,2,2,16,16,128]{5,4,3,2,1,0:T(8,128)(2,1)S(1)}, u32[]{:S(2)}, u32[]{:S(2)}) collective-permute-start(bf16[2,2,2,16,16,128]{5,4,3,2,1,0:T(8,128)(2,1)S(1)} %get-tuple-element.23), channel_id=1, source_target_pairs={{0,0},{1,1},{2,2},{3,3},{4,8},{5,9},{6,10},{7,11},{8,4},{9,5},{10,... | collective-permute-start | bytes 1572872 | tf_op jit(solution)/shard_map/ppermute | solution.py:304
  47.0 0.6 partial.2.refs_9_
  47.6 0.0 collective-permute-done.9.refs_3_.refs_7_
  47.6 1.3 %collective-permute-start.11 = (bf16[2,2,2,16,16,128]{5,4,3,2,1,0:T(8,128)(2,1)S(1)}, bf16[2,2,2,16,16,128]{5,4,3,2,1,0:T(8,128)(2,1)S(1)}, u32[]{:S(2)}, u32[]{:S(2)}) collective-permute-start(bf16[2,2,2,16,16,128]{5,4,3,2,1,0:T(8,128)(2,1)S(1)} %collective-permute-done.10.refs_3_), channel_id=1, source_target_pairs={{0,128},{252,124},{1,129},{253,125},{2,130},{254,126},{3,131},{255... | collective-permute-start | bytes 1572872 | tf_op jit(solution)/shard_map/ppermute | solution.py:377
  48.9 3.8 %partial.3.refs_3_ = f32[33,32,8,128]{3,2,1,0:T(8,128)S(1)} custom-call(s32[2]{0:T(128)S(1)} %pad_add_fusion.refs_0_.flags_ref, bf16[2,2,2,32,16,128]{5,4,3,2,1,0:T(8,128)(2,1)S(1)} %get-tuple-element.26.refs_0_.refs_5_, bf16[2,2,2,32,16,128]{5,4,3,2,1,0:T(8,128)(2,1)S(1)} %collective-permute-done.7.refs_1_.refs_6_, ...), custom_call_target="tpu_custom_call" | custom-call | flops 17160000 | bytes 4290000 | tf_op jit(solution)/shard_map/partial/pallas_call | solution.py:270
  52.7 0.0 collective-permute-done.2.refs_1_
  52.7 3.9 %collective-permute-done.3.refs_2_ = bf16[2,2,2,16,16,128]{5,4,3,2,1,0:T(8,128)(2,1)S(1)} collective-permute-done((bf16[2,2,2,16,16,128]{5,4,3,2,1,0:T(8,128)(2,1)S(1)}, bf16[2,2,2,16,16,128]{5,4,3,2,1,0:T(8,128)(2,1)S(1)}, u32[]{:S(2)}, u32[]{:S(2)}) %collective-permute-start.3) | collective-permute-done | bytes 524320 | tf_op jit(solution)/shard_map/ppermute | solution.py:304
  56.6 5.9 %image.2.refs_10_ = f32[4,65,32,256]{3,2,1,0:T(8,128)} custom-call(s32[2]{0:T(128)S(1)} %pad_add_fusion.refs_0_.flags_ref, bf16[2,2,2,32,16,128]{5,4,3,2,1,0:T(8,128)(2,1)S(1)} %collective-permute-done.1.refs_1_.refs_0_, bf16[2,2,2,16,16,128]{5,4,3,2,1,0:T(8,128)(2,1)S(1)} %collective-permute-done.2.refs_1_, ...), custom_call_target="tpu_custom_call" | custom-call | flops 17160000 | bytes 4290000 | tf_op jit(solution)/shard_map/image/pallas_call | solution.py:270
  62.6 0.0 collective-permute-done.4.refs_3_
  62.6 3.6 %collective-permute-done.5.refs_4_ = bf16[2,2,2,16,16,128]{5,4,3,2,1,0:T(8,128)(2,1)S(1)} collective-permute-done((bf16[2,2,2,16,16,128]{5,4,3,2,1,0:T(8,128)(2,1)S(1)}, bf16[2,2,2,16,16,128]{5,4,3,2,1,0:T(8,128)(2,1)S(1)}, u32[]{:S(2)}, u32[]{:S(2)}) %collective-permute-start.5) | collective-permute-done | bytes 524320 | tf_op jit(solution)/shard_map/ppermute | solution.py:304
  66.2 0.0 collective-permute-done.11.refs_8_
  66.2 8.8 %image.3 = f32[4,65,32,256]{3,2,1,0:T(8,128)} custom-call(s32[2]{0:T(128)S(1)} %pad_add_fusion.refs_0_.flags_ref, bf16[2,2,2,32,16,128]{5,4,3,2,1,0:T(8,128)(2,1)S(1)} %collective-permute-done.1.refs_1_.refs_0_, bf16[2,2,2,16,16,128]{5,4,3,2,1,0:T(8,128)(2,1)S(1)} %collective-permute-done.2.refs_1_, ...), custom_call_target="tpu_custom_call", output_to_operand_aliasing={{}: (11, {})} | custom-call | flops 16640000 | bytes 4160000 | tf_op jit(solution)/shard_map/image/pallas_call | solution.py:270
Async XLA Ops:
  1.7 2.0 %collective-permute-start = (bf16[2,2,32,16,128]{4,3,2,1,0:T(8,128)(2,1)S(1)}, bf16[2,2,32,16,128]{4,3,2,1,0:T(8,128)(2,1)S(1)}, u32[]{:S(2)}, u32[]{:S(2)}) collective-permute-start(bf16[2,2,32,16,128]{4,3,2,1,0:T(8,128)(2,1)S(1)} %get-tuple-element.19), channel_id=1, source_target_pairs={{0,1},{1,0},{2,3},{3,2},{4,5},{5,4},{6,7},{7,6},{8,9},{9,8},{10,11... | collective-permute-start | bytes 1572872 | tf_op jit(solution)/shard_map/ppermute | solution.py:297
  1.8 4.9 %collective-permute-start.6 = (bf16[2,2,32,16,128]{4,3,2,1,0:T(8,128)(2,1)S(1)}, bf16[2,2,32,16,128]{4,3,2,1,0:T(8,128)(2,1)S(1)}, u32[]{:S(2)}, u32[]{:S(2)}) collective-permute-start(bf16[2,2,32,16,128]{4,3,2,1,0:T(8,128)(2,1)S(1)} %get-tuple-element.25), channel_id=1, source_target_pairs={{0,1},{1,0},{2,3},{3,2},{4,5},{5,4},{6,7},{7,6},{8,9},{9,8},{10,11... | collective-permute-start | bytes 1572872 | tf_op jit(solution)/shard_map/ppermute | solution.py:297
  4.3 26.8 %collective-permute-start.1 = (bf16[2,2,2,32,16,128]{5,4,3,2,1,0:T(8,128)(2,1)S(1)}, bf16[2,2,2,32,16,128]{5,4,3,2,1,0:T(8,128)(2,1)S(1)}, u32[]{:S(2)}, u32[]{:S(2)}) collective-permute-start(bf16[2,2,2,32,16,128]{5,4,3,2,1,0:T(8,128)(2,1)S(1)} %pack.3.refs_2_), channel_id=1, source_target_pairs={{0,2},{1,3},{2,0},{3,1},{4,6},{5,7},{6,4},{7,5},{8,10},{9,11},{10,... | collective-permute-start | bytes 3145736 | tf_op jit(solution)/shard_map/ppermute | solution.py:297
  7.4 36.5 %collective-permute-start.7 = (bf16[2,2,2,32,16,128]{5,4,3,2,1,0:T(8,128)(2,1)S(1)}, bf16[2,2,2,32,16,128]{5,4,3,2,1,0:T(8,128)(2,1)S(1)}, u32[]{:S(2)}, u32[]{:S(2)}) collective-permute-start(bf16[2,2,2,32,16,128]{5,4,3,2,1,0:T(8,128)(2,1)S(1)} %get-tuple-element.26.refs_0_.refs_5_), channel_id=1, source_target_pairs={{0,4},{1,5},{2,6},{3,7},{4,0},{5,1},{6,2},{7,3},{8,12},{9,13},{10,... | collective-permute-start | bytes 3145736 | tf_op jit(solution)/shard_map/ppermute | solution.py:304
  9.0 20.2 %collective-permute-start.8 = (bf16[2,2,2,16,16,128]{5,4,3,2,1,0:T(8,128)(2,1)S(1)}, bf16[2,2,2,16,16,128]{5,4,3,2,1,0:T(8,128)(2,1)S(1)}, u32[]{:S(2)}, u32[]{:S(2)}) collective-permute-start(bf16[2,2,2,16,16,128]{5,4,3,2,1,0:T(8,128)(2,1)S(1)} %get-tuple-element.27), channel_id=1, source_target_pairs={{0,124},{1,125},{2,126},{3,127},{4,8},{5,9},{6,10},{7,11},{8,4},{9... | collective-permute-start | bytes 1572872 | tf_op jit(solution)/shard_map/ppermute | solution.py:304
  16.4 27.4 %collective-permute-start.10 = (bf16[2,2,2,16,16,128]{5,4,3,2,1,0:T(8,128)(2,1)S(1)}, bf16[2,2,2,16,16,128]{5,4,3,2,1,0:T(8,128)(2,1)S(1)}, u32[]{:S(2)}, u32[]{:S(2)}) collective-permute-start(bf16[2,2,2,16,16,128]{5,4,3,2,1,0:T(8,128)(2,1)S(1)} %get-tuple-element.28), channel_id=1, source_target_pairs={{0,124},{1,125},{2,126},{3,127},{4,8},{5,9},{6,10},{7,11},{8,4},{9... | collective-permute-start | bytes 1572872 | tf_op jit(solution)/shard_map/ppermute | solution.py:304
  29.2 18.4 %collective-permute-start.9 = (bf16[2,2,2,16,16,128]{5,4,3,2,1,0:T(8,128)(2,1)S(1)}, bf16[2,2,2,16,16,128]{5,4,3,2,1,0:T(8,128)(2,1)S(1)}, u32[]{:S(2)}, u32[]{:S(2)}) collective-permute-start(bf16[2,2,2,16,16,128]{5,4,3,2,1,0:T(8,128)(2,1)S(1)} %collective-permute-done.8.refs_2_), channel_id=1, source_target_pairs={{0,128},{252,124},{1,129},{253,125},{2,130},{254,126},{3,131},{255... | collective-permute-start | bytes 1572872 | tf_op jit(solution)/shard_map/ppermute | solution.py:330
  31.9 20.8 %collective-permute-start.2 = (bf16[2,2,2,16,16,128]{5,4,3,2,1,0:T(8,128)(2,1)S(1)}, bf16[2,2,2,16,16,128]{5,4,3,2,1,0:T(8,128)(2,1)S(1)}, u32[]{:S(2)}, u32[]{:S(2)}) collective-permute-start(bf16[2,2,2,16,16,128]{5,4,3,2,1,0:T(8,128)(2,1)S(1)} %get-tuple-element.20), channel_id=1, source_target_pairs={{0,4},{1,5},{2,6},{3,7},{4,0},{5,1},{6,2},{7,3},{8,12},{9,13},{10,... | collective-permute-start | bytes 1572872 | tf_op jit(solution)/shard_map/ppermute | solution.py:304
  33.5 23.1 %collective-permute-start.3 = (bf16[2,2,2,16,16,128]{5,4,3,2,1,0:T(8,128)(2,1)S(1)}, bf16[2,2,2,16,16,128]{5,4,3,2,1,0:T(8,128)(2,1)S(1)}, u32[]{:S(2)}, u32[]{:S(2)}) collective-permute-start(bf16[2,2,2,16,16,128]{5,4,3,2,1,0:T(8,128)(2,1)S(1)} %get-tuple-element.21), channel_id=1, source_target_pairs={{0,0},{1,1},{2,2},{3,3},{4,8},{5,9},{6,10},{7,11},{8,4},{9,5},{10,... | collective-permute-start | bytes 1572872 | tf_op jit(solution)/shard_map/ppermute | solution.py:304
  43.8 18.7 %collective-permute-start.4 = (bf16[2,2,2,16,16,128]{5,4,3,2,1,0:T(8,128)(2,1)S(1)}, bf16[2,2,2,16,16,128]{5,4,3,2,1,0:T(8,128)(2,1)S(1)}, u32[]{:S(2)}, u32[]{:S(2)}) collective-permute-start(bf16[2,2,2,16,16,128]{5,4,3,2,1,0:T(8,128)(2,1)S(1)} %get-tuple-element.22), channel_id=1, source_target_pairs={{0,4},{1,5},{2,6},{3,7},{4,0},{5,1},{6,2},{7,3},{8,12},{9,13},{10,... | collective-permute-start | bytes 1572872 | tf_op jit(solution)/shard_map/ppermute | solution.py:304
  43.9 22.2 %collective-permute-start.5 = (bf16[2,2,2,16,16,128]{5,4,3,2,1,0:T(8,128)(2,1)S(1)}, bf16[2,2,2,16,16,128]{5,4,3,2,1,0:T(8,128)(2,1)S(1)}, u32[]{:S(2)}, u32[]{:S(2)}) collective-permute-start(bf16[2,2,2,16,16,128]{5,4,3,2,1,0:T(8,128)(2,1)S(1)} %get-tuple-element.23), channel_id=1, source_target_pairs={{0,0},{1,1},{2,2},{3,3},{4,8},{5,9},{6,10},{7,11},{8,4},{9,5},{10,... | collective-permute-start | bytes 1572872 | tf_op jit(solution)/shard_map/ppermute | solution.py:304
  47.6 18.6 %collective-permute-start.11 = (bf16[2,2,2,16,16,128]{5,4,3,2,1,0:T(8,128)(2,1)S(1)}, bf16[2,2,2,16,16,128]{5,4,3,2,1,0:T(8,128)(2,1)S(1)}, u32[]{:S(2)}, u32[]{:S(2)}) collective-permute-start(bf16[2,2,2,16,16,128]{5,4,3,2,1,0:T(8,128)(2,1)S(1)} %collective-permute-done.10.refs_3_), channel_id=1, source_target_pairs={{0,128},{252,124},{1,129},{253,125},{2,130},{254,126},{3,131},{255... | collective-permute-start | bytes 1572872 | tf_op jit(solution)/shard_map/ppermute | solution.py:377

commit v14 on v13

--- a/solution.py
+++ b/solution.py
@@ -127,17 +127,17 @@
 def sum_body(plan, count, groups, bands, first, last, flags_ref, *refs):
     blocks, refs = refs[:count], refs[count:]
     befores = ()
-    if last:
+    if last in (1, 2):
         befores, refs = refs[: len(bands)], refs[len(bands) :]
-    if last == 2:
+    if last >= 2:
         refs = refs[1:]
+    last = last % 3
     outs = refs[: 1 if last else len(bands)]
     fields = refs[len(outs)]
     if last:
         turn, stage, sems = refs[len(outs) + 1 :]
         out_ref = outs[0]
     cells = stage.shape[4 - 1] if last else outs[0].shape[1]
-    total_freqs = 2 * groups
 
     def fill(index, part, at, length, to, group):
         start, to = by_parity(flags_ref, at), by_parity(flags_ref, to)
@@ -163,14 +163,14 @@
         else:
             pl.when(functools.reduce(jnp.logical_or, [flags_ref[1] == value for value in values]))(place)
 
-    def tile(before, out, k0, row0, rows, x0, slot):
+    def tile(before, out, k0, row0, rows, x0, slot, fresh, freqs):
         s0 = x0 + 2 * HMAX - k0 - (rows - 1)
         r0 = x0 + k0
-        if first:
+        if fresh:
             total = [[None] * TX for _ in range(rows)]
         else:
             total = [[before[row0 + j, x0 + i] for i in range(TX)] for j in range(rows)]
-        for f in range(total_freqs):
+        for f in range(freqs):
             for c in range(2):
                 s = [fields[0, s0 + i, f, 8 * c : 8 * c + 8] for i in range(TX + rows - 1)]
                 r = [fields[1, r0 + i, f, 8 * c : 8 * c + 8] for i in range(TX + rows - 1)]
@@ -204,11 +204,18 @@
             return k0 if not jump else k0 + jnp.where(step >= jump_at, jump, 0)
 
         def rows_of(k0, row0, rows, slot):
-            def x_step(xt, _):
-                tile(before, out, k0, row0, rows, xt * TX, slot)
+            def x_step(start, fresh, freqs, xt, _):
+                tile(before, out, k0, row0, rows, (start + xt) * TX, slot, fresh, freqs)
                 return 0
 
-            lax.fori_loop(0, cells // TX, x_step, 0)
+            if first == "half":
+                middle = cells // TX // 2
+                beside = functools.partial(x_step, by_parity(flags_ref, (0, middle)), True, 2 * groups)
+                lax.fori_loop(0, middle, beside, 0)
+                other = functools.partial(x_step, by_parity(flags_ref, (middle, 0)), False, 4)
+                lax.fori_loop(0, middle, other, 0)
+            else:
+                lax.fori_loop(0, cells // TX, functools.partial(x_step, 0, first, 2 * groups), 0)
 
         def h_step(step, _):
             slot = lax.rem(step, SLOTS)
@@ -267,8 +274,12 @@
     else:
         out_shape = [pltpu.VMEM((height, cells, 8, LANES), jnp.float32) for height in heights]
         out_specs = [vmem] * len(heights)
+        if image is not None:
+            operands.append(image)
+            in_specs.append(vmem)
+            aliases = {len(operands): 0}
     return pl.pallas_call(
-        functools.partial(sum_kernel, variants, len(blocks), bands, last),
+        functools.partial(sum_kernel, variants, len(blocks), bands, last if image is None or last else 3),
         in_specs=in_specs,
         out_specs=out_specs,
         out_shape=out_shape,
@@ -375,6 +386,11 @@
     far_sums = summed(flags, blocks, ((False, plan, True, 2),), (FAR_BAND,), (), cells, 0)
     far_over, *far_sums = lax.optimization_barrier((first_far_b, *far_sums))
     far_over = lax.ppermute(far_over, "slab", over_middle)
+    plan = first_groups(0, 1, None, None, 2, None, 0, True)
+    plan = [entry for entry in plan if entry[-1] != (0,)] + [(*zero, far_at_b, g, (1,)) for g in range(2)]
+    far_sums = summed(
+        flags, (own, whole_a, near_over), ((True, plan, True, 2),), (FAR_BAND,), (), cells, 0, far_sums[0]
+    )
     plan = last_groups(0, 1, 2, None, None, False)
     image = summed(flags, (far_own, near_a, near_b), ((None, plan, False, 2),), (NEAR_BAND,), near_sums, cells, 1)
     plan = last_groups(0, 1, 2, 3, 4, True)
@@ -382,7 +398,7 @@
     crossing = [entry for entry in crossing if entry[0] is not None or entry[5] < 2]
     crossing = [entry for entry in crossing if entry[-1] != (0,)]
     blocks = (far_own, near_a, near_b, far_a, far_b, own, whole_a, near_over, far_over)
-    variants = ((False, plan, False, 2), (True, crossing, True, 4))
+    variants = ((False, plan, False, 2), (True, crossing, "half", 4))
     return summed(flags, blocks, variants, (FAR_BAND,), far_sums, cells, 2, image)
 
 

time: 75.1 us -> 74.1 us (0.987)
  waiting for transfers between devices: 22.2 us -> 18.3 us
  Pallas kernels: 22.9 us -> 25.9 us
    ppermute x7, waiting for transfers between devices: 20.2 us -> 16.3 us  [trade(): return lax.ppermute(value, ('slab', 'freq'), pairs)]
    pallas_call x4 -> x5, Pallas kernels: 19 us -> 22 us  [summed(): pl.pallas_call(functools.partial(sum_kernel, variants, len(blocks), bands...]
  transfers between devices with their start and end apart: 12 -> 12, of which waited for: 5 -> 4; matrix products, arithmetic and copies ran while one was open for 0% -> 0% of each run, Pallas kernels for 17% -> 22%
where the time goes in v14:
time: 74.1 us; the launch traced here: 73.9 us
  starting transfers between devices  29.6 us (40%)
  Pallas kernels  25.9 us (35%)
  waiting for transfers between devices  18.3 us (25%)
    ppermute x7, starting transfers between devices, trade(): return lax.ppermute(value, ('slab', 'freq'), pairs)  24 us
    pallas_call x5, Pallas kernels, summed(): pl.pallas_call(functools.partial(sum_kernel, variants, len(blocks), bands...  22 us
    ppermute x7, waiting for transfers between devices, trade(): return lax.ppermute(value, ('slab', 'freq'), pairs)  16.3 us
    ppermute x3, starting transfers between devices, swap(): return lax.ppermute(part, 'freq', [(g, g ^ d) for g in range(GROUPS)])  2.96 us
    pallas_call x3, Pallas kernels, pack(): pl.pallas_call(functools.partial(pack_kernel, copies, len(arrays)), in_sp...  2.24 us
    ppermute x3, waiting for transfers between devices, swap(): return lax.ppermute(part, 'freq', [(g, g ^ d) for g in range(GROUPS)])  1.94 us
    pallas_call x1, Pallas kernels, regrouped(): pl.pallas_call(regroup_kernel, in_specs=[pl.BlockSpec(memory_space=pltpu....  1.66 us
  transfers between devices with their start and end apart: 12, of which 4 were waited for; matrix products, arithmetic and copies ran while one was open for 0% of the time, Pallas kernels for 22%

profile of v14, /device:TPU:8, one launch (start us, length us, event | category | flops | bytes accessed | tf_op | source)
XLA Modules:
  0.0 73.9 jit_solution(11331827917926142990)
XLA Ops:
  0.0 1.7 %regroup.1 = (bf16[2,2,32,16,128]{4,3,2,1,0:T(8,128)(2,1)S(1)}, bf16[2,2,32,16,128]{4,3,2,1,0:T(8,128)(2,1)S(1)}, bf16[2,2,32,16,128]{4,3,2,1,0:T(8,128)(2,1)S(1)}, bf16[2,2,32,16,128]{4,3,2,1,0:T(8,128)(2,1)S(1)}) custom-call(s32[1]{0:T(128)} %bitcast.2.group_ref, bf16[2,2,32,16,256]{4,3,2,1,0:T(8,128)(2,1)} %source_ref.1, ...), custom_call_target="tpu_custom_call" | custom-call | bytes 4194304 | tf_op jit(solution)/shard_map/regroup/pallas_call | solution.py:65
  1.7 0.1 collective-permute-start
  1.8 0.5 collective-permute-start.6
  2.3 0.1 pad_add_fusion.refs_0_.flags_ref
  2.3 1.3 %collective-permute-done.refs_2_ = bf16[2,2,32,16,128]{4,3,2,1,0:T(8,128)(2,1)S(1)} collective-permute-done((bf16[2,2,32,16,128]{4,3,2,1,0:T(8,128)(2,1)S(1)}, bf16[2,2,32,16,128]{4,3,2,1,0:T(8,128)(2,1)S(1)}, u32[]{:S(2)}, u32[]{:S(2)}) %collective-permute-start) | collective-permute-done | bytes 524320 | tf_op jit(solution)/shard_map/ppermute | solution.py:308
  3.7 0.6 pack.3.refs_2_
  4.3 2.4 %collective-permute-start.1 = (bf16[2,2,2,32,16,128]{5,4,3,2,1,0:T(8,128)(2,1)S(1)}, bf16[2,2,2,32,16,128]{5,4,3,2,1,0:T(8,128)(2,1)S(1)}, u32[]{:S(2)}, u32[]{:S(2)}) collective-permute-start(bf16[2,2,2,32,16,128]{5,4,3,2,1,0:T(8,128)(2,1)S(1)} %pack.3.refs_2_), channel_id=1, source_target_pairs={{0,2},{1,3},{2,0},{3,1},{4,6},{5,7},{6,4},{7,5},{8,10},{9,11},{10,... | collective-permute-start | bytes 3145736 | tf_op jit(solution)/shard_map/ppermute | solution.py:308
  6.7 0.0 collective-permute-done.6.refs_2_
  6.7 0.8 %pack.5 = (bf16[2,2,2,32,16,128]{5,4,3,2,1,0:T(8,128)(2,1)S(1)}, bf16[2,2,2,16,16,128]{5,4,3,2,1,0:T(8,128)(2,1)S(1)}, bf16[2,2,2,16,16,128]{5,4,3,2,1,0:T(8,128)(2,1)S(1)}) custom-call(s32[2]{0:T(128)S(1)} %pad_add_fusion.refs_0_.flags_ref, bf16[2,2,32,16,128]{4,3,2,1,0:T(8,128)(2,1)S(1)} %get-tuple-element.24.refs_1_, ...), custom_call_target="tpu_custom_call" | custom-call | bytes 2097152 | tf_op jit(solution)/shard_map/pack/pallas_call | solution.py:107
  7.4 1.6 %collective-permute-start.7 = (bf16[2,2,2,32,16,128]{5,4,3,2,1,0:T(8,128)(2,1)S(1)}, bf16[2,2,2,32,16,128]{5,4,3,2,1,0:T(8,128)(2,1)S(1)}, u32[]{:S(2)}, u32[]{:S(2)}) collective-permute-start(bf16[2,2,2,32,16,128]{5,4,3,2,1,0:T(8,128)(2,1)S(1)} %get-tuple-element.26.refs_0_.refs_5_), channel_id=1, source_target_pairs={{0,4},{1,5},{2,6},{3,7},{4,0},{5,1},{6,2},{7,3},{8,12},{9,13},{10,... | collective-permute-start | bytes 3145736 | tf_op jit(solution)/shard_map/ppermute | solution.py:315
  9.0 7.4 %collective-permute-start.8 = (bf16[2,2,2,16,16,128]{5,4,3,2,1,0:T(8,128)(2,1)S(1)}, bf16[2,2,2,16,16,128]{5,4,3,2,1,0:T(8,128)(2,1)S(1)}, u32[]{:S(2)}, u32[]{:S(2)}) collective-permute-start(bf16[2,2,2,16,16,128]{5,4,3,2,1,0:T(8,128)(2,1)S(1)} %get-tuple-element.27), channel_id=1, source_target_pairs={{0,124},{1,125},{2,126},{3,127},{4,8},{5,9},{6,10},{7,11},{8,4},{9... | collective-permute-start | bytes 1572872 | tf_op jit(solution)/shard_map/ppermute | solution.py:315
  16.4 0.0 collective-permute-start.10
  16.4 12.8 %collective-permute-done.8.refs_2_ = bf16[2,2,2,16,16,128]{5,4,3,2,1,0:T(8,128)(2,1)S(1)} collective-permute-done((bf16[2,2,2,16,16,128]{5,4,3,2,1,0:T(8,128)(2,1)S(1)}, bf16[2,2,2,16,16,128]{5,4,3,2,1,0:T(8,128)(2,1)S(1)}, u32[]{:S(2)}, u32[]{:S(2)}) %collective-permute-start.8) | collective-permute-done | bytes 524320 | tf_op jit(solution)/shard_map/ppermute | solution.py:315
  29.2 1.3 %collective-permute-start.9 = (bf16[2,2,2,16,16,128]{5,4,3,2,1,0:T(8,128)(2,1)S(1)}, bf16[2,2,2,16,16,128]{5,4,3,2,1,0:T(8,128)(2,1)S(1)}, u32[]{:S(2)}, u32[]{:S(2)}) collective-permute-start(bf16[2,2,2,16,16,128]{5,4,3,2,1,0:T(8,128)(2,1)S(1)} %collective-permute-done.8.refs_2_), channel_id=1, source_target_pairs={{0,128},{252,124},{1,129},{253,125},{2,130},{254,126},{3,131},{255... | collective-permute-start | bytes 1572872 | tf_op jit(solution)/shard_map/ppermute | solution.py:341
  30.5 0.6 collective-permute-done.1.refs_1_.refs_0_
  31.1 0.8 %pack.4 = (bf16[2,2,2,16,16,128]{5,4,3,2,1,0:T(8,128)(2,1)S(1)}, bf16[2,2,2,16,16,128]{5,4,3,2,1,0:T(8,128)(2,1)S(1)}, bf16[2,2,2,16,16,128]{5,4,3,2,1,0:T(8,128)(2,1)S(1)}, bf16[2,2,2,16,16,128]{5,4,3,2,1,0:T(8,128)(2,1)S(1)}) custom-call(s32[2]{0:T(128)S(1)} %pad_add_fusion.refs_0_.flags_ref, ...), custom_call_target="tpu_custom_call" | custom-call | bytes 2097152 | tf_op jit(solution)/shard_map/pack/pallas_call | solution.py:107
  31.9 1.6 %collective-permute-start.2 = (bf16[2,2,2,16,16,128]{5,4,3,2,1,0:T(8,128)(2,1)S(1)}, bf16[2,2,2,16,16,128]{5,4,3,2,1,0:T(8,128)(2,1)S(1)}, u32[]{:S(2)}, u32[]{:S(2)}) collective-permute-start(bf16[2,2,2,16,16,128]{5,4,3,2,1,0:T(8,128)(2,1)S(1)} %get-tuple-element.20), channel_id=1, source_target_pairs={{0,4},{1,5},{2,6},{3,7},{4,0},{5,1},{6,2},{7,3},{8,12},{9,13},{10,... | collective-permute-start | bytes 1572872 | tf_op jit(solution)/shard_map/ppermute | solution.py:315
  33.5 10.3 %collective-permute-start.3 = (bf16[2,2,2,16,16,128]{5,4,3,2,1,0:T(8,128)(2,1)S(1)}, bf16[2,2,2,16,16,128]{5,4,3,2,1,0:T(8,128)(2,1)S(1)}, u32[]{:S(2)}, u32[]{:S(2)}) collective-permute-start(bf16[2,2,2,16,16,128]{5,4,3,2,1,0:T(8,128)(2,1)S(1)} %get-tuple-element.21), channel_id=1, source_target_pairs={{0,0},{1,1},{2,2},{3,3},{4,8},{5,9},{6,10},{7,11},{8,4},{9,5},{10,... | collective-permute-start | bytes 1572872 | tf_op jit(solution)/shard_map/ppermute | solution.py:315
  43.8 0.0 collective-permute-done.10.refs_3_
  43.8 0.1 collective-permute-start.4
  43.9 0.0 collective-permute-done.7.refs_1_.refs_6_
  43.9 3.1 %collective-permute-start.5 = (bf16[2,2,2,16,16,128]{5,4,3,2,1,0:T(8,128)(2,1)S(1)}, bf16[2,2,2,16,16,128]{5,4,3,2,1,0:T(8,128)(2,1)S(1)}, u32[]{:S(2)}, u32[]{:S(2)}) collective-permute-start(bf16[2,2,2,16,16,128]{5,4,3,2,1,0:T(8,128)(2,1)S(1)} %get-tuple-element.23), channel_id=1, source_target_pairs={{0,0},{1,1},{2,2},{3,3},{4,8},{5,9},{6,10},{7,11},{8,4},{9,5},{10,... | collective-permute-start | bytes 1572872 | tf_op jit(solution)/shard_map/ppermute | solution.py:315
  47.0 0.6 partial.3.refs_3_
  47.6 0.0 collective-permute-done.9.refs_2_.refs_3_.refs_7_
  47.6 1.3 %collective-permute-start.11 = (bf16[2,2,2,16,16,128]{5,4,3,2,1,0:T(8,128)(2,1)S(1)}, bf16[2,2,2,16,16,128]{5,4,3,2,1,0:T(8,128)(2,1)S(1)}, u32[]{:S(2)}, u32[]{:S(2)}) collective-permute-start(bf16[2,2,2,16,16,128]{5,4,3,2,1,0:T(8,128)(2,1)S(1)} %collective-permute-done.10.refs_3_), channel_id=1, source_target_pairs={{0,128},{252,124},{1,129},{253,125},{2,130},{254,126},{3,131},{255... | collective-permute-start | bytes 1572872 | tf_op jit(solution)/shard_map/ppermute | solution.py:388
  48.9 3.9 %partial.4.refs_9_ = f32[32,32,8,128]{3,2,1,0:T(8,128)S(1)} custom-call(s32[2]{0:T(128)S(1)} %pad_add_fusion.refs_0_.flags_ref, bf16[2,2,2,32,16,128]{5,4,3,2,1,0:T(8,128)(2,1)S(1)} %get-tuple-element.26.refs_0_.refs_5_, bf16[2,2,2,32,16,128]{5,4,3,2,1,0:T(8,128)(2,1)S(1)} %collective-permute-done.7.refs_1_.refs_6_, ...), custom_call_target="tpu_custom_call", output_to_operand_aliasing={{}: (4, {})} | custom-call | flops 16640000 | bytes 4160000 | tf_op jit(solution)/shard_map/partial/pallas_call | solution.py:281
  52.8 3.8 %partial.5.refs_3_ = f32[33,32,8,128]{3,2,1,0:T(8,128)S(1)} custom-call(s32[2]{0:T(128)S(1)} %pad_add_fusion.refs_0_.flags_ref, bf16[2,2,2,32,16,128]{5,4,3,2,1,0:T(8,128)(2,1)S(1)} %get-tuple-element.26.refs_0_.refs_5_, bf16[2,2,2,32,16,128]{5,4,3,2,1,0:T(8,128)(2,1)S(1)} %collective-permute-done.7.refs_1_.refs_6_, ...), custom_call_target="tpu_custom_call" | custom-call | flops 17160000 | bytes 4290000 | tf_op jit(solution)/shard_map/partial/pallas_call | solution.py:281
  56.7 0.0 collective-permute-done.2.refs_1_
  56.7 0.0 collective-permute-done.3.refs_2_
  56.7 5.9 %image.2.refs_10_ = f32[4,65,32,256]{3,2,1,0:T(8,128)} custom-call(s32[2]{0:T(128)S(1)} %pad_add_fusion.refs_0_.flags_ref, bf16[2,2,2,32,16,128]{5,4,3,2,1,0:T(8,128)(2,1)S(1)} %collective-permute-done.1.refs_1_.refs_0_, bf16[2,2,2,16,16,128]{5,4,3,2,1,0:T(8,128)(2,1)S(1)} %collective-permute-done.2.refs_1_, ...), custom_call_target="tpu_custom_call" | custom-call | flops 17160000 | bytes 4290000 | tf_op jit(solution)/shard_map/image/pallas_call | solution.py:281
  62.6 0.0 collective-permute-done.4.refs_3_
  62.6 3.5 %collective-permute-done.5.refs_4_ = bf16[2,2,2,16,16,128]{5,4,3,2,1,0:T(8,128)(2,1)S(1)} collective-permute-done((bf16[2,2,2,16,16,128]{5,4,3,2,1,0:T(8,128)(2,1)S(1)}, bf16[2,2,2,16,16,128]{5,4,3,2,1,0:T(8,128)(2,1)S(1)}, u32[]{:S(2)}, u32[]{:S(2)}) %collective-permute-start.5) | collective-permute-done | bytes 524320 | tf_op jit(solution)/shard_map/ppermute | solution.py:315
  66.2 0.0 collective-permute-done.11.refs_8_
  66.2 7.8 %image.3 = f32[4,65,32,256]{3,2,1,0:T(8,128)} custom-call(s32[2]{0:T(128)S(1)} %pad_add_fusion.refs_0_.flags_ref, bf16[2,2,2,32,16,128]{5,4,3,2,1,0:T(8,128)(2,1)S(1)} %collective-permute-done.1.refs_1_.refs_0_, bf16[2,2,2,16,16,128]{5,4,3,2,1,0:T(8,128)(2,1)S(1)} %collective-permute-done.2.refs_1_, ...), custom_call_target="tpu_custom_call", output_to_operand_aliasing={{}: (11, {})} | custom-call | flops 16640000 | bytes 4160000 | tf_op jit(solution)/shard_map/image/pallas_call | solution.py:281
Async XLA Ops:
  1.7 2.0 %collective-permute-start = (bf16[2,2,32,16,128]{4,3,2,1,0:T(8,128)(2,1)S(1)}, bf16[2,2,32,16,128]{4,3,2,1,0:T(8,128)(2,1)S(1)}, u32[]{:S(2)}, u32[]{:S(2)}) collective-permute-start(bf16[2,2,32,16,128]{4,3,2,1,0:T(8,128)(2,1)S(1)} %get-tuple-element.19), channel_id=1, source_target_pairs={{0,1},{1,0},{2,3},{3,2},{4,5},{5,4},{6,7},{7,6},{8,9},{9,8},{10,11... | collective-permute-start | bytes 1572872 | tf_op jit(solution)/shard_map/ppermute | solution.py:308
  1.8 4.9 %collective-permute-start.6 = (bf16[2,2,32,16,128]{4,3,2,1,0:T(8,128)(2,1)S(1)}, bf16[2,2,32,16,128]{4,3,2,1,0:T(8,128)(2,1)S(1)}, u32[]{:S(2)}, u32[]{:S(2)}) collective-permute-start(bf16[2,2,32,16,128]{4,3,2,1,0:T(8,128)(2,1)S(1)} %get-tuple-element.25), channel_id=1, source_target_pairs={{0,1},{1,0},{2,3},{3,2},{4,5},{5,4},{6,7},{7,6},{8,9},{9,8},{10,11... | collective-permute-start | bytes 1572872 | tf_op jit(solution)/shard_map/ppermute | solution.py:308
  4.3 26.8 %collective-permute-start.1 = (bf16[2,2,2,32,16,128]{5,4,3,2,1,0:T(8,128)(2,1)S(1)}, bf16[2,2,2,32,16,128]{5,4,3,2,1,0:T(8,128)(2,1)S(1)}, u32[]{:S(2)}, u32[]{:S(2)}) collective-permute-start(bf16[2,2,2,32,16,128]{5,4,3,2,1,0:T(8,128)(2,1)S(1)} %pack.3.refs_2_), channel_id=1, source_target_pairs={{0,2},{1,3},{2,0},{3,1},{4,6},{5,7},{6,4},{7,5},{8,10},{9,11},{10,... | collective-permute-start | bytes 3145736 | tf_op jit(solution)/shard_map/ppermute | solution.py:308
  7.4 36.5 %collective-permute-start.7 = (bf16[2,2,2,32,16,128]{5,4,3,2,1,0:T(8,128)(2,1)S(1)}, bf16[2,2,2,32,16,128]{5,4,3,2,1,0:T(8,128)(2,1)S(1)}, u32[]{:S(2)}, u32[]{:S(2)}) collective-permute-start(bf16[2,2,2,32,16,128]{5,4,3,2,1,0:T(8,128)(2,1)S(1)} %get-tuple-element.26.refs_0_.refs_5_), channel_id=1, source_target_pairs={{0,4},{1,5},{2,6},{3,7},{4,0},{5,1},{6,2},{7,3},{8,12},{9,13},{10,... | collective-permute-start | bytes 3145736 | tf_op jit(solution)/shard_map/ppermute | solution.py:315
  9.0 20.2 %collective-permute-start.8 = (bf16[2,2,2,16,16,128]{5,4,3,2,1,0:T(8,128)(2,1)S(1)}, bf16[2,2,2,16,16,128]{5,4,3,2,1,0:T(8,128)(2,1)S(1)}, u32[]{:S(2)}, u32[]{:S(2)}) collective-permute-start(bf16[2,2,2,16,16,128]{5,4,3,2,1,0:T(8,128)(2,1)S(1)} %get-tuple-element.27), channel_id=1, source_target_pairs={{0,124},{1,125},{2,126},{3,127},{4,8},{5,9},{6,10},{7,11},{8,4},{9... | collective-permute-start | bytes 1572872 | tf_op jit(solution)/shard_map/ppermute | solution.py:315
  16.4 27.4 %collective-permute-start.10 = (bf16[2,2,2,16,16,128]{5,4,3,2,1,0:T(8,128)(2,1)S(1)}, bf16[2,2,2,16,16,128]{5,4,3,2,1,0:T(8,128)(2,1)S(1)}, u32[]{:S(2)}, u32[]{:S(2)}) collective-permute-start(bf16[2,2,2,16,16,128]{5,4,3,2,1,0:T(8,128)(2,1)S(1)} %get-tuple-element.28), channel_id=1, source_target_pairs={{0,124},{1,125},{2,126},{3,127},{4,8},{5,9},{6,10},{7,11},{8,4},{9... | collective-permute-start | bytes 1572872 | tf_op jit(solution)/shard_map/ppermute | solution.py:315
  29.2 18.4 %collective-permute-start.9 = (bf16[2,2,2,16,16,128]{5,4,3,2,1,0:T(8,128)(2,1)S(1)}, bf16[2,2,2,16,16,128]{5,4,3,2,1,0:T(8,128)(2,1)S(1)}, u32[]{:S(2)}, u32[]{:S(2)}) collective-permute-start(bf16[2,2,2,16,16,128]{5,4,3,2,1,0:T(8,128)(2,1)S(1)} %collective-permute-done.8.refs_2_), channel_id=1, source_target_pairs={{0,128},{252,124},{1,129},{253,125},{2,130},{254,126},{3,131},{255... | collective-permute-start | bytes 1572872 | tf_op jit(solution)/shard_map/ppermute | solution.py:341
  31.9 24.7 %collective-permute-start.2 = (bf16[2,2,2,16,16,128]{5,4,3,2,1,0:T(8,128)(2,1)S(1)}, bf16[2,2,2,16,16,128]{5,4,3,2,1,0:T(8,128)(2,1)S(1)}, u32[]{:S(2)}, u32[]{:S(2)}) collective-permute-start(bf16[2,2,2,16,16,128]{5,4,3,2,1,0:T(8,128)(2,1)S(1)} %get-tuple-element.20), channel_id=1, source_target_pairs={{0,4},{1,5},{2,6},{3,7},{4,0},{5,1},{6,2},{7,3},{8,12},{9,13},{10,... | collective-permute-start | bytes 1572872 | tf_op jit(solution)/shard_map/ppermute | solution.py:315
  33.5 23.1 %collective-permute-start.3 = (bf16[2,2,2,16,16,128]{5,4,3,2,1,0:T(8,128)(2,1)S(1)}, bf16[2,2,2,16,16,128]{5,4,3,2,1,0:T(8,128)(2,1)S(1)}, u32[]{:S(2)}, u32[]{:S(2)}) collective-permute-start(bf16[2,2,2,16,16,128]{5,4,3,2,1,0:T(8,128)(2,1)S(1)} %get-tuple-element.21), channel_id=1, source_target_pairs={{0,0},{1,1},{2,2},{3,3},{4,8},{5,9},{6,10},{7,11},{8,4},{9,5},{10,... | collective-permute-start | bytes 1572872 | tf_op jit(solution)/shard_map/ppermute | solution.py:315
  43.8 18.8 %collective-permute-start.4 = (bf16[2,2,2,16,16,128]{5,4,3,2,1,0:T(8,128)(2,1)S(1)}, bf16[2,2,2,16,16,128]{5,4,3,2,1,0:T(8,128)(2,1)S(1)}, u32[]{:S(2)}, u32[]{:S(2)}) collective-permute-start(bf16[2,2,2,16,16,128]{5,4,3,2,1,0:T(8,128)(2,1)S(1)} %get-tuple-element.22), channel_id=1, source_target_pairs={{0,4},{1,5},{2,6},{3,7},{4,0},{5,1},{6,2},{7,3},{8,12},{9,13},{10,... | collective-permute-start | bytes 1572872 | tf_op jit(solution)/shard_map/ppermute | solution.py:315
  43.9 22.2 %collective-permute-start.5 = (bf16[2,2,2,16,16,128]{5,4,3,2,1,0:T(8,128)(2,1)S(1)}, bf16[2,2,2,16,16,128]{5,4,3,2,1,0:T(8,128)(2,1)S(1)}, u32[]{:S(2)}, u32[]{:S(2)}) collective-permute-start(bf16[2,2,2,16,16,128]{5,4,3,2,1,0:T(8,128)(2,1)S(1)} %get-tuple-element.23), channel_id=1, source_target_pairs={{0,0},{1,1},{2,2},{3,3},{4,8},{5,9},{6,10},{7,11},{8,4},{9,5},{10,... | collective-permute-start | bytes 1572872 | tf_op jit(solution)/shard_map/ppermute | solution.py:315
  47.6 18.6 %collective-permute-start.11 = (bf16[2,2,2,16,16,128]{5,4,3,2,1,0:T(8,128)(2,1)S(1)}, bf16[2,2,2,16,16,128]{5,4,3,2,1,0:T(8,128)(2,1)S(1)}, u32[]{:S(2)}, u32[]{:S(2)}) collective-permute-start(bf16[2,2,2,16,16,128]{5,4,3,2,1,0:T(8,128)(2,1)S(1)} %collective-permute-done.10.refs_3_), channel_id=1, source_target_pairs={{0,128},{252,124},{1,129},{253,125},{2,130},{254,126},{3,131},{255... | collective-permute-start | bytes 1572872 | tf_op jit(solution)/shard_map/ppermute | solution.py:388

commit v15 on v14

--- a/solution.py
+++ b/solution.py
@@ -348,8 +348,10 @@
             copies += [(False, 0, slot, at, out, slot), (True, 1, slot, at, out, slot)]
     near_a, near_b, far_a, far_b = pack(flags, (far_own, turned_own), copies, (half,) * 4)
     turned = (middle - 1, middle)
-    near_a, near_b = trade(near_a, side_a), trade(near_b, side_b, turned)
-    far_a, far_b = trade(far_a, side_a), trade(far_b, side_b, turned)
+    near_b = trade(near_b, side_b, turned)
+    near_a = trade(near_a, side_a)
+    far_b = trade(far_b, side_b, turned)
+    far_a = trade(far_a, side_a)
 
     near_at_a, near_at_b = (2 * cells, rest), (rest, 2 * cells)
     far_at_a, far_at_b = (2 * cells + NEAR, 0), (0, 2 * cells + NEAR)
@@ -391,13 +393,13 @@
     far_sums = summed(
         flags, (own, whole_a, near_over), ((True, plan, True, 2),), (FAR_BAND,), (), cells, 0, far_sums[0]
     )
-    plan = last_groups(0, 1, 2, None, None, False)
-    image = summed(flags, (far_own, near_a, near_b), ((None, plan, False, 2),), (NEAR_BAND,), near_sums, cells, 1)
-    plan = last_groups(0, 1, 2, 3, 4, True)
+    plan = last_groups(0, 2, 1, None, None, False)
+    image = summed(flags, (far_own, near_b, near_a), ((None, plan, False, 2),), (NEAR_BAND,), near_sums, cells, 1)
+    plan = last_groups(0, 2, 1, 4, 3, True)
     crossing = plan + first_groups(5, 6, None, None, 7, 8, 2, True)
     crossing = [entry for entry in crossing if entry[0] is not None or entry[5] < 2]
     crossing = [entry for entry in crossing if entry[-1] != (0,)]
-    blocks = (far_own, near_a, near_b, far_a, far_b, own, whole_a, near_over, far_over)
+    blocks = (far_own, near_b, near_a, far_b, far_a, own, whole_a, near_over, far_over)
     variants = ((False, plan, False, 2), (True, crossing, "half", 4))
     return summed(flags, blocks, variants, (FAR_BAND,), far_sums, cells, 2, image)
 

time: 74.1 us -> 75 us (1.012)
  waiting for transfers between devices: 18.3 us -> 19.2 us
    ppermute x7, waiting for transfers between devices: 16.3 us -> 17.3 us  [trade(): return lax.ppermute(value, ('slab', 'freq'), pairs)]
  transfers between devices with their start and end apart: 12 -> 12, of which waited for: 4 -> 6; matrix products, arithmetic and copies ran while one was open for 0% -> 0% of each run, Pallas kernels for 22% -> 22%
where the time goes in v15:
time: 75 us; the launch traced here: 74.9 us
  starting transfers between devices  29.6 us (39%)
  Pallas kernels  25.9 us (35%)
  waiting for transfers between devices  19.2 us (26%)
    ppermute x7, starting transfers between devices, trade(): return lax.ppermute(value, ('slab', 'freq'), pairs)  24 us
    pallas_call x5, Pallas kernels, summed(): pl.pallas_call(functools.partial(sum_kernel, variants, len(blocks), bands...  22 us
    ppermute x7, waiting for transfers between devices, trade(): return lax.ppermute(value, ('slab', 'freq'), pairs)  17.3 us
    ppermute x3, starting transfers between devices, swap(): return lax.ppermute(part, 'freq', [(g, g ^ d) for g in range(GROUPS)])  2.96 us
    pallas_call x3, Pallas kernels, pack(): pl.pallas_call(functools.partial(pack_kernel, copies, len(arrays)), in_sp...  2.24 us
    ppermute x3, waiting for transfers between devices, swap(): return lax.ppermute(part, 'freq', [(g, g ^ d) for g in range(GROUPS)])  1.94 us
    pallas_call x1, Pallas kernels, regrouped(): pl.pallas_call(regroup_kernel, in_specs=[pl.BlockSpec(memory_space=pltpu....  1.66 us
  transfers between devices with their start and end apart: 12, of which 6 were waited for; matrix products, arithmetic and copies ran while one was open for 0% of the time, Pallas kernels for 22%

profile of v15, /device:TPU:8, one launch (start us, length us, event | category | flops | bytes accessed | tf_op | source)
XLA Modules:
  0.0 74.9 jit_solution(14492768865390179790)
XLA Ops:
  0.0 1.7 %regroup.1 = (bf16[2,2,32,16,128]{4,3,2,1,0:T(8,128)(2,1)S(1)}, bf16[2,2,32,16,128]{4,3,2,1,0:T(8,128)(2,1)S(1)}, bf16[2,2,32,16,128]{4,3,2,1,0:T(8,128)(2,1)S(1)}, bf16[2,2,32,16,128]{4,3,2,1,0:T(8,128)(2,1)S(1)}) custom-call(s32[1]{0:T(128)} %bitcast.2.group_ref, bf16[2,2,32,16,256]{4,3,2,1,0:T(8,128)(2,1)} %source_ref.1, ...), custom_call_target="tpu_custom_call" | custom-call | bytes 4194304 | tf_op jit(solution)/shard_map/regroup/pallas_call | solution.py:65
  1.7 0.1 collective-permute-start
  1.8 0.5 collective-permute-start.6
  2.3 0.1 pad_add_fusion.refs_0_.flags_ref
  2.3 1.3 %collective-permute-done.refs_2_ = bf16[2,2,32,16,128]{4,3,2,1,0:T(8,128)(2,1)S(1)} collective-permute-done((bf16[2,2,32,16,128]{4,3,2,1,0:T(8,128)(2,1)S(1)}, bf16[2,2,32,16,128]{4,3,2,1,0:T(8,128)(2,1)S(1)}, u32[]{:S(2)}, u32[]{:S(2)}) %collective-permute-start) | collective-permute-done | bytes 524320 | tf_op jit(solution)/shard_map/ppermute | solution.py:308
  3.7 0.6 pack.3.refs_2_
  4.3 2.4 %collective-permute-start.1 = (bf16[2,2,2,32,16,128]{5,4,3,2,1,0:T(8,128)(2,1)S(1)}, bf16[2,2,2,32,16,128]{5,4,3,2,1,0:T(8,128)(2,1)S(1)}, u32[]{:S(2)}, u32[]{:S(2)}) collective-permute-start(bf16[2,2,2,32,16,128]{5,4,3,2,1,0:T(8,128)(2,1)S(1)} %pack.3.refs_2_), channel_id=1, source_target_pairs={{0,2},{1,3},{2,0},{3,1},{4,6},{5,7},{6,4},{7,5},{8,10},{9,11},{10,... | collective-permute-start | bytes 3145736 | tf_op jit(solution)/shard_map/ppermute | solution.py:308
  6.7 0.0 collective-permute-done.6.refs_2_
  6.7 0.8 %pack.5 = (bf16[2,2,2,32,16,128]{5,4,3,2,1,0:T(8,128)(2,1)S(1)}, bf16[2,2,2,16,16,128]{5,4,3,2,1,0:T(8,128)(2,1)S(1)}, bf16[2,2,2,16,16,128]{5,4,3,2,1,0:T(8,128)(2,1)S(1)}) custom-call(s32[2]{0:T(128)S(1)} %pad_add_fusion.refs_0_.flags_ref, bf16[2,2,32,16,128]{4,3,2,1,0:T(8,128)(2,1)S(1)} %get-tuple-element.24.refs_1_, ...), custom_call_target="tpu_custom_call" | custom-call | bytes 2097152 | tf_op jit(solution)/shard_map/pack/pallas_call | solution.py:107
  7.4 1.6 %collective-permute-start.7 = (bf16[2,2,2,32,16,128]{5,4,3,2,1,0:T(8,128)(2,1)S(1)}, bf16[2,2,2,32,16,128]{5,4,3,2,1,0:T(8,128)(2,1)S(1)}, u32[]{:S(2)}, u32[]{:S(2)}) collective-permute-start(bf16[2,2,2,32,16,128]{5,4,3,2,1,0:T(8,128)(2,1)S(1)} %get-tuple-element.26.refs_0_.refs_5_), channel_id=1, source_target_pairs={{0,4},{1,5},{2,6},{3,7},{4,0},{5,1},{6,2},{7,3},{8,12},{9,13},{10,... | collective-permute-start | bytes 3145736 | tf_op jit(solution)/shard_map/ppermute | solution.py:315
  9.0 7.4 %collective-permute-start.8 = (bf16[2,2,2,16,16,128]{5,4,3,2,1,0:T(8,128)(2,1)S(1)}, bf16[2,2,2,16,16,128]{5,4,3,2,1,0:T(8,128)(2,1)S(1)}, u32[]{:S(2)}, u32[]{:S(2)}) collective-permute-start(bf16[2,2,2,16,16,128]{5,4,3,2,1,0:T(8,128)(2,1)S(1)} %get-tuple-element.27), channel_id=1, source_target_pairs={{0,124},{1,125},{2,126},{3,127},{4,8},{5,9},{6,10},{7,11},{8,4},{9... | collective-permute-start | bytes 1572872 | tf_op jit(solution)/shard_map/ppermute | solution.py:315
  16.4 0.0 collective-permute-start.10
  16.4 12.8 %collective-permute-done.8.refs_2_ = bf16[2,2,2,16,16,128]{5,4,3,2,1,0:T(8,128)(2,1)S(1)} collective-permute-done((bf16[2,2,2,16,16,128]{5,4,3,2,1,0:T(8,128)(2,1)S(1)}, bf16[2,2,2,16,16,128]{5,4,3,2,1,0:T(8,128)(2,1)S(1)}, u32[]{:S(2)}, u32[]{:S(2)}) %collective-permute-start.8) | collective-permute-done | bytes 524320 | tf_op jit(solution)/shard_map/ppermute | solution.py:315
  29.2 1.3 %collective-permute-start.9 = (bf16[2,2,2,16,16,128]{5,4,3,2,1,0:T(8,128)(2,1)S(1)}, bf16[2,2,2,16,16,128]{5,4,3,2,1,0:T(8,128)(2,1)S(1)}, u32[]{:S(2)}, u32[]{:S(2)}) collective-permute-start(bf16[2,2,2,16,16,128]{5,4,3,2,1,0:T(8,128)(2,1)S(1)} %collective-permute-done.8.refs_2_), channel_id=1, source_target_pairs={{0,128},{252,124},{1,129},{253,125},{2,130},{254,126},{3,131},{255... | collective-permute-start | bytes 1572872 | tf_op jit(solution)/shard_map/ppermute | solution.py:341
  30.5 0.6 collective-permute-done.1.refs_1_.refs_0_
  31.1 0.8 %pack.4 = (bf16[2,2,2,16,16,128]{5,4,3,2,1,0:T(8,128)(2,1)S(1)}, bf16[2,2,2,16,16,128]{5,4,3,2,1,0:T(8,128)(2,1)S(1)}, bf16[2,2,2,16,16,128]{5,4,3,2,1,0:T(8,128)(2,1)S(1)}, bf16[2,2,2,16,16,128]{5,4,3,2,1,0:T(8,128)(2,1)S(1)}) custom-call(s32[2]{0:T(128)S(1)} %pad_add_fusion.refs_0_.flags_ref, ...), custom_call_target="tpu_custom_call" | custom-call | bytes 2097152 | tf_op jit(solution)/shard_map/pack/pallas_call | solution.py:107
  31.9 11.0 %collective-permute-start.2 = (bf16[2,2,2,16,16,128]{5,4,3,2,1,0:T(8,128)(2,1)S(1)}, bf16[2,2,2,16,16,128]{5,4,3,2,1,0:T(8,128)(2,1)S(1)}, u32[]{:S(2)}, u32[]{:S(2)}) collective-permute-start(bf16[2,2,2,16,16,128]{5,4,3,2,1,0:T(8,128)(2,1)S(1)} %get-tuple-element.20), channel_id=1, source_target_pairs={{0,0},{1,1},{2,2},{3,3},{4,8},{5,9},{6,10},{7,11},{8,4},{9,5},{10,... | collective-permute-start | bytes 1572872 | tf_op jit(solution)/shard_map/ppermute | solution.py:315
  42.9 0.1 collective-permute-start.3
  43.0 0.0 collective-permute-done.10.refs_3_
  43.0 3.2 %collective-permute-start.4 = (bf16[2,2,2,16,16,128]{5,4,3,2,1,0:T(8,128)(2,1)S(1)}, bf16[2,2,2,16,16,128]{5,4,3,2,1,0:T(8,128)(2,1)S(1)}, u32[]{:S(2)}, u32[]{:S(2)}) collective-permute-start(bf16[2,2,2,16,16,128]{5,4,3,2,1,0:T(8,128)(2,1)S(1)} %get-tuple-element.22), channel_id=1, source_target_pairs={{0,0},{1,1},{2,2},{3,3},{4,8},{5,9},{6,10},{7,11},{8,4},{9,5},{10,... | collective-permute-start | bytes 1572872 | tf_op jit(solution)/shard_map/ppermute | solution.py:315
  46.3 0.0 collective-permute-done.7.refs_1_.refs_6_
  46.3 0.8 %collective-permute-start.5 = (bf16[2,2,2,16,16,128]{5,4,3,2,1,0:T(8,128)(2,1)S(1)}, bf16[2,2,2,16,16,128]{5,4,3,2,1,0:T(8,128)(2,1)S(1)}, u32[]{:S(2)}, u32[]{:S(2)}) collective-permute-start(bf16[2,2,2,16,16,128]{5,4,3,2,1,0:T(8,128)(2,1)S(1)} %get-tuple-element.23), channel_id=1, source_target_pairs={{0,4},{1,5},{2,6},{3,7},{4,0},{5,1},{6,2},{7,3},{8,12},{9,13},{10,... | collective-permute-start | bytes 1572872 | tf_op jit(solution)/shard_map/ppermute | solution.py:315
  47.0 0.5 partial.3.refs_3_
  47.6 0.0 collective-permute-done.9.refs_2_.refs_3_.refs_7_
  47.6 1.3 %collective-permute-start.11 = (bf16[2,2,2,16,16,128]{5,4,3,2,1,0:T(8,128)(2,1)S(1)}, bf16[2,2,2,16,16,128]{5,4,3,2,1,0:T(8,128)(2,1)S(1)}, u32[]{:S(2)}, u32[]{:S(2)}) collective-permute-start(bf16[2,2,2,16,16,128]{5,4,3,2,1,0:T(8,128)(2,1)S(1)} %collective-permute-done.10.refs_3_), channel_id=1, source_target_pairs={{0,128},{252,124},{1,129},{253,125},{2,130},{254,126},{3,131},{255... | collective-permute-start | bytes 1572872 | tf_op jit(solution)/shard_map/ppermute | solution.py:390
  48.9 3.9 %partial.4.refs_9_ = f32[32,32,8,128]{3,2,1,0:T(8,128)S(1)} custom-call(s32[2]{0:T(128)S(1)} %pad_add_fusion.refs_0_.flags_ref, bf16[2,2,2,32,16,128]{5,4,3,2,1,0:T(8,128)(2,1)S(1)} %get-tuple-element.26.refs_0_.refs_5_, bf16[2,2,2,32,16,128]{5,4,3,2,1,0:T(8,128)(2,1)S(1)} %collective-permute-done.7.refs_1_.refs_6_, ...), custom_call_target="tpu_custom_call", output_to_operand_aliasing={{}: (4, {})} | custom-call | flops 16640000 | bytes 4160000 | tf_op jit(solution)/shard_map/partial/pallas_call | solution.py:281
  52.8 3.8 %partial.5.refs_3_ = f32[33,32,8,128]{3,2,1,0:T(8,128)S(1)} custom-call(s32[2]{0:T(128)S(1)} %pad_add_fusion.refs_0_.flags_ref, bf16[2,2,2,32,16,128]{5,4,3,2,1,0:T(8,128)(2,1)S(1)} %get-tuple-element.26.refs_0_.refs_5_, bf16[2,2,2,32,16,128]{5,4,3,2,1,0:T(8,128)(2,1)S(1)} %collective-permute-done.7.refs_1_.refs_6_, ...), custom_call_target="tpu_custom_call" | custom-call | flops 17160000 | bytes 4290000 | tf_op jit(solution)/shard_map/partial/pallas_call | solution.py:281
  56.7 0.0 collective-permute-done.2.refs_1_
  56.7 1.2 %collective-permute-done.3.refs_2_ = bf16[2,2,2,16,16,128]{5,4,3,2,1,0:T(8,128)(2,1)S(1)} collective-permute-done((bf16[2,2,2,16,16,128]{5,4,3,2,1,0:T(8,128)(2,1)S(1)}, bf16[2,2,2,16,16,128]{5,4,3,2,1,0:T(8,128)(2,1)S(1)}, u32[]{:S(2)}, u32[]{:S(2)}) %collective-permute-start.3) | collective-permute-done | bytes 524320 | tf_op jit(solution)/shard_map/ppermute | solution.py:315
  57.9 5.9 %image.2.refs_10_ = f32[4,65,32,256]{3,2,1,0:T(8,128)} custom-call(s32[2]{0:T(128)S(1)} %pad_add_fusion.refs_0_.flags_ref, bf16[2,2,2,32,16,128]{5,4,3,2,1,0:T(8,128)(2,1)S(1)} %collective-permute-done.1.refs_1_.refs_0_, bf16[2,2,2,16,16,128]{5,4,3,2,1,0:T(8,128)(2,1)S(1)} %collective-permute-done.2.refs_1_, ...), custom_call_target="tpu_custom_call" | custom-call | flops 17160000 | bytes 4290000 | tf_op jit(solution)/shard_map/image/pallas_call | solution.py:281
  63.8 1.7 %collective-permute-done.4.refs_3_ = bf16[2,2,2,16,16,128]{5,4,3,2,1,0:T(8,128)(2,1)S(1)} collective-permute-done((bf16[2,2,2,16,16,128]{5,4,3,2,1,0:T(8,128)(2,1)S(1)}, bf16[2,2,2,16,16,128]{5,4,3,2,1,0:T(8,128)(2,1)S(1)}, u32[]{:S(2)}, u32[]{:S(2)}) %collective-permute-start.4) | collective-permute-done | bytes 524320 | tf_op jit(solution)/shard_map/ppermute | solution.py:315
  65.5 1.6 %collective-permute-done.5.refs_4_ = bf16[2,2,2,16,16,128]{5,4,3,2,1,0:T(8,128)(2,1)S(1)} collective-permute-done((bf16[2,2,2,16,16,128]{5,4,3,2,1,0:T(8,128)(2,1)S(1)}, bf16[2,2,2,16,16,128]{5,4,3,2,1,0:T(8,128)(2,1)S(1)}, u32[]{:S(2)}, u32[]{:S(2)}) %collective-permute-start.5) | collective-permute-done | bytes 524320 | tf_op jit(solution)/shard_map/ppermute | solution.py:315
  67.1 0.0 collective-permute-done.11.refs_8_
  67.1 7.8 %image.3 = f32[4,65,32,256]{3,2,1,0:T(8,128)} custom-call(s32[2]{0:T(128)S(1)} %pad_add_fusion.refs_0_.flags_ref, bf16[2,2,2,32,16,128]{5,4,3,2,1,0:T(8,128)(2,1)S(1)} %collective-permute-done.1.refs_1_.refs_0_, bf16[2,2,2,16,16,128]{5,4,3,2,1,0:T(8,128)(2,1)S(1)} %collective-permute-done.2.refs_1_, ...), custom_call_target="tpu_custom_call", output_to_operand_aliasing={{}: (11, {})} | custom-call | flops 16640000 | bytes 4160000 | tf_op jit(solution)/shard_map/image/pallas_call | solution.py:281
Async XLA Ops:
  1.7 2.0 %collective-permute-start = (bf16[2,2,32,16,128]{4,3,2,1,0:T(8,128)(2,1)S(1)}, bf16[2,2,32,16,128]{4,3,2,1,0:T(8,128)(2,1)S(1)}, u32[]{:S(2)}, u32[]{:S(2)}) collective-permute-start(bf16[2,2,32,16,128]{4,3,2,1,0:T(8,128)(2,1)S(1)} %get-tuple-element.19), channel_id=1, source_target_pairs={{0,1},{1,0},{2,3},{3,2},{4,5},{5,4},{6,7},{7,6},{8,9},{9,8},{10,11... | collective-permute-start | bytes 1572872 | tf_op jit(solution)/shard_map/ppermute | solution.py:308
  1.8 4.9 %collective-permute-start.6 = (bf16[2,2,32,16,128]{4,3,2,1,0:T(8,128)(2,1)S(1)}, bf16[2,2,32,16,128]{4,3,2,1,0:T(8,128)(2,1)S(1)}, u32[]{:S(2)}, u32[]{:S(2)}) collective-permute-start(bf16[2,2,32,16,128]{4,3,2,1,0:T(8,128)(2,1)S(1)} %get-tuple-element.25), channel_id=1, source_target_pairs={{0,1},{1,0},{2,3},{3,2},{4,5},{5,4},{6,7},{7,6},{8,9},{9,8},{10,11... | collective-permute-start | bytes 1572872 | tf_op jit(solution)/shard_map/ppermute | solution.py:308
  4.3 26.8 %collective-permute-start.1 = (bf16[2,2,2,32,16,128]{5,4,3,2,1,0:T(8,128)(2,1)S(1)}, bf16[2,2,2,32,16,128]{5,4,3,2,1,0:T(8,128)(2,1)S(1)}, u32[]{:S(2)}, u32[]{:S(2)}) collective-permute-start(bf16[2,2,2,32,16,128]{5,4,3,2,1,0:T(8,128)(2,1)S(1)} %pack.3.refs_2_), channel_id=1, source_target_pairs={{0,2},{1,3},{2,0},{3,1},{4,6},{5,7},{6,4},{7,5},{8,10},{9,11},{10,... | collective-permute-start | bytes 3145736 | tf_op jit(solution)/shard_map/ppermute | solution.py:308
  7.4 38.8 %collective-permute-start.7 = (bf16[2,2,2,32,16,128]{5,4,3,2,1,0:T(8,128)(2,1)S(1)}, bf16[2,2,2,32,16,128]{5,4,3,2,1,0:T(8,128)(2,1)S(1)}, u32[]{:S(2)}, u32[]{:S(2)}) collective-permute-start(bf16[2,2,2,32,16,128]{5,4,3,2,1,0:T(8,128)(2,1)S(1)} %get-tuple-element.26.refs_0_.refs_5_), channel_id=1, source_target_pairs={{0,4},{1,5},{2,6},{3,7},{4,0},{5,1},{6,2},{7,3},{8,12},{9,13},{10,... | collective-permute-start | bytes 3145736 | tf_op jit(solution)/shard_map/ppermute | solution.py:315
  9.0 20.2 %collective-permute-start.8 = (bf16[2,2,2,16,16,128]{5,4,3,2,1,0:T(8,128)(2,1)S(1)}, bf16[2,2,2,16,16,128]{5,4,3,2,1,0:T(8,128)(2,1)S(1)}, u32[]{:S(2)}, u32[]{:S(2)}) collective-permute-start(bf16[2,2,2,16,16,128]{5,4,3,2,1,0:T(8,128)(2,1)S(1)} %get-tuple-element.27), channel_id=1, source_target_pairs={{0,124},{1,125},{2,126},{3,127},{4,8},{5,9},{6,10},{7,11},{8,4},{9... | collective-permute-start | bytes 1572872 | tf_op jit(solution)/shard_map/ppermute | solution.py:315
  16.4 26.6 %collective-permute-start.10 = (bf16[2,2,2,16,16,128]{5,4,3,2,1,0:T(8,128)(2,1)S(1)}, bf16[2,2,2,16,16,128]{5,4,3,2,1,0:T(8,128)(2,1)S(1)}, u32[]{:S(2)}, u32[]{:S(2)}) collective-permute-start(bf16[2,2,2,16,16,128]{5,4,3,2,1,0:T(8,128)(2,1)S(1)} %get-tuple-element.28), channel_id=1, source_target_pairs={{0,124},{1,125},{2,126},{3,127},{4,8},{5,9},{6,10},{7,11},{8,4},{9... | collective-permute-start | bytes 1572872 | tf_op jit(solution)/shard_map/ppermute | solution.py:315
  29.2 18.4 %collective-permute-start.9 = (bf16[2,2,2,16,16,128]{5,4,3,2,1,0:T(8,128)(2,1)S(1)}, bf16[2,2,2,16,16,128]{5,4,3,2,1,0:T(8,128)(2,1)S(1)}, u32[]{:S(2)}, u32[]{:S(2)}) collective-permute-start(bf16[2,2,2,16,16,128]{5,4,3,2,1,0:T(8,128)(2,1)S(1)} %collective-permute-done.8.refs_2_), channel_id=1, source_target_pairs={{0,128},{252,124},{1,129},{253,125},{2,130},{254,126},{3,131},{255... | collective-permute-start | bytes 1572872 | tf_op jit(solution)/shard_map/ppermute | solution.py:341
  31.9 24.7 %collective-permute-start.2 = (bf16[2,2,2,16,16,128]{5,4,3,2,1,0:T(8,128)(2,1)S(1)}, bf16[2,2,2,16,16,128]{5,4,3,2,1,0:T(8,128)(2,1)S(1)}, u32[]{:S(2)}, u32[]{:S(2)}) collective-permute-start(bf16[2,2,2,16,16,128]{5,4,3,2,1,0:T(8,128)(2,1)S(1)} %get-tuple-element.20), channel_id=1, source_target_pairs={{0,0},{1,1},{2,2},{3,3},{4,8},{5,9},{6,10},{7,11},{8,4},{9,5},{10,... | collective-permute-start | bytes 1572872 | tf_op jit(solution)/shard_map/ppermute | solution.py:315
  42.9 14.9 %collective-permute-start.3 = (bf16[2,2,2,16,16,128]{5,4,3,2,1,0:T(8,128)(2,1)S(1)}, bf16[2,2,2,16,16,128]{5,4,3,2,1,0:T(8,128)(2,1)S(1)}, u32[]{:S(2)}, u32[]{:S(2)}) collective-permute-start(bf16[2,2,2,16,16,128]{5,4,3,2,1,0:T(8,128)(2,1)S(1)} %get-tuple-element.21), channel_id=1, source_target_pairs={{0,4},{1,5},{2,6},{3,7},{4,0},{5,1},{6,2},{7,3},{8,12},{9,13},{10,... | collective-permute-start | bytes 1572872 | tf_op jit(solution)/shard_map/ppermute | solution.py:315
  43.0 22.5 %collective-permute-start.4 = (bf16[2,2,2,16,16,128]{5,4,3,2,1,0:T(8,128)(2,1)S(1)}, bf16[2,2,2,16,16,128]{5,4,3,2,1,0:T(8,128)(2,1)S(1)}, u32[]{:S(2)}, u32[]{:S(2)}) collective-permute-start(bf16[2,2,2,16,16,128]{5,4,3,2,1,0:T(8,128)(2,1)S(1)} %get-tuple-element.22), channel_id=1, source_target_pairs={{0,0},{1,1},{2,2},{3,3},{4,8},{5,9},{6,10},{7,11},{8,4},{9,5},{10,... | collective-permute-start | bytes 1572872 | tf_op jit(solution)/shard_map/ppermute | solution.py:315
  46.3 20.8 %collective-permute-start.5 = (bf16[2,2,2,16,16,128]{5,4,3,2,1,0:T(8,128)(2,1)S(1)}, bf16[2,2,2,16,16,128]{5,4,3,2,1,0:T(8,128)(2,1)S(1)}, u32[]{:S(2)}, u32[]{:S(2)}) collective-permute-start(bf16[2,2,2,16,16,128]{5,4,3,2,1,0:T(8,128)(2,1)S(1)} %get-tuple-element.23), channel_id=1, source_target_pairs={{0,4},{1,5},{2,6},{3,7},{4,0},{5,1},{6,2},{7,3},{8,12},{9,13},{10,... | collective-permute-start | bytes 1572872 | tf_op jit(solution)/shard_map/ppermute | solution.py:315
  47.6 19.5 %collective-permute-start.11 = (bf16[2,2,2,16,16,128]{5,4,3,2,1,0:T(8,128)(2,1)S(1)}, bf16[2,2,2,16,16,128]{5,4,3,2,1,0:T(8,128)(2,1)S(1)}, u32[]{:S(2)}, u32[]{:S(2)}) collective-permute-start(bf16[2,2,2,16,16,128]{5,4,3,2,1,0:T(8,128)(2,1)S(1)} %collective-permute-done.10.refs_3_), channel_id=1, source_target_pairs={{0,128},{252,124},{1,129},{253,125},{2,130},{254,126},{3,131},{255... | collective-permute-start | bytes 1572872 | tf_op jit(solution)/shard_map/ppermute | solution.py:390

commit v16 on v14

--- a/solution.py
+++ b/solution.py
@@ -348,7 +348,9 @@
             copies += [(False, 0, slot, at, out, slot), (True, 1, slot, at, out, slot)]
     near_a, near_b, far_a, far_b = pack(flags, (far_own, turned_own), copies, (half,) * 4)
     turned = (middle - 1, middle)
-    near_a, near_b = trade(near_a, side_a), trade(near_b, side_b, turned)
+    near_b = trade(near_b, side_b, turned)
+    near_a, whole_a = lax.optimization_barrier((near_a, whole_a))
+    near_a = trade(near_a, side_a)
     far_a, far_b = trade(far_a, side_a), trade(far_b, side_b, turned)
 
     near_at_a, near_at_b = (2 * cells, rest), (rest, 2 * cells)

time: 74.1 us -> 74.1 us (level)
  transfers between devices with their start and end apart: 12 -> 12, of which waited for: 4 -> 5; matrix products, arithmetic and copies ran while one was open for 0% -> 0% of each run, Pallas kernels for 22% -> 22%
where the time goes in v16:
time: 74.1 us; the launch traced here: 73.9 us
  starting transfers between devices  29.1 us (39%)
  Pallas kernels  25.9 us (35%)
  waiting for transfers between devices  18.8 us (25%)
    ppermute x7, starting transfers between devices, trade(): return lax.ppermute(value, ('slab', 'freq'), pairs)  23.5 us
    pallas_call x5, Pallas kernels, summed(): pl.pallas_call(functools.partial(sum_kernel, variants, len(blocks), bands...  22 us
    ppermute x7, waiting for transfers between devices, trade(): return lax.ppermute(value, ('slab', 'freq'), pairs)  16.8 us
    ppermute x3, starting transfers between devices, swap(): return lax.ppermute(part, 'freq', [(g, g ^ d) for g in range(GROUPS)])  2.96 us
    pallas_call x3, Pallas kernels, pack(): pl.pallas_call(functools.partial(pack_kernel, copies, len(arrays)), in_sp...  2.24 us
    ppermute x3, waiting for transfers between devices, swap(): return lax.ppermute(part, 'freq', [(g, g ^ d) for g in range(GROUPS)])  1.94 us
    pallas_call x1, Pallas kernels, regrouped(): pl.pallas_call(regroup_kernel, in_specs=[pl.BlockSpec(memory_space=pltpu....  1.66 us
  transfers between devices with their start and end apart: 12, of which 5 were waited for; matrix products, arithmetic and copies ran while one was open for 0% of the time, Pallas kernels for 22%

profile of v16, /device:TPU:8, one launch (start us, length us, event | category | flops | bytes accessed | tf_op | source)
XLA Modules:
  0.0 73.9 jit_solution(12229050291666642573)
XLA Ops:
  0.0 1.7 %regroup.1 = (bf16[2,2,32,16,128]{4,3,2,1,0:T(8,128)(2,1)S(1)}, bf16[2,2,32,16,128]{4,3,2,1,0:T(8,128)(2,1)S(1)}, bf16[2,2,32,16,128]{4,3,2,1,0:T(8,128)(2,1)S(1)}, bf16[2,2,32,16,128]{4,3,2,1,0:T(8,128)(2,1)S(1)}) custom-call(s32[1]{0:T(128)} %bitcast.2.group_ref, bf16[2,2,32,16,256]{4,3,2,1,0:T(8,128)(2,1)} %source_ref.1, ...), custom_call_target="tpu_custom_call" | custom-call | bytes 4194304 | tf_op jit(solution)/shard_map/regroup/pallas_call | solution.py:65
  1.7 0.1 collective-permute-start
  1.8 0.5 collective-permute-start.2
  2.3 0.1 pad_add_fusion.refs_0_.flags_ref
  2.3 1.3 %collective-permute-done.refs_2_ = bf16[2,2,32,16,128]{4,3,2,1,0:T(8,128)(2,1)S(1)} collective-permute-done((bf16[2,2,32,16,128]{4,3,2,1,0:T(8,128)(2,1)S(1)}, bf16[2,2,32,16,128]{4,3,2,1,0:T(8,128)(2,1)S(1)}, u32[]{:S(2)}, u32[]{:S(2)}) %collective-permute-start) | collective-permute-done | bytes 524320 | tf_op jit(solution)/shard_map/ppermute | solution.py:308
  3.7 0.6 pack.3.refs_2_
  4.3 2.4 %collective-permute-start.1 = (bf16[2,2,2,32,16,128]{5,4,3,2,1,0:T(8,128)(2,1)S(1)}, bf16[2,2,2,32,16,128]{5,4,3,2,1,0:T(8,128)(2,1)S(1)}, u32[]{:S(2)}, u32[]{:S(2)}) collective-permute-start(bf16[2,2,2,32,16,128]{5,4,3,2,1,0:T(8,128)(2,1)S(1)} %pack.3.refs_2_), channel_id=1, source_target_pairs={{0,2},{1,3},{2,0},{3,1},{4,6},{5,7},{6,4},{7,5},{8,10},{9,11},{10,... | collective-permute-start | bytes 3145736 | tf_op jit(solution)/shard_map/ppermute | solution.py:308
  6.7 0.0 collective-permute-done.2.refs_2_
  6.7 0.8 %pack.5 = (bf16[2,2,2,32,16,128]{5,4,3,2,1,0:T(8,128)(2,1)S(1)}, bf16[2,2,2,16,16,128]{5,4,3,2,1,0:T(8,128)(2,1)S(1)}, bf16[2,2,2,16,16,128]{5,4,3,2,1,0:T(8,128)(2,1)S(1)}) custom-call(s32[2]{0:T(128)S(1)} %pad_add_fusion.refs_0_.flags_ref, bf16[2,2,32,16,128]{4,3,2,1,0:T(8,128)(2,1)S(1)} %get-tuple-element.23.refs_1_, ...), custom_call_target="tpu_custom_call" | custom-call | bytes 2097152 | tf_op jit(solution)/shard_map/pack/pallas_call | solution.py:107
  7.4 1.6 %collective-permute-start.3 = (bf16[2,2,2,32,16,128]{5,4,3,2,1,0:T(8,128)(2,1)S(1)}, bf16[2,2,2,32,16,128]{5,4,3,2,1,0:T(8,128)(2,1)S(1)}, u32[]{:S(2)}, u32[]{:S(2)}) collective-permute-start(bf16[2,2,2,32,16,128]{5,4,3,2,1,0:T(8,128)(2,1)S(1)} %get-tuple-element.25.refs_0_.refs_5_), channel_id=1, source_target_pairs={{0,4},{1,5},{2,6},{3,7},{4,0},{5,1},{6,2},{7,3},{8,12},{9,13},{10,... | collective-permute-start | bytes 3145736 | tf_op jit(solution)/shard_map/ppermute | solution.py:315
  9.0 7.4 %collective-permute-start.8 = (bf16[2,2,2,16,16,128]{5,4,3,2,1,0:T(8,128)(2,1)S(1)}, bf16[2,2,2,16,16,128]{5,4,3,2,1,0:T(8,128)(2,1)S(1)}, u32[]{:S(2)}, u32[]{:S(2)}) collective-permute-start(bf16[2,2,2,16,16,128]{5,4,3,2,1,0:T(8,128)(2,1)S(1)} %get-tuple-element.31), channel_id=1, source_target_pairs={{0,124},{1,125},{2,126},{3,127},{4,8},{5,9},{6,10},{7,11},{8,4},{9... | collective-permute-start | bytes 1572872 | tf_op jit(solution)/shard_map/ppermute | solution.py:315
  16.4 0.0 collective-permute-start.10
  16.4 12.8 %collective-permute-done.8.refs_2_ = bf16[2,2,2,16,16,128]{5,4,3,2,1,0:T(8,128)(2,1)S(1)} collective-permute-done((bf16[2,2,2,16,16,128]{5,4,3,2,1,0:T(8,128)(2,1)S(1)}, bf16[2,2,2,16,16,128]{5,4,3,2,1,0:T(8,128)(2,1)S(1)}, u32[]{:S(2)}, u32[]{:S(2)}) %collective-permute-start.8) | collective-permute-done | bytes 524320 | tf_op jit(solution)/shard_map/ppermute | solution.py:315
  29.2 1.3 %collective-permute-start.9 = (bf16[2,2,2,16,16,128]{5,4,3,2,1,0:T(8,128)(2,1)S(1)}, bf16[2,2,2,16,16,128]{5,4,3,2,1,0:T(8,128)(2,1)S(1)}, u32[]{:S(2)}, u32[]{:S(2)}) collective-permute-start(bf16[2,2,2,16,16,128]{5,4,3,2,1,0:T(8,128)(2,1)S(1)} %collective-permute-done.8.refs_2_), channel_id=1, source_target_pairs={{0,128},{252,124},{1,129},{253,125},{2,130},{254,126},{3,131},{255... | collective-permute-start | bytes 1572872 | tf_op jit(solution)/shard_map/ppermute | solution.py:341
  30.5 0.6 collective-permute-done.1.refs_1_.refs_0_
  31.1 0.8 %pack.4 = (bf16[2,2,2,16,16,128]{5,4,3,2,1,0:T(8,128)(2,1)S(1)}, bf16[2,2,2,16,16,128]{5,4,3,2,1,0:T(8,128)(2,1)S(1)}, bf16[2,2,2,16,16,128]{5,4,3,2,1,0:T(8,128)(2,1)S(1)}, bf16[2,2,2,16,16,128]{5,4,3,2,1,0:T(8,128)(2,1)S(1)}) custom-call(s32[2]{0:T(128)S(1)} %pad_add_fusion.refs_0_.flags_ref, ...), custom_call_target="tpu_custom_call" | custom-call | bytes 2097152 | tf_op jit(solution)/shard_map/pack/pallas_call | solution.py:107
  31.9 0.5 collective-permute-done.3.refs_1_.refs_6_
  32.5 1.5 %collective-permute-start.4 = (bf16[2,2,2,16,16,128]{5,4,3,2,1,0:T(8,128)(2,1)S(1)}, bf16[2,2,2,16,16,128]{5,4,3,2,1,0:T(8,128)(2,1)S(1)}, u32[]{:S(2)}, u32[]{:S(2)}) collective-permute-start(bf16[2,2,2,16,16,128]{5,4,3,2,1,0:T(8,128)(2,1)S(1)} %get-tuple-element.26), channel_id=1, source_target_pairs={{0,4},{1,5},{2,6},{3,7},{4,0},{5,1},{6,2},{7,3},{8,12},{9,13},{10,... | collective-permute-start | bytes 1572872 | tf_op jit(solution)/shard_map/ppermute | solution.py:315
  33.9 9.9 %collective-permute-start.5 = (bf16[2,2,2,16,16,128]{5,4,3,2,1,0:T(8,128)(2,1)S(1)}, bf16[2,2,2,16,16,128]{5,4,3,2,1,0:T(8,128)(2,1)S(1)}, u32[]{:S(2)}, u32[]{:S(2)}) collective-permute-start(bf16[2,2,2,16,16,128]{5,4,3,2,1,0:T(8,128)(2,1)S(1)} %get-tuple-element.27), channel_id=1, source_target_pairs={{0,0},{1,1},{2,2},{3,3},{4,8},{5,9},{6,10},{7,11},{8,4},{9,5},{10,... | collective-permute-start | bytes 1572872 | tf_op jit(solution)/shard_map/ppermute | solution.py:315
  43.8 0.1 collective-permute-start.6
  43.9 0.0 collective-permute-done.10.refs_3_
  43.9 3.1 %collective-permute-start.7 = (bf16[2,2,2,16,16,128]{5,4,3,2,1,0:T(8,128)(2,1)S(1)}, bf16[2,2,2,16,16,128]{5,4,3,2,1,0:T(8,128)(2,1)S(1)}, u32[]{:S(2)}, u32[]{:S(2)}) collective-permute-start(bf16[2,2,2,16,16,128]{5,4,3,2,1,0:T(8,128)(2,1)S(1)} %get-tuple-element.29), channel_id=1, source_target_pairs={{0,0},{1,1},{2,2},{3,3},{4,8},{5,9},{6,10},{7,11},{8,4},{9,5},{10,... | collective-permute-start | bytes 1572872 | tf_op jit(solution)/shard_map/ppermute | solution.py:315
  47.0 0.6 partial.3.refs_3_
  47.6 0.0 collective-permute-done.9.refs_2_.refs_3_.refs_7_
  47.6 1.3 %collective-permute-start.11 = (bf16[2,2,2,16,16,128]{5,4,3,2,1,0:T(8,128)(2,1)S(1)}, bf16[2,2,2,16,16,128]{5,4,3,2,1,0:T(8,128)(2,1)S(1)}, u32[]{:S(2)}, u32[]{:S(2)}) collective-permute-start(bf16[2,2,2,16,16,128]{5,4,3,2,1,0:T(8,128)(2,1)S(1)} %collective-permute-done.10.refs_3_), channel_id=1, source_target_pairs={{0,128},{252,124},{1,129},{253,125},{2,130},{254,126},{3,131},{255... | collective-permute-start | bytes 1572872 | tf_op jit(solution)/shard_map/ppermute | solution.py:390
  48.9 3.9 %partial.4.refs_9_ = f32[32,32,8,128]{3,2,1,0:T(8,128)S(1)} custom-call(s32[2]{0:T(128)S(1)} %pad_add_fusion.refs_0_.flags_ref, bf16[2,2,2,32,16,128]{5,4,3,2,1,0:T(8,128)(2,1)S(1)} %get-tuple-element.25.refs_0_.refs_5_, bf16[2,2,2,32,16,128]{5,4,3,2,1,0:T(8,128)(2,1)S(1)} %collective-permute-done.3.refs_1_.refs_6_, ...), custom_call_target="tpu_custom_call", output_to_operand_aliasing={{}: (4, {})} | custom-call | flops 16640000 | bytes 4160000 | tf_op jit(solution)/shard_map/partial/pallas_call | solution.py:281
  52.8 3.8 %partial.5.refs_3_ = f32[33,32,8,128]{3,2,1,0:T(8,128)S(1)} custom-call(s32[2]{0:T(128)S(1)} %pad_add_fusion.refs_0_.flags_ref, bf16[2,2,2,32,16,128]{5,4,3,2,1,0:T(8,128)(2,1)S(1)} %get-tuple-element.25.refs_0_.refs_5_, bf16[2,2,2,32,16,128]{5,4,3,2,1,0:T(8,128)(2,1)S(1)} %collective-permute-done.3.refs_1_.refs_6_, ...), custom_call_target="tpu_custom_call" | custom-call | flops 17160000 | bytes 4290000 | tf_op jit(solution)/shard_map/partial/pallas_call | solution.py:281
  56.7 0.0 collective-permute-done.4.refs_1_
  56.7 0.0 collective-permute-done.5.refs_2_
  56.7 5.9 %image.2.refs_10_ = f32[4,65,32,256]{3,2,1,0:T(8,128)} custom-call(s32[2]{0:T(128)S(1)} %pad_add_fusion.refs_0_.flags_ref, bf16[2,2,2,32,16,128]{5,4,3,2,1,0:T(8,128)(2,1)S(1)} %collective-permute-done.1.refs_1_.refs_0_, bf16[2,2,2,16,16,128]{5,4,3,2,1,0:T(8,128)(2,1)S(1)} %collective-permute-done.4.refs_1_, ...), custom_call_target="tpu_custom_call" | custom-call | flops 17160000 | bytes 4290000 | tf_op jit(solution)/shard_map/image/pallas_call | solution.py:281
  62.6 0.0 collective-permute-done.6.refs_3_
  62.6 3.6 %collective-permute-done.7.refs_4_ = bf16[2,2,2,16,16,128]{5,4,3,2,1,0:T(8,128)(2,1)S(1)} collective-permute-done((bf16[2,2,2,16,16,128]{5,4,3,2,1,0:T(8,128)(2,1)S(1)}, bf16[2,2,2,16,16,128]{5,4,3,2,1,0:T(8,128)(2,1)S(1)}, u32[]{:S(2)}, u32[]{:S(2)}) %collective-permute-start.7) | collective-permute-done | bytes 524320 | tf_op jit(solution)/shard_map/ppermute | solution.py:315
  66.2 0.0 collective-permute-done.11.refs_8_
  66.2 7.8 %image.3 = f32[4,65,32,256]{3,2,1,0:T(8,128)} custom-call(s32[2]{0:T(128)S(1)} %pad_add_fusion.refs_0_.flags_ref, bf16[2,2,2,32,16,128]{5,4,3,2,1,0:T(8,128)(2,1)S(1)} %collective-permute-done.1.refs_1_.refs_0_, bf16[2,2,2,16,16,128]{5,4,3,2,1,0:T(8,128)(2,1)S(1)} %collective-permute-done.4.refs_1_, ...), custom_call_target="tpu_custom_call", output_to_operand_aliasing={{}: (11, {})} | custom-call | flops 16640000 | bytes 4160000 | tf_op jit(solution)/shard_map/image/pallas_call | solution.py:281
Async XLA Ops:
  1.7 2.0 %collective-permute-start = (bf16[2,2,32,16,128]{4,3,2,1,0:T(8,128)(2,1)S(1)}, bf16[2,2,32,16,128]{4,3,2,1,0:T(8,128)(2,1)S(1)}, u32[]{:S(2)}, u32[]{:S(2)}) collective-permute-start(bf16[2,2,32,16,128]{4,3,2,1,0:T(8,128)(2,1)S(1)} %get-tuple-element.21), channel_id=1, source_target_pairs={{0,1},{1,0},{2,3},{3,2},{4,5},{5,4},{6,7},{7,6},{8,9},{9,8},{10,11... | collective-permute-start | bytes 1572872 | tf_op jit(solution)/shard_map/ppermute | solution.py:308
  1.8 4.9 %collective-permute-start.2 = (bf16[2,2,32,16,128]{4,3,2,1,0:T(8,128)(2,1)S(1)}, bf16[2,2,32,16,128]{4,3,2,1,0:T(8,128)(2,1)S(1)}, u32[]{:S(2)}, u32[]{:S(2)}) collective-permute-start(bf16[2,2,32,16,128]{4,3,2,1,0:T(8,128)(2,1)S(1)} %get-tuple-element.24), channel_id=1, source_target_pairs={{0,1},{1,0},{2,3},{3,2},{4,5},{5,4},{6,7},{7,6},{8,9},{9,8},{10,11... | collective-permute-start | bytes 1572872 | tf_op jit(solution)/shard_map/ppermute | solution.py:308
  4.3 26.8 %collective-permute-start.1 = (bf16[2,2,2,32,16,128]{5,4,3,2,1,0:T(8,128)(2,1)S(1)}, bf16[2,2,2,32,16,128]{5,4,3,2,1,0:T(8,128)(2,1)S(1)}, u32[]{:S(2)}, u32[]{:S(2)}) collective-permute-start(bf16[2,2,2,32,16,128]{5,4,3,2,1,0:T(8,128)(2,1)S(1)} %pack.3.refs_2_), channel_id=1, source_target_pairs={{0,2},{1,3},{2,0},{3,1},{4,6},{5,7},{6,4},{7,5},{8,10},{9,11},{10,... | collective-permute-start | bytes 3145736 | tf_op jit(solution)/shard_map/ppermute | solution.py:308
  7.4 25.0 %collective-permute-start.3 = (bf16[2,2,2,32,16,128]{5,4,3,2,1,0:T(8,128)(2,1)S(1)}, bf16[2,2,2,32,16,128]{5,4,3,2,1,0:T(8,128)(2,1)S(1)}, u32[]{:S(2)}, u32[]{:S(2)}) collective-permute-start(bf16[2,2,2,32,16,128]{5,4,3,2,1,0:T(8,128)(2,1)S(1)} %get-tuple-element.25.refs_0_.refs_5_), channel_id=1, source_target_pairs={{0,4},{1,5},{2,6},{3,7},{4,0},{5,1},{6,2},{7,3},{8,12},{9,13},{10,... | collective-permute-start | bytes 3145736 | tf_op jit(solution)/shard_map/ppermute | solution.py:315
  9.0 20.2 %collective-permute-start.8 = (bf16[2,2,2,16,16,128]{5,4,3,2,1,0:T(8,128)(2,1)S(1)}, bf16[2,2,2,16,16,128]{5,4,3,2,1,0:T(8,128)(2,1)S(1)}, u32[]{:S(2)}, u32[]{:S(2)}) collective-permute-start(bf16[2,2,2,16,16,128]{5,4,3,2,1,0:T(8,128)(2,1)S(1)} %get-tuple-element.31), channel_id=1, source_target_pairs={{0,124},{1,125},{2,126},{3,127},{4,8},{5,9},{6,10},{7,11},{8,4},{9... | collective-permute-start | bytes 1572872 | tf_op jit(solution)/shard_map/ppermute | solution.py:315
  16.4 27.5 %collective-permute-start.10 = (bf16[2,2,2,16,16,128]{5,4,3,2,1,0:T(8,128)(2,1)S(1)}, bf16[2,2,2,16,16,128]{5,4,3,2,1,0:T(8,128)(2,1)S(1)}, u32[]{:S(2)}, u32[]{:S(2)}) collective-permute-start(bf16[2,2,2,16,16,128]{5,4,3,2,1,0:T(8,128)(2,1)S(1)} %get-tuple-element.32), channel_id=1, source_target_pairs={{0,124},{1,125},{2,126},{3,127},{4,8},{5,9},{6,10},{7,11},{8,4},{9... | collective-permute-start | bytes 1572872 | tf_op jit(solution)/shard_map/ppermute | solution.py:315
  29.2 18.4 %collective-permute-start.9 = (bf16[2,2,2,16,16,128]{5,4,3,2,1,0:T(8,128)(2,1)S(1)}, bf16[2,2,2,16,16,128]{5,4,3,2,1,0:T(8,128)(2,1)S(1)}, u32[]{:S(2)}, u32[]{:S(2)}) collective-permute-start(bf16[2,2,2,16,16,128]{5,4,3,2,1,0:T(8,128)(2,1)S(1)} %collective-permute-done.8.refs_2_), channel_id=1, source_target_pairs={{0,128},{252,124},{1,129},{253,125},{2,130},{254,126},{3,131},{255... | collective-permute-start | bytes 1572872 | tf_op jit(solution)/shard_map/ppermute | solution.py:341
  32.5 24.2 %collective-permute-start.4 = (bf16[2,2,2,16,16,128]{5,4,3,2,1,0:T(8,128)(2,1)S(1)}, bf16[2,2,2,16,16,128]{5,4,3,2,1,0:T(8,128)(2,1)S(1)}, u32[]{:S(2)}, u32[]{:S(2)}) collective-permute-start(bf16[2,2,2,16,16,128]{5,4,3,2,1,0:T(8,128)(2,1)S(1)} %get-tuple-element.26), channel_id=1, source_target_pairs={{0,4},{1,5},{2,6},{3,7},{4,0},{5,1},{6,2},{7,3},{8,12},{9,13},{10,... | collective-permute-start | bytes 1572872 | tf_op jit(solution)/shard_map/ppermute | solution.py:315
  33.9 22.7 %collective-permute-start.5 = (bf16[2,2,2,16,16,128]{5,4,3,2,1,0:T(8,128)(2,1)S(1)}, bf16[2,2,2,16,16,128]{5,4,3,2,1,0:T(8,128)(2,1)S(1)}, u32[]{:S(2)}, u32[]{:S(2)}) collective-permute-start(bf16[2,2,2,16,16,128]{5,4,3,2,1,0:T(8,128)(2,1)S(1)} %get-tuple-element.27), channel_id=1, source_target_pairs={{0,0},{1,1},{2,2},{3,3},{4,8},{5,9},{6,10},{7,11},{8,4},{9,5},{10,... | collective-permute-start | bytes 1572872 | tf_op jit(solution)/shard_map/ppermute | solution.py:315
  43.8 18.8 %collective-permute-start.6 = (bf16[2,2,2,16,16,128]{5,4,3,2,1,0:T(8,128)(2,1)S(1)}, bf16[2,2,2,16,16,128]{5,4,3,2,1,0:T(8,128)(2,1)S(1)}, u32[]{:S(2)}, u32[]{:S(2)}) collective-permute-start(bf16[2,2,2,16,16,128]{5,4,3,2,1,0:T(8,128)(2,1)S(1)} %get-tuple-element.28), channel_id=1, source_target_pairs={{0,4},{1,5},{2,6},{3,7},{4,0},{5,1},{6,2},{7,3},{8,12},{9,13},{10,... | collective-permute-start | bytes 1572872 | tf_op jit(solution)/shard_map/ppermute | solution.py:315
  43.9 22.2 %collective-permute-start.7 = (bf16[2,2,2,16,16,128]{5,4,3,2,1,0:T(8,128)(2,1)S(1)}, bf16[2,2,2,16,16,128]{5,4,3,2,1,0:T(8,128)(2,1)S(1)}, u32[]{:S(2)}, u32[]{:S(2)}) collective-permute-start(bf16[2,2,2,16,16,128]{5,4,3,2,1,0:T(8,128)(2,1)S(1)} %get-tuple-element.29), channel_id=1, source_target_pairs={{0,0},{1,1},{2,2},{3,3},{4,8},{5,9},{6,10},{7,11},{8,4},{9,5},{10,... | collective-permute-start | bytes 1572872 | tf_op jit(solution)/shard_map/ppermute | solution.py:315
  47.6 18.6 %collective-permute-start.11 = (bf16[2,2,2,16,16,128]{5,4,3,2,1,0:T(8,128)(2,1)S(1)}, bf16[2,2,2,16,16,128]{5,4,3,2,1,0:T(8,128)(2,1)S(1)}, u32[]{:S(2)}, u32[]{:S(2)}) collective-permute-start(bf16[2,2,2,16,16,128]{5,4,3,2,1,0:T(8,128)(2,1)S(1)} %collective-permute-done.10.refs_3_), channel_id=1, source_target_pairs={{0,128},{252,124},{1,129},{253,125},{2,130},{254,126},{3,131},{255... | collective-permute-start | bytes 1572872 | tf_op jit(solution)/shard_map/ppermute | solution.py:390
